TPU v7x, 32 devices: a whole 2x2x4 slice. The times are simulated.
32 devices in a mesh: grp: 2 (over y), pas: 4 (over x, core), fsdp: 4 (over z).
Axes of the slice: x: 2, y: 2, z: 4, core: 2. Of those that a mesh axis runs over, the one named last changes fastest.
Arguments:
- passages: bfloat16 [32, 128, 4096], P(('grp', 'pas'), None, 'fsdp'), parts along dimension 0, may hold values from -3 to 3
- cotangent: bfloat16 [32, 128, 4096], P(('grp', 'pas'), None, 'fsdp'), parts along dimension 0, may hold values from -6 to 6
- passage_counts: int32 [8], P(('grp', 'pas')), parts along dimension 0, may hold values from 1 to 4, 8 in all
- norm_gain: float32 [4096], replicated, may hold values from 0.1 to 1.9
- w_query: bfloat16 [4096, 4096], P('pas', 'fsdp'), may hold values from -0.25 to 0.25
- w_key: bfloat16 [4096, 4096], P('pas', 'fsdp')
- w_value: bfloat16 [4096, 4096], P('pas', 'fsdp'), may hold values from -0.09375 to 0.09375
- w_out: bfloat16 [4096, 4096], P('fsdp', 'pas'), may hold values from -0.29882812 to 0.29882812
Outputs:
- encoded: bfloat16 [32, 128, 4096], P(('grp', 'pas'), None, 'fsdp'), parts along dimension 0
- input_grad: bfloat16 [32, 128, 4096], P(('grp', 'pas'), None, 'fsdp'), parts along dimension 0
- gain_grad: float32 [8192], P(('grp', 'fsdp')), parts along dimension 0
There are 2 independent parts, one for each index of `grp`. A program takes and returns all parts, laid end to end along the dimension named above; an argument that names none is the same for every part. Nothing has to cross between parts.
Inputs may be any that keep to these rules, and one draw needn't show every extreme that they name: `passage_counts`: counts are 1 or more; the 4 counts of a group sum to 8, and one of them equals 4.
All inputs are finite; a program needn't handle non-finite values.
Results may differ from a plain program's by a relative error of at most 0.012.
Values may be sent and summed in bfloat16 or wider, within the bound.
No kernel may reach another device: no remote copies, remote signals or barrier semaphores. Data moves between devices by JAX's collectives and lax.ppermute only.
A program may use at most 128 MiB of HBM per device.

v0:
```python
import jax
import jax.numpy as jnp
from jax import lax
from jax.sharding import PartitionSpec as P

HD = 64
BAL = 2


EPSILON = 1e-06


def entering(shard, axis, combine, identity):
    length, position = (lax.axis_size(axis), lax.axis_index(axis))
    everything = lax.all_gather(shard, axis)
    start = jnp.broadcast_to(jnp.asarray(identity, shard.dtype), shard.shape)

    def lap(k, before):
        reached = k < position
        new = combine(before, everything[k])
        return jnp.where(reached, new, before)

    return lax.fori_loop(0, length, lap, start)


def add_counts(earlier, later):
    return earlier + later


def body(passages, cotangent, passage_counts, norm_gain, w_query, w_key, w_value, w_out):
    peer_total = lax.axis_size("pas")
    slots, seq_len, part_width = passages.shape
    flat_width = seq_len * part_width
    own_count = passage_counts[0]
    first_rank = entering(passage_counts, "pas", add_counts, jnp.zeros_like(passage_counts))[0]
    slot_index = jnp.arange(slots, dtype=jnp.int32)
    slot_rank = first_rank + slot_index
    is_live = slot_index < own_count
    peer_index = jnp.arange(peer_total, dtype=jnp.int32)
    routing_mask = is_live[None, :] & ((slot_rank % peer_total)[None, :] == peer_index[:, None])
    routing = routing_mask.astype(jnp.bfloat16)
    sent_rank = jnp.max(jnp.where(routing_mask, slot_rank[None, :], -1), axis=1).astype(jnp.int32)
    send_tokens = jnp.dot(
        routing, passages.reshape(slots, flat_width), preferred_element_type=jnp.float32
    ).astype(jnp.bfloat16)
    send_grads = jnp.dot(
        routing, cotangent.reshape(slots, flat_width), preferred_element_type=jnp.float32
    ).astype(jnp.bfloat16)
    got_tokens, got_grads, got_rank = (
        lax.all_to_all(send_tokens, "pas", split_axis=0, concat_axis=0, tiled=True),
        lax.all_to_all(send_grads, "pas", split_axis=0, concat_axis=0, tiled=True),
        lax.all_to_all(sent_rank, "pas", split_axis=0, concat_axis=0, tiled=True),
    )
    picked_mask = (got_rank[None, :] >= 0) & (
        got_rank[None, :] // peer_total == jnp.arange(BAL, dtype=jnp.int32)[:, None]
    )
    picked = picked_mask.astype(jnp.bfloat16)
    returned = jnp.transpose(picked)
    local_tokens = (
        jnp.dot(picked, got_tokens, preferred_element_type=jnp.float32)
        .astype(jnp.bfloat16)
        .reshape(BAL, seq_len, part_width)
    )
    local_grads = (
        jnp.dot(picked, got_grads, preferred_element_type=jnp.float32)
        .astype(jnp.bfloat16)
        .reshape(BAL, seq_len, part_width)
    )
    query_w, key_w, value_w, out_w = (
        lax.all_gather(w_query, "pas", axis=0, tiled=True),
        lax.all_gather(w_key, "pas", axis=0, tiled=True),
        lax.all_gather(w_value, "pas", axis=0, tiled=True),
        lax.all_gather(w_out, "pas", axis=1, tiled=True),
    )
    full_tokens = lax.all_gather(local_tokens, "fsdp", axis=2, tiled=True)
    width = full_tokens.shape[2]
    feature_start = lax.axis_index("fsdp") * part_width
    full_f32 = full_tokens.astype(jnp.float32)
    inverse = lax.rsqrt(jnp.mean(full_f32 * full_f32, axis=-1, keepdims=True) + EPSILON)
    unit_rows = full_f32 * inverse
    normed = (unit_rows * norm_gain).astype(jnp.bfloat16)
    local_cols = query_w.shape[1]
    head_count = local_cols // HD
    flat_rows = normed.reshape(BAL * seq_len, width)

    def project(weight):
        result = jnp.dot(flat_rows, weight, preferred_element_type=jnp.float32).astype(jnp.bfloat16)
        return result.reshape(BAL, seq_len, head_count, HD)

    query = project(query_w)
    keys = project(key_w)
    values = project(value_w)
    scores = jnp.einsum("blhe,bmhe->bhlm", query, keys, preferred_element_type=jnp.float32)
    probs = jax.nn.softmax(scores, axis=-1)
    probs_low = probs.astype(jnp.bfloat16)
    context = jnp.einsum(
        "bhlm,bmhe->blhe", probs_low, values, preferred_element_type=jnp.float32
    ).astype(jnp.bfloat16)
    context_rows = context.reshape(BAL * seq_len, local_cols)
    partial_out = jnp.dot(context_rows, out_w, preferred_element_type=jnp.float32).reshape(
        BAL, seq_len, width
    )
    attention = lax.psum_scatter(
        partial_out.astype(jnp.bfloat16), "fsdp", scatter_dimension=2, tiled=True
    ).astype(jnp.float32)
    states = (local_tokens.astype(jnp.float32) + attention).astype(jnp.bfloat16)
    states_back = jnp.dot(
        returned, states.reshape(BAL, flat_width), preferred_element_type=jnp.float32
    ).astype(jnp.bfloat16)
    states_home = lax.all_to_all(states_back, "pas", split_axis=0, concat_axis=0, tiled=True)
    upstream_rows = lax.all_gather(local_grads, "fsdp", axis=2, tiled=True).reshape(
        BAL * seq_len, width
    )
    d_context = jnp.einsum(
        "td,cd->tc", upstream_rows, out_w, preferred_element_type=jnp.float32
    ).astype(jnp.bfloat16)
    d_context = d_context.reshape(BAL, seq_len, head_count, HD)
    d_values = jnp.einsum(
        "bhlm,blhe->bmhe", probs_low, d_context, preferred_element_type=jnp.float32
    ).astype(jnp.bfloat16)
    d_probs = jnp.einsum("blhe,bmhe->bhlm", d_context, values, preferred_element_type=jnp.float32)
    d_scores = (probs * (d_probs - jnp.sum(d_probs * probs, axis=-1, keepdims=True))).astype(
        jnp.bfloat16
    )
    d_query = jnp.einsum(
        "bhlm,bmhe->blhe", d_scores, keys, preferred_element_type=jnp.float32
    ).astype(jnp.bfloat16)
    d_keys = jnp.einsum(
        "bhlm,blhe->bmhe", d_scores, query, preferred_element_type=jnp.float32
    ).astype(jnp.bfloat16)

    def back_project(grad, weight):
        grad_rows = grad.reshape(BAL * seq_len, local_cols)
        return jnp.einsum("tc,dc->td", grad_rows, weight, preferred_element_type=jnp.float32)

    d_normed = (
        back_project(d_query, query_w)
        + back_project(d_keys, key_w)
        + back_project(d_values, value_w)
    )
    d_normed_part = lax.psum_scatter(
        d_normed.reshape(BAL, seq_len, width).astype(jnp.bfloat16),
        "fsdp",
        scatter_dimension=2,
        tiled=True,
    ).astype(jnp.float32)
    unit_part = lax.dynamic_slice_in_dim(unit_rows, feature_start, part_width, 2)
    gain_part = lax.dynamic_slice_in_dim(norm_gain, feature_start, part_width, 0)
    d_unit = d_normed_part * gain_part
    row_total = lax.psum(jnp.sum(d_unit * unit_part, axis=-1, keepdims=True), "fsdp")
    row_mean = row_total / width
    d_tokens = inverse * (d_unit - unit_part * row_mean)
    grads_local = (local_grads.astype(jnp.float32) + d_tokens).astype(jnp.bfloat16)
    gain_grad = lax.psum(jnp.sum(d_normed_part * unit_part, axis=(0, 1)), "pas")
    grads_back = jnp.dot(
        returned, grads_local.reshape(BAL, flat_width), preferred_element_type=jnp.float32
    ).astype(jnp.bfloat16)
    grads_home = lax.all_to_all(grads_back, "pas", split_axis=0, concat_axis=0, tiled=True)
    routing_back = jnp.transpose(routing)
    encoded = (
        jnp.dot(routing_back, states_home, preferred_element_type=jnp.float32)
        .astype(jnp.bfloat16)
        .reshape(slots, seq_len, part_width)
    )
    input_grad = (
        jnp.dot(routing_back, grads_home, preferred_element_type=jnp.float32)
        .astype(jnp.bfloat16)
        .reshape(slots, seq_len, part_width)
    )
    return (encoded, input_grad, gain_grad)


def solution(mesh):
    placed = (
        P(("grp", "pas"), None, "fsdp"),
        P(("grp", "pas"), None, "fsdp"),
        P(("grp", "pas")),
        P(),
        P("pas", "fsdp"),
        P("pas", "fsdp"),
        P("pas", "fsdp"),
        P("fsdp", "pas"),
    )
    return jax.shard_map(
        body,
        mesh=mesh,
        in_specs=placed,
        out_specs=(
            P(("grp", "pas"), None, "fsdp"),
            P(("grp", "pas"), None, "fsdp"),
            P(("grp", "fsdp")),
        ),
        check_vma=False,
    )
```

profile of v0, /device:TPU:0, one launch (start us, length us, event | category | flops | bytes accessed | tf_op | source)
XLA Modules:
  0.0 536.4 jit_solution(14253019655738050172)
XLA Ops:
  7.8 1.2 dynamic-slice
  9.8 6.3 %all-reduce = s32[4]{0:T(128)S(1)} all-reduce(s32[4]{0:T(128)S(1)} %dynamic-update-slice), channel_id=2, replica_groups=mesh['grp'=2,'pas'=4,'fsdp'=4] {'pas'}, use_global_device_ids=true, to_apply=%add | all-reduce | flops 4 | bytes 32
  16.2 4.7 while.13
  21.7 3.2 all-to-all-start
  24.9 2.0 copy.136
  28.2 2.1 reduce.1
  30.3 2.0 reshape.191
  32.3 3.5 all-to-all-start.1
  36.1 14.2 %all-to-all-done.1 = bf16[4,2,65536]{2,1,0:T(2,128)(2,1)S(1)} async-done(((bf16[4,2,65536]{2,1,0:T(2,128)(2,1)}), bf16[4,2,65536]{2,1,0:T(2,128)(2,1)S(1)}, u32[]{:S(2)}, u32[]{:S(2)}) %all-to-all-start.1) | async-done | bytes 1048608 | tf_op jit(solution)/shard_map/all_to_all | solution.py:50
  50.3 0.9 reshape.192
  51.2 1.4 convolution_convert_fusion.7
  53.5 0.9 copy.186
  58.6 2.1 reduce.3
  60.7 1.1 reshape.195
  61.8 17.1 %all_to_all.60 = bf16[4,2,65536]{2,1,0:T(2,128)(2,1)S(1)} all-to-all(bf16[4,2,65536]{2,1,0:T(2,128)(2,1)S(1)} %reshape.195), channel_id=1, replica_groups=mesh['grp'=2,'pas'=4,'fsdp'=4] {'pas'}, dimensions={0} | all-to-all | bytes 2097152 | tf_op jit(solution)/shard_map/all_to_all | solution.py:51
  78.9 0.9 reshape.196
  79.9 1.4 convolution_convert_fusion.6
  82.1 0.9 copy.185
  83.1 17.7 %all-gather.8.cloned.1.call-done = bf16[2,128,4096]{2,1,0:T(8,128)(2,1)} async-done(((bf16[2,128,1024]{2,1,0:T(8,128)(2,1)}), bf16[2,128,4096]{2,1,0:T(8,128)(2,1)}) %all-gather.8.cloned.1.call-update) | async-done | bytes 2097168 | tf_op jit(solution)/shard_map/all_gather | solution.py:75
  100.8 2.2 fusion.11
  103.1 2.9 convert_multiply_fusion
  106.0 53.4 %all-gather.10.cloned.1.call-done = bf16[4096,1024]{1,0:T(8,128)(2,1)} async-done(((bf16[1024,1024]{1,0:T(8,128)(2,1)}), bf16[4096,1024]{1,0:T(8,128)(2,1)}) %all-gather.10.cloned.1.call-update) | async-done | bytes 8388624 | tf_op jit(solution)/shard_map/all_gather | solution.py:72
  159.4 6.5 %convolution_convert_fusion.11 = bf16[256,1024]{1,0:T(8,128)(2,1)} fusion(bf16[256,4096]{1,0:T(8,128)(2,1)S(1)} %bitcast.137, bf16[4096,1024]{1,0:T(8,128)(2,1)} %all-gather.10.cloned.1.call-done), kind=kOutput, calls=%fused_computation.32 | convolution fusion | flops 2147745792 | bytes 11010048 | tf_op jit(solution)/shard_map/dot_general | solution.py:87
  165.9 1.8 reshape.186
  167.7 1.6 copy.101
  169.3 50.0 %all-gather.12.cloned.1.call-done = bf16[4096,1024]{1,0:T(8,128)(2,1)} async-done(((bf16[1024,1024]{1,0:T(8,128)(2,1)}), bf16[4096,1024]{1,0:T(8,128)(2,1)}) %all-gather.12.cloned.1.call-update) | async-done | bytes 8388624 | tf_op jit(solution)/shard_map/all_gather | solution.py:70
  219.3 5.7 %convolution_convert_fusion.10 = bf16[256,1024]{1,0:T(8,128)(2,1)S(1)} fusion(bf16[256,4096]{1,0:T(8,128)(2,1)S(1)} %bitcast.138, bf16[4096,1024]{1,0:T(8,128)(2,1)} %all-gather.12.cloned.1.call-done), kind=kOutput, calls=%fused_computation.31 | convolution fusion | flops 2147745792 | bytes 11010048 | tf_op jit(solution)/shard_map/dot_general | solution.py:87
  225.7 0.9 copy.99
  226.5 52.5 %all-gather.14.cloned.1.call-done = bf16[4096,1024]{1,0:T(8,128)(2,1)} async-done(((bf16[1024,1024]{1,0:T(8,128)(2,1)}), bf16[4096,1024]{1,0:T(8,128)(2,1)}) %all-gather.14.cloned.1.call-update) | async-done | bytes 8388624 | tf_op jit(solution)/shard_map/all_gather | solution.py:71
  279.0 6.3 %convolution_convert_fusion.9 = bf16[256,1024]{1,0:T(8,128)(2,1)S(1)} fusion(bf16[256,4096]{1,0:T(8,128)(2,1)} %bitcast.139, bf16[4096,1024]{1,0:T(8,128)(2,1)} %all-gather.14.cloned.1.call-done), kind=kOutput, calls=%fused_computation.30 | convolution fusion | flops 2147745792 | bytes 11010048 | tf_op jit(solution)/shard_map/dot_general | solution.py:87
  286.0 0.9 copy.100
  287.7 2.3 convolution_convert_fusion.15
  290.1 48.7 %all-gather.16.cloned.1.call-done = bf16[1024,4096]{1,0:T(8,128)(2,1)} async-done(((bf16[1024,1024]{1,0:T(8,128)(2,1)}), bf16[1024,4096]{1,0:T(8,128)(2,1)}) %all-gather.16.cloned.1.call-update) | async-done | bytes 8388624 | tf_op jit(solution)/shard_map/all_gather | solution.py:73
  338.8 7.3 %fusion.7 = bf16[2,128,4096]{2,1,0:T(8,128)(2,1)} fusion(bf16[2,128,1024]{1,2,0:T(8,128)(2,1)} %bitcast.160, bf16[1024,4096]{1,0:T(8,128)(2,1)} %all-gather.16.cloned.1.call-done), kind=kOutput, calls=%fused_computation.20 | convolution fusion | flops 2148532224 | bytes 11010048 | tf_op jit(solution)/shard_map/dot_general | solution.py:100
  346.1 40.1 %all-gather.18.cloned.1.call-done = bf16[2,128,4096]{2,1,0:T(8,128)(2,1)} async-done(((bf16[2,128,1024]{2,1,0:T(8,128)(2,1)}), bf16[2,128,4096]{2,1,0:T(8,128)(2,1)}) %all-gather.18.cloned.1.call-update) | async-done | bytes 2097168 | tf_op jit(solution)/shard_map/all_gather | solution.py:111
  386.2 7.2 %convolution_convert_fusion.8 = bf16[256,1024]{1,0:T(8,128)(2,1)} fusion(bf16[256,4096]{1,0:T(8,128)(2,1)} %bitcast.167, bf16[1024,4096]{1,0:T(8,128)(2,1)} %all-gather.16.cloned.1.call-done), kind=kOutput, calls=%fused_computation.29 | convolution fusion | flops 2147745792 | bytes 11010048 | tf_op jit(solution)/shard_map/td,cd->tc/dot_general | solution.py:114
  393.4 11.0 %reshape.189 = bf16[2,128,16,64]{3,2,1,0:T(8,128)(2,1)} reshape(bf16[256,1024]{1,0:T(8,128)(2,1)} %convolution_convert_fusion.8) | data formatting | bytes 1048576 | tf_op jit(solution)/shard_map/reshape | solution.py:117
  404.3 2.8 copy.107
  407.1 1.7 multiply_reduce_fusion
  411.9 0.8 fusion.16
  413.3 2.5 fusion.36
  415.8 6.1 %convolution_add_fusion.1 = f32[256,4096]{1,0:T(8,128)S(1)} fusion(f32[256,4096]{1,0:T(8,128)S(1)} %fusion.36, bf16[4096,1024]{1,0:T(8,128)(2,1)} %all-gather.14.cloned.1.call-done, bf16[128,8,2,128]{3,2,1,0:T(2,128)(2,1)S(1)} %bitcast.156), kind=kOutput, calls=%fused_computation.19 | convolution fusion | flops 2148532224 | bytes 17301504 | tf_op jit(solution)/shard_map/tc,dc->td/dot_general | solution.py:134
  421.9 3.8 fusion.10
  425.8 5.3 reduce-scatter.3.cloned.1.call-done
  431.1 1.4 fusion.30
  433.1 1.1 fusion.2
  434.2 2.1 reduce.2
  436.3 2.0 reshape.193
  438.3 3.6 all-to-all-start.2
  441.9 34.7 %reduce-scatter.5.cloned.1.call-done = bf16[2,128,1024]{2,1,0:T(8,128)(2,1)} async-done(((bf16[2,128,4096]{2,1,0:T(8,128)(2,1)}), bf16[2,128,1024]{2,1,0:T(8,128)(2,1)}) %reduce-scatter.5.cloned.1.call-update) | async-done | bytes 524304 | tf_op jit(solution)/shard_map/reduce_scatter | solution.py:141
  476.7 1.7 fusion.21
  478.4 9.8 %psum.14 = f32[2,128,1]{1,0,2:T(2,128)S(1)} all-reduce(f32[2,128,1]{1,0,2:T(2,128)S(1)} %bitcast.161), channel_id=1, replica_groups=mesh['grp'=2,'pas'=4,'fsdp'=4] {'fsdp'}, use_global_device_ids=true, to_apply=%region_10.11 | all-reduce | flops 256 | bytes 2048 | tf_op jit(solution)/shard_map/psum | solution.py:150
  488.2 1.7 fusion.31
  490.4 1.1 fusion.4
  491.5 2.1 reduce.4
  493.6 2.0 reshape.197
  495.6 3.5 all-to-all-start.4
  499.2 16.4 %psum.15 = f32[1024]{0:T(1024)} all-reduce(f32[1024]{0:T(1024)S(1)} %get-tuple-element.83), channel_id=1, replica_groups=mesh['grp'=2,'pas'=4,'fsdp'=4] {'pas'}, use_global_device_ids=true, to_apply=%region_12.13 | all-reduce | flops 1024 | bytes 8192 | tf_op jit(solution)/shard_map/psum | solution.py:154
  515.6 2.3 reshape.194
  517.9 3.2 convolution_convert_fusion.3
  521.1 1.3 copy.184
  522.4 2.3 reshape.198
  524.7 3.2 convolution_convert_fusion
  527.9 1.3 copy.183
  (79 shorter events, 18.0 us)
Async XLA Ops:
  21.7 10.7 %all-to-all-start = ((s32[4,1,1]{2,1,0:T(1,128)}), s32[4,1,1]{2,1,0:T(1,128)S(1)}, u32[]{:S(2)}, u32[]{:S(2)}) async-start(s32[4,1,1]{2,1,0:T(1,128)} %copy.94), calls=%async_computation | async-start | bytes 4096 | tf_op jit(solution)/shard_map/all_to_all | solution.py:52
  32.3 18.0 %all-to-all-start.1 = ((bf16[4,2,65536]{2,1,0:T(2,128)(2,1)}), bf16[4,2,65536]{2,1,0:T(2,128)(2,1)S(1)}, u32[]{:S(2)}, u32[]{:S(2)}) async-start(bf16[4,2,65536]{2,1,0:T(2,128)(2,1)} %reshape.191), calls=%async_computation.1 | async-start | bytes 2097152 | tf_op jit(solution)/shard_map/all_to_all | solution.py:50
  35.8 65.0 %all-gather.8.cloned.1.call-start = ((), (), s32[]{:S(2)}) async-start(), calls=%async_computation.7 | async-start | bytes 2621440 | tf_op jit(solution)/shard_map/all_gather | solution.py:75
  52.6 0.8 copy-start.2
  54.4 105.0 %all-gather.10.cloned.1.call-start = ((), (), s32[]{:S(2)}) async-start(), calls=%async_computation.8 | async-start | bytes 10485760 | tf_op jit(solution)/shard_map/all_gather | solution.py:72
  55.2 164.1 %all-gather.12.cloned.1.call-start = ((), (), s32[]{:S(2)}) async-start(), calls=%async_computation.9 | async-start | bytes 10485760 | tf_op jit(solution)/shard_map/all_gather | solution.py:70
  55.9 1.2 copy-start.6
  55.9 223.1 %all-gather.14.cloned.1.call-start = ((), (), s32[]{:S(2)}) async-start(), calls=%async_computation.10 | async-start | bytes 10485760 | tf_op jit(solution)/shard_map/all_gather | solution.py:71
  56.5 282.3 %all-gather.16.cloned.1.call-start = ((), (), s32[]{:S(2)}) async-start(), calls=%async_computation.11 | async-start | bytes 10485760 | tf_op jit(solution)/shard_map/all_gather | solution.py:73
  57.1 329.1 %all-gather.18.cloned.1.call-start = ((), (), s32[]{:S(2)}) async-start(), calls=%async_computation.13 | async-start | bytes 2621440 | tf_op jit(solution)/shard_map/all_gather | solution.py:111
  81.3 0.8 copy-start.4
  81.3 21.8 %copy-start.8 = (f32[4096]{0:T(1024)S(1)}, f32[4096]{0:T(1024)}, u32[]{:S(2)}) copy-start(f32[4096]{0:T(1024)} %param.13) | copy-start | bytes 49156
  83.0 348.1 %reduce-scatter.3.cloned.1.call-start = ((), (), s32[]{:S(2)}) async-start(), calls=%async_computation.12 | async-start | bytes 2621440 | tf_op jit(solution)/shard_map/reduce_scatter | solution.py:103
  100.8 2.3 copy-start
  106.0 113.3 %copy-start.1 = (bf16[2,128,4096]{2,1,0:T(8,128)(2,1)}, bf16[2,128,4096]{2,1,0:T(8,128)(2,1)S(1)}, u32[]{:S(2)}) copy-start(bf16[2,128,4096]{2,1,0:T(8,128)(2,1)S(1)} %get-tuple-element.96) | copy-start | bytes 6291460
  346.0 130.6 %reduce-scatter.5.cloned.1.call-start = ((), (), s32[]{:S(2)}) async-start(), calls=%async_computation.14 | async-start | bytes 2621440 | tf_op jit(solution)/shard_map/reduce_scatter | solution.py:141
  408.9 4.4 slice-start.2
  409.9 2.0 copy-start.7
  410.5 2.8 slice-start.3
  413.3 8.6 %slice-start = ((s8[8388608]{0:T(1024)(128)(4,1)}), s8[4194304]{0:T(1024)(128)(4,1)S(1)}, s32[]{:S(2)}) async-start(s8[8388608]{0:T(1024)(128)(4,1)} %bitcast.163), calls=%async_computation.15 | async-start | bytes 8388608
  415.8 6.1 %slice-start.1 = ((s8[8388608]{0:T(1024)(128)(4,1)}), s8[4194304]{0:T(1024)(128)(4,1)S(1)}, s32[]{:S(2)}) async-start(s8[8388608]{0:T(1024)(128)(4,1)} %bitcast.163), calls=%async_computation.16 | async-start | bytes 8388608
  425.7 5.4 copy-start.3
  438.3 49.9 %copy-start.5 = (bf16[2,131072]{1,0:T(2,128)(2,1)S(1)}, bf16[2,131072]{1,0:T(2,128)(2,1)}, u32[]{:S(2)}) copy-start(bf16[2,131072]{1,0:T(2,128)(2,1)} %copy-done.4) | copy-start | bytes 1572868
  438.3 57.3 %all-to-all-start.2 = ((bf16[4,2,65536]{2,1,0:T(2,128)(2,1)}), bf16[4,2,65536]{2,1,0:T(2,128)(2,1)S(1)}, u32[]{:S(2)}, u32[]{:S(2)}) async-start(bf16[4,2,65536]{2,1,0:T(2,128)(2,1)} %reshape.193), calls=%async_computation.3 | async-start | bytes 2097152 | tf_op jit(solution)/shard_map/all_to_all | solution.py:110
  495.6 26.7 %all-to-all-start.4 = ((bf16[4,2,65536]{2,1,0:T(2,128)(2,1)}), bf16[4,2,65536]{2,1,0:T(2,128)(2,1)S(1)}, u32[]{:S(2)}, u32[]{:S(2)}) async-start(bf16[4,2,65536]{2,1,0:T(2,128)(2,1)} %reshape.197), calls=%async_computation.6 | async-start | bytes 2097152 | tf_op jit(solution)/shard_map/all_to_all | solution.py:158
Sparse Core Ops, SparseCore 0:
  54.5 46.2 all-gather.7
  102.4 56.9 all-gather.9
  161.0 58.2 all-gather.11
  220.7 58.2 all-gather.13
  280.4 58.2 all-gather.15
  340.2 45.9 all-gather.17
  388.5 42.5 reduce-scatter.2
  433.5 43.1 reduce-scatter.4
where the time goes:
time: 546 us; the launch traced here: 536 us
  waiting for transfers between devices  319 us (58%)
  matrix products  65.1 us (12%)
  local copies, waits for them, and re-layouts  51 us (9%)
  blocking collectives  49.8 us (9%)
  other arithmetic  19.1 us (3%)
  between operations  15.7 us (3%)
  starting transfers between devices  14.2 us (3%)
    all_gather x1, waiting for transfers between devices, body(): lax.all_gather(w_value, 'pas', axis=0, tiled=True)  53.4 us
    all_gather x1, waiting for transfers between devices, body(): lax.all_gather(w_key, 'pas', axis=0, tiled=True)  52.5 us
    all_gather x1, waiting for transfers between devices, body(): lax.all_gather(w_query, 'pas', axis=0, tiled=True)  50 us
    all_gather x1, waiting for transfers between devices, body(): lax.all_gather(w_out, 'pas', axis=1, tiled=True)  48.7 us
    all_gather x1, waiting for transfers between devices, body(): lax.all_gather(local_grads, 'fsdp', axis=2, tiled=True)  40.1 us
    reduce_scatter x1, waiting for transfers between devices, body(): lax.psum_scatter(d_normed.reshape(BAL, seq_len, width).astype(jnp.bfloat1...  34.7 us
    unnamed x45, local copies, waits for them, and re-layouts  25.6 us
    dot_general x3, matrix products, project(): jnp.dot(flat_rows, weight, preferred_element_type=jnp.float32)  18.6 us
  transfers between devices with their start and end apart: 12, of which 9 were waited for; matrix products, arithmetic and copies ran while one was open for 22% of the time, Pallas kernels for 0%

commit v1 on v0

--- a/solution.py
+++ b/solution.py
@@ -1,13 +1,14 @@
 import jax
 import jax.numpy as jnp
 from jax import lax
+from jax.experimental import pallas as pl
+from jax.experimental.pallas import tpu as pltpu
 from jax.sharding import PartitionSpec as P
 
 HD = 64
 BAL = 2
-
-
 EPSILON = 1e-06
+VMEM_LIMIT = 50 * 2**20
 
 
 def entering(shard, axis, combine, identity):
@@ -27,7 +28,7 @@
     return earlier + later
 
 
-def body(passages, cotangent, passage_counts, norm_gain, w_query, w_key, w_value, w_out):
+def general_body(passages, cotangent, passage_counts, norm_gain, w_query, w_key, w_value, w_out):
     peer_total = lax.axis_size("pas")
     slots, seq_len, part_width = passages.shape
     flat_width = seq_len * part_width
@@ -170,6 +171,281 @@
     return (encoded, input_grad, gain_grad)
 
 
+def swap(array, axis, bit):
+    return lax.ppermute(array, axis, [(i, i ^ bit) for i in range(lax.axis_size(axis))])
+
+
+def dot_nn(a, b):
+    return jnp.dot(a, b, preferred_element_type=jnp.float32)
+
+
+def dot_nt(a, b):
+    return lax.dot_general(a, b, (((1,), (1,)), ((), ())), preferred_element_type=jnp.float32)
+
+
+def dot_tn(a, b):
+    return lax.dot_general(a, b, (((0,), (0,)), ((), ())), preferred_element_type=jnp.float32)
+
+
+def halves(at):
+    first = pl.multiple_of(at * 512, 512)
+    second = pl.multiple_of((1 - at) * 512, 512)
+    return pl.ds(first, 512), pl.ds(second, 512)
+
+
+def project_kernel(pos, rows, own, core, xh, yh, xch, ych, out):
+    b = pos[0]
+    near, far = halves(pos[1])
+    total = dot_nn(rows[b], own[...]) + dot_nn(rows[b ^ 1], core[...])
+    total += dot_nn(rows[b ^ 2, :, near], xh[...]) + dot_nn(rows[b ^ 2, :, far], yh[...])
+    total += dot_nn(rows[b ^ 3, :, near], xch[...]) + dot_nn(rows[b ^ 3, :, far], ych[...])
+    out[...] = total.astype(out.dtype)
+
+
+def project_out_kernel(pos, rows, own, core, xh, yh, xch, ych, out):
+    b = pos[0]
+    near, far = halves(pos[1])
+    total = dot_nt(rows[b], own[...]) + dot_nt(rows[b ^ 1], core[...])
+    total += dot_nt(rows[b ^ 2, :, near], xh[...]) + dot_nt(rows[b ^ 2, :, far], yh[...])
+    total += dot_nt(rows[b ^ 3, :, near], xch[...]) + dot_nt(rows[b ^ 3, :, far], ych[...])
+    out[...] = total.astype(out.dtype)
+
+
+def half_at(at, step):
+    return pl.ds(pl.multiple_of(at * 512 + step * 128, 128), 128)
+
+
+def emit_kernel(pos, ctx, own, core, xh, yh, xch, ych, out):
+    b = pos[0]
+    step = pl.program_id(0)
+    whole = pl.ds(pl.multiple_of(step * 256, 256), 256)
+    near, far = half_at(pos[1], step), half_at(1 - pos[1], step)
+    rows = ctx[...]
+    out[b, :, whole] = dot_nn(rows, own[...]).astype(out.dtype)
+    out[b ^ 1, :, whole] = dot_nn(rows, core[...]).astype(out.dtype)
+    two = dot_nn(rows, jnp.concatenate([xh[...], yh[...]], axis=1)).astype(out.dtype)
+    out[b ^ 2, :, near] = two[:, :128]
+    out[b ^ 2, :, far] = two[:, 128:]
+    two = dot_nn(rows, jnp.concatenate([xch[...], ych[...]], axis=1)).astype(out.dtype)
+    out[b ^ 3, :, near] = two[:, :128]
+    out[b ^ 3, :, far] = two[:, 128:]
+
+
+def back_kernel(pos, dq, dk, dv, *refs):
+    weights, out = refs[:18], refs[18]
+    b = pos[0]
+    step = pl.program_id(0)
+    whole = pl.ds(pl.multiple_of(step * 256, 256), 256)
+    near, far = half_at(pos[1], step), half_at(1 - pos[1], step)
+    grads = (dq[...], dk[...], dv[...])
+
+    def total(pick):
+        return sum(dot_nt(g, pick(weights[6 * i : 6 * i + 6])) for i, g in enumerate(grads))
+
+    out[b, :, whole] = total(lambda w: w[0][...]).astype(out.dtype)
+    out[b ^ 1, :, whole] = total(lambda w: w[1][...]).astype(out.dtype)
+    two = total(lambda w: jnp.concatenate([w[2][...], w[3][...]], axis=0)).astype(out.dtype)
+    out[b ^ 2, :, near] = two[:, :128]
+    out[b ^ 2, :, far] = two[:, 128:]
+    two = total(lambda w: jnp.concatenate([w[4][...], w[5][...]], axis=0)).astype(out.dtype)
+    out[b ^ 3, :, near] = two[:, :128]
+    out[b ^ 3, :, far] = two[:, 128:]
+
+
+def attention_kernel(q_ref, k_ref, v_ref, dc_ref, ctx_ref, dq_ref, dk_ref, dv_ref):
+    seq = q_ref.shape[0]
+    lane = lax.broadcasted_iota(jnp.int32, (seq, 128), 1)
+    first = lane < HD
+    mask0 = jnp.where(first, 1.0, 0.0).astype(jnp.bfloat16)
+    mask1 = jnp.where(first, 0.0, 1.0).astype(jnp.bfloat16)
+    for pair in range(q_ref.shape[1] // 128):
+        at = pl.ds(pair * 128, 128)
+        q, k, v, dc = q_ref[:, at], k_ref[:, at], v_ref[:, at], dc_ref[:, at]
+        keys = jnp.concatenate([k * mask0, k * mask1], axis=0)
+        values = jnp.concatenate([v * mask0, v * mask1], axis=0)
+        scores = dot_nt(q, keys)
+        d_probs = dot_nt(dc, values)
+        probs, d_scores = [], []
+        for h in range(2):
+            s = scores[:, h * seq : (h + 1) * seq]
+            dp = d_probs[:, h * seq : (h + 1) * seq]
+            e = jnp.exp(s - jnp.max(s, axis=-1, keepdims=True))
+            p = e / jnp.sum(e, axis=-1, keepdims=True)
+            ds = p * (dp - jnp.sum(dp * p, axis=-1, keepdims=True))
+            probs.append(p.astype(jnp.bfloat16))
+            d_scores.append(ds.astype(jnp.bfloat16))
+        low = jnp.concatenate(probs, axis=1)
+        ds = jnp.concatenate(d_scores, axis=1)
+        ctx_ref[:, at] = dot_nn(low, values).astype(jnp.bfloat16)
+        dq_ref[:, at] = dot_nn(ds, keys).astype(jnp.bfloat16)
+        both = dot_tn(low, dc)
+        dv_ref[:, at] = jnp.where(first, both[:seq], both[seq:]).astype(jnp.bfloat16)
+        both = dot_tn(ds, q)
+        dk_ref[:, at] = jnp.where(first, both[:seq], both[seq:]).astype(jnp.bfloat16)
+
+
+def whole_spec(array):
+    zeros = (0,) * array.ndim
+    return pl.BlockSpec(array.shape, lambda j, pos: zeros)
+
+
+def call(kernel, pos, rows, pieces, tile, out_shape, out_tile):
+    def cut(array):
+        shape = list(array.shape)
+        shape[tile] //= 4
+        return pl.BlockSpec(tuple(shape), lambda j, pos: (j, 0) if tile == 0 else (0, j))
+
+    flops = 2 * 256 * sum(p.size for p in pieces)
+    size = 2 * sum(p.size for p in pieces)
+    return pl.pallas_call(
+        kernel,
+        grid_spec=pltpu.PrefetchScalarGridSpec(
+            num_scalar_prefetch=1,
+            grid=(4,),
+            in_specs=[whole_spec(r) for r in rows] + [cut(p) for p in pieces],
+            out_specs=out_tile,
+        ),
+        out_shape=out_shape,
+        cost_estimate=pl.CostEstimate(flops=flops, bytes_accessed=size, transcendentals=0),
+        compiler_params=pltpu.CompilerParams(vmem_limit_bytes=VMEM_LIMIT),
+    )(pos, *rows, *pieces)
+
+
+def attend(query, keys, values, d_context):
+    rows, cols = query.shape
+    spec = pl.BlockSpec((rows // BAL, cols // 2), lambda i, j: (i, j))
+    shape = jax.ShapeDtypeStruct(query.shape, jnp.bfloat16)
+    return pl.pallas_call(
+        attention_kernel,
+        grid=(BAL, 2),
+        in_specs=[spec] * 4,
+        out_specs=[spec] * 4,
+        out_shape=[shape] * 4,
+        cost_estimate=pl.CostEstimate(
+            flops=32 * 12 * 128 * 128 * 128, bytes_accessed=8 * 2 * query.size, transcendentals=2**19
+        ),
+        compiler_params=pltpu.CompilerParams(vmem_limit_bytes=VMEM_LIMIT),
+    )(query, keys, values, d_context)
+
+
+def fetch_weight(weight, group, axis):
+    half = lax.dynamic_slice_in_dim(weight, group * 512, 512, axis)
+    core = swap(weight, "pas", 1)
+    xh = swap(half, "pas", 2)
+    yh = swap(xh, "grp", 1)
+    xch = swap(xh, "pas", 1)
+    ych = swap(yh, "pas", 1)
+    return [weight, core, xh, yh, xch, ych]
+
+
+def fast_body(passages, cotangent, passage_counts, norm_gain, w_query, w_key, w_value, w_out):
+    me = lax.axis_index("pas")
+    group = lax.axis_index("grp")
+    feature = lax.axis_index("fsdp")
+    seq = passages.shape[1]
+    pos = jnp.stack([me, group]).astype(jnp.int32)
+
+    counts = lax.all_gather(passage_counts, "pas", axis=0, tiled=True)
+    index = jnp.arange(4, dtype=jnp.int32)
+    single = counts == 1
+    source = jnp.sum(jnp.where(counts == 4, index, 0))
+    rank = lambda d: jnp.minimum(jnp.sum((single & (index < d)).astype(jnp.int32)), 1)
+    host0 = jnp.min(jnp.where(single, index, 4))
+    host1 = jnp.max(jnp.where(single, index, -1))
+    own_count = passage_counts[0]
+    relation = me ^ source
+
+    def second(array):
+        extra = array[2:4]
+        extra_core = swap(extra, "pas", 1)
+        there = rank(me ^ 2)
+        picked = jnp.where(source == me, extra, extra_core)
+        sent = jnp.where(there == 0, picked[0], picked[1])
+        got_x = swap(sent, "pas", 2)
+        from_core = jnp.where(rank(me) == 0, extra_core[0], extra_core[1])
+        foreign = jnp.where(relation == 1, from_core, got_x)
+        return jnp.where(own_count >= 2, array[1], foreign)
+
+    tokens = jnp.concatenate([passages[0], second(passages)], axis=0)
+    grads = jnp.concatenate([cotangent[0], second(cotangent)], axis=0)
+
+    key_w = fetch_weight(w_key, group, 0)
+    query_w = fetch_weight(w_query, group, 0)
+    value_w = fetch_weight(w_value, group, 0)
+    out_w = fetch_weight(w_out, group, 1)
+
+    all_tokens = lax.all_gather(tokens, "fsdp", axis=0)
+    all_grads = lax.all_gather(grads, "fsdp", axis=0)
+
+    tokens_f32 = all_tokens.astype(jnp.float32)
+    width = norm_gain.shape[0]
+    gain = norm_gain.reshape(4, 1, 1024)
+    inverse = lax.rsqrt(
+        jnp.sum(tokens_f32 * tokens_f32, axis=(0, 2), keepdims=True) / width + EPSILON
+    )
+    normed = (tokens_f32 * inverse * gain).astype(jnp.bfloat16)
+
+    rows_shape = jax.ShapeDtypeStruct((2 * seq, 1024), jnp.bfloat16)
+    rows_tile = pl.BlockSpec((2 * seq, 256), lambda j, pos: (0, j))
+    wide_shape = jax.ShapeDtypeStruct((4, 2 * seq, 1024), jnp.bfloat16)
+    wide_tile = pl.BlockSpec((4, 2 * seq, 1024), lambda j, pos: (0, 0, 0))
+
+    def project(pieces):
+        return call(project_kernel, pos, [normed], pieces, 1, rows_shape, rows_tile)
+
+    keys = project(key_w)
+    query = project(query_w)
+    values = project(value_w)
+    d_context = call(project_out_kernel, pos, [all_grads], out_w, 0, rows_shape, rows_tile)
+    context, d_query, d_keys, d_values = attend(query, keys, values, d_context)
+    d_normed = call(
+        back_kernel, pos, [d_query, d_keys, d_values], query_w + key_w + value_w, 0, wide_shape, wide_tile
+    )
+    partial_out = call(emit_kernel, pos, [context], out_w, 1, wide_shape, wide_tile)
+
+    d_part = lax.psum_scatter(d_normed, "fsdp", scatter_dimension=0).astype(jnp.float32)
+    attention = lax.psum_scatter(partial_out, "fsdp", scatter_dimension=0).astype(jnp.float32)
+
+    row_total = jnp.sum(
+        d_normed.astype(jnp.float32) * gain * (tokens_f32 * inverse), axis=(0, 2)
+    ).reshape(2, seq)
+    row_total += swap(row_total, "fsdp", 1)
+    row_total += swap(row_total, "fsdp", 2)
+    row_mean = row_total.reshape(2 * seq, 1) / width
+
+    gain_part = lax.dynamic_slice_in_dim(norm_gain, feature * 1024, 1024, 0)
+    inverse_rows = inverse.reshape(2 * seq, 1)
+    unit_part = tokens.astype(jnp.float32) * inverse_rows
+    d_tokens = inverse_rows * (d_part * gain_part - unit_part * row_mean)
+    input_local = (grads.astype(jnp.float32) + d_tokens).astype(jnp.bfloat16)
+    states = (tokens.astype(jnp.float32) + attention).astype(jnp.bfloat16)
+    gain_grad = jnp.sum(d_part * unit_part, axis=0).reshape(8, 128)
+    gain_grad += swap(gain_grad, "pas", 1)
+    gain_grad += swap(gain_grad, "pas", 2)
+
+    def home(local):
+        local = local.reshape(2, seq, 1024)
+        back = local[1]
+        over_x = swap(back, "pas", 2)
+        over_core = swap(jnp.stack([back, over_x]), "pas", 1)
+
+        def pick(host):
+            way = host ^ me
+            return jnp.where(way == 1, over_core[0], jnp.where(way == 2, over_x, over_core[1]))
+
+        zero = jnp.zeros_like(back)
+        return jnp.stack(
+            [
+                local[0],
+                jnp.where(own_count >= 2, back, zero),
+                jnp.where(own_count == 4, pick(host0), zero),
+                jnp.where(own_count == 4, pick(host1), zero),
+            ]
+        )
+
+    return home(states), home(input_local), gain_grad.reshape(1024)
+
+
 def solution(mesh):
     placed = (
         P(("grp", "pas"), None, "fsdp"),
@@ -181,8 +457,10 @@
         P("pas", "fsdp"),
         P("fsdp", "pas"),
     )
+    sizes = dict(mesh.shape)
+    fast = sizes["grp"] == 2 and sizes["pas"] == 4 and sizes["fsdp"] == 4
     return jax.shard_map(
-        body,
+        fast_body if fast else general_body,
         mesh=mesh,
         in_specs=placed,
         out_specs=(

time: 546 us -> 373 us (0.68); the launches traced: 536 us -> 372 us
  waiting for transfers between devices: 319 us -> 233 us
  matrix products: 65.1 us -> 0 us
  Pallas kernels: 0 us -> 55.7 us
  blocking collectives: 49.8 us -> 5.92 us
  local copies, waits for them, and re-layouts: 51 us -> 17.4 us
  starting transfers between devices: 14.2 us -> 22.5 us
    all_gather x6 -> x2, waiting for transfers between devices: 262 us -> 0.02 us  [the longest x1 0.02 us: fast_body(): all_grads = lax.all_gather(grads, 'fsdp', axis=0)]
    ppermute x0 -> x32, waiting for transfers between devices: none -> 172 us  [swap(): lax.ppermute(array, axis, [(i, i ^ bit) for i in range(lax.axis_size(axis...]
    dot_general x21 -> x0, matrix products: 64.3 us -> none  [the longest x3 18.6 us: project(): jnp.dot(flat_rows, weight, preferred_element_type=jnp.float32)]
    pallas_call x0 -> x7, Pallas kernels: none -> 55.7 us  [the longest x6 47.1 us: call(): pl.pallas_call(kernel, grid_spec=pltpu.PrefetchScalarGridSpec(num_scalar_...]
    psum x2 -> x0, blocking collectives: 26.3 us -> none  [the longest x1 16.4 us: body(): gain_grad = lax.psum(jnp.sum(d_normed_part * unit_part, axis=(0, 1)), 'pas')]
    ppermute x0 -> x32, starting transfers between devices: none -> 22.1 us  [swap(): lax.ppermute(array, axis, [(i, i ^ bit) for i in range(lax.axis_size(axis...]
    reduce_scatter x2, waiting for transfers between devices: 40.1 us -> 60.7 us  [the longest x1 45.5 us: fast_body(): lax.psum_scatter(d_normed, 'fsdp', scatter_dimension=0).astype(jnp.float32)]
    reshape x8 -> x0, local copies, waits for them, and re-layouts: 20.2 us -> none  [the longest x2 13.8 us: body(): d_context = d_context.reshape(BAL, seq_len, head_count, HD)]
  transfers between devices with their start and end apart: 12 -> 36, of which waited for: 9 -> 13; matrix products, arithmetic and copies ran while one was open for 22% -> 5% of each run, Pallas kernels for 0% -> 9%
where the time goes in v1:
time: 373 us; the launch traced here: 372 us
  waiting for transfers between devices  233 us (62%)
  Pallas kernels  55.7 us (15%)
  starting transfers between devices  22.5 us (6%)
  between operations  18.7 us (5%)
  other arithmetic  18.6 us (5%)
  local copies, waits for them, and re-layouts  17.4 us (5%)
  blocking collectives  5.92 us (2%)
    ppermute x32, waiting for transfers between devices, swap(): lax.ppermute(array, axis, [(i, i ^ bit) for i in range(lax.axis_size(axis...  172 us
    pallas_call x6, Pallas kernels, call(): pl.pallas_call(kernel, grid_spec=pltpu.PrefetchScalarGridSpec(num_scalar_...  47.1 us
    reduce_scatter x1, waiting for transfers between devices, fast_body(): lax.psum_scatter(d_normed, 'fsdp', scatter_dimension=0).astype(jnp.float32)  45.5 us
    ppermute x32, starting transfers between devices, swap(): lax.ppermute(array, axis, [(i, i ^ bit) for i in range(lax.axis_size(axis...  22.1 us
    reduce_scatter x1, waiting for transfers between devices, fast_body(): lax.psum_scatter(partial_out, 'fsdp', scatter_dimension=0)  15.3 us
    unnamed x73, local copies, waits for them, and re-layouts  12.4 us
    pallas_call x1, Pallas kernels, attend(): pl.pallas_call(attention_kernel, grid=(BAL, 2), in_specs=[spec] * 4, out_...  8.63 us
  transfers between devices with their start and end apart: 36, of which 13 were waited for; matrix products, arithmetic and copies ran while one was open for 5% of the time, Pallas kernels for 9%

profile of v1, /device:TPU:0, one launch (start us, length us, event | category | flops | bytes accessed | tf_op | source)
XLA Modules:
  0.0 371.9 jit_solution(6461346590801524506)
XLA Ops:
  7.2 1.2 slice.84
  9.6 1.2 dynamic-slice
  10.9 0.8 dynamic-update-slice
  11.6 5.9 %all-reduce = s32[4]{0:T(128)S(1)} all-reduce(s32[4]{0:T(128)S(1)} %dynamic-update-slice), channel_id=1, replica_groups=mesh['grp'=2,'pas'=4,'fsdp'=4] {'pas'}, use_global_device_ids=true, to_apply=%add | all-reduce | flops 4 | bytes 32
  17.5 0.8 select_reduce_fusion.1
  19.6 1.1 broadcast_select_fusion.1
  20.7 0.7 fusion.16
  21.5 0.9 collective-permute-start.1
  23.7 5.8 %collective-permute-done.1 = bf16[128,1024]{1,0:T(8,128)(2,1)S(1)} collective-permute-done((bf16[128,1024]{1,0:T(8,128)(2,1)}, bf16[128,1024]{1,0:T(8,128)(2,1)S(1)}, u32[]{:S(2)}, u32[]{:S(2)}) %collective-permute-start.1) | collective-permute-done | bytes 262176 | tf_op jit(solution)/shard_map/ppermute | solution.py:175
  29.5 0.7 copy-done.33
  30.2 1.0 fusion.19
  31.2 0.9 pad_maximum_fusion.2
  32.2 0.8 slice.91
  33.5 1.4 constant_dynamic-slice_fusion.2
  35.0 0.6 collective-permute-start.8
  35.6 1.3 constant_dynamic-slice_fusion.1
  36.9 1.5 collective-permute-start.13
  38.6 0.6 collective-permute-start.20
  39.3 2.6 collective-permute-start.18
  42.0 68.7 %collective-permute-done.18 = bf16[128,1024]{1,0:T(8,128)(2,1)S(1)} collective-permute-done((bf16[128,1024]{1,0:T(8,128)(2,1)S(1)}, bf16[128,1024]{1,0:T(8,128)(2,1)S(1)}, u32[]{:S(2)}, u32[]{:S(2)}) %collective-permute-start.18) | collective-permute-done | bytes 262176 | tf_op jit(solution)/shard_map/ppermute | solution.py:175
  111.3 1.2 collective-permute-start.9
  113.0 22.0 %collective-permute-done.3.xh.refs_2_ = bf16[512,1024]{1,0:T(8,128)(2,1)} collective-permute-done((bf16[512,1024]{1,0:T(8,128)(2,1)S(1)}, bf16[512,1024]{1,0:T(8,128)(2,1)}, u32[]{:S(2)}, u32[]{:S(2)}) %collective-permute-start.3) | collective-permute-done | bytes 1048608 | tf_op jit(solution)/shard_map/ppermute | solution.py:175
  135.0 1.5 collective-permute-start.14
  136.5 1.0 copy-done.4
  137.5 1.1 fusion.15
  138.6 1.0 copy-done.6
  140.1 1.5 collective-permute-start.4
  141.7 0.9 pad_maximum_fusion.3
  142.6 18.6 %collective-permute-done.14.yh.refs_15_ = bf16[512,1024]{1,0:T(8,128)(2,1)} collective-permute-done((bf16[512,1024]{1,0:T(8,128)(2,1)S(1)}, bf16[512,1024]{1,0:T(8,128)(2,1)}, u32[]{:S(2)}, u32[]{:S(2)}) %collective-permute-start.14) | collective-permute-done | bytes 1048608 | tf_op jit(solution)/shard_map/ppermute | solution.py:175
  161.8 21.8 %collective-permute-done.21.yh = bf16[1024,512]{1,0:T(8,128)(2,1)S(1)} collective-permute-done((bf16[1024,512]{1,0:T(8,128)(2,1)S(1)}, bf16[1024,512]{1,0:T(8,128)(2,1)S(1)}, u32[]{:S(2)}, u32[]{:S(2)}) %collective-permute-start.21) | collective-permute-done | bytes 1048608 | tf_op jit(solution)/shard_map/ppermute | solution.py:175
  183.6 19.8 %collective-permute-done.4.yh.refs_3_ = bf16[512,1024]{1,0:T(8,128)(2,1)} collective-permute-done((bf16[512,1024]{1,0:T(8,128)(2,1)}, bf16[512,1024]{1,0:T(8,128)(2,1)}, u32[]{:S(2)}, u32[]{:S(2)}) %collective-permute-start.4) | collective-permute-done | bytes 1048608 | tf_op jit(solution)/shard_map/ppermute | solution.py:175
  204.0 2.2 fusion.4
  206.8 2.1 fusion.2.rows
  209.1 6.3 %shard_map.104.k_ref = bf16[256,1024]{1,0:T(8,128)(2,1)S(1)} custom-call(s32[2]{0:T(128)S(1)} %pad_add_fusion.pos, bf16[4,256,1024]{2,1,0:T(8,128)(2,1)} %fusion.2.rows, bf16[1024,1024]{1,0:T(8,128)(2,1)} %refs_6_.1, bf16[1024,1024]{1,0:T(8,128)(2,1)} %collective-permute-done.7.core.refs_7_, bf16[512,1024]{1,0:T(8,128)(2,1)S(1)} %copy-done.1, ...), custom_call_target="tpu_custom_call" | custom-call | flops 2147483648 | bytes 8388608 | tf_op jit(solution)/shard_map/pallas_call | solution.py:300
  215.4 6.7 %shard_map.105.v_ref = bf16[256,1024]{1,0:T(8,128)(2,1)S(1)} custom-call(s32[2]{0:T(128)S(1)} %pad_add_fusion.pos, bf16[4,256,1024]{2,1,0:T(8,128)(2,1)} %fusion.2.rows, bf16[1024,1024]{1,0:T(8,128)(2,1)} %refs_12_.1, bf16[1024,1024]{1,0:T(8,128)(2,1)} %collective-permute-done.12.core.refs_13_, bf16[512,1024]{1,0:T(8,128)(2,1)S(1)} %copy-done.3, ...), custom_call_target="tpu_custom_call" | custom-call | flops 2147483648 | bytes 8388608 | tf_op jit(solution)/shard_map/pallas_call | solution.py:300
  222.1 0.8 copy-done.16
  222.9 7.2 %shard_map.103.q_ref = bf16[256,1024]{1,0:T(8,128)(2,1)S(1)} custom-call(s32[2]{0:T(128)S(1)} %pad_add_fusion.pos, bf16[4,256,1024]{2,1,0:T(8,128)(2,1)} %fusion.2.rows, bf16[1024,1024]{1,0:T(8,128)(2,1)} %refs_0_.1, bf16[1024,1024]{1,0:T(8,128)(2,1)} %collective-permute-done.2.core.refs_1_, bf16[512,1024]{1,0:T(8,128)(2,1)} %collective-permute-done.3.xh.refs_2_, ...), custom_call_target="tpu_custom_call" | custom-call | flops 2147483648 | bytes 8388608 | tf_op jit(solution)/shard_map/pallas_call | solution.py:300
  230.2 0.8 copy-done.18
  231.0 6.4 %shard_map.106.dc_ref = bf16[256,1024]{1,0:T(8,128)(2,1)S(1)} custom-call(s32[2]{0:T(128)S(1)} %pad_add_fusion.pos, bf16[4,256,1024]{2,1,0:T(8,128)(2,1)} %bitcast.100, bf16[1024,1024]{1,0:T(8,128)(2,1)} %own.9, bf16[1024,1024]{1,0:T(8,128)(2,1)} %collective-permute-done.19.core, bf16[1024,512]{1,0:T(8,128)(2,1)S(1)} %collective-permute-done.20.xh, ...), custom_call_target="tpu_custom_call" | custom-call | flops 2147483648 | bytes 8388608 | tf_op jit(solution)/shard_map/pallas_call | solution.py:300
  237.4 0.8 copy-done.20
  238.3 8.6 %shard_map.107 = (bf16[256,1024]{1,0:T(8,128)(2,1)S(1)}, bf16[256,1024]{1,0:T(8,128)(2,1)S(1)}, bf16[256,1024]{1,0:T(8,128)(2,1)S(1)}, bf16[256,1024]{1,0:T(8,128)(2,1)S(1)}) custom-call(bf16[256,1024]{1,0:T(8,128)(2,1)S(1)} %copy-done.19, bf16[256,1024]{1,0:T(8,128)(2,1)S(1)} %copy-done.15, bf16[256,1024]{1,0:T(8,128)(2,1)S(1)} %copy-done.17, ...), custom_call_target="tpu_custom_call" | custom-call | flops 805306368 | bytes 4194304 | tf_op jit(solution)/shard_map/pallas_call | solution.py:318
  246.9 0.8 copy-done.8
  247.7 0.8 copy-done.10
  248.5 0.8 copy-done.12
  249.3 7.0 %shard_map.108 = bf16[4,256,1024]{2,1,0:T(8,128)(2,1)} custom-call(s32[2]{0:T(128)S(1)} %pad_add_fusion.pos, bf16[256,1024]{1,0:T(8,128)(2,1)S(1)} %get-tuple-element.7.ctx, bf16[1024,1024]{1,0:T(8,128)(2,1)} %own.9, bf16[1024,1024]{1,0:T(8,128)(2,1)} %collective-permute-done.19.core, bf16[1024,512]{1,0:T(8,128)(2,1)S(1)} %collective-permute-done.20.xh, ...), custom_call_target="tpu_custom_call" | custom-call | flops 2147483648 | bytes 8388608 | tf_op jit(solution)/shard_map/pallas_call | solution.py:300
  256.6 0.8 copy-done.9
  257.7 13.5 %shard_map.109 = bf16[4,256,1024]{2,1,0:T(8,128)(2,1)} custom-call(s32[2]{0:T(128)S(1)} %pad_add_fusion.pos, bf16[256,1024]{1,0:T(8,128)(2,1)S(1)} %copy-done.9, bf16[256,1024]{1,0:T(8,128)(2,1)S(1)} %copy-done.11, bf16[256,1024]{1,0:T(8,128)(2,1)S(1)} %copy-done.13, bf16[1024,1024]{1,0:T(8,128)(2,1)} %refs_0_.1, ...), custom_call_target="tpu_custom_call" | custom-call | flops 6442450944 | bytes 25165824 | tf_op jit(solution)/shard_map/pallas_call | solution.py:300
  271.2 1.6 copy-done.22
  272.7 2.6 fusion.3
  275.4 1.8 collective-permute-start.26
  277.2 3.1 collective-permute-done.26
  280.2 1.7 collective-permute-start.27
  281.9 4.0 %collective-permute-done.27 = f32[2,128]{1,0:T(2,128)S(1)} collective-permute-done((f32[2,128]{1,0:T(2,128)S(1)}, f32[2,128]{1,0:T(2,128)S(1)}, u32[]{:S(2)}, u32[]{:S(2)}) %collective-permute-start.27) | collective-permute-done | bytes 1056 | tf_op jit(solution)/shard_map/ppermute | solution.py:175
  285.9 15.3 %reduce-scatter.3.cloned.1.call-done = bf16[1,256,1024]{2,1,0:T(8,128)(2,1)} async-done(((bf16[4,256,1024]{2,1,0:T(8,128)(2,1)}), bf16[1,256,1024]{2,1,0:T(8,128)(2,1)}) %reduce-scatter.3.cloned.1.call-update) | async-done | bytes 524304 | tf_op jit(solution)/shard_map/reduce_scatter | solution.py:407
  301.2 45.5 %reduce-scatter.5.cloned.1.call-done = bf16[1,256,1024]{2,1,0:T(8,128)(2,1)} async-done(((bf16[4,256,1024]{2,1,0:T(8,128)(2,1)}), bf16[1,256,1024]{2,1,0:T(8,128)(2,1)}) %reduce-scatter.5.cloned.1.call-update) | async-done | bytes 524304 | tf_op jit(solution)/shard_map/reduce_scatter | solution.py:406
  346.7 1.8 fusion.11
  348.6 1.5 collective-permute-start.28
  351.5 0.6 collective-permute-start.24
  352.1 5.8 %collective-permute-done.28 = bf16[128,1024]{1,0:T(8,128)(2,1)S(1)} collective-permute-done((bf16[128,1024]{1,0:T(8,128)(2,1)S(1)}, bf16[128,1024]{1,0:T(8,128)(2,1)S(1)}, u32[]{:S(2)}, u32[]{:S(2)}) %collective-permute-start.28) | collective-permute-done | bytes 262176 | tf_op jit(solution)/shard_map/ppermute | solution.py:175
  358.0 1.5 collective-permute-start.31
  359.6 2.6 collective-permute-done.24
  362.3 0.6 add_bitcast_fusion
  363.0 1.1 pad_maximum_fusion.1
  364.3 1.1 pad_maximum_fusion
  (129 shorter events, 6.5 us)
Async XLA Ops:
  7.2 16.5 %copy-start.25 = (bf16[4,128,1024]{2,1,0:T(8,128)(2,1)S(1)}, bf16[4,128,1024]{2,1,0:T(8,128)(2,1)}, u32[]{:S(2)}) copy-start(bf16[4,128,1024]{2,1,0:T(8,128)(2,1)} %param.8) | copy-start | bytes 3145732
  7.2 16.5 %copy-start.26 = (bf16[4,128,1024]{2,1,0:T(8,128)(2,1)S(1)}, bf16[4,128,1024]{2,1,0:T(8,128)(2,1)}, u32[]{:S(2)}) copy-start(bf16[4,128,1024]{2,1,0:T(8,128)(2,1)} %param.9) | copy-start | bytes 3145732
  7.2 196.8 %all-gather.5.cloned.1.call-start = ((), (), s32[]{:S(2)}) async-start(), calls=%async_computation.4 | async-start | bytes 2621440 | tf_op jit(solution)/shard_map/all_gather | solution.py:377
  8.5 11.2 %collective-permute-start = (bf16[2,128,1024]{2,1,0:T(8,128)(2,1)S(1)}, bf16[2,128,1024]{2,1,0:T(8,128)(2,1)S(1)}, u32[]{:S(2)}, u32[]{:S(2)}) collective-permute-start(bf16[2,128,1024]{2,1,0:T(8,128)(2,1)S(1)} %slice.84), channel_id=1, source_target_pairs={{0,4},{4,0},{8,12},{12,8},{1,5},{5,1},{9,13},{13,9},{2,6},{6,2},{1... | collective-permute-start | bytes 1572872 | tf_op jit(solution)/shard_map/ppermute | solution.py:175
  21.5 8.0 %collective-permute-start.1 = (bf16[128,1024]{1,0:T(8,128)(2,1)}, bf16[128,1024]{1,0:T(8,128)(2,1)S(1)}, u32[]{:S(2)}, u32[]{:S(2)}) collective-permute-start(bf16[128,1024]{1,0:T(8,128)(2,1)} %fusion.16), channel_id=1, source_target_pairs={{0,8},{4,12},{8,0},{12,4},{1,9},{5,13},{9,1},{13,5},{2,10},{6,14},... | collective-permute-start | bytes 786440 | tf_op jit(solution)/shard_map/ppermute | solution.py:175
  23.7 11.3 %copy-start.27 = (bf16[128,1024]{1,0:T(8,128)(2,1)}, bf16[128,1024]{1,0:T(8,128)(2,1)S(1)}, u32[]{:S(2)}) copy-start(bf16[128,1024]{1,0:T(8,128)(2,1)S(1)} %get-tuple-element.32) | copy-start | bytes 786436
  31.2 3.8 %copy-start.29 = (bf16[128,1024]{1,0:T(8,128)(2,1)}, bf16[128,1024]{1,0:T(8,128)(2,1)S(1)}, u32[]{:S(2)}) copy-start(bf16[128,1024]{1,0:T(8,128)(2,1)S(1)} %fusion.19) | copy-start | bytes 786436
  32.1 198.8 %all-gather.7.cloned.1.call-start = ((), (), s32[]{:S(2)}) async-start(), calls=%async_computation.5 | async-start | bytes 2621440 | tf_op jit(solution)/shard_map/all_gather | solution.py:378
  33.0 6.2 %collective-permute-start.17 = (bf16[2,128,1024]{2,1,0:T(8,128)(2,1)}, bf16[2,128,1024]{2,1,0:T(8,128)(2,1)}, u32[]{:S(2)}, u32[]{:S(2)}) collective-permute-start(bf16[2,128,1024]{2,1,0:T(8,128)(2,1)} %slice.91), channel_id=1, source_target_pairs={{0,4},{4,0},{8,12},{12,8},{1,5},{5,1},{9,13},{13,9},{2,6},{6,2},{1... | collective-permute-start | bytes 1572872 | tf_op jit(solution)/shard_map/ppermute | solution.py:175
  33.0 107.1 %collective-permute-start.7 = (bf16[1024,1024]{1,0:T(8,128)(2,1)}, bf16[1024,1024]{1,0:T(8,128)(2,1)}, u32[]{:S(2)}, u32[]{:S(2)}) collective-permute-start(bf16[1024,1024]{1,0:T(8,128)(2,1)} %refs_6_.1), channel_id=1, source_target_pairs={{0,4},{4,0},{8,12},{12,8},{1,5},{5,1},{9,13},{13,9},{2,6},{6,2},{1... | collective-permute-start | bytes 6291464 | tf_op jit(solution)/shard_map/ppermute | solution.py:175
  33.5 4.9 %copy-start.23 = (bf16[1024,1024]{1,0:T(8,128)(2,1)S(1)}, bf16[1024,1024]{1,0:T(8,128)(2,1)}, u32[]{:S(2)}) copy-start(bf16[1024,1024]{1,0:T(8,128)(2,1)} %own.9) | copy-start | bytes 6291460
  35.0 76.3 %collective-permute-start.8 = (bf16[512,1024]{1,0:T(8,128)(2,1)S(1)}, bf16[512,1024]{1,0:T(8,128)(2,1)S(1)}, u32[]{:S(2)}, u32[]{:S(2)}) collective-permute-start(bf16[512,1024]{1,0:T(8,128)(2,1)S(1)} %constant_dynamic-slice_fusion.2), channel_id=1, source_target_pairs={{0,8},{4,12},{8,0},{12,4},{1,9},{5,13},{9,1},{13,5},{2,10},{6,14},... | collective-permute-start | bytes 3145736 | tf_op jit(solution)/shard_map/ppermute | solution.py:175
  36.9 5.0 %copy-start.24 = (bf16[1024,1024]{1,0:T(8,128)(2,1)S(1)}, bf16[1024,1024]{1,0:T(8,128)(2,1)}, u32[]{:S(2)}) copy-start(bf16[1024,1024]{1,0:T(8,128)(2,1)} %refs_0_.1) | copy-start | bytes 6291460
  36.9 75.6 %collective-permute-start.13 = (bf16[512,1024]{1,0:T(8,128)(2,1)S(1)}, bf16[512,1024]{1,0:T(8,128)(2,1)S(1)}, u32[]{:S(2)}, u32[]{:S(2)}) collective-permute-start(bf16[512,1024]{1,0:T(8,128)(2,1)S(1)} %constant_dynamic-slice_fusion.1), channel_id=1, source_target_pairs={{0,8},{4,12},{8,0},{12,4},{1,9},{5,13},{9,1},{13,5},{2,10},{6,14},... | collective-permute-start | bytes 3145736 | tf_op jit(solution)/shard_map/ppermute | solution.py:175
  38.6 73.9 %collective-permute-start.20 = (bf16[1024,512]{1,0:T(8,128)(2,1)S(1)}, bf16[1024,512]{1,0:T(8,128)(2,1)S(1)}, u32[]{:S(2)}, u32[]{:S(2)}) collective-permute-start(bf16[1024,512]{1,0:T(8,128)(2,1)S(1)} %constant_dynamic-slice_fusion), channel_id=1, source_target_pairs={{0,8},{4,12},{8,0},{12,4},{1,9},{5,13},{9,1},{13,5},{2,10},{6,14},... | collective-permute-start | bytes 3145736 | tf_op jit(solution)/shard_map/ppermute | solution.py:175
  39.3 164.0 %copy-start.34 = (f32[4096]{0:T(1024)S(1)}, f32[4096]{0:T(1024)}, u32[]{:S(2)}) copy-start(f32[4096]{0:T(1024)} %param.11) | copy-start | bytes 49156
  39.3 71.4 %collective-permute-start.18 = (bf16[128,1024]{1,0:T(8,128)(2,1)S(1)}, bf16[128,1024]{1,0:T(8,128)(2,1)S(1)}, u32[]{:S(2)}, u32[]{:S(2)}) collective-permute-start(bf16[128,1024]{1,0:T(8,128)(2,1)S(1)} %fusion.12), channel_id=1, source_target_pairs={{0,8},{4,12},{8,0},{12,4},{1,9},{5,13},{9,1},{13,5},{2,10},{6,14},... | collective-permute-start | bytes 786440 | tf_op jit(solution)/shard_map/ppermute | solution.py:175
  110.7 24.3 %collective-permute-start.3 = (bf16[512,1024]{1,0:T(8,128)(2,1)S(1)}, bf16[512,1024]{1,0:T(8,128)(2,1)}, u32[]{:S(2)}, u32[]{:S(2)}) collective-permute-start(bf16[512,1024]{1,0:T(8,128)(2,1)S(1)} %constant_dynamic-slice_fusion.3), channel_id=1, source_target_pairs={{0,8},{4,12},{8,0},{12,4},{1,9},{5,13},{9,1},{13,5},{2,10},{6,14},... | collective-permute-start | bytes 3145736 | tf_op jit(solution)/shard_map/ppermute | solution.py:175
  111.3 27.3 %copy-start = (bf16[512,1024]{1,0:T(8,128)(2,1)}, bf16[512,1024]{1,0:T(8,128)(2,1)S(1)}, u32[]{:S(2)}) copy-start(bf16[512,1024]{1,0:T(8,128)(2,1)S(1)} %collective-permute-done.8.xh.refs_8_) | copy-start | bytes 3145732
  111.3 25.3 %collective-permute-start.9 = (bf16[512,1024]{1,0:T(8,128)(2,1)S(1)}, bf16[512,1024]{1,0:T(8,128)(2,1)S(1)}, u32[]{:S(2)}, u32[]{:S(2)}) collective-permute-start(bf16[512,1024]{1,0:T(8,128)(2,1)S(1)} %collective-permute-done.8.xh.refs_8_), channel_id=1, source_target_pairs={{0,16},{16,0},{1,17},{17,1},{2,18},{18,2},{3,19},{19,3},{4,20},{20... | collective-permute-start | bytes 3145736 | tf_op jit(solution)/shard_map/ppermute | solution.py:175
  112.5 93.7 %copy-start.2 = (bf16[512,1024]{1,0:T(8,128)(2,1)}, bf16[512,1024]{1,0:T(8,128)(2,1)S(1)}, u32[]{:S(2)}) copy-start(bf16[512,1024]{1,0:T(8,128)(2,1)S(1)} %collective-permute-done.13.xh.refs_14_) | copy-start | bytes 3145732
  112.5 26.1 %collective-permute-start.10 = (bf16[512,1024]{1,0:T(8,128)(2,1)S(1)}, bf16[512,1024]{1,0:T(8,128)(2,1)S(1)}, u32[]{:S(2)}, u32[]{:S(2)}) collective-permute-start(bf16[512,1024]{1,0:T(8,128)(2,1)S(1)} %collective-permute-done.8.xh.refs_8_), channel_id=1, source_target_pairs={{0,4},{4,0},{8,12},{12,8},{1,5},{5,1},{9,13},{13,9},{2,6},{6,2},{1... | collective-permute-start | bytes 3145736 | tf_op jit(solution)/shard_map/ppermute | solution.py:175
  112.5 49.2 %collective-permute-start.12 = (bf16[1024,1024]{1,0:T(8,128)(2,1)}, bf16[1024,1024]{1,0:T(8,128)(2,1)}, u32[]{:S(2)}, u32[]{:S(2)}) collective-permute-start(bf16[1024,1024]{1,0:T(8,128)(2,1)} %refs_12_.1), channel_id=1, source_target_pairs={{0,4},{4,0},{8,12},{12,8},{1,5},{5,1},{9,13},{13,9},{2,6},{6,2},{1... | collective-permute-start | bytes 6291464 | tf_op jit(solution)/shard_map/ppermute | solution.py:175
  135.0 26.2 %collective-permute-start.14 = (bf16[512,1024]{1,0:T(8,128)(2,1)S(1)}, bf16[512,1024]{1,0:T(8,128)(2,1)}, u32[]{:S(2)}, u32[]{:S(2)}) collective-permute-start(bf16[512,1024]{1,0:T(8,128)(2,1)S(1)} %collective-permute-done.13.xh.refs_14_), channel_id=1, source_target_pairs={{0,16},{16,0},{1,17},{17,1},{2,18},{18,2},{3,19},{19,3},{4,20},{20... | collective-permute-start | bytes 3145736 | tf_op jit(solution)/shard_map/ppermute | solution.py:175
  136.5 1.0 copy-start.4
  137.5 23.7 %collective-permute-start.15 = (bf16[512,1024]{1,0:T(8,128)(2,1)S(1)}, bf16[512,1024]{1,0:T(8,128)(2,1)}, u32[]{:S(2)}, u32[]{:S(2)}) collective-permute-start(bf16[512,1024]{1,0:T(8,128)(2,1)S(1)} %collective-permute-done.13.xh.refs_14_), channel_id=1, source_target_pairs={{0,4},{4,0},{8,12},{12,8},{1,5},{5,1},{9,13},{13,9},{2,6},{6,2},{1... | collective-permute-start | bytes 3145736 | tf_op jit(solution)/shard_map/ppermute | solution.py:175
  138.6 3.1 copy-start.31
  138.6 1.0 copy-start.6
  139.6 43.9 %collective-permute-start.21 = (bf16[1024,512]{1,0:T(8,128)(2,1)S(1)}, bf16[1024,512]{1,0:T(8,128)(2,1)S(1)}, u32[]{:S(2)}, u32[]{:S(2)}) collective-permute-start(bf16[1024,512]{1,0:T(8,128)(2,1)S(1)} %collective-permute-done.20.xh), channel_id=1, source_target_pairs={{0,16},{16,0},{1,17},{17,1},{2,18},{18,2},{3,19},{19,3},{4,20},{20... | collective-permute-start | bytes 3145736 | tf_op jit(solution)/shard_map/ppermute | solution.py:175
  140.1 63.2 %collective-permute-start.4 = (bf16[512,1024]{1,0:T(8,128)(2,1)}, bf16[512,1024]{1,0:T(8,128)(2,1)}, u32[]{:S(2)}, u32[]{:S(2)}) collective-permute-start(bf16[512,1024]{1,0:T(8,128)(2,1)} %collective-permute-done.3.xh.refs_2_), channel_id=1, source_target_pairs={{0,16},{16,0},{1,17},{17,1},{2,18},{18,2},{3,19},{19,3},{4,20},{20... | collective-permute-start | bytes 3145736 | tf_op jit(solution)/shard_map/ppermute | solution.py:175
  142.6 158.7 %reduce-scatter.3.cloned.1.call-start = ((), (), s32[]{:S(2)}) async-start(), calls=%async_computation.2 | async-start | bytes 2621440 | tf_op jit(solution)/shard_map/reduce_scatter | solution.py:407
  161.2 42.2 %collective-permute-start.5 = (bf16[512,1024]{1,0:T(8,128)(2,1)}, bf16[512,1024]{1,0:T(8,128)(2,1)}, u32[]{:S(2)}, u32[]{:S(2)}) collective-permute-start(bf16[512,1024]{1,0:T(8,128)(2,1)} %collective-permute-done.3.xh.refs_2_), channel_id=1, source_target_pairs={{0,4},{4,0},{8,12},{12,8},{1,5},{5,1},{9,13},{13,9},{2,6},{6,2},{1... | collective-permute-start | bytes 3145736 | tf_op jit(solution)/shard_map/ppermute | solution.py:175
  161.2 61.7 %collective-permute-start.2 = (bf16[1024,1024]{1,0:T(8,128)(2,1)}, bf16[1024,1024]{1,0:T(8,128)(2,1)}, u32[]{:S(2)}, u32[]{:S(2)}) collective-permute-start(bf16[1024,1024]{1,0:T(8,128)(2,1)} %refs_0_.1), channel_id=1, source_target_pairs={{0,4},{4,0},{8,12},{12,8},{1,5},{5,1},{9,13},{13,9},{2,6},{6,2},{1... | collective-permute-start | bytes 6291464 | tf_op jit(solution)/shard_map/ppermute | solution.py:175
  161.7 44.5 %collective-permute-start.11 = (bf16[512,1024]{1,0:T(8,128)(2,1)}, bf16[512,1024]{1,0:T(8,128)(2,1)}, u32[]{:S(2)}, u32[]{:S(2)}) collective-permute-start(bf16[512,1024]{1,0:T(8,128)(2,1)} %copy-done.4), channel_id=1, source_target_pairs={{0,4},{4,0},{8,12},{12,8},{1,5},{5,1},{9,13},{13,9},{2,6},{6,2},{1... | collective-permute-start | bytes 3145736 | tf_op jit(solution)/shard_map/ppermute | solution.py:175
  183.6 22.8 %collective-permute-start.16 = (bf16[512,1024]{1,0:T(8,128)(2,1)}, bf16[512,1024]{1,0:T(8,128)(2,1)}, u32[]{:S(2)}, u32[]{:S(2)}) collective-permute-start(bf16[512,1024]{1,0:T(8,128)(2,1)} %collective-permute-done.14.yh.refs_15_), channel_id=1, source_target_pairs={{0,4},{4,0},{8,12},{12,8},{1,5},{5,1},{9,13},{13,9},{2,6},{6,2},{1... | collective-permute-start | bytes 3145736 | tf_op jit(solution)/shard_map/ppermute | solution.py:175
  203.3 27.6 %collective-permute-start.19 = (bf16[1024,1024]{1,0:T(8,128)(2,1)}, bf16[1024,1024]{1,0:T(8,128)(2,1)}, u32[]{:S(2)}, u32[]{:S(2)}) collective-permute-start(bf16[1024,1024]{1,0:T(8,128)(2,1)} %own.9), channel_id=1, source_target_pairs={{0,4},{4,0},{8,12},{12,8},{1,5},{5,1},{9,13},{13,9},{2,6},{6,2},{1... | collective-permute-start | bytes 6291464 | tf_op jit(solution)/shard_map/ppermute | solution.py:175
  203.4 19.5 %collective-permute-start.6 = (bf16[512,1024]{1,0:T(8,128)(2,1)}, bf16[512,1024]{1,0:T(8,128)(2,1)}, u32[]{:S(2)}, u32[]{:S(2)}) collective-permute-start(bf16[512,1024]{1,0:T(8,128)(2,1)} %collective-permute-done.4.yh.refs_3_), channel_id=1, source_target_pairs={{0,4},{4,0},{8,12},{12,8},{1,5},{5,1},{9,13},{13,9},{2,6},{6,2},{1... | collective-permute-start | bytes 3145736 | tf_op jit(solution)/shard_map/ppermute | solution.py:175
  204.0 2.8 copy-start.21
  206.2 24.7 %collective-permute-start.22 = (bf16[1024,512]{1,0:T(8,128)(2,1)S(1)}, bf16[1024,512]{1,0:T(8,128)(2,1)S(1)}, u32[]{:S(2)}, u32[]{:S(2)}) collective-permute-start(bf16[1024,512]{1,0:T(8,128)(2,1)S(1)} %collective-permute-done.20.xh), channel_id=1, source_target_pairs={{0,4},{4,0},{8,12},{12,8},{1,5},{5,1},{9,13},{13,9},{2,6},{6,2},{1... | collective-permute-start | bytes 3145736 | tf_op jit(solution)/shard_map/ppermute | solution.py:175
  206.3 24.6 %collective-permute-start.23 = (bf16[1024,512]{1,0:T(8,128)(2,1)S(1)}, bf16[1024,512]{1,0:T(8,128)(2,1)}, u32[]{:S(2)}, u32[]{:S(2)}) collective-permute-start(bf16[1024,512]{1,0:T(8,128)(2,1)S(1)} %collective-permute-done.21.yh), channel_id=1, source_target_pairs={{0,4},{4,0},{8,12},{12,8},{1,5},{5,1},{9,13},{13,9},{2,6},{6,2},{1... | collective-permute-start | bytes 3145736 | tf_op jit(solution)/shard_map/ppermute | solution.py:175
  206.8 2.1 copy-start.1
  206.8 2.1 copy-start.5
  206.8 2.2 copy-start.7
  209.1 6.4 %copy-start.3 = (bf16[512,1024]{1,0:T(8,128)(2,1)S(1)}, bf16[512,1024]{1,0:T(8,128)(2,1)}, u32[]{:S(2)}) copy-start(bf16[512,1024]{1,0:T(8,128)(2,1)} %copy-done.2) | copy-start | bytes 3145732
  215.4 6.7 %copy-start.14 = (bf16[256,1024]{1,0:T(8,128)(2,1)}, bf16[256,1024]{1,0:T(8,128)(2,1)S(1)}, u32[]{:S(2)}) copy-start(bf16[256,1024]{1,0:T(8,128)(2,1)S(1)} %shard_map.104.k_ref) | copy-start | bytes 1572868
  231.0 7.3 %copy-start.15 = (bf16[256,1024]{1,0:T(8,128)(2,1)S(1)}, bf16[256,1024]{1,0:T(8,128)(2,1)}, u32[]{:S(2)}) copy-start(bf16[256,1024]{1,0:T(8,128)(2,1)} %copy-done.14) | copy-start | bytes 1572868
  231.0 7.3 %copy-start.17 = (bf16[256,1024]{1,0:T(8,128)(2,1)S(1)}, bf16[256,1024]{1,0:T(8,128)(2,1)}, u32[]{:S(2)}) copy-start(bf16[256,1024]{1,0:T(8,128)(2,1)} %copy-done.16) | copy-start | bytes 1572868
  231.0 7.3 %copy-start.19 = (bf16[256,1024]{1,0:T(8,128)(2,1)S(1)}, bf16[256,1024]{1,0:T(8,128)(2,1)}, u32[]{:S(2)}) copy-start(bf16[256,1024]{1,0:T(8,128)(2,1)} %copy-done.18) | copy-start | bytes 1572868
  256.3 1.0 copy-start.9
  256.3 1.2 copy-start.11
  256.3 1.4 copy-start.13
  256.4 90.3 %reduce-scatter.5.cloned.1.call-start = ((), (), s32[]{:S(2)}) async-start(), calls=%async_computation.3 | async-start | bytes 2621440 | tf_op jit(solution)/shard_map/reduce_scatter | solution.py:406
  271.1 1.6 copy-start.22
  272.7 73.9 %copy-start.28 = (bf16[128,1024]{1,0:T(8,128)(2,1)S(1)}, bf16[128,1024]{1,0:T(8,128)(2,1)}, u32[]{:S(2)}) copy-start(bf16[128,1024]{1,0:T(8,128)(2,1)} %copy-done.27) | copy-start | bytes 786436
  272.7 73.9 %copy-start.30 = (bf16[128,1024]{1,0:T(8,128)(2,1)S(1)}, bf16[128,1024]{1,0:T(8,128)(2,1)}, u32[]{:S(2)}) copy-start(bf16[128,1024]{1,0:T(8,128)(2,1)} %copy-done.29) | copy-start | bytes 786436
  272.7 73.9 %copy-start.32 = (bf16[128,1024]{1,0:T(8,128)(2,1)S(1)}, bf16[128,1024]{1,0:T(8,128)(2,1)}, u32[]{:S(2)}) copy-start(bf16[128,1024]{1,0:T(8,128)(2,1)} %copy-done.31) | copy-start | bytes 786436
  275.4 4.8 %collective-permute-start.26 = (f32[2,128]{1,0:T(2,128)S(1)}, f32[2,128]{1,0:T(2,128)S(1)}, u32[]{:S(2)}, u32[]{:S(2)}) collective-permute-start(f32[2,128]{1,0:T(2,128)S(1)} %bitcast.104), channel_id=1, source_target_pairs={{0,1},{1,0},{2,3},{3,2},{4,5},{5,4},{6,7},{7,6},{8,9},{9,8},{10,11... | collective-permute-start | bytes 3080 | tf_op jit(solution)/shard_map/ppermute | solution.py:175
  280.2 5.7 %collective-permute-start.27 = (f32[2,128]{1,0:T(2,128)S(1)}, f32[2,128]{1,0:T(2,128)S(1)}, u32[]{:S(2)}, u32[]{:S(2)}) collective-permute-start(f32[2,128]{1,0:T(2,128)S(1)} %bitcast_add_fusion.1), channel_id=1, source_target_pairs={{0,2},{1,3},{2,0},{3,1},{4,6},{5,7},{6,4},{7,5},{8,10},{9,11},{10,... | collective-permute-start | bytes 3080 | tf_op jit(solution)/shard_map/ppermute | solution.py:175
  348.6 9.3 %collective-permute-start.28 = (bf16[128,1024]{1,0:T(8,128)(2,1)S(1)}, bf16[128,1024]{1,0:T(8,128)(2,1)S(1)}, u32[]{:S(2)}, u32[]{:S(2)}) collective-permute-start(bf16[128,1024]{1,0:T(8,128)(2,1)S(1)} %get-tuple-element.26), channel_id=1, source_target_pairs={{0,8},{4,12},{8,0},{12,4},{1,9},{5,13},{9,1},{13,5},{2,10},{6,14},... | collective-permute-start | bytes 786440 | tf_op jit(solution)/shard_map/ppermute | solution.py:175
  351.3 6.7 %collective-permute-start.30 = (f32[8,128]{1,0:T(8,128)S(1)}, f32[8,128]{1,0:T(8,128)S(1)}, u32[]{:S(2)}, u32[]{:S(2)}) collective-permute-start(f32[8,128]{1,0:T(8,128)S(1)} %bitcast.103), channel_id=1, source_target_pairs={{0,4},{4,0},{8,12},{12,8},{1,5},{5,1},{9,13},{13,9},{2,6},{6,2},{1... | collective-permute-start | bytes 12296 | tf_op jit(solution)/shard_map/ppermute | solution.py:175
  351.5 10.7 %collective-permute-start.24 = (bf16[128,1024]{1,0:T(8,128)(2,1)S(1)}, bf16[128,1024]{1,0:T(8,128)(2,1)S(1)}, u32[]{:S(2)}, u32[]{:S(2)}) collective-permute-start(bf16[128,1024]{1,0:T(8,128)(2,1)S(1)} %get-tuple-element.30), channel_id=1, source_target_pairs={{0,8},{4,12},{8,0},{12,4},{1,9},{5,13},{9,1},{13,5},{2,10},{6,14},... | collective-permute-start | bytes 786440 | tf_op jit(solution)/shard_map/ppermute | solution.py:175
  357.9 5.0 %collective-permute-start.29 = (bf16[2,128,1024]{2,1,0:T(8,128)(2,1)S(1)}, bf16[2,128,1024]{2,1,0:T(8,128)(2,1)S(1)}, u32[]{:S(2)}, u32[]{:S(2)}) collective-permute-start(bf16[2,128,1024]{2,1,0:T(8,128)(2,1)S(1)} %pad_maximum_fusion.5), channel_id=1, source_target_pairs={{0,4},{4,0},{8,12},{12,8},{1,5},{5,1},{9,13},{13,9},{2,6},{6,2},{1... | collective-permute-start | bytes 1572872 | tf_op jit(solution)/shard_map/ppermute | solution.py:175
  358.0 4.3 %collective-permute-start.31 = (f32[8,128]{1,0:T(8,128)S(1)}, f32[8,128]{1,0:T(8,128)S(1)}, u32[]{:S(2)}, u32[]{:S(2)}) collective-permute-start(f32[8,128]{1,0:T(8,128)S(1)} %bitcast_add_fusion), channel_id=1, source_target_pairs={{0,8},{4,12},{8,0},{12,4},{1,9},{5,13},{9,1},{13,5},{2,10},{6,14},... | collective-permute-start | bytes 12296 | tf_op jit(solution)/shard_map/ppermute | solution.py:175
  362.2 2.0 collective-permute-start.25
  (7 other events, 5.5 us)
Sparse Core Ops, SparseCore 0:
  32.3 46.2 all-gather.4
  142.7 45.8 all-gather.6
  256.5 44.6 reduce-scatter.2
  303.5 43.1 reduce-scatter.4

commit v2 on v0

--- a/solution.py
+++ b/solution.py
@@ -1,13 +1,14 @@
 import jax
 import jax.numpy as jnp
 from jax import lax
+from jax.experimental import pallas as pl
+from jax.experimental.pallas import tpu as pltpu
 from jax.sharding import PartitionSpec as P
 
 HD = 64
 BAL = 2
-
-
 EPSILON = 1e-06
+VMEM_LIMIT = 50 * 2**20
 
 
 def entering(shard, axis, combine, identity):
@@ -27,7 +28,7 @@
     return earlier + later
 
 
-def body(passages, cotangent, passage_counts, norm_gain, w_query, w_key, w_value, w_out):
+def general_body(passages, cotangent, passage_counts, norm_gain, w_query, w_key, w_value, w_out):
     peer_total = lax.axis_size("pas")
     slots, seq_len, part_width = passages.shape
     flat_width = seq_len * part_width
@@ -170,6 +171,361 @@
     return (encoded, input_grad, gain_grad)
 
 
+def swap(array, axis, bit):
+    return lax.ppermute(array, axis, [(i, i ^ bit) for i in range(lax.axis_size(axis))])
+
+
+def dot_nn(a, b):
+    return jnp.dot(a, b, preferred_element_type=jnp.float32)
+
+
+def dot_nt(a, b):
+    return lax.dot_general(a, b, (((1,), (1,)), ((), ())), preferred_element_type=jnp.float32)
+
+
+def dot_tn(a, b):
+    return lax.dot_general(a, b, (((0,), (0,)), ((), ())), preferred_element_type=jnp.float32)
+
+
+def stream(weights, pos, held, sems):
+    started = {}
+    for i in range(4):
+        for w, pieces in enumerate(weights):
+            piece = pieces[i]
+            if isinstance(piece, list):
+                parts = []
+                for j, chunk in enumerate(piece):
+                    size = chunk.shape[0]
+                    at = pl.multiple_of((j ^ (2 * pos[1])) * size, size)
+                    parts.append((chunk, held.at[w, i, pl.ds(at, size)], sems.at[w, i, j]))
+            else:
+                parts = [(piece, held.at[w, i], sems.at[w, i, 0])]
+            started[w, i] = [pltpu.make_async_copy(*part) for part in parts]
+            for copy in started[w, i]:
+                copy.start()
+
+    def ready(w, i):
+        for copy in started[w, i]:
+            copy.wait()
+        return held[w, i]
+
+    return ready
+
+
+def project_kernel(weights, pos, dense, out, held, sems):
+    ready = stream(weights, pos, held, sems)
+    total = 0.0
+    for i in range(4):
+        total += dot_nn(dense[0][pos[0] ^ i], ready(0, i))
+    out[...] = total.astype(out.dtype)
+
+
+def project_out_kernel(weights, pos, dense, out, held, sems):
+    ready = stream(weights, pos, held, sems)
+    total = 0.0
+    for i in range(4):
+        total += dot_nt(dense[0][pos[0] ^ i], ready(0, i))
+    out[...] = total.astype(out.dtype)
+
+
+def emit_kernel(weights, pos, dense, out, held, sems):
+    ready = stream(weights, pos, held, sems)
+    rows = dense[0][...]
+    for i in range(4):
+        out[pos[0] ^ i] = dot_nn(rows, ready(0, i)).astype(out.dtype)
+
+
+def back_kernel(weights, pos, dense, out, held, sems):
+    ready = stream(weights, pos, held, sems)
+    grads = [d[...] for d in dense]
+    for i in range(4):
+        total = sum(dot_nt(g, ready(w, i)) for w, g in enumerate(grads))
+        out[pos[0] ^ i] = total.astype(out.dtype)
+
+
+def call(kernel, pos, dense, weights, out_shape):
+    flat, tree = jax.tree.flatten(weights)
+    count = len(weights)
+
+    def run(pos_ref, *refs):
+        dense_refs = refs[: len(dense)]
+        weight_refs = jax.tree.unflatten(tree, refs[len(dense) : len(dense) + len(flat)])
+        out, held, sems = refs[len(dense) + len(flat) :]
+        kernel(weight_refs, pos_ref, dense_refs, out, held, sems)
+
+    size = count * 2**22
+    return pl.pallas_call(
+        run,
+        in_specs=[pl.BlockSpec(memory_space=pltpu.SMEM)]
+        + [pl.BlockSpec(memory_space=pltpu.VMEM)] * len(dense)
+        + [pl.BlockSpec(memory_space=pl.ANY)] * len(flat),
+        out_specs=pl.BlockSpec(memory_space=pltpu.VMEM),
+        out_shape=out_shape,
+        scratch_shapes=[
+            pltpu.VMEM((count, 4, 1024, 1024), jnp.bfloat16),
+            pltpu.SemaphoreType.DMA((count, 4, 4)),
+        ],
+        cost_estimate=pl.CostEstimate(flops=512 * size, bytes_accessed=2 * size, transcendentals=0),
+        compiler_params=pltpu.CompilerParams(vmem_limit_bytes=VMEM_LIMIT),
+    )(pos, *dense, *flat)
+
+
+def head_pairs(width):
+    return [pl.ds(pair * 128, 128) for pair in range(width // 128)]
+
+
+def first_head(seq):
+    return lax.broadcasted_iota(jnp.int32, (seq, 128), 1) < HD
+
+
+def split_heads(array):
+    first = first_head(array.shape[0])
+    mask0 = jnp.where(first, 1.0, 0.0).astype(array.dtype)
+    mask1 = jnp.where(first, 0.0, 1.0).astype(array.dtype)
+    return jnp.concatenate([array * mask0, array * mask1], axis=0)
+
+
+def join_heads(both):
+    seq = both.shape[0] // 2
+    return jnp.where(first_head(seq), both[:seq], both[seq:])
+
+
+def softmax_pair(scores):
+    seq = scores.shape[0]
+    probs = []
+    for h in range(2):
+        s = scores[:, h * seq : (h + 1) * seq]
+        e = jnp.exp(s - jnp.max(s, axis=-1, keepdims=True))
+        probs.append(e / jnp.sum(e, axis=-1, keepdims=True))
+    return probs
+
+
+def attention_kernel(q_ref, k_ref, v_ref, ctx_ref):
+    for at in head_pairs(q_ref.shape[1]):
+        probs = softmax_pair(dot_nt(q_ref[:, at], split_heads(k_ref[:, at])))
+        low = jnp.concatenate([p.astype(jnp.bfloat16) for p in probs], axis=1)
+        ctx_ref[:, at] = dot_nn(low, split_heads(v_ref[:, at])).astype(jnp.bfloat16)
+
+
+def attention_back_kernel(q_ref, k_ref, v_ref, dc_ref, dq_ref, dk_ref, dv_ref):
+    seq = q_ref.shape[0]
+    for at in head_pairs(q_ref.shape[1]):
+        q, dc = q_ref[:, at], dc_ref[:, at]
+        keys = split_heads(k_ref[:, at])
+        probs = softmax_pair(dot_nt(q, keys))
+        d_probs = dot_nt(dc, split_heads(v_ref[:, at]))
+        d_scores = []
+        for h in range(2):
+            dp = d_probs[:, h * seq : (h + 1) * seq]
+            ds = probs[h] * (dp - jnp.sum(dp * probs[h], axis=-1, keepdims=True))
+            d_scores.append(ds.astype(jnp.bfloat16))
+        low = jnp.concatenate([p.astype(jnp.bfloat16) for p in probs], axis=1)
+        ds = jnp.concatenate(d_scores, axis=1)
+        dq_ref[:, at] = dot_nn(ds, keys).astype(jnp.bfloat16)
+        dv_ref[:, at] = join_heads(dot_tn(low, dc)).astype(jnp.bfloat16)
+        dk_ref[:, at] = join_heads(dot_tn(ds, q)).astype(jnp.bfloat16)
+
+
+def attend(kernel, arrays, outputs):
+    rows, cols = arrays[0].shape
+    spec = pl.BlockSpec((rows // BAL, cols // 2), lambda i, j: (i, j))
+    shape = jax.ShapeDtypeStruct((rows, cols), jnp.bfloat16)
+    many = len(arrays) + outputs
+    return pl.pallas_call(
+        kernel,
+        grid=(BAL, 2),
+        in_specs=[spec] * len(arrays),
+        out_specs=[spec] * outputs,
+        out_shape=[shape] * outputs,
+        cost_estimate=pl.CostEstimate(
+            flops=32 * 8 * 128 * 128 * 128, bytes_accessed=many * 2 * rows * cols, transcendentals=2**19
+        ),
+        compiler_params=pltpu.CompilerParams(vmem_limit_bytes=VMEM_LIMIT),
+    )(*arrays)
+
+
+ANYWHERE = pl.BlockSpec(memory_space=pl.ANY)
+
+
+def cut(weight, block, earlier):
+    def copy(block_ref, rows, *refs):
+        refs[-1][...] = rows[...]
+
+    return pl.pallas_call(
+        copy,
+        grid_spec=pltpu.PrefetchScalarGridSpec(
+            num_scalar_prefetch=1,
+            grid=(1,),
+            in_specs=[pl.BlockSpec((256, 1024), lambda i, block: (block[0], 0))]
+            + [ANYWHERE] * len(earlier),
+            out_specs=pl.BlockSpec((256, 1024), lambda i, block: (0, 0)),
+        ),
+        out_shape=jax.ShapeDtypeStruct((256, 1024), weight.dtype),
+        cost_estimate=pl.CostEstimate(flops=0, bytes_accessed=2**20, transcendentals=0),
+    )(block.reshape(1), weight, *earlier)
+
+
+def after(array, *earlier):
+    def nothing(*refs):
+        pass
+
+    return pl.pallas_call(
+        nothing,
+        in_specs=[ANYWHERE] * (1 + len(earlier)),
+        out_specs=ANYWHERE,
+        out_shape=jax.ShapeDtypeStruct(array.shape, array.dtype),
+        input_output_aliases={0: 0},
+    )(array, *earlier)
+
+
+def far_block(chunks, group):
+    low, high = jnp.concatenate(chunks[:2]), jnp.concatenate(chunks[2:])
+    return jnp.where(group == 0, jnp.concatenate([low, high]), jnp.concatenate([high, low]))
+
+
+def fast_body(passages, cotangent, passage_counts, norm_gain, w_query, w_key, w_value, w_out):
+    me = lax.axis_index("pas")
+    group = lax.axis_index("grp")
+    feature = lax.axis_index("fsdp")
+    seq = passages.shape[1]
+    pos = jnp.stack([me, group]).astype(jnp.int32)
+
+    counts = lax.all_gather(passage_counts, "pas", axis=0, tiled=True)
+    index = jnp.arange(4, dtype=jnp.int32)
+    single = counts == 1
+    source = jnp.sum(jnp.where(counts == 4, index, 0))
+    rank = lambda d: jnp.minimum(jnp.sum((single & (index < d)).astype(jnp.int32)), 1)
+    host0 = jnp.min(jnp.where(single, index, 4))
+    host1 = jnp.max(jnp.where(single, index, -1))
+    own_count = passage_counts[0]
+    relation = me ^ source
+
+    def send_second(array):
+        extra = array[2:4]
+        extra_core = swap(extra, "pas", 1)
+        there = rank(me ^ 2)
+        picked = jnp.where(source == me, extra, extra_core)
+        return extra_core, jnp.where(there == 0, picked[0], picked[1])
+
+    def second(array, extra_core, got_x):
+        from_core = jnp.where(rank(me) == 0, extra_core[0], extra_core[1])
+        foreign = jnp.where(relation == 1, from_core, got_x)
+        return jnp.where(own_count >= 2, array[1], foreign)
+
+    weights = (w_key, w_query, w_value, w_out)
+    over_x, over_y = [], []
+
+    def send(*earlier):
+        i = len(over_x)
+        chunk = cut(weights[i // 2], group * 2 + i % 2, earlier)
+        over_x.append(swap(chunk, "pas", 2))
+
+    def forward():
+        over_y.append(swap(over_x[len(over_y)], "grp", 1))
+
+    def fetch(i):
+        far = far_block(over_x[i : i + 2] + over_y[i : i + 2], group)
+        return [weights[i // 2], swap(weights[i // 2], "pas", 1), far, swap(far, "pas", 1)]
+
+    send()
+    tokens_core, tokens_sent = send_second(passages)
+    grads_core, grads_sent = send_second(cotangent)
+    tokens_x = swap(tokens_sent, "pas", 2)
+    grads_x = swap(grads_sent, "pas", 2)
+    tokens = jnp.concatenate([passages[0], second(passages, tokens_core, tokens_x)], axis=0)
+    grads = jnp.concatenate([cotangent[0], second(cotangent, grads_core, grads_x)], axis=0)
+    all_tokens = lax.all_gather(tokens, "fsdp", axis=0)
+    all_grads = lax.all_gather(grads, "fsdp", axis=0)
+
+    tokens_f32 = all_tokens.astype(jnp.float32)
+    width = norm_gain.shape[0]
+    gain = norm_gain.reshape(4, 1, 1024)
+    inverse = lax.rsqrt(
+        jnp.sum(tokens_f32 * tokens_f32, axis=(0, 2), keepdims=True) / width + EPSILON
+    )
+    normed = (tokens_f32 * inverse * gain).astype(jnp.bfloat16)
+
+    rows_shape = jax.ShapeDtypeStruct((2 * seq, 1024), jnp.bfloat16)
+    wide_shape = jax.ShapeDtypeStruct((4, 2 * seq, 1024), jnp.bfloat16)
+
+    def project(w):
+        return call(project_kernel, pos, [normed], [w], rows_shape)
+
+    send(tokens_sent, grads_sent)
+    forward()
+    send(over_x[0], tokens_x, grads_x)
+    forward()
+    send(over_x[1], over_y[0], grads)
+    key_w = fetch(0)
+    forward()
+    send(over_x[2], over_y[1])
+    forward()
+    send(over_x[3], over_y[2])
+    query_w = fetch(2)
+    forward()
+    keys = project(key_w)
+    send(over_x[4], over_y[3], keys)
+    forward()
+    query = project(query_w)
+    send(over_x[5], over_y[4], query)
+    value_w = fetch(4)
+    forward()
+    forward()
+    far = over_x[6:] + over_y[6:]
+    out_w = [w_out, swap(w_out, "pas", 1), far, [swap(c, "pas", 1) for c in far]]
+    values = project(value_w)
+    (context,) = attend(attention_kernel, (query, keys, values), 1)
+    partial_out = call(emit_kernel, pos, [context], [out_w], wide_shape)
+    attention = lax.psum_scatter(partial_out, "fsdp", scatter_dimension=0)
+    d_context = call(project_out_kernel, pos, [after(all_grads, partial_out)], [out_w], rows_shape)
+    d_query, d_keys, d_values = attend(attention_back_kernel, (query, keys, values, d_context), 3)
+    d_normed = call(
+        back_kernel, pos, [d_query, d_keys, d_values], [query_w, key_w, value_w], wide_shape
+    )
+
+    d_normed = after(d_normed, attention)
+    d_part = lax.psum_scatter(d_normed, "fsdp", scatter_dimension=0).astype(jnp.float32)
+
+    row_total = jnp.sum(
+        d_normed.astype(jnp.float32) * gain * (tokens_f32 * inverse), axis=(0, 2)
+    ).reshape(2, seq)
+    row_total += swap(row_total, "fsdp", 1)
+    row_total += swap(row_total, "fsdp", 2)
+    row_mean = row_total.reshape(2 * seq, 1) / width
+
+    gain_part = lax.dynamic_slice_in_dim(norm_gain, feature * 1024, 1024, 0)
+    inverse_rows = inverse.reshape(2 * seq, 1)
+    unit_part = tokens.astype(jnp.float32) * inverse_rows
+    d_tokens = inverse_rows * (d_part * gain_part - unit_part * row_mean)
+    input_local = (grads.astype(jnp.float32) + d_tokens).astype(jnp.bfloat16)
+    states = (tokens.astype(jnp.float32) + attention.astype(jnp.float32)).astype(jnp.bfloat16)
+    gain_grad = jnp.sum(d_part * unit_part, axis=0).reshape(8, 128)
+    gain_grad += swap(gain_grad, "pas", 1)
+    gain_grad += swap(gain_grad, "pas", 2)
+
+    def home(local):
+        local = local.reshape(2, seq, 1024)
+        back = local[1]
+        over_x = swap(back, "pas", 2)
+        over_core = swap(jnp.stack([back, over_x]), "pas", 1)
+
+        def pick(host):
+            way = host ^ me
+            return jnp.where(way == 1, over_core[0], jnp.where(way == 2, over_x, over_core[1]))
+
+        zero = jnp.zeros_like(back)
+        return jnp.stack(
+            [
+                local[0],
+                jnp.where(own_count >= 2, back, zero),
+                jnp.where(own_count == 4, pick(host0), zero),
+                jnp.where(own_count == 4, pick(host1), zero),
+            ]
+        )
+
+    return home(states), home(input_local), gain_grad.reshape(1024)
+
+
 def solution(mesh):
     placed = (
         P(("grp", "pas"), None, "fsdp"),
@@ -181,8 +537,10 @@
         P("pas", "fsdp"),
         P("fsdp", "pas"),
     )
+    sizes = dict(mesh.shape)
+    fast = sizes["grp"] == 2 and sizes["pas"] == 4 and sizes["fsdp"] == 4
     return jax.shard_map(
-        body,
+        fast_body if fast else general_body,
         mesh=mesh,
         in_specs=placed,
         out_specs=(

time: 546 us -> 323 us (0.59); the launches traced: 536 us -> 322 us
  waiting for transfers between devices: 319 us -> 155 us
  Pallas kernels: 0 us -> 67.7 us
  matrix products: 65.1 us -> 0 us
  blocking collectives: 49.8 us -> 5.92 us
  local copies, waits for them, and re-layouts: 51 us -> 16.6 us
  starting transfers between devices: 14.2 us -> 29.7 us
  other arithmetic: 19.1 us -> 28.3 us
    all_gather x6 -> x2, waiting for transfers between devices: 262 us -> 0.02 us  [the longest x1 0.02 us: fast_body(): all_grads = lax.all_gather(grads, 'fsdp', axis=0)]
    ppermute x0 -> x39, waiting for transfers between devices: none -> 107 us  [swap(): lax.ppermute(array, axis, [(i, i ^ bit) for i in range(lax.axis_size(axis...]
    pallas_call x0 -> x18, Pallas kernels: none -> 67.7 us  [the longest x6 40.8 us: call(): pl.pallas_call(run, in_specs=[pl.BlockSpec(memory_space=pltpu.SMEM)] + [p...]
    dot_general x21 -> x0, matrix products: 64.3 us -> none  [the longest x3 18.6 us: project(): jnp.dot(flat_rows, weight, preferred_element_type=jnp.float32)]
    ppermute x0 -> x39, starting transfers between devices: none -> 29.1 us  [swap(): lax.ppermute(array, axis, [(i, i ^ bit) for i in range(lax.axis_size(axis...]
    psum x2 -> x0, blocking collectives: 26.3 us -> none  [the longest x1 16.4 us: body(): gain_grad = lax.psum(jnp.sum(d_normed_part * unit_part, axis=(0, 1)), 'pas')]
    reshape x8 -> x0, local copies, waits for them, and re-layouts: 20.2 us -> none  [the longest x2 13.8 us: body(): d_context = d_context.reshape(BAL, seq_len, head_count, HD)]
    all_to_all x1 -> x0, blocking collectives: 17.1 us -> none  [body(): lax.all_to_all(send_grads, 'pas', split_axis=0, concat_axis=0, tiled=True)]
  transfers between devices with their start and end apart: 12 -> 43, of which waited for: 9 -> 21; matrix products, arithmetic and copies ran while one was open for 22% -> 8% of each run, Pallas kernels for 0% -> 21%
where the time goes in v2:
time: 323 us; the launch traced here: 322 us
  waiting for transfers between devices  155 us (48%)
  Pallas kernels  67.7 us (21%)
  starting transfers between devices  29.7 us (9%)
  other arithmetic  28.3 us (9%)
  between operations  18.8 us (6%)
  local copies, waits for them, and re-layouts  16.6 us (5%)
  blocking collectives  5.92 us (2%)
    ppermute x39, waiting for transfers between devices, swap(): lax.ppermute(array, axis, [(i, i ^ bit) for i in range(lax.axis_size(axis...  107 us
    pallas_call x6, Pallas kernels, call(): pl.pallas_call(run, in_specs=[pl.BlockSpec(memory_space=pltpu.SMEM)] + [p...  40.8 us
    reduce_scatter x1, waiting for transfers between devices, fast_body(): lax.psum_scatter(d_normed, 'fsdp', scatter_dimension=0).astype(jnp.float32)  32.7 us
    ppermute x39, starting transfers between devices, swap(): lax.ppermute(array, axis, [(i, i ^ bit) for i in range(lax.axis_size(axis...  29.1 us
    pallas_call x8, Pallas kernels, cut(): pl.pallas_call(copy, grid_spec=pltpu.PrefetchScalarGridSpec(num_scalar_pr...  15.2 us
    reduce_scatter x1, waiting for transfers between devices, fast_body(): attention = lax.psum_scatter(partial_out, 'fsdp', scatter_dimension=0)  14.9 us
    unnamed x81, local copies, waits for them, and re-layouts  14.6 us
    pallas_call x2, Pallas kernels, attend(): pl.pallas_call(kernel, grid=(BAL, 2), in_specs=[spec] * len(arrays), out_...  11.6 us
  transfers between devices with their start and end apart: 43, of which 21 were waited for; matrix products, arithmetic and copies ran while one was open for 8% of the time, Pallas kernels for 21%

profile of v2, /device:TPU:0, one launch (start us, length us, event | category | flops | bytes accessed | tf_op | source)
XLA Modules:
  0.0 322.0 jit_solution(9619703959933537200)
XLA Ops:
  7.2 1.2 slice.84
  9.6 1.2 dynamic-slice
  11.6 5.9 %all-reduce = s32[4]{0:T(128)S(1)} all-reduce(s32[4]{0:T(128)S(1)} %dynamic-update-slice), channel_id=1, replica_groups=mesh['grp'=2,'pas'=4,'fsdp'=4] {'pas'}, use_global_device_ids=true, to_apply=%add | all-reduce | flops 4 | bytes 32
  22.5 1.9 shard_map.103
  24.3 1.2 collective-permute-start.3
  26.8 2.7 collective-permute-done.1.refs_1_
  30.5 1.1 broadcast_select_fusion
  32.4 1.9 shard_map.105
  34.3 2.0 collective-permute-start.5
  36.3 4.5 %collective-permute-done.3.refs_0_ = bf16[256,1024]{1,0:T(8,128)(2,1)} collective-permute-done((bf16[256,1024]{1,0:T(8,128)(2,1)}, bf16[256,1024]{1,0:T(8,128)(2,1)}, u32[]{:S(2)}, u32[]{:S(2)}) %collective-permute-start.3) | collective-permute-done | bytes 524320 | tf_op jit(solution)/shard_map/ppermute | solution.py:175
  40.8 1.5 collective-permute-start.8
  42.4 14.3 %collective-permute-done.5.refs_2_ = bf16[128,1024]{1,0:T(8,128)(2,1)S(1)} collective-permute-done((bf16[128,1024]{1,0:T(8,128)(2,1)S(1)}, bf16[128,1024]{1,0:T(8,128)(2,1)S(1)}, u32[]{:S(2)}, u32[]{:S(2)}) %collective-permute-start.5) | collective-permute-done | bytes 262176 | tf_op jit(solution)/shard_map/ppermute | solution.py:175
  57.4 1.9 shard_map.104
  59.8 1.2 fusion.14
  61.0 1.5 collective-permute-start.14
  63.4 2.1 shard_map.106
  65.4 1.5 collective-permute-start.9
  67.0 7.5 %collective-permute-done.6.refs_0_ = bf16[256,1024]{1,0:T(8,128)(2,1)} collective-permute-done((bf16[256,1024]{1,0:T(8,128)(2,1)}, bf16[256,1024]{1,0:T(8,128)(2,1)}, u32[]{:S(2)}, u32[]{:S(2)}) %collective-permute-start.6) | collective-permute-done | bytes 524320 | tf_op jit(solution)/shard_map/ppermute | solution.py:175
  74.5 1.5 collective-permute-start.10
  76.0 1.9 shard_map.109
  78.4 7.3 %collective-permute-done.9.refs_0_ = bf16[256,1024]{1,0:T(8,128)(2,1)} collective-permute-done((bf16[256,1024]{1,0:T(8,128)(2,1)}, bf16[256,1024]{1,0:T(8,128)(2,1)}, u32[]{:S(2)}, u32[]{:S(2)}) %collective-permute-start.9) | collective-permute-done | bytes 524320 | tf_op jit(solution)/shard_map/ppermute | solution.py:175
  85.7 1.5 collective-permute-start.11
  87.2 3.7 %maximum_select_fusion.1.refs_3_.refs_9_ = bf16[1024,1024]{1,0:T(8,128)(2,1)} fusion(bf16[256,1024]{1,0:T(8,128)(2,1)} %collective-permute-done.14.refs_1_, bf16[256,1024]{1,0:T(8,128)(2,1)} %collective-permute-done.8.refs_1_, bf16[256,1024]{1,0:T(8,128)(2,1)} %copy-done.31, bf16[256,1024]{1,0:T(8,128)(2,1)} %collective-permute-done.3.refs_0_, pred[]{:T(512)S(6)} %eq.58), kind=kLoop, calls=%fused_computation.8 | loop fusion | flops 17825792 | bytes 4194305 | tf_op jit(solution)/shard_map/jit(_where)/select_n | solution.py:383
  90.9 1.9 shard_map.110
  93.3 3.8 %collective-permute-done.11.refs_1_ = bf16[256,1024]{1,0:T(8,128)(2,1)S(1)} collective-permute-done((bf16[256,1024]{1,0:T(8,128)(2,1)}, bf16[256,1024]{1,0:T(8,128)(2,1)S(1)}, u32[]{:S(2)}, u32[]{:S(2)}) %collective-permute-start.11) | collective-permute-done | bytes 524320 | tf_op jit(solution)/shard_map/ppermute | solution.py:175
  97.1 1.6 collective-permute-start.19
  98.7 3.2 %maximum_select_fusion.refs_3_.refs_5_ = bf16[1024,1024]{1,0:T(8,128)(2,1)} fusion(bf16[256,1024]{1,0:T(8,128)(2,1)S(1)} %collective-permute-done.11.refs_1_, bf16[256,1024]{1,0:T(8,128)(2,1)} %collective-permute-done.10.refs_1_, bf16[256,1024]{1,0:T(8,128)(2,1)} %collective-permute-done.9.refs_0_, bf16[256,1024]{1,0:T(8,128)(2,1)} %collective-permute-done.6.refs_0_, ...), kind=kLoop, calls=%fused_computation.7 | loop fusion | flops 17825792 | bytes 4194305 | tf_op jit(solution)/shard_map/jit(_where)/select_n | solution.py:383
  101.9 5.5 %collective-permute-done.18.refs_0_ = bf16[256,1024]{1,0:T(8,128)(2,1)} collective-permute-done((bf16[256,1024]{1,0:T(8,128)(2,1)}, bf16[256,1024]{1,0:T(8,128)(2,1)}, u32[]{:S(2)}, u32[]{:S(2)}) %collective-permute-start.18) | collective-permute-done | bytes 524320 | tf_op jit(solution)/shard_map/ppermute | solution.py:175
  107.4 4.0 %collective-permute-done.19.refs_1_ = bf16[256,1024]{1,0:T(8,128)(2,1)S(1)} collective-permute-done((bf16[256,1024]{1,0:T(8,128)(2,1)S(1)}, bf16[256,1024]{1,0:T(8,128)(2,1)S(1)}, u32[]{:S(2)}, u32[]{:S(2)}) %collective-permute-start.19) | collective-permute-done | bytes 524320 | tf_op jit(solution)/shard_map/ppermute | solution.py:175
  112.2 1.5 collective-permute-start.20
  114.1 11.8 %collective-permute-done.20 = bf16[256,1024]{1,0:T(8,128)(2,1)S(1)} collective-permute-done((bf16[256,1024]{1,0:T(8,128)(2,1)}, bf16[256,1024]{1,0:T(8,128)(2,1)S(1)}, u32[]{:S(2)}, u32[]{:S(2)}) %collective-permute-start.20) | collective-permute-done | bytes 524320 | tf_op jit(solution)/shard_map/ppermute | solution.py:175
  126.0 3.2 maximum_select_fusion.2.refs_3_.refs_13_
  129.6 2.3 fusion.4
  132.8 5.4 %shard_map.108.k_ref.refs_2_ = bf16[256,1024]{1,0:T(8,128)(2,1)S(1)} custom-call(s32[2]{0:T(128)S(1)} %pad_add_fusion.pos_ref, bf16[4,256,1024]{2,1,0:T(8,128)(2,1)S(1)} %fusion.2.refs_0_, bf16[1024,1024]{1,0:T(8,128)(2,1)} %refs_7_.1, bf16[1024,1024]{1,0:T(8,128)(2,1)} %collective-permute-done.13.refs_2_.refs_8_, ...), custom_call_target="tpu_custom_call" | custom-call | flops 2147483648 | bytes 8388608 | tf_op jit(solution)/shard_map/pallas_call | solution.py:257
  139.0 1.9 shard_map.113
  140.9 1.2 collective-permute-start.23
  142.1 5.4 %shard_map.107.q_ref.refs_2_ = bf16[256,1024]{1,0:T(8,128)(2,1)S(1)} custom-call(s32[2]{0:T(128)S(1)} %pad_add_fusion.pos_ref, bf16[4,256,1024]{2,1,0:T(8,128)(2,1)S(1)} %fusion.2.refs_0_, bf16[1024,1024]{1,0:T(8,128)(2,1)} %refs_3_.1, bf16[1024,1024]{1,0:T(8,128)(2,1)} %collective-permute-done.2.refs_2_.refs_4_, ...), custom_call_target="tpu_custom_call" | custom-call | flops 2147483648 | bytes 8388608 | tf_op jit(solution)/shard_map/pallas_call | solution.py:257
  148.4 1.9 shard_map.114
  151.0 4.9 %collective-permute-done.23.refs_3_ = bf16[256,1024]{1,0:T(8,128)(2,1)} collective-permute-done((bf16[256,1024]{1,0:T(8,128)(2,1)}, bf16[256,1024]{1,0:T(8,128)(2,1)}, u32[]{:S(2)}, u32[]{:S(2)}) %collective-permute-start.23) | collective-permute-done | bytes 524320 | tf_op jit(solution)/shard_map/ppermute | solution.py:175
  155.9 1.5 collective-permute-start.25
  157.5 9.3 %collective-permute-done.24.refs_4_ = bf16[256,1024]{1,0:T(8,128)(2,1)S(1)} collective-permute-done((bf16[256,1024]{1,0:T(8,128)(2,1)}, bf16[256,1024]{1,0:T(8,128)(2,1)S(1)}, u32[]{:S(2)}, u32[]{:S(2)}) %collective-permute-start.24) | collective-permute-done | bytes 524320 | tf_op jit(solution)/shard_map/ppermute | solution.py:175
  166.7 1.5 collective-permute-start.26
  168.2 1.4 collective-permute-done.25.refs_5_
  170.1 10.5 %collective-permute-done.26.refs_6_ = bf16[256,1024]{1,0:T(8,128)(2,1)S(1)} collective-permute-done((bf16[256,1024]{1,0:T(8,128)(2,1)S(1)}, bf16[256,1024]{1,0:T(8,128)(2,1)S(1)}, u32[]{:S(2)}, u32[]{:S(2)}) %collective-permute-start.26) | collective-permute-done | bytes 524320 | tf_op jit(solution)/shard_map/ppermute | solution.py:175
  180.6 5.4 %shard_map.111.v_ref = bf16[256,1024]{1,0:T(8,128)(2,1)S(1)} custom-call(s32[2]{0:T(128)S(1)} %pad_add_fusion.pos_ref, bf16[4,256,1024]{2,1,0:T(8,128)(2,1)S(1)} %fusion.2.refs_0_, bf16[1024,1024]{1,0:T(8,128)(2,1)} %refs_11_.1, bf16[1024,1024]{1,0:T(8,128)(2,1)} %collective-permute-done.16.refs_2_.refs_12_, ...), custom_call_target="tpu_custom_call" | custom-call | flops 2147483648 | bytes 8388608 | tf_op jit(solution)/shard_map/pallas_call | solution.py:257
  186.0 3.8 %shard_map.112.refs_0_ = bf16[256,1024]{1,0:T(8,128)(2,1)S(1)} custom-call(bf16[256,1024]{1,0:T(8,128)(2,1)S(1)} %copy-done.5, bf16[256,1024]{1,0:T(8,128)(2,1)S(1)} %copy-done.3, bf16[256,1024]{1,0:T(8,128)(2,1)S(1)} %shard_map.111.v_ref), custom_call_target="tpu_custom_call" | custom-call | flops 536870912 | bytes 2097152 | tf_op jit(solution)/shard_map/pallas_call | solution.py:334
  192.3 6.4 %shard_map.115.refs_1_ = bf16[4,256,1024]{2,1,0:T(8,128)(2,1)} custom-call(s32[2]{0:T(128)S(1)} %pad_add_fusion.pos_ref, bf16[256,1024]{1,0:T(8,128)(2,1)S(1)} %shard_map.112.refs_0_, bf16[1024,1024]{1,0:T(8,128)(2,1)} %refs_1_.9, bf16[1024,1024]{1,0:T(8,128)(2,1)} %collective-permute-done.22.refs_2_, bf16[256,1024]{1,0:T(8,128)(2,1)} %collective-permute-done.23.refs_3_, ...), custom_call_target="tpu_custom_call" | custom-call | flops 2147483648 | bytes 8388608 | tf_op jit(solution)/shard_map/pallas_call | solution.py:257
  203.2 6.6 %shard_map.117.dc_ref = bf16[256,1024]{1,0:T(8,128)(2,1)S(1)} custom-call(s32[2]{0:T(128)S(1)} %pad_add_fusion.pos_ref, bf16[4,256,1024]{2,1,0:T(8,128)(2,1)} %shard_map.116.refs_0_, bf16[1024,1024]{1,0:T(8,128)(2,1)} %refs_1_.9, bf16[1024,1024]{1,0:T(8,128)(2,1)} %collective-permute-done.22.refs_2_, bf16[256,1024]{1,0:T(8,128)(2,1)} %collective-permute-done.23.refs_3_, ...), custom_call_target="tpu_custom_call" | custom-call | flops 2147483648 | bytes 8388608 | tf_op jit(solution)/shard_map/pallas_call | solution.py:257
  209.9 7.9 %shard_map.118 = (bf16[256,1024]{1,0:T(8,128)(2,1)S(1)}, bf16[256,1024]{1,0:T(8,128)(2,1)S(1)}, bf16[256,1024]{1,0:T(8,128)(2,1)S(1)}) custom-call(bf16[256,1024]{1,0:T(8,128)(2,1)S(1)} %copy-done.5, bf16[256,1024]{1,0:T(8,128)(2,1)S(1)} %copy-done.3, bf16[256,1024]{1,0:T(8,128)(2,1)S(1)} %copy-done.7, bf16[256,1024]{1,0:T(8,128)(2,1)S(1)} %shard_map.117.dc_ref), custom_call_target="tpu_custom_call" | custom-call | flops 536870912 | bytes 3670016 | tf_op jit(solution)/shard_map/pallas_call | solution.py:334
  217.8 11.4 %shard_map.119.refs_0_ = bf16[4,256,1024]{2,1,0:T(8,128)(2,1)S(1)} custom-call(s32[2]{0:T(128)S(1)} %pad_add_fusion.pos_ref, bf16[256,1024]{1,0:T(8,128)(2,1)S(1)} %get-tuple-element.6.refs_0_, bf16[256,1024]{1,0:T(8,128)(2,1)S(1)} %get-tuple-element.7.refs_1_, bf16[256,1024]{1,0:T(8,128)(2,1)S(1)} %get-tuple-element.8.refs_2_, bf16[1024,1024]{1,0:T(8,128)(2,1)} %refs_3_.1, ...), custom_call_target="tpu_custom_call" | custom-call | flops 6442450944 | bytes 25165824 | tf_op jit(solution)/shard_map/pallas_call | solution.py:257
  229.2 1.4 copy-done
  230.6 14.9 %reduce-scatter.3.cloned.1.call-done = bf16[1,256,1024]{2,1,0:T(8,128)(2,1)} async-done(((bf16[4,256,1024]{2,1,0:T(8,128)(2,1)}), bf16[1,256,1024]{2,1,0:T(8,128)(2,1)}) %reduce-scatter.3.cloned.1.call-update) | async-done | bytes 524304 | tf_op jit(solution)/shard_map/reduce_scatter | solution.py:479
  245.5 1.6 copy-done.1
  247.1 2.6 fusion.3
  249.8 3.6 %collective-permute-done.33 = f32[2,128]{1,0:T(2,128)S(1)} collective-permute-done((f32[2,128]{1,0:T(2,128)S(1)}, f32[2,128]{1,0:T(2,128)S(1)}, u32[]{:S(2)}, u32[]{:S(2)}) %collective-permute-start.33) | collective-permute-done | bytes 1056 | tf_op jit(solution)/shard_map/ppermute | solution.py:175
  253.4 1.7 collective-permute-start.34
  255.1 3.2 %collective-permute-done.34 = f32[2,128]{1,0:T(2,128)S(1)} collective-permute-done((f32[2,128]{1,0:T(2,128)S(1)}, f32[2,128]{1,0:T(2,128)S(1)}, u32[]{:S(2)}, u32[]{:S(2)}) %collective-permute-start.34) | collective-permute-done | bytes 1056 | tf_op jit(solution)/shard_map/ppermute | solution.py:175
  258.4 32.7 %reduce-scatter.5.cloned.1.call-done = bf16[1,256,1024]{2,1,0:T(8,128)(2,1)} async-done(((bf16[4,256,1024]{2,1,0:T(8,128)(2,1)}), bf16[1,256,1024]{2,1,0:T(8,128)(2,1)}) %reduce-scatter.5.cloned.1.call-update) | async-done | bytes 524304 | tf_op jit(solution)/shard_map/reduce_scatter | solution.py:487
  291.1 1.8 fusion.11
  293.0 1.5 collective-permute-start.31
  295.2 7.1 %collective-permute-done.31 = bf16[128,1024]{1,0:T(8,128)(2,1)S(1)} collective-permute-done((bf16[128,1024]{1,0:T(8,128)(2,1)S(1)}, bf16[128,1024]{1,0:T(8,128)(2,1)S(1)}, u32[]{:S(2)}, u32[]{:S(2)}) %collective-permute-start.31) | collective-permute-done | bytes 262176 | tf_op jit(solution)/shard_map/ppermute | solution.py:175
  302.4 4.2 %collective-permute-done.35 = bf16[128,1024]{1,0:T(8,128)(2,1)S(1)} collective-permute-done((bf16[128,1024]{1,0:T(8,128)(2,1)S(1)}, bf16[128,1024]{1,0:T(8,128)(2,1)S(1)}, u32[]{:S(2)}, u32[]{:S(2)}) %collective-permute-start.35) | collective-permute-done | bytes 262176 | tf_op jit(solution)/shard_map/ppermute | solution.py:175
  309.0 1.5 collective-permute-start.38
  313.3 1.1 pad_maximum_fusion.1
  (161 shorter events, 28.2 us)
Async XLA Ops:
  7.2 14.5 %copy-start.21 = (bf16[4,128,1024]{2,1,0:T(8,128)(2,1)S(1)}, bf16[4,128,1024]{2,1,0:T(8,128)(2,1)}, u32[]{:S(2)}) copy-start(bf16[4,128,1024]{2,1,0:T(8,128)(2,1)} %param.9) | copy-start | bytes 3145732
  7.2 122.5 %all-gather.5.cloned.1.call-start = ((), (), s32[]{:S(2)}) async-start(), calls=%async_computation.4 | async-start | bytes 2621440 | tf_op jit(solution)/shard_map/all_gather | solution.py:437
  8.4 11.1 %collective-permute-start = (bf16[2,128,1024]{2,1,0:T(8,128)(2,1)S(1)}, bf16[2,128,1024]{2,1,0:T(8,128)(2,1)S(1)}, u32[]{:S(2)}, u32[]{:S(2)}) collective-permute-start(bf16[2,128,1024]{2,1,0:T(8,128)(2,1)S(1)} %slice.84), channel_id=1, source_target_pairs={{0,4},{4,0},{8,12},{12,8},{1,5},{5,1},{9,13},{13,9},{2,6},{6,2},{1... | collective-permute-start | bytes 1572872 | tf_op jit(solution)/shard_map/ppermute | solution.py:175
  20.6 6.1 %copy-start.20 = (bf16[4,128,1024]{2,1,0:T(8,128)(2,1)S(1)}, bf16[4,128,1024]{2,1,0:T(8,128)(2,1)}, u32[]{:S(2)}) copy-start(bf16[4,128,1024]{2,1,0:T(8,128)(2,1)} %param.8) | copy-start | bytes 3145732
  20.7 6.1 %copy-start.35 = (bf16[128,1024]{1,0:T(8,128)(2,1)}, bf16[128,1024]{1,0:T(8,128)(2,1)S(1)}, u32[]{:S(2)}) copy-start(bf16[128,1024]{1,0:T(8,128)(2,1)S(1)} %fusion.16.refs_0_) | copy-start | bytes 786436
  20.7 8.8 %collective-permute-start.1 = (bf16[128,1024]{1,0:T(8,128)(2,1)S(1)}, bf16[128,1024]{1,0:T(8,128)(2,1)S(1)}, u32[]{:S(2)}, u32[]{:S(2)}) collective-permute-start(bf16[128,1024]{1,0:T(8,128)(2,1)S(1)} %fusion.16.refs_0_), channel_id=1, source_target_pairs={{0,8},{4,12},{8,0},{12,4},{1,9},{5,13},{9,1},{13,5},{2,10},{6,14},... | collective-permute-start | bytes 786440 | tf_op jit(solution)/shard_map/ppermute | solution.py:175
  22.5 8.1 %collective-permute-start.4 = (bf16[2,128,1024]{2,1,0:T(8,128)(2,1)}, bf16[2,128,1024]{2,1,0:T(8,128)(2,1)}, u32[]{:S(2)}, u32[]{:S(2)}) collective-permute-start(bf16[2,128,1024]{2,1,0:T(8,128)(2,1)} %slice.89), channel_id=1, source_target_pairs={{0,4},{4,0},{8,12},{12,8},{1,5},{5,1},{9,13},{13,9},{2,6},{6,2},{1... | collective-permute-start | bytes 1572872 | tf_op jit(solution)/shard_map/ppermute | solution.py:175
  24.3 16.5 %collective-permute-start.3 = (bf16[256,1024]{1,0:T(8,128)(2,1)}, bf16[256,1024]{1,0:T(8,128)(2,1)}, u32[]{:S(2)}, u32[]{:S(2)}) collective-permute-start(bf16[256,1024]{1,0:T(8,128)(2,1)} %shard_map.103), channel_id=1, source_target_pairs={{0,8},{4,12},{8,0},{12,4},{1,9},{5,13},{9,1},{13,5},{2,10},{6,14},... | collective-permute-start | bytes 1572872 | tf_op jit(solution)/shard_map/ppermute | solution.py:175
  29.5 4.8 %copy-start.24 = (bf16[128,1024]{1,0:T(8,128)(2,1)}, bf16[128,1024]{1,0:T(8,128)(2,1)S(1)}, u32[]{:S(2)}) copy-start(bf16[128,1024]{1,0:T(8,128)(2,1)S(1)} %fusion.19) | copy-start | bytes 786436
  30.5 170.2 %all-gather.7.cloned.1.call-start = ((), (), s32[]{:S(2)}) async-start(), calls=%async_computation.5 | async-start | bytes 2621440 | tf_op jit(solution)/shard_map/all_gather | solution.py:438
  34.3 26.7 %collective-permute-start.7 = (bf16[256,1024]{1,0:T(8,128)(2,1)}, bf16[256,1024]{1,0:T(8,128)(2,1)S(1)}, u32[]{:S(2)}, u32[]{:S(2)}) collective-permute-start(bf16[256,1024]{1,0:T(8,128)(2,1)} %shard_map.105), channel_id=1, source_target_pairs={{0,8},{4,12},{8,0},{12,4},{1,9},{5,13},{9,1},{13,5},{2,10},{6,14},... | collective-permute-start | bytes 1572872 | tf_op jit(solution)/shard_map/ppermute | solution.py:175
  34.3 22.4 %collective-permute-start.5 = (bf16[128,1024]{1,0:T(8,128)(2,1)S(1)}, bf16[128,1024]{1,0:T(8,128)(2,1)S(1)}, u32[]{:S(2)}, u32[]{:S(2)}) collective-permute-start(bf16[128,1024]{1,0:T(8,128)(2,1)S(1)} %copy-done.37), channel_id=1, source_target_pairs={{0,8},{4,12},{8,0},{12,4},{1,9},{5,13},{9,1},{13,5},{2,10},{6,14},... | collective-permute-start | bytes 786440 | tf_op jit(solution)/shard_map/ppermute | solution.py:175
  40.8 22.5 %collective-permute-start.8 = (bf16[256,1024]{1,0:T(8,128)(2,1)}, bf16[256,1024]{1,0:T(8,128)(2,1)}, u32[]{:S(2)}, u32[]{:S(2)}) collective-permute-start(bf16[256,1024]{1,0:T(8,128)(2,1)} %collective-permute-done.3.refs_0_), channel_id=1, source_target_pairs={{0,16},{16,0},{1,17},{17,1},{2,18},{18,2},{3,19},{19,3},{4,20},{20... | collective-permute-start | bytes 1572872 | tf_op jit(solution)/shard_map/ppermute | solution.py:175
  42.4 20.2 %copy-start.22 = (bf16[128,1024]{1,0:T(8,128)(2,1)}, bf16[128,1024]{1,0:T(8,128)(2,1)S(1)}, u32[]{:S(2)}) copy-start(bf16[128,1024]{1,0:T(8,128)(2,1)S(1)} %slice_bitcast_fusion.6) | copy-start | bytes 786436
  59.3 15.2 %collective-permute-start.6 = (bf16[256,1024]{1,0:T(8,128)(2,1)}, bf16[256,1024]{1,0:T(8,128)(2,1)}, u32[]{:S(2)}, u32[]{:S(2)}) collective-permute-start(bf16[256,1024]{1,0:T(8,128)(2,1)} %shard_map.104), channel_id=1, source_target_pairs={{0,8},{4,12},{8,0},{12,4},{1,9},{5,13},{9,1},{13,5},{2,10},{6,14},... | collective-permute-start | bytes 1572872 | tf_op jit(solution)/shard_map/ppermute | solution.py:175
  61.0 2.4 copy-start.26
  61.0 2.4 copy-start.31
  61.0 14.9 %collective-permute-start.14 = (bf16[256,1024]{1,0:T(8,128)(2,1)S(1)}, bf16[256,1024]{1,0:T(8,128)(2,1)}, u32[]{:S(2)}, u32[]{:S(2)}) collective-permute-start(bf16[256,1024]{1,0:T(8,128)(2,1)S(1)} %collective-permute-done.7.refs_0_), channel_id=1, source_target_pairs={{0,16},{16,0},{1,17},{17,1},{2,18},{18,2},{3,19},{19,3},{4,20},{20... | collective-permute-start | bytes 1572872 | tf_op jit(solution)/shard_map/ppermute | solution.py:175
  63.4 12.6 %copy-start.18 = (bf16[1024,1024]{1,0:T(8,128)(2,1)S(1)}, bf16[1024,1024]{1,0:T(8,128)(2,1)}, u32[]{:S(2)}) copy-start(bf16[1024,1024]{1,0:T(8,128)(2,1)} %refs_7_.1) | copy-start | bytes 6291460
  65.4 20.2 %collective-permute-start.9 = (bf16[256,1024]{1,0:T(8,128)(2,1)}, bf16[256,1024]{1,0:T(8,128)(2,1)}, u32[]{:S(2)}, u32[]{:S(2)}) collective-permute-start(bf16[256,1024]{1,0:T(8,128)(2,1)} %shard_map.106), channel_id=1, source_target_pairs={{0,8},{4,12},{8,0},{12,4},{1,9},{5,13},{9,1},{13,5},{2,10},{6,14},... | collective-permute-start | bytes 1572872 | tf_op jit(solution)/shard_map/ppermute | solution.py:175
  74.5 16.4 %collective-permute-start.10 = (bf16[256,1024]{1,0:T(8,128)(2,1)}, bf16[256,1024]{1,0:T(8,128)(2,1)}, u32[]{:S(2)}, u32[]{:S(2)}) collective-permute-start(bf16[256,1024]{1,0:T(8,128)(2,1)} %collective-permute-done.6.refs_0_), channel_id=1, source_target_pairs={{0,16},{16,0},{1,17},{17,1},{2,18},{18,2},{3,19},{19,3},{4,20},{20... | collective-permute-start | bytes 1572872 | tf_op jit(solution)/shard_map/ppermute | solution.py:175
  76.0 53.1 %collective-permute-start.13 = (bf16[1024,1024]{1,0:T(8,128)(2,1)S(1)}, bf16[1024,1024]{1,0:T(8,128)(2,1)}, u32[]{:S(2)}, u32[]{:S(2)}) collective-permute-start(bf16[1024,1024]{1,0:T(8,128)(2,1)S(1)} %copy-done.18), channel_id=1, source_target_pairs={{0,4},{4,0},{8,12},{12,8},{1,5},{5,1},{9,13},{13,9},{2,6},{6,2},{1... | collective-permute-start | bytes 6291464 | tf_op jit(solution)/shard_map/ppermute | solution.py:175
  77.9 19.2 %collective-permute-start.17 = (bf16[256,1024]{1,0:T(8,128)(2,1)}, bf16[256,1024]{1,0:T(8,128)(2,1)S(1)}, u32[]{:S(2)}, u32[]{:S(2)}) collective-permute-start(bf16[256,1024]{1,0:T(8,128)(2,1)} %shard_map.109), channel_id=1, source_target_pairs={{0,8},{4,12},{8,0},{12,4},{1,9},{5,13},{9,1},{13,5},{2,10},{6,14},... | collective-permute-start | bytes 1572872 | tf_op jit(solution)/shard_map/ppermute | solution.py:175
  85.7 11.4 %collective-permute-start.11 = (bf16[256,1024]{1,0:T(8,128)(2,1)}, bf16[256,1024]{1,0:T(8,128)(2,1)S(1)}, u32[]{:S(2)}, u32[]{:S(2)}) collective-permute-start(bf16[256,1024]{1,0:T(8,128)(2,1)} %collective-permute-done.9.refs_0_), channel_id=1, source_target_pairs={{0,16},{16,0},{1,17},{17,1},{2,18},{18,2},{3,19},{19,3},{4,20},{20... | collective-permute-start | bytes 1572872 | tf_op jit(solution)/shard_map/ppermute | solution.py:175
  90.9 41.0 %collective-permute-start.15 = (bf16[1024,1024]{1,0:T(8,128)(2,1)}, bf16[1024,1024]{1,0:T(8,128)(2,1)}, u32[]{:S(2)}, u32[]{:S(2)}) collective-permute-start(bf16[1024,1024]{1,0:T(8,128)(2,1)} %maximum_select_fusion.1.refs_3_.refs_9_), channel_id=1, source_target_pairs={{0,4},{4,0},{8,12},{12,8},{1,5},{5,1},{9,13},{13,9},{2,6},{6,2},{1... | collective-permute-start | bytes 6291464 | tf_op jit(solution)/shard_map/ppermute | solution.py:175
  92.8 21.0 %copy-start.38 = (f32[4096]{0:T(1024)S(1)}, f32[4096]{0:T(1024)}, u32[]{:S(2)}) copy-start(f32[4096]{0:T(1024)} %param.11) | copy-start | bytes 49156
  92.8 14.6 %collective-permute-start.18 = (bf16[256,1024]{1,0:T(8,128)(2,1)}, bf16[256,1024]{1,0:T(8,128)(2,1)}, u32[]{:S(2)}, u32[]{:S(2)}) collective-permute-start(bf16[256,1024]{1,0:T(8,128)(2,1)} %shard_map.110), channel_id=1, source_target_pairs={{0,8},{4,12},{8,0},{12,4},{1,9},{5,13},{9,1},{13,5},{2,10},{6,14},... | collective-permute-start | bytes 1572872 | tf_op jit(solution)/shard_map/ppermute | solution.py:175
  97.1 4.8 %copy-start.29 = (bf16[256,1024]{1,0:T(8,128)(2,1)}, bf16[256,1024]{1,0:T(8,128)(2,1)S(1)}, u32[]{:S(2)}) copy-start(bf16[256,1024]{1,0:T(8,128)(2,1)S(1)} %collective-permute-done.11.refs_1_) | copy-start | bytes 1572868
  97.1 43.9 %collective-permute-start.2 = (bf16[1024,1024]{1,0:T(8,128)(2,1)}, bf16[1024,1024]{1,0:T(8,128)(2,1)}, u32[]{:S(2)}, u32[]{:S(2)}) collective-permute-start(bf16[1024,1024]{1,0:T(8,128)(2,1)} %refs_3_.1), channel_id=1, source_target_pairs={{0,4},{4,0},{8,12},{12,8},{1,5},{5,1},{9,13},{13,9},{2,6},{6,2},{1... | collective-permute-start | bytes 6291464 | tf_op jit(solution)/shard_map/ppermute | solution.py:175
  97.1 28.9 %copy-start.28 = (bf16[256,1024]{1,0:T(8,128)(2,1)}, bf16[256,1024]{1,0:T(8,128)(2,1)S(1)}, u32[]{:S(2)}) copy-start(bf16[256,1024]{1,0:T(8,128)(2,1)S(1)} %collective-permute-done.17.refs_0_) | copy-start | bytes 1572868
  97.1 14.3 %collective-permute-start.19 = (bf16[256,1024]{1,0:T(8,128)(2,1)S(1)}, bf16[256,1024]{1,0:T(8,128)(2,1)S(1)}, u32[]{:S(2)}, u32[]{:S(2)}) collective-permute-start(bf16[256,1024]{1,0:T(8,128)(2,1)S(1)} %collective-permute-done.17.refs_0_), channel_id=1, source_target_pairs={{0,16},{16,0},{1,17},{17,1},{2,18},{18,2},{3,19},{19,3},{4,20},{20... | collective-permute-start | bytes 1572872 | tf_op jit(solution)/shard_map/ppermute | solution.py:175
  107.4 34.7 %collective-permute-start.12 = (bf16[1024,1024]{1,0:T(8,128)(2,1)}, bf16[1024,1024]{1,0:T(8,128)(2,1)}, u32[]{:S(2)}, u32[]{:S(2)}) collective-permute-start(bf16[1024,1024]{1,0:T(8,128)(2,1)} %maximum_select_fusion.refs_3_.refs_5_), channel_id=1, source_target_pairs={{0,4},{4,0},{8,12},{12,8},{1,5},{5,1},{9,13},{13,9},{2,6},{6,2},{1... | collective-permute-start | bytes 6291464 | tf_op jit(solution)/shard_map/ppermute | solution.py:175
  112.2 13.7 %collective-permute-start.20 = (bf16[256,1024]{1,0:T(8,128)(2,1)}, bf16[256,1024]{1,0:T(8,128)(2,1)S(1)}, u32[]{:S(2)}, u32[]{:S(2)}) collective-permute-start(bf16[256,1024]{1,0:T(8,128)(2,1)} %collective-permute-done.18.refs_0_), channel_id=1, source_target_pairs={{0,16},{16,0},{1,17},{17,1},{2,18},{18,2},{3,19},{19,3},{4,20},{20... | collective-permute-start | bytes 1572872 | tf_op jit(solution)/shard_map/ppermute | solution.py:175
  113.9 131.6 %reduce-scatter.3.cloned.1.call-start = ((), (), s32[]{:S(2)}) async-start(), calls=%async_computation.2 | async-start | bytes 2621440 | tf_op jit(solution)/shard_map/reduce_scatter | solution.py:479
  125.9 42.3 %collective-permute-start.16 = (bf16[1024,1024]{1,0:T(8,128)(2,1)}, bf16[1024,1024]{1,0:T(8,128)(2,1)}, u32[]{:S(2)}, u32[]{:S(2)}) collective-permute-start(bf16[1024,1024]{1,0:T(8,128)(2,1)} %refs_11_.1), channel_id=1, source_target_pairs={{0,4},{4,0},{8,12},{12,8},{1,5},{5,1},{9,13},{13,9},{2,6},{6,2},{1... | collective-permute-start | bytes 6291464 | tf_op jit(solution)/shard_map/ppermute | solution.py:175
  129.1 40.5 %collective-permute-start.21 = (bf16[1024,1024]{1,0:T(8,128)(2,1)}, bf16[1024,1024]{1,0:T(8,128)(2,1)}, u32[]{:S(2)}, u32[]{:S(2)}) collective-permute-start(bf16[1024,1024]{1,0:T(8,128)(2,1)} %maximum_select_fusion.2.refs_3_.refs_13_), channel_id=1, source_target_pairs={{0,4},{4,0},{8,12},{12,8},{1,5},{5,1},{9,13},{13,9},{2,6},{6,2},{1... | collective-permute-start | bytes 6291464 | tf_op jit(solution)/shard_map/ppermute | solution.py:175
  129.6 2.4 copy-start.19
  131.9 58.7 %collective-permute-start.22 = (bf16[1024,1024]{1,0:T(8,128)(2,1)}, bf16[1024,1024]{1,0:T(8,128)(2,1)}, u32[]{:S(2)}, u32[]{:S(2)}) collective-permute-start(bf16[1024,1024]{1,0:T(8,128)(2,1)} %refs_1_.9), channel_id=1, source_target_pairs={{0,4},{4,0},{8,12},{12,8},{1,5},{5,1},{9,13},{13,9},{2,6},{6,2},{1... | collective-permute-start | bytes 6291464 | tf_op jit(solution)/shard_map/ppermute | solution.py:175
  140.9 15.0 %collective-permute-start.23 = (bf16[256,1024]{1,0:T(8,128)(2,1)}, bf16[256,1024]{1,0:T(8,128)(2,1)}, u32[]{:S(2)}, u32[]{:S(2)}) collective-permute-start(bf16[256,1024]{1,0:T(8,128)(2,1)} %shard_map.113), channel_id=1, source_target_pairs={{0,8},{4,12},{8,0},{12,4},{1,9},{5,13},{9,1},{13,5},{2,10},{6,14},... | collective-permute-start | bytes 1572872 | tf_op jit(solution)/shard_map/ppermute | solution.py:175
  150.2 35.8 %copy-start.3 = (bf16[256,1024]{1,0:T(8,128)(2,1)S(1)}, bf16[256,1024]{1,0:T(8,128)(2,1)}, u32[]{:S(2)}) copy-start(bf16[256,1024]{1,0:T(8,128)(2,1)} %copy-done.2) | copy-start | bytes 1572868
  150.2 35.8 %copy-start.5 = (bf16[256,1024]{1,0:T(8,128)(2,1)S(1)}, bf16[256,1024]{1,0:T(8,128)(2,1)}, u32[]{:S(2)}) copy-start(bf16[256,1024]{1,0:T(8,128)(2,1)} %copy-done.4) | copy-start | bytes 1572868
  150.2 16.5 %collective-permute-start.24 = (bf16[256,1024]{1,0:T(8,128)(2,1)}, bf16[256,1024]{1,0:T(8,128)(2,1)S(1)}, u32[]{:S(2)}, u32[]{:S(2)}) collective-permute-start(bf16[256,1024]{1,0:T(8,128)(2,1)} %shard_map.114), channel_id=1, source_target_pairs={{0,8},{4,12},{8,0},{12,4},{1,9},{5,13},{9,1},{13,5},{2,10},{6,14},... | collective-permute-start | bytes 1572872 | tf_op jit(solution)/shard_map/ppermute | solution.py:175
  155.9 13.7 %collective-permute-start.25 = (bf16[256,1024]{1,0:T(8,128)(2,1)}, bf16[256,1024]{1,0:T(8,128)(2,1)S(1)}, u32[]{:S(2)}, u32[]{:S(2)}) collective-permute-start(bf16[256,1024]{1,0:T(8,128)(2,1)} %collective-permute-done.23.refs_3_), channel_id=1, source_target_pairs={{0,16},{16,0},{1,17},{17,1},{2,18},{18,2},{3,19},{19,3},{4,20},{20... | collective-permute-start | bytes 1572872 | tf_op jit(solution)/shard_map/ppermute | solution.py:175
  166.7 24.0 %copy-start.8 = (bf16[256,1024]{1,0:T(8,128)(2,1)}, bf16[256,1024]{1,0:T(8,128)(2,1)S(1)}, u32[]{:S(2)}) copy-start(bf16[256,1024]{1,0:T(8,128)(2,1)S(1)} %collective-permute-done.24.refs_4_) | copy-start | bytes 1572868
  166.7 13.9 %collective-permute-start.26 = (bf16[256,1024]{1,0:T(8,128)(2,1)S(1)}, bf16[256,1024]{1,0:T(8,128)(2,1)S(1)}, u32[]{:S(2)}, u32[]{:S(2)}) collective-permute-start(bf16[256,1024]{1,0:T(8,128)(2,1)S(1)} %collective-permute-done.24.refs_4_), channel_id=1, source_target_pairs={{0,16},{16,0},{1,17},{17,1},{2,18},{18,2},{3,19},{19,3},{4,20},{20... | collective-permute-start | bytes 1572872 | tf_op jit(solution)/shard_map/ppermute | solution.py:175
  168.2 22.4 %collective-permute-start.27 = (bf16[256,1024]{1,0:T(8,128)(2,1)}, bf16[256,1024]{1,0:T(8,128)(2,1)S(1)}, u32[]{:S(2)}, u32[]{:S(2)}) collective-permute-start(bf16[256,1024]{1,0:T(8,128)(2,1)} %collective-permute-done.23.refs_3_), channel_id=1, source_target_pairs={{0,4},{4,0},{8,12},{12,8},{1,5},{5,1},{9,13},{13,9},{2,6},{6,2},{1... | collective-permute-start | bytes 1572872 | tf_op jit(solution)/shard_map/ppermute | solution.py:175
  169.6 21.1 %copy-start.10 = (bf16[256,1024]{1,0:T(8,128)(2,1)}, bf16[256,1024]{1,0:T(8,128)(2,1)S(1)}, u32[]{:S(2)}) copy-start(bf16[256,1024]{1,0:T(8,128)(2,1)S(1)} %collective-permute-done.25.refs_5_) | copy-start | bytes 1572868
  169.6 21.0 %collective-permute-start.28 = (bf16[256,1024]{1,0:T(8,128)(2,1)S(1)}, bf16[256,1024]{1,0:T(8,128)(2,1)S(1)}, u32[]{:S(2)}, u32[]{:S(2)}) collective-permute-start(bf16[256,1024]{1,0:T(8,128)(2,1)S(1)} %collective-permute-done.24.refs_4_), channel_id=1, source_target_pairs={{0,4},{4,0},{8,12},{12,8},{1,5},{5,1},{9,13},{13,9},{2,6},{6,2},{1... | collective-permute-start | bytes 1572872 | tf_op jit(solution)/shard_map/ppermute | solution.py:175
  169.6 21.0 %collective-permute-start.29 = (bf16[256,1024]{1,0:T(8,128)(2,1)S(1)}, bf16[256,1024]{1,0:T(8,128)(2,1)S(1)}, u32[]{:S(2)}, u32[]{:S(2)}) collective-permute-start(bf16[256,1024]{1,0:T(8,128)(2,1)S(1)} %collective-permute-done.25.refs_5_), channel_id=1, source_target_pairs={{0,4},{4,0},{8,12},{12,8},{1,5},{5,1},{9,13},{13,9},{2,6},{6,2},{1... | collective-permute-start | bytes 1572872 | tf_op jit(solution)/shard_map/ppermute | solution.py:175
  180.6 10.1 %copy-start.12 = (bf16[256,1024]{1,0:T(8,128)(2,1)}, bf16[256,1024]{1,0:T(8,128)(2,1)S(1)}, u32[]{:S(2)}) copy-start(bf16[256,1024]{1,0:T(8,128)(2,1)S(1)} %collective-permute-done.26.refs_6_) | copy-start | bytes 1572868
  180.6 10.1 %collective-permute-start.30 = (bf16[256,1024]{1,0:T(8,128)(2,1)S(1)}, bf16[256,1024]{1,0:T(8,128)(2,1)S(1)}, u32[]{:S(2)}, u32[]{:S(2)}) collective-permute-start(bf16[256,1024]{1,0:T(8,128)(2,1)S(1)} %collective-permute-done.26.refs_6_), channel_id=1, source_target_pairs={{0,4},{4,0},{8,12},{12,8},{1,5},{5,1},{9,13},{13,9},{2,6},{6,2},{1... | collective-permute-start | bytes 1572872 | tf_op jit(solution)/shard_map/ppermute | solution.py:175
  200.4 90.7 %reduce-scatter.5.cloned.1.call-start = ((), (), s32[]{:S(2)}) async-start(), calls=%async_computation.3 | async-start | bytes 2621440 | tf_op jit(solution)/shard_map/reduce_scatter | solution.py:487
  203.2 6.7 %copy-start.7 = (bf16[256,1024]{1,0:T(8,128)(2,1)S(1)}, bf16[256,1024]{1,0:T(8,128)(2,1)}, u32[]{:S(2)}) copy-start(bf16[256,1024]{1,0:T(8,128)(2,1)} %copy-done.6) | copy-start | bytes 1572868
  247.1 44.0 %copy-start.23 = (bf16[128,1024]{1,0:T(8,128)(2,1)S(1)}, bf16[128,1024]{1,0:T(8,128)(2,1)}, u32[]{:S(2)}) copy-start(bf16[128,1024]{1,0:T(8,128)(2,1)} %copy-done.22) | copy-start | bytes 786436
  247.1 44.0 %copy-start.25 = (bf16[128,1024]{1,0:T(8,128)(2,1)S(1)}, bf16[128,1024]{1,0:T(8,128)(2,1)}, u32[]{:S(2)}) copy-start(bf16[128,1024]{1,0:T(8,128)(2,1)} %copy-done.24) | copy-start | bytes 786436
  247.1 44.0 %copy-start.27 = (bf16[128,1024]{1,0:T(8,128)(2,1)S(1)}, bf16[128,1024]{1,0:T(8,128)(2,1)}, u32[]{:S(2)}) copy-start(bf16[128,1024]{1,0:T(8,128)(2,1)} %copy-done.26) | copy-start | bytes 786436
  249.8 3.6 %collective-permute-start.33 = (f32[2,128]{1,0:T(2,128)S(1)}, f32[2,128]{1,0:T(2,128)S(1)}, u32[]{:S(2)}, u32[]{:S(2)}) collective-permute-start(f32[2,128]{1,0:T(2,128)S(1)} %bitcast.106), channel_id=1, source_target_pairs={{0,1},{1,0},{2,3},{3,2},{4,5},{5,4},{6,7},{7,6},{8,9},{9,8},{10,11... | collective-permute-start | bytes 3080 | tf_op jit(solution)/shard_map/ppermute | solution.py:175
  253.4 5.0 %collective-permute-start.34 = (f32[2,128]{1,0:T(2,128)S(1)}, f32[2,128]{1,0:T(2,128)S(1)}, u32[]{:S(2)}, u32[]{:S(2)}) collective-permute-start(f32[2,128]{1,0:T(2,128)S(1)} %bitcast_add_fusion.1), channel_id=1, source_target_pairs={{0,2},{1,3},{2,0},{3,1},{4,6},{5,7},{6,4},{7,5},{8,10},{9,11},{10,... | collective-permute-start | bytes 3080 | tf_op jit(solution)/shard_map/ppermute | solution.py:175
  293.0 9.3 %collective-permute-start.31 = (bf16[128,1024]{1,0:T(8,128)(2,1)S(1)}, bf16[128,1024]{1,0:T(8,128)(2,1)S(1)}, u32[]{:S(2)}, u32[]{:S(2)}) collective-permute-start(bf16[128,1024]{1,0:T(8,128)(2,1)S(1)} %get-tuple-element.28), channel_id=1, source_target_pairs={{0,8},{4,12},{8,0},{12,4},{1,9},{5,13},{9,1},{13,5},{2,10},{6,14},... | collective-permute-start | bytes 786440 | tf_op jit(solution)/shard_map/ppermute | solution.py:175
  294.6 12.0 %collective-permute-start.35 = (bf16[128,1024]{1,0:T(8,128)(2,1)S(1)}, bf16[128,1024]{1,0:T(8,128)(2,1)S(1)}, u32[]{:S(2)}, u32[]{:S(2)}) collective-permute-start(bf16[128,1024]{1,0:T(8,128)(2,1)S(1)} %get-tuple-element.24), channel_id=1, source_target_pairs={{0,8},{4,12},{8,0},{12,4},{1,9},{5,13},{9,1},{13,5},{2,10},{6,14},... | collective-permute-start | bytes 786440 | tf_op jit(solution)/shard_map/ppermute | solution.py:175
  302.3 10.9 %collective-permute-start.32 = (bf16[2,128,1024]{2,1,0:T(8,128)(2,1)S(1)}, bf16[2,128,1024]{2,1,0:T(8,128)(2,1)S(1)}, u32[]{:S(2)}, u32[]{:S(2)}) collective-permute-start(bf16[2,128,1024]{2,1,0:T(8,128)(2,1)S(1)} %pad_maximum_fusion.4), channel_id=1, source_target_pairs={{0,4},{4,0},{8,12},{12,8},{1,5},{5,1},{9,13},{13,9},{2,6},{6,2},{1... | collective-permute-start | bytes 1572872 | tf_op jit(solution)/shard_map/ppermute | solution.py:175
  307.4 5.8 %collective-permute-start.36 = (bf16[2,128,1024]{2,1,0:T(8,128)(2,1)}, bf16[2,128,1024]{2,1,0:T(8,128)(2,1)S(1)}, u32[]{:S(2)}, u32[]{:S(2)}) collective-permute-start(bf16[2,128,1024]{2,1,0:T(8,128)(2,1)} %pad_maximum_fusion.5), channel_id=1, source_target_pairs={{0,4},{4,0},{8,12},{12,8},{1,5},{5,1},{9,13},{13,9},{2,6},{6,2},{1... | collective-permute-start | bytes 1572872 | tf_op jit(solution)/shard_map/ppermute | solution.py:175
  307.4 1.5 collective-permute-start.37
  309.0 3.6 %collective-permute-start.38 = (f32[8,128]{1,0:T(8,128)S(1)}, f32[8,128]{1,0:T(8,128)S(1)}, u32[]{:S(2)}, u32[]{:S(2)}) collective-permute-start(f32[8,128]{1,0:T(8,128)S(1)} %bitcast_add_fusion), channel_id=1, source_target_pairs={{0,8},{4,12},{8,0},{12,4},{1,9},{5,13},{9,1},{13,5},{2,10},{6,14},... | collective-permute-start | bytes 12296 | tf_op jit(solution)/shard_map/ppermute | solution.py:175
  (18 other events, 20.3 us)
Sparse Core Ops, SparseCore 0:
  30.6 46.2 all-gather.4
  114.0 45.9 all-gather.6
  200.5 44.9 reduce-scatter.2
  247.8 43.2 reduce-scatter.4

commit v3 on v2

--- a/solution.py
+++ b/solution.py
@@ -171,6 +171,9 @@
     return (encoded, input_grad, gain_grad)
 
 
+ANYWHERE = pl.BlockSpec(memory_space=pl.ANY)
+
+
 def swap(array, axis, bit):
     return lax.ppermute(array, axis, [(i, i ^ bit) for i in range(lax.axis_size(axis))])
 
@@ -185,6 +188,15 @@
 
 def dot_tn(a, b):
     return lax.dot_general(a, b, (((0,), (0,)), ((), ())), preferred_element_type=jnp.float32)
+
+
+def places(group, count):
+    first, second = group * 512, (1 - group) * 512
+    if count == 4:
+        rows = [first, first + 256, second, second + 256]
+    else:
+        rows = [first, first + 256, 384, second, second + 256, 896]
+    return [pl.multiple_of(r, 128) for r in rows]
 
 
 def stream(weights, pos, held, sems):
@@ -194,10 +206,14 @@
             piece = pieces[i]
             if isinstance(piece, list):
                 parts = []
-                for j, chunk in enumerate(piece):
-                    size = chunk.shape[0]
-                    at = pl.multiple_of((j ^ (2 * pos[1])) * size, size)
-                    parts.append((chunk, held.at[w, i, pl.ds(at, size)], sems.at[w, i, j]))
+                for j, (chunk, at) in enumerate(zip(piece, places(pos[1], len(piece)))):
+                    size = 128 if len(piece) == 6 and j % 3 else 256
+                    source = chunk
+                    if j == 5:
+                        source = chunk.at[pl.ds(128, 128)]
+                    elif len(piece) == 6 and j == 2:
+                        source = chunk.at[pl.ds(0, 128)]
+                    parts.append((source, held.at[w, i, pl.ds(at, size)], sems.at[w, i, j]))
             else:
                 parts = [(piece, held.at[w, i], sems.at[w, i, 0])]
             started[w, i] = [pltpu.make_async_copy(*part) for part in parts]
@@ -243,14 +259,14 @@
         out[pos[0] ^ i] = total.astype(out.dtype)
 
 
-def call(kernel, pos, dense, weights, out_shape):
+def call(kernel, pos, dense, weights, out_shape, *earlier):
     flat, tree = jax.tree.flatten(weights)
     count = len(weights)
 
     def run(pos_ref, *refs):
         dense_refs = refs[: len(dense)]
         weight_refs = jax.tree.unflatten(tree, refs[len(dense) : len(dense) + len(flat)])
-        out, held, sems = refs[len(dense) + len(flat) :]
+        out, held, sems = refs[-3:]
         kernel(weight_refs, pos_ref, dense_refs, out, held, sems)
 
     size = count * 2**22
@@ -258,16 +274,16 @@
         run,
         in_specs=[pl.BlockSpec(memory_space=pltpu.SMEM)]
         + [pl.BlockSpec(memory_space=pltpu.VMEM)] * len(dense)
-        + [pl.BlockSpec(memory_space=pl.ANY)] * len(flat),
+        + [ANYWHERE] * (len(flat) + len(earlier)),
         out_specs=pl.BlockSpec(memory_space=pltpu.VMEM),
         out_shape=out_shape,
         scratch_shapes=[
             pltpu.VMEM((count, 4, 1024, 1024), jnp.bfloat16),
-            pltpu.SemaphoreType.DMA((count, 4, 4)),
+            pltpu.SemaphoreType.DMA((count, 4, 6)),
         ],
         cost_estimate=pl.CostEstimate(flops=512 * size, bytes_accessed=2 * size, transcendentals=0),
         compiler_params=pltpu.CompilerParams(vmem_limit_bytes=VMEM_LIMIT),
-    )(pos, *dense, *flat)
+    )(pos, *dense, *flat, *earlier)
 
 
 def head_pairs(width):
@@ -344,25 +360,66 @@
     )(*arrays)
 
 
-ANYWHERE = pl.BlockSpec(memory_space=pl.ANY)
-
-
-def cut(weight, block, earlier):
-    def copy(block_ref, rows, *refs):
-        refs[-1][...] = rows[...]
+def cut(weight, block, rows, earlier):
+    def copy(block_ref, source, *refs):
+        refs[-1][...] = source[...]
 
     return pl.pallas_call(
         copy,
         grid_spec=pltpu.PrefetchScalarGridSpec(
             num_scalar_prefetch=1,
             grid=(1,),
-            in_specs=[pl.BlockSpec((256, 1024), lambda i, block: (block[0], 0))]
+            in_specs=[pl.BlockSpec((rows, 1024), lambda i, block: (block[0], 0))]
             + [ANYWHERE] * len(earlier),
-            out_specs=pl.BlockSpec((256, 1024), lambda i, block: (0, 0)),
+            out_specs=pl.BlockSpec((rows, 1024), lambda i, block: (0, 0)),
         ),
+        out_shape=jax.ShapeDtypeStruct((rows, 1024), weight.dtype),
+        cost_estimate=pl.CostEstimate(flops=0, bytes_accessed=4096 * rows, transcendentals=0),
+    )(block.reshape(1), weight, *earlier)
+
+
+def cut_ends(weight, earlier):
+    def copy(low, high, *refs):
+        refs[-1][0:128] = low[...]
+        refs[-1][128:256] = high[...]
+
+    return pl.pallas_call(
+        copy,
+        grid=(1,),
+        in_specs=[
+            pl.BlockSpec((128, 1024), lambda i: (3, 0)),
+            pl.BlockSpec((128, 1024), lambda i: (7, 0)),
+        ]
+        + [ANYWHERE] * len(earlier),
+        out_specs=pl.BlockSpec((256, 1024), lambda i: (0, 0)),
         out_shape=jax.ShapeDtypeStruct((256, 1024), weight.dtype),
         cost_estimate=pl.CostEstimate(flops=0, bytes_accessed=2**20, transcendentals=0),
-    )(block.reshape(1), weight, *earlier)
+    )(weight, weight, *earlier)
+
+
+def finish(d_part, tokens, grads, inverse, row_mean, gain, *earlier):
+    def kernel(d_ref, x_ref, g_ref, inverse_ref, mean_ref, gain_ref, *refs):
+        grad_out, gain_out = refs[-2:]
+        d = d_ref[...].astype(jnp.float32)
+        scale = inverse_ref[...]
+        unit = x_ref[...].astype(jnp.float32) * scale
+        d_tokens = scale * (d * gain_ref[...] - unit * mean_ref[...])
+        grad_out[...] = (g_ref[...].astype(jnp.float32) + d_tokens).astype(grad_out.dtype)
+        gain_out[...] = jnp.sum(d * unit, axis=0, keepdims=True)
+
+    return pl.pallas_call(
+        kernel,
+        in_specs=[pl.BlockSpec(memory_space=pltpu.VMEM)] * 6 + [ANYWHERE] * len(earlier),
+        out_specs=[pl.BlockSpec(memory_space=pltpu.VMEM)] * 2,
+        out_shape=[
+            jax.ShapeDtypeStruct(grads.shape, grads.dtype),
+            jax.ShapeDtypeStruct((1, grads.shape[1]), jnp.float32),
+        ],
+        cost_estimate=pl.CostEstimate(
+            flops=8 * grads.size, bytes_accessed=8 * grads.size, transcendentals=0
+        ),
+        compiler_params=pltpu.CompilerParams(vmem_limit_bytes=VMEM_LIMIT),
+    )(d_part, tokens, grads, inverse, row_mean, gain, *earlier)
 
 
 def after(array, *earlier):
@@ -390,7 +447,9 @@
     seq = passages.shape[1]
     pos = jnp.stack([me, group]).astype(jnp.int32)
 
-    counts = lax.all_gather(passage_counts, "pas", axis=0, tiled=True)
+    first_chunk = cut(w_key, group * 2, 256, ())
+
+    counts = lax.all_gather(after(passage_counts, first_chunk), "pas", axis=0, tiled=True)
     index = jnp.arange(4, dtype=jnp.int32)
     single = counts == 1
     source = jnp.sum(jnp.where(counts == 4, index, 0))
@@ -413,15 +472,26 @@
         return jnp.where(own_count >= 2, array[1], foreign)
 
     weights = (w_key, w_query, w_value, w_out)
-    over_x, over_y = [], []
+    over_x, over_y, cuts = [], [], []
 
     def send(*earlier):
         i = len(over_x)
-        chunk = cut(weights[i // 2], group * 2 + i % 2, earlier)
+        if i == 8:
+            chunk = cut_ends(w_out, earlier)
+        elif i == 7:
+            chunk = cut(w_out, group * 4 + 2, 128, earlier)
+        elif i == 0:
+            chunk = first_chunk
+        else:
+            chunk = cut(weights[i // 2], group * 2 + i % 2, 256, earlier)
+        cuts.append(chunk)
         over_x.append(swap(chunk, "pas", 2))
 
-    def forward():
-        over_y.append(swap(over_x[len(over_y)], "grp", 1))
+    def forward(*earlier):
+        i = len(over_y)
+        if earlier:
+            over_x[i] = after(over_x[i], *earlier)
+        over_y.append(swap(over_x[i], "grp", 1))
 
     def fetch(i):
         far = far_block(over_x[i : i + 2] + over_y[i : i + 2], group)
@@ -433,6 +503,8 @@
     tokens_x = swap(tokens_sent, "pas", 2)
     grads_x = swap(grads_sent, "pas", 2)
     tokens = jnp.concatenate([passages[0], second(passages, tokens_core, tokens_x)], axis=0)
+    send(tokens_sent)
+    tokens = after(tokens, cuts[1])
     grads = jnp.concatenate([cotangent[0], second(cotangent, grads_core, grads_x)], axis=0)
     all_tokens = lax.all_gather(tokens, "fsdp", axis=0)
     all_grads = lax.all_gather(grads, "fsdp", axis=0)
@@ -448,32 +520,35 @@
     rows_shape = jax.ShapeDtypeStruct((2 * seq, 1024), jnp.bfloat16)
     wide_shape = jax.ShapeDtypeStruct((4, 2 * seq, 1024), jnp.bfloat16)
 
-    def project(w):
-        return call(project_kernel, pos, [normed], [w], rows_shape)
-
-    send(tokens_sent, grads_sent)
+    def project(w, *earlier):
+        return call(project_kernel, pos, [normed], [w], rows_shape, *earlier)
+
+    send(over_x[0], tokens_x)
+    forward(cuts[2])
+    send(over_x[1], grads_sent)
+    forward(cuts[3])
+    key_w = fetch(0)
+    send(over_x[2], over_y[0])
+    forward(cuts[4])
+    send(over_x[3], over_y[1], grads)
+    forward(cuts[5])
+    query_w = fetch(2)
+    send(over_x[4], over_y[2])
+    forward(cuts[6])
+    send(over_x[5], over_y[3])
+    forward(cuts[7])
+    send(over_x[6], over_y[4])
+    forward(cuts[8])
+    keys = project(key_w)
+    query = project(query_w)
+    over_x[8] = after(over_x[8], over_y[5], keys, query)
     forward()
-    send(over_x[0], tokens_x, grads_x)
-    forward()
-    send(over_x[1], over_y[0], grads)
-    key_w = fetch(0)
-    forward()
-    send(over_x[2], over_y[1])
-    forward()
-    send(over_x[3], over_y[2])
-    query_w = fetch(2)
-    forward()
-    keys = project(key_w)
-    send(over_x[4], over_y[3], keys)
-    forward()
-    query = project(query_w)
-    send(over_x[5], over_y[4], query)
-    value_w = fetch(4)
-    forward()
-    forward()
-    far = over_x[6:] + over_y[6:]
-    out_w = [w_out, swap(w_out, "pas", 1), far, [swap(c, "pas", 1) for c in far]]
-    values = project(value_w)
+    far = over_x[4:6] + over_y[4:6]
+    value_w = [w_value, swap(w_value, "pas", 1), far, [swap(c, "pas", 1) for c in far]]
+    far = over_x[6:9] + over_y[6:8]
+    far_core = [swap(c, "pas", 1) for c in far]
+    out_w = [w_out, swap(w_out, "pas", 1), far + far[2:3], far_core + far_core[2:3]]
+    values = project(value_w, all_grads)
     (context,) = attend(attention_kernel, (query, keys, values), 1)
     partial_out = call(emit_kernel, pos, [context], [out_w], wide_shape)
     attention = lax.psum_scatter(partial_out, "fsdp", scatter_dimension=0)
@@ -484,7 +559,7 @@
     )
 
     d_normed = after(d_normed, attention)
-    d_part = lax.psum_scatter(d_normed, "fsdp", scatter_dimension=0).astype(jnp.float32)
+    d_part = lax.psum_scatter(d_normed, "fsdp", scatter_dimension=0)
 
     row_total = jnp.sum(
         d_normed.astype(jnp.float32) * gain * (tokens_f32 * inverse), axis=(0, 2)
@@ -494,15 +569,7 @@
     row_mean = row_total.reshape(2 * seq, 1) / width
 
     gain_part = lax.dynamic_slice_in_dim(norm_gain, feature * 1024, 1024, 0)
-    inverse_rows = inverse.reshape(2 * seq, 1)
-    unit_part = tokens.astype(jnp.float32) * inverse_rows
-    d_tokens = inverse_rows * (d_part * gain_part - unit_part * row_mean)
-    input_local = (grads.astype(jnp.float32) + d_tokens).astype(jnp.bfloat16)
-    states = (tokens.astype(jnp.float32) + attention.astype(jnp.float32)).astype(jnp.bfloat16)
-    gain_grad = jnp.sum(d_part * unit_part, axis=0).reshape(8, 128)
-    gain_grad += swap(gain_grad, "pas", 1)
-    gain_grad += swap(gain_grad, "pas", 2)
-
+    states = (tokens.astype(jnp.float32) + attention.reshape(2 * seq, 1024).astype(jnp.float32)).astype(jnp.bfloat16)
     def home(local):
         local = local.reshape(2, seq, 1024)
         back = local[1]
@@ -523,7 +590,21 @@
             ]
         )
 
-    return home(states), home(input_local), gain_grad.reshape(1024)
+    encoded = home(states)
+    input_local, gain_grad = finish(
+        d_part.reshape(2 * seq, 1024),
+        tokens,
+        grads,
+        inverse.reshape(2 * seq, 1),
+        row_mean,
+        gain_part.reshape(1, 1024),
+        encoded,
+    )
+    input_grad = home(input_local)
+    gain_grad = gain_grad.reshape(8, 128)
+    gain_grad += swap(gain_grad, "pas", 1)
+    gain_grad += swap(gain_grad, "pas", 2)
+    return encoded, input_grad, gain_grad.reshape(1024)
 
 
 def solution(mesh):

time: 323 us -> 301 us (0.932)
  waiting for transfers between devices: 155 us -> 135 us
  other arithmetic: 28.3 us -> 17.5 us
  starting transfers between devices: 29.7 us -> 36.5 us
  Pallas kernels: 67.7 us -> 73.4 us
  local copies, waits for them, and re-layouts: 16.6 us -> 12.9 us
    ppermute x39 -> x44, waiting for transfers between devices: 107 us -> 91.3 us  [swap(): lax.ppermute(array, axis, [(i, i ^ bit) for i in range(lax.axis_size(axis...]
    ppermute x39 -> x44, starting transfers between devices: 29.1 us -> 36.2 us  [swap(): lax.ppermute(array, axis, [(i, i ^ bit) for i in range(lax.axis_size(axis...]
    reduce_scatter x1, waiting for transfers between devices: 32.7 us -> 26.5 us  [fast_body(): d_part = lax.psum_scatter(d_normed, 'fsdp', scatter_dimension=0)]
    unnamed x81 -> x83, local copies, waits for them, and re-layouts: 14.6 us -> 10.5 us
    select_n x3 -> x2, other arithmetic: 10.1 us -> 6.68 us  [far_block(): jnp.where(group == 0, jnp.concatenate([low, high]), jnp.concatenate([high...]
  transfers between devices with their start and end apart: 43 -> 48, of which waited for: 21 -> 20; matrix products, arithmetic and copies ran while one was open for 8% -> 6% of each run, Pallas kernels for 21% -> 22%
where the time goes in v3:
time: 301 us; the launch traced here: 300 us
  waiting for transfers between devices  135 us (45%)
  Pallas kernels  73.4 us (24%)
  starting transfers between devices  36.5 us (12%)
  between operations  19.1 us (6%)
  other arithmetic  17.5 us (6%)
  local copies, waits for them, and re-layouts  12.9 us (4%)
  blocking collectives  5.92 us (2%)
    ppermute x44, waiting for transfers between devices, swap(): lax.ppermute(array, axis, [(i, i ^ bit) for i in range(lax.axis_size(axis...  91.3 us
    pallas_call x6, Pallas kernels, call(): pl.pallas_call(run, in_specs=[pl.BlockSpec(memory_space=pltpu.SMEM)] + [p...  43.9 us
    ppermute x44, starting transfers between devices, swap(): lax.ppermute(array, axis, [(i, i ^ bit) for i in range(lax.axis_size(axis...  36.2 us
    reduce_scatter x1, waiting for transfers between devices, fast_body(): d_part = lax.psum_scatter(d_normed, 'fsdp', scatter_dimension=0)  26.5 us
    reduce_scatter x1, waiting for transfers between devices, fast_body(): attention = lax.psum_scatter(partial_out, 'fsdp', scatter_dimension=0)  17 us
    pallas_call x8, Pallas kernels, cut(): pl.pallas_call(copy, grid_spec=pltpu.PrefetchScalarGridSpec(num_scalar_pr...  15 us
    pallas_call x2, Pallas kernels, attend(): pl.pallas_call(kernel, grid=(BAL, 2), in_specs=[spec] * len(arrays), out_...  11.6 us
    unnamed x83, local copies, waits for them, and re-layouts  10.5 us
  transfers between devices with their start and end apart: 48, of which 20 were waited for; matrix products, arithmetic and copies ran while one was open for 6% of the time, Pallas kernels for 22%

profile of v3, /device:TPU:0, one launch (start us, length us, event | category | flops | bytes accessed | tf_op | source)
XLA Modules:
  0.0 300.2 jit_solution(12905307736610484653)
XLA Ops:
  7.2 1.2 slice.84
  9.6 1.9 shard_map.103.refs_1_
  12.6 1.4 dynamic-update-slice
  14.0 5.9 %all-reduce = s32[4]{0:T(128)S(1)} all-reduce(s32[4]{0:T(128)S(1)} %dynamic-update-slice), channel_id=1, replica_groups=mesh['grp'=2,'pas'=4,'fsdp'=4] {'pas'}, use_global_device_ids=true, to_apply=%add | all-reduce | flops 4 | bytes 32
  24.4 1.9 shard_map.105.refs_1_
  26.3 3.7 %collective-permute-done.1.refs_1_ = bf16[128,1024]{1,0:T(8,128)(2,1)S(1)} collective-permute-done((bf16[128,1024]{1,0:T(8,128)(2,1)S(1)}, bf16[128,1024]{1,0:T(8,128)(2,1)S(1)}, u32[]{:S(2)}, u32[]{:S(2)}) %collective-permute-start.1) | collective-permute-done | bytes 262176 | tf_op jit(solution)/shard_map/ppermute | solution.py:178
  32.5 1.5 collective-permute-start.6
  34.0 12.2 %collective-permute-done.3.refs_0_ = bf16[256,1024]{1,0:T(8,128)(2,1)S(1)} collective-permute-done((bf16[256,1024]{1,0:T(8,128)(2,1)}, bf16[256,1024]{1,0:T(8,128)(2,1)S(1)}, u32[]{:S(2)}, u32[]{:S(2)}) %collective-permute-start.3) | collective-permute-done | bytes 524320 | tf_op jit(solution)/shard_map/ppermute | solution.py:178
  46.9 1.9 shard_map.107.refs_1_
  48.8 1.5 collective-permute-start.5
  51.8 4.7 %collective-permute-done.6.refs_0_ = bf16[256,1024]{1,0:T(8,128)(2,1)S(1)} collective-permute-done((bf16[256,1024]{1,0:T(8,128)(2,1)}, bf16[256,1024]{1,0:T(8,128)(2,1)S(1)}, u32[]{:S(2)}, u32[]{:S(2)}) %collective-permute-start.6) | collective-permute-done | bytes 524320 | tf_op jit(solution)/shard_map/ppermute | solution.py:178
  57.3 1.9 shard_map.111.refs_1_
  59.2 2.5 collective-permute-start.9
  61.7 2.0 collective-permute-start.10
  63.7 4.0 %collective-permute-done.4.refs_0_ = bf16[256,1024]{1,0:T(8,128)(2,1)S(1)} collective-permute-done((bf16[256,1024]{1,0:T(8,128)(2,1)}, bf16[256,1024]{1,0:T(8,128)(2,1)S(1)}, u32[]{:S(2)}, u32[]{:S(2)}) %collective-permute-start.4) | collective-permute-done | bytes 524320 | tf_op jit(solution)/shard_map/ppermute | solution.py:178
  68.5 1.9 shard_map.109.refs_1_
  70.4 2.4 collective-permute-start.11
  72.8 10.4 %collective-permute-done.10 = bf16[128,1024]{1,0:T(8,128)(2,1)} collective-permute-done((bf16[128,1024]{1,0:T(8,128)(2,1)S(1)}, bf16[128,1024]{1,0:T(8,128)(2,1)}, u32[]{:S(2)}, u32[]{:S(2)}) %collective-permute-start.10) | collective-permute-done | bytes 262176 | tf_op jit(solution)/shard_map/ppermute | solution.py:178
  83.3 1.0 fusion.7
  86.2 2.0 shard_map.113.refs_1_
  88.2 1.5 collective-permute-start.12
  89.8 9.2 %collective-permute-done.17.refs_0_ = bf16[256,1024]{1,0:T(8,128)(2,1)S(1)} collective-permute-done((bf16[256,1024]{1,0:T(8,128)(2,1)}, bf16[256,1024]{1,0:T(8,128)(2,1)S(1)}, u32[]{:S(2)}, u32[]{:S(2)}) %collective-permute-start.17) | collective-permute-done | bytes 524320 | tf_op jit(solution)/shard_map/ppermute | solution.py:178
  99.3 3.3 %collective-permute-done.12.refs_1_ = bf16[256,1024]{1,0:T(8,128)(2,1)} collective-permute-done((bf16[256,1024]{1,0:T(8,128)(2,1)}, bf16[256,1024]{1,0:T(8,128)(2,1)}, u32[]{:S(2)}, u32[]{:S(2)}) %collective-permute-start.12) | collective-permute-done | bytes 524320 | tf_op jit(solution)/shard_map/ppermute | solution.py:178
  102.6 1.5 collective-permute-start.18
  104.1 3.5 %maximum_select_fusion.1.refs_3_.refs_9_ = bf16[1024,1024]{1,0:T(8,128)(2,1)} fusion(bf16[256,1024]{1,0:T(8,128)(2,1)} %copy-done.29, bf16[256,1024]{1,0:T(8,128)(2,1)} %copy-done.31, bf16[256,1024]{1,0:T(8,128)(2,1)} %shard_map.112, bf16[256,1024]{1,0:T(8,128)(2,1)} %shard_map.108, pred[]{:T(512)S(6)} %eq.57), kind=kLoop, calls=%fused_computation.8 | loop fusion | flops 17825792 | bytes 4194305 | tf_op jit(solution)/shard_map/jit(_where)/select_n | solution.py:440
  107.6 3.2 %maximum_select_fusion.refs_3_.refs_5_ = bf16[1024,1024]{1,0:T(8,128)(2,1)} fusion(bf16[256,1024]{1,0:T(8,128)(2,1)} %collective-permute-done.12.refs_1_, bf16[256,1024]{1,0:T(8,128)(2,1)} %collective-permute-done.11.refs_1_, bf16[256,1024]{1,0:T(8,128)(2,1)S(1)} %copy-done.20, bf16[256,1024]{1,0:T(8,128)(2,1)S(1)} %copy-done.22, pred[]{:T(512)S(6)} %eq.57), kind=kLoop, calls=%fused_computation.7 | loop fusion | flops 17825792 | bytes 4194305 | tf_op jit(solution)/shard_map/jit(_where)/select_n | solution.py:440
  110.8 5.3 %collective-permute-done.18.refs_0_ = bf16[256,1024]{1,0:T(8,128)(2,1)} collective-permute-done((bf16[256,1024]{1,0:T(8,128)(2,1)}, bf16[256,1024]{1,0:T(8,128)(2,1)}, u32[]{:S(2)}, u32[]{:S(2)}) %collective-permute-start.18) | collective-permute-done | bytes 524320 | tf_op jit(solution)/shard_map/ppermute | solution.py:178
  116.7 1.9 shard_map.117.refs_1_
  118.6 1.9 collective-permute-start.19
  120.5 1.5 collective-permute-start.26
  122.0 1.7 shard_map.119.refs_1_
  123.7 9.2 %collective-permute-done.19.refs_5_.refs_1_.refs_15_ = bf16[256,1024]{1,0:T(8,128)(2,1)} collective-permute-done((bf16[256,1024]{1,0:T(8,128)(2,1)}, bf16[256,1024]{1,0:T(8,128)(2,1)}, u32[]{:S(2)}, u32[]{:S(2)}) %collective-permute-start.19) | collective-permute-done | bytes 524320 | tf_op jit(solution)/shard_map/ppermute | solution.py:178
  132.9 1.5 collective-permute-start.27
  134.4 1.7 collective-permute-start.20
  136.2 1.9 shard_map.123.refs_1_
  138.1 2.2 fusion.4
  140.7 1.5 collective-permute-start.28
  143.1 4.6 %collective-permute-done.20.refs_6_.refs_1_.refs_16_ = bf16[256,1024]{1,0:T(8,128)(2,1)} collective-permute-done((bf16[256,1024]{1,0:T(8,128)(2,1)}, bf16[256,1024]{1,0:T(8,128)(2,1)}, u32[]{:S(2)}, u32[]{:S(2)}) %collective-permute-start.20) | collective-permute-done | bytes 524320 | tf_op jit(solution)/shard_map/ppermute | solution.py:178
  147.7 1.4 collective-permute-start.29
  149.9 3.2 %collective-permute-done.28.refs_0_ = bf16[256,1024]{1,0:T(8,128)(2,1)S(1)} collective-permute-done((bf16[256,1024]{1,0:T(8,128)(2,1)S(1)}, bf16[256,1024]{1,0:T(8,128)(2,1)S(1)}, u32[]{:S(2)}, u32[]{:S(2)}) %collective-permute-start.28) | collective-permute-done | bytes 524320 | tf_op jit(solution)/shard_map/ppermute | solution.py:178
  153.1 1.3 collective-permute-start.30
  154.9 5.5 %shard_map.116.k_ref.refs_2_ = bf16[256,1024]{1,0:T(8,128)(2,1)S(1)} custom-call(s32[2]{0:T(128)S(1)} %pad_add_fusion.pos_ref, bf16[4,256,1024]{2,1,0:T(8,128)(2,1)S(1)} %fusion.2.refs_0_, bf16[1024,1024]{1,0:T(8,128)(2,1)} %refs_7_.1, bf16[1024,1024]{1,0:T(8,128)(2,1)} %collective-permute-done.14.refs_2_.refs_8_, ...), custom_call_target="tpu_custom_call" | custom-call | flops 2147483648 | bytes 8388608 | tf_op jit(solution)/shard_map/pallas_call | solution.py:273
  161.2 5.5 %shard_map.115.q_ref.refs_3_ = bf16[256,1024]{1,0:T(8,128)(2,1)S(1)} custom-call(s32[2]{0:T(128)S(1)} %pad_add_fusion.pos_ref, bf16[4,256,1024]{2,1,0:T(8,128)(2,1)S(1)} %fusion.2.refs_0_, bf16[1024,1024]{1,0:T(8,128)(2,1)} %refs_3_.1, bf16[1024,1024]{1,0:T(8,128)(2,1)} %collective-permute-done.2.refs_2_.refs_4_, ...), custom_call_target="tpu_custom_call" | custom-call | flops 2147483648 | bytes 8388608 | tf_op jit(solution)/shard_map/pallas_call | solution.py:273
  169.4 6.7 %shard_map.121.v_ref = bf16[256,1024]{1,0:T(8,128)(2,1)S(1)} custom-call(s32[2]{0:T(128)S(1)} %pad_add_fusion.pos_ref, bf16[4,256,1024]{2,1,0:T(8,128)(2,1)} %copy-done, bf16[1024,1024]{1,0:T(8,128)(2,1)} %refs_11_.1, bf16[1024,1024]{1,0:T(8,128)(2,1)} %collective-permute-done.16.refs_2_.refs_12_, bf16[256,1024]{1,0:T(8,128)(2,1)S(1)} %copy-done.5, ...), custom_call_target="tpu_custom_call" | custom-call | flops 2147483648 | bytes 8388608 | tf_op jit(solution)/shard_map/pallas_call | solution.py:273
  176.1 3.8 %shard_map.122.refs_0_ = bf16[256,1024]{1,0:T(8,128)(2,1)S(1)} custom-call(bf16[256,1024]{1,0:T(8,128)(2,1)S(1)} %copy-done.10, bf16[256,1024]{1,0:T(8,128)(2,1)S(1)} %copy-done.8, bf16[256,1024]{1,0:T(8,128)(2,1)S(1)} %shard_map.121.v_ref), custom_call_target="tpu_custom_call" | custom-call | flops 536870912 | bytes 2097152 | tf_op jit(solution)/shard_map/pallas_call | solution.py:350
  179.9 6.6 %shard_map.126.refs_1_ = bf16[4,256,1024]{2,1,0:T(8,128)(2,1)} custom-call(s32[2]{0:T(128)S(1)} %pad_add_fusion.pos_ref, bf16[256,1024]{1,0:T(8,128)(2,1)S(1)} %shard_map.122.refs_0_, bf16[1024,1024]{1,0:T(8,128)(2,1)} %refs_1_.9, bf16[1024,1024]{1,0:T(8,128)(2,1)} %collective-permute-done.25.refs_2_, bf16[256,1024]{1,0:T(8,128)(2,1)} %shard_map.124.refs_3_, ...), custom_call_target="tpu_custom_call" | custom-call | flops 2147483648 | bytes 8388608 | tf_op jit(solution)/shard_map/pallas_call | solution.py:273
  186.6 6.7 %shard_map.128.dc_ref = bf16[256,1024]{1,0:T(8,128)(2,1)S(1)} custom-call(s32[2]{0:T(128)S(1)} %pad_add_fusion.pos_ref, bf16[4,256,1024]{2,1,0:T(8,128)(2,1)} %shard_map.127.refs_0_, bf16[1024,1024]{1,0:T(8,128)(2,1)} %refs_1_.9, bf16[1024,1024]{1,0:T(8,128)(2,1)} %collective-permute-done.25.refs_2_, bf16[256,1024]{1,0:T(8,128)(2,1)} %shard_map.124.refs_3_, ...), custom_call_target="tpu_custom_call" | custom-call | flops 2147483648 | bytes 8388608 | tf_op jit(solution)/shard_map/pallas_call | solution.py:273
  193.3 7.9 %shard_map.129 = (bf16[256,1024]{1,0:T(8,128)(2,1)S(1)}, bf16[256,1024]{1,0:T(8,128)(2,1)S(1)}, bf16[256,1024]{1,0:T(8,128)(2,1)S(1)}) custom-call(bf16[256,1024]{1,0:T(8,128)(2,1)S(1)} %copy-done.10, bf16[256,1024]{1,0:T(8,128)(2,1)S(1)} %copy-done.8, bf16[256,1024]{1,0:T(8,128)(2,1)S(1)} %shard_map.121.v_ref, bf16[256,1024]{1,0:T(8,128)(2,1)S(1)} %shard_map.128.dc_ref), custom_call_target="tpu_custom_call" | custom-call | flops 536870912 | bytes 3670016 | tf_op jit(solution)/shard_map/pallas_call | solution.py:350
  201.1 13.0 %shard_map.130.refs_0_ = bf16[4,256,1024]{2,1,0:T(8,128)(2,1)} custom-call(s32[2]{0:T(128)S(1)} %pad_add_fusion.pos_ref, bf16[256,1024]{1,0:T(8,128)(2,1)S(1)} %get-tuple-element.8.refs_0_, bf16[256,1024]{1,0:T(8,128)(2,1)S(1)} %get-tuple-element.9.refs_1_, bf16[256,1024]{1,0:T(8,128)(2,1)S(1)} %get-tuple-element.10.refs_2_, bf16[1024,1024]{1,0:T(8,128)(2,1)} %refs_3_.1, ...), custom_call_target="tpu_custom_call" | custom-call | flops 6442450944 | bytes 25165824 | tf_op jit(solution)/shard_map/pallas_call | solution.py:273
  214.2 17.0 %reduce-scatter.3.cloned.1.call-done = bf16[1,256,1024]{2,1,0:T(8,128)(2,1)} async-done(((bf16[4,256,1024]{2,1,0:T(8,128)(2,1)}), bf16[1,256,1024]{2,1,0:T(8,128)(2,1)}) %reduce-scatter.3.cloned.1.call-update) | async-done | bytes 524304 | tf_op jit(solution)/shard_map/reduce_scatter | solution.py:554
  231.2 1.0 copy-done.3
  232.7 1.5 collective-permute-start.36
  234.2 6.4 %collective-permute-done.36 = bf16[128,1024]{1,0:T(8,128)(2,1)S(1)} collective-permute-done((bf16[128,1024]{1,0:T(8,128)(2,1)S(1)}, bf16[128,1024]{1,0:T(8,128)(2,1)S(1)}, u32[]{:S(2)}, u32[]{:S(2)}) %collective-permute-start.36) | collective-permute-done | bytes 262176 | tf_op jit(solution)/shard_map/ppermute | solution.py:178
  241.8 3.6 %collective-permute-done.38 = f32[2,128]{1,0:T(2,128)S(1)} collective-permute-done((f32[2,128]{1,0:T(2,128)S(1)}, f32[2,128]{1,0:T(2,128)S(1)}, u32[]{:S(2)}, u32[]{:S(2)}) %collective-permute-start.38) | collective-permute-done | bytes 1056 | tf_op jit(solution)/shard_map/ppermute | solution.py:178
  245.4 1.9 collective-permute-start.39
  248.8 1.1 collective-permute-done.39
  250.2 26.5 %reduce-scatter.5.cloned.1.call-done = bf16[1,256,1024]{2,1,0:T(8,128)(2,1)} async-done(((bf16[4,256,1024]{2,1,0:T(8,128)(2,1)}), bf16[1,256,1024]{2,1,0:T(8,128)(2,1)}) %reduce-scatter.5.cloned.1.call-update) | async-done | bytes 524304 | tf_op jit(solution)/shard_map/reduce_scatter | solution.py:562
  276.7 1.0 copy-done.14
  278.3 1.5 collective-permute-start.40
  279.9 6.4 %collective-permute-done.40 = bf16[128,1024]{1,0:T(8,128)(2,1)S(1)} collective-permute-done((bf16[128,1024]{1,0:T(8,128)(2,1)S(1)}, bf16[128,1024]{1,0:T(8,128)(2,1)S(1)}, u32[]{:S(2)}, u32[]{:S(2)}) %collective-permute-start.40) | collective-permute-done | bytes 262176 | tf_op jit(solution)/shard_map/ppermute | solution.py:178
  286.9 1.4 collective-permute-done.42
  288.3 1.5 collective-permute-start.43
  289.7 2.1 collective-permute-done.43
  292.5 1.1 pad_maximum_fusion.1
  (187 shorter events, 22.6 us)
Async XLA Ops:
  7.2 14.8 %copy-start.25 = (bf16[4,128,1024]{2,1,0:T(8,128)(2,1)S(1)}, bf16[4,128,1024]{2,1,0:T(8,128)(2,1)}, u32[]{:S(2)}) copy-start(bf16[4,128,1024]{2,1,0:T(8,128)(2,1)} %param.8) | copy-start | bytes 3145732
  7.2 130.9 %all-gather.5.cloned.1.call-start = ((), (), s32[]{:S(2)}) async-start(), calls=%async_computation.4 | async-start | bytes 2621440 | tf_op jit(solution)/shard_map/all_gather | solution.py:509
  8.4 13.6 %collective-permute-start = (bf16[2,128,1024]{2,1,0:T(8,128)(2,1)S(1)}, bf16[2,128,1024]{2,1,0:T(8,128)(2,1)S(1)}, u32[]{:S(2)}, u32[]{:S(2)}) collective-permute-start(bf16[2,128,1024]{2,1,0:T(8,128)(2,1)S(1)} %slice.84), channel_id=1, source_target_pairs={{0,4},{4,0},{8,12},{12,8},{1,5},{5,1},{9,13},{13,9},{2,6},{6,2},{1... | collective-permute-start | bytes 1572872 | tf_op jit(solution)/shard_map/ppermute | solution.py:178
  22.1 7.9 %collective-permute-start.1 = (bf16[128,1024]{1,0:T(8,128)(2,1)S(1)}, bf16[128,1024]{1,0:T(8,128)(2,1)S(1)}, u32[]{:S(2)}, u32[]{:S(2)}) collective-permute-start(bf16[128,1024]{1,0:T(8,128)(2,1)S(1)} %fusion.9.refs_0_), channel_id=1, source_target_pairs={{0,8},{4,12},{8,0},{12,4},{1,9},{5,13},{9,1},{13,5},{2,10},{6,14},... | collective-permute-start | bytes 786440 | tf_op jit(solution)/shard_map/ppermute | solution.py:178
  31.0 137.7 %all-gather.7.cloned.1.call-start = ((), (), s32[]{:S(2)}) async-start(), calls=%async_computation.5 | async-start | bytes 2621440 | tf_op jit(solution)/shard_map/all_gather | solution.py:510
  31.0 15.1 %collective-permute-start.3 = (bf16[256,1024]{1,0:T(8,128)(2,1)}, bf16[256,1024]{1,0:T(8,128)(2,1)S(1)}, u32[]{:S(2)}, u32[]{:S(2)}) collective-permute-start(bf16[256,1024]{1,0:T(8,128)(2,1)} %shard_map.103.refs_1_), channel_id=1, source_target_pairs={{0,8},{4,12},{8,0},{12,4},{1,9},{5,13},{9,1},{13,5},{2,10},{6,14},... | collective-permute-start | bytes 1572872 | tf_op jit(solution)/shard_map/ppermute | solution.py:178
  32.5 18.4 %collective-permute-start.7 = (bf16[2,128,1024]{2,1,0:T(8,128)(2,1)}, bf16[2,128,1024]{2,1,0:T(8,128)(2,1)S(1)}, u32[]{:S(2)}, u32[]{:S(2)}) collective-permute-start(bf16[2,128,1024]{2,1,0:T(8,128)(2,1)} %slice.89), channel_id=1, source_target_pairs={{0,4},{4,0},{8,12},{12,8},{1,5},{5,1},{9,13},{13,9},{2,6},{6,2},{1... | collective-permute-start | bytes 1572872 | tf_op jit(solution)/shard_map/ppermute | solution.py:178
  32.5 23.9 %collective-permute-start.6 = (bf16[256,1024]{1,0:T(8,128)(2,1)}, bf16[256,1024]{1,0:T(8,128)(2,1)S(1)}, u32[]{:S(2)}, u32[]{:S(2)}) collective-permute-start(bf16[256,1024]{1,0:T(8,128)(2,1)} %shard_map.105.refs_1_), channel_id=1, source_target_pairs={{0,8},{4,12},{8,0},{12,4},{1,9},{5,13},{9,1},{13,5},{2,10},{6,14},... | collective-permute-start | bytes 1572872 | tf_op jit(solution)/shard_map/ppermute | solution.py:178
  48.8 12.9 %collective-permute-start.5 = (bf16[256,1024]{1,0:T(8,128)(2,1)}, bf16[256,1024]{1,0:T(8,128)(2,1)S(1)}, u32[]{:S(2)}, u32[]{:S(2)}) collective-permute-start(bf16[256,1024]{1,0:T(8,128)(2,1)} %shard_map.108), channel_id=1, source_target_pairs={{0,16},{16,0},{1,17},{17,1},{2,18},{18,2},{3,19},{19,3},{4,20},{20... | collective-permute-start | bytes 1572872 | tf_op jit(solution)/shard_map/ppermute | solution.py:178
  50.3 65.8 %collective-permute-start.14 = (bf16[1024,1024]{1,0:T(8,128)(2,1)}, bf16[1024,1024]{1,0:T(8,128)(2,1)}, u32[]{:S(2)}, u32[]{:S(2)}) collective-permute-start(bf16[1024,1024]{1,0:T(8,128)(2,1)} %refs_7_.1), channel_id=1, source_target_pairs={{0,4},{4,0},{8,12},{12,8},{1,5},{5,1},{9,13},{13,9},{2,6},{6,2},{1... | collective-permute-start | bytes 6291464 | tf_op jit(solution)/shard_map/ppermute | solution.py:178
  50.3 17.4 %collective-permute-start.4 = (bf16[256,1024]{1,0:T(8,128)(2,1)}, bf16[256,1024]{1,0:T(8,128)(2,1)S(1)}, u32[]{:S(2)}, u32[]{:S(2)}) collective-permute-start(bf16[256,1024]{1,0:T(8,128)(2,1)} %shard_map.107.refs_1_), channel_id=1, source_target_pairs={{0,8},{4,12},{8,0},{12,4},{1,9},{5,13},{9,1},{13,5},{2,10},{6,14},... | collective-permute-start | bytes 1572872 | tf_op jit(solution)/shard_map/ppermute | solution.py:178
  50.9 8.2 %copy-start.32 = (bf16[2,128,1024]{2,1,0:T(8,128)(2,1)}, bf16[2,128,1024]{2,1,0:T(8,128)(2,1)S(1)}, u32[]{:S(2)}) copy-start(bf16[2,128,1024]{2,1,0:T(8,128)(2,1)S(1)} %collective-permute-done.7) | copy-start | bytes 1572868
  51.8 9.9 %copy-start.36 = (bf16[128,1024]{1,0:T(8,128)(2,1)S(1)}, bf16[128,1024]{1,0:T(8,128)(2,1)}, u32[]{:S(2)}) copy-start(bf16[128,1024]{1,0:T(8,128)(2,1)} %fusion.8.refs_1_) | copy-start | bytes 786436
  59.2 25.1 %collective-permute-start.9 = (bf16[256,1024]{1,0:T(8,128)(2,1)}, bf16[256,1024]{1,0:T(8,128)(2,1)S(1)}, u32[]{:S(2)}, u32[]{:S(2)}) collective-permute-start(bf16[256,1024]{1,0:T(8,128)(2,1)} %shard_map.112), channel_id=1, source_target_pairs={{0,16},{16,0},{1,17},{17,1},{2,18},{18,2},{3,19},{19,3},{4,20},{20... | collective-permute-start | bytes 1572872 | tf_op jit(solution)/shard_map/ppermute | solution.py:178
  61.6 23.5 %collective-permute-start.8 = (bf16[256,1024]{1,0:T(8,128)(2,1)}, bf16[256,1024]{1,0:T(8,128)(2,1)S(1)}, u32[]{:S(2)}, u32[]{:S(2)}) collective-permute-start(bf16[256,1024]{1,0:T(8,128)(2,1)} %shard_map.111.refs_1_), channel_id=1, source_target_pairs={{0,8},{4,12},{8,0},{12,4},{1,9},{5,13},{9,1},{13,5},{2,10},{6,14},... | collective-permute-start | bytes 1572872 | tf_op jit(solution)/shard_map/ppermute | solution.py:178
  61.7 21.6 %collective-permute-start.10 = (bf16[128,1024]{1,0:T(8,128)(2,1)S(1)}, bf16[128,1024]{1,0:T(8,128)(2,1)}, u32[]{:S(2)}, u32[]{:S(2)}) collective-permute-start(bf16[128,1024]{1,0:T(8,128)(2,1)S(1)} %copy-done.36), channel_id=1, source_target_pairs={{0,8},{4,12},{8,0},{12,4},{1,9},{5,13},{9,1},{13,5},{2,10},{6,14},... | collective-permute-start | bytes 786440 | tf_op jit(solution)/shard_map/ppermute | solution.py:178
  70.4 12.9 %copy-start.33 = (bf16[2,128,1024]{2,1,0:T(8,128)(2,1)S(1)}, bf16[2,128,1024]{2,1,0:T(8,128)(2,1)}, u32[]{:S(2)}) copy-start(bf16[2,128,1024]{2,1,0:T(8,128)(2,1)} %copy-done.32) | copy-start | bytes 1572868
  70.4 17.9 %collective-permute-start.11 = (bf16[256,1024]{1,0:T(8,128)(2,1)}, bf16[256,1024]{1,0:T(8,128)(2,1)}, u32[]{:S(2)}, u32[]{:S(2)}) collective-permute-start(bf16[256,1024]{1,0:T(8,128)(2,1)} %shard_map.110), channel_id=1, source_target_pairs={{0,16},{16,0},{1,17},{17,1},{2,18},{18,2},{3,19},{19,3},{4,20},{20... | collective-permute-start | bytes 1572872 | tf_op jit(solution)/shard_map/ppermute | solution.py:178
  83.3 35.3 %collective-permute-start.2 = (bf16[1024,1024]{1,0:T(8,128)(2,1)}, bf16[1024,1024]{1,0:T(8,128)(2,1)}, u32[]{:S(2)}, u32[]{:S(2)}) collective-permute-start(bf16[1024,1024]{1,0:T(8,128)(2,1)} %refs_3_.1), channel_id=1, source_target_pairs={{0,4},{4,0},{8,12},{12,8},{1,5},{5,1},{9,13},{13,9},{2,6},{6,2},{1... | collective-permute-start | bytes 6291464 | tf_op jit(solution)/shard_map/ppermute | solution.py:178
  84.3 36.2 %collective-permute-start.16 = (bf16[1024,1024]{1,0:T(8,128)(2,1)}, bf16[1024,1024]{1,0:T(8,128)(2,1)}, u32[]{:S(2)}, u32[]{:S(2)}) collective-permute-start(bf16[1024,1024]{1,0:T(8,128)(2,1)} %refs_11_.1), channel_id=1, source_target_pairs={{0,4},{4,0},{8,12},{12,8},{1,5},{5,1},{9,13},{13,9},{2,6},{6,2},{1... | collective-permute-start | bytes 6291464 | tf_op jit(solution)/shard_map/ppermute | solution.py:178
  85.1 13.9 %collective-permute-start.17 = (bf16[256,1024]{1,0:T(8,128)(2,1)}, bf16[256,1024]{1,0:T(8,128)(2,1)S(1)}, u32[]{:S(2)}, u32[]{:S(2)}) collective-permute-start(bf16[256,1024]{1,0:T(8,128)(2,1)} %shard_map.109.refs_1_), channel_id=1, source_target_pairs={{0,8},{4,12},{8,0},{12,4},{1,9},{5,13},{9,1},{13,5},{2,10},{6,14},... | collective-permute-start | bytes 1572872 | tf_op jit(solution)/shard_map/ppermute | solution.py:178
  86.2 12.8 %copy-start.15 = (bf16[1024,1024]{1,0:T(8,128)(2,1)S(1)}, bf16[1024,1024]{1,0:T(8,128)(2,1)}, u32[]{:S(2)}) copy-start(bf16[1024,1024]{1,0:T(8,128)(2,1)} %refs_1_.9) | copy-start | bytes 6291460
  88.2 14.4 %collective-permute-start.12 = (bf16[256,1024]{1,0:T(8,128)(2,1)}, bf16[256,1024]{1,0:T(8,128)(2,1)}, u32[]{:S(2)}, u32[]{:S(2)}) collective-permute-start(bf16[256,1024]{1,0:T(8,128)(2,1)} %shard_map.114), channel_id=1, source_target_pairs={{0,16},{16,0},{1,17},{17,1},{2,18},{18,2},{3,19},{19,3},{4,20},{20... | collective-permute-start | bytes 1572872 | tf_op jit(solution)/shard_map/ppermute | solution.py:178
  99.0 8.6 %copy-start.4 = (bf16[256,1024]{1,0:T(8,128)(2,1)}, bf16[256,1024]{1,0:T(8,128)(2,1)S(1)}, u32[]{:S(2)}) copy-start(bf16[256,1024]{1,0:T(8,128)(2,1)S(1)} %collective-permute-done.17.refs_0_) | copy-start | bytes 1572868
  99.0 24.7 %collective-permute-start.25 = (bf16[1024,1024]{1,0:T(8,128)(2,1)S(1)}, bf16[1024,1024]{1,0:T(8,128)(2,1)}, u32[]{:S(2)}, u32[]{:S(2)}) collective-permute-start(bf16[1024,1024]{1,0:T(8,128)(2,1)S(1)} %copy-done.15), channel_id=1, source_target_pairs={{0,4},{4,0},{8,12},{12,8},{1,5},{5,1},{9,13},{13,9},{2,6},{6,2},{1... | collective-permute-start | bytes 6291464 | tf_op jit(solution)/shard_map/ppermute | solution.py:178
  99.0 8.6 %copy-start.20 = (bf16[256,1024]{1,0:T(8,128)(2,1)S(1)}, bf16[256,1024]{1,0:T(8,128)(2,1)}, u32[]{:S(2)}) copy-start(bf16[256,1024]{1,0:T(8,128)(2,1)} %shard_map.114) | copy-start | bytes 1572868
  99.0 132.2 %reduce-scatter.3.cloned.1.call-start = ((), (), s32[]{:S(2)}) async-start(), calls=%async_computation.2 | async-start | bytes 2621440 | tf_op jit(solution)/shard_map/reduce_scatter | solution.py:554
  99.3 8.4 %copy-start.22 = (bf16[256,1024]{1,0:T(8,128)(2,1)S(1)}, bf16[256,1024]{1,0:T(8,128)(2,1)}, u32[]{:S(2)}) copy-start(bf16[256,1024]{1,0:T(8,128)(2,1)} %shard_map.110) | copy-start | bytes 1572868
  102.6 13.6 %collective-permute-start.18 = (bf16[256,1024]{1,0:T(8,128)(2,1)}, bf16[256,1024]{1,0:T(8,128)(2,1)}, u32[]{:S(2)}, u32[]{:S(2)}) collective-permute-start(bf16[256,1024]{1,0:T(8,128)(2,1)} %shard_map.113.refs_1_), channel_id=1, source_target_pairs={{0,8},{4,12},{8,0},{12,4},{1,9},{5,13},{9,1},{13,5},{2,10},{6,14},... | collective-permute-start | bytes 1572872 | tf_op jit(solution)/shard_map/ppermute | solution.py:178
  116.2 38.2 %collective-permute-start.15 = (bf16[1024,1024]{1,0:T(8,128)(2,1)}, bf16[1024,1024]{1,0:T(8,128)(2,1)}, u32[]{:S(2)}, u32[]{:S(2)}) collective-permute-start(bf16[1024,1024]{1,0:T(8,128)(2,1)} %maximum_select_fusion.1.refs_3_.refs_9_), channel_id=1, source_target_pairs={{0,4},{4,0},{8,12},{12,8},{1,5},{5,1},{9,13},{13,9},{2,6},{6,2},{1... | collective-permute-start | bytes 6291464 | tf_op jit(solution)/shard_map/ppermute | solution.py:178
  116.2 38.2 %collective-permute-start.13 = (bf16[1024,1024]{1,0:T(8,128)(2,1)}, bf16[1024,1024]{1,0:T(8,128)(2,1)}, u32[]{:S(2)}, u32[]{:S(2)}) collective-permute-start(bf16[1024,1024]{1,0:T(8,128)(2,1)} %maximum_select_fusion.refs_3_.refs_5_), channel_id=1, source_target_pairs={{0,4},{4,0},{8,12},{12,8},{1,5},{5,1},{9,13},{13,9},{2,6},{6,2},{1... | collective-permute-start | bytes 6291464 | tf_op jit(solution)/shard_map/ppermute | solution.py:178
  118.6 14.4 %collective-permute-start.19 = (bf16[256,1024]{1,0:T(8,128)(2,1)}, bf16[256,1024]{1,0:T(8,128)(2,1)}, u32[]{:S(2)}, u32[]{:S(2)}) collective-permute-start(bf16[256,1024]{1,0:T(8,128)(2,1)} %shard_map.118.refs_3_.refs_13_), channel_id=1, source_target_pairs={{0,16},{16,0},{1,17},{17,1},{2,18},{18,2},{3,19},{19,3},{4,20},{20... | collective-permute-start | bytes 1572872 | tf_op jit(solution)/shard_map/ppermute | solution.py:178
  120.5 13.9 %collective-permute-start.26 = (bf16[256,1024]{1,0:T(8,128)(2,1)}, bf16[256,1024]{1,0:T(8,128)(2,1)}, u32[]{:S(2)}, u32[]{:S(2)}) collective-permute-start(bf16[256,1024]{1,0:T(8,128)(2,1)} %shard_map.117.refs_1_), channel_id=1, source_target_pairs={{0,8},{4,12},{8,0},{12,4},{1,9},{5,13},{9,1},{13,5},{2,10},{6,14},... | collective-permute-start | bytes 1572872 | tf_op jit(solution)/shard_map/ppermute | solution.py:178
  122.0 14.2 %copy-start.38 = (f32[4096]{0:T(1024)S(1)}, f32[4096]{0:T(1024)}, u32[]{:S(2)}) copy-start(f32[4096]{0:T(1024)} %param.11) | copy-start | bytes 49156
  123.7 18.6 %collective-permute-start.21 = (bf16[256,1024]{1,0:T(8,128)(2,1)S(1)}, bf16[256,1024]{1,0:T(8,128)(2,1)S(1)}, u32[]{:S(2)}, u32[]{:S(2)}) collective-permute-start(bf16[256,1024]{1,0:T(8,128)(2,1)S(1)} %copy-done.5), channel_id=1, source_target_pairs={{0,4},{4,0},{8,12},{12,8},{1,5},{5,1},{9,13},{13,9},{2,6},{6,2},{1... | collective-permute-start | bytes 1572872 | tf_op jit(solution)/shard_map/ppermute | solution.py:178
  132.9 7.8 %collective-permute-start.27 = (bf16[128,1024]{1,0:T(8,128)(2,1)}, bf16[128,1024]{1,0:T(8,128)(2,1)S(1)}, u32[]{:S(2)}, u32[]{:S(2)}) collective-permute-start(bf16[128,1024]{1,0:T(8,128)(2,1)} %shard_map.119.refs_1_), channel_id=1, source_target_pairs={{0,8},{4,12},{8,0},{12,4},{1,9},{5,13},{9,1},{13,5},{2,10},{6,14},... | collective-permute-start | bytes 786440 | tf_op jit(solution)/shard_map/ppermute | solution.py:178
  134.4 13.3 %collective-permute-start.20 = (bf16[256,1024]{1,0:T(8,128)(2,1)}, bf16[256,1024]{1,0:T(8,128)(2,1)}, u32[]{:S(2)}, u32[]{:S(2)}) collective-permute-start(bf16[256,1024]{1,0:T(8,128)(2,1)} %shard_map.120.refs_4_.refs_14_), channel_id=1, source_target_pairs={{0,16},{16,0},{1,17},{17,1},{2,18},{18,2},{3,19},{19,3},{4,20},{20... | collective-permute-start | bytes 1572872 | tf_op jit(solution)/shard_map/ppermute | solution.py:178
  138.1 11.1 %copy-start.17 = (bf16[1024,1024]{1,0:T(8,128)(2,1)S(1)}, bf16[1024,1024]{1,0:T(8,128)(2,1)}, u32[]{:S(2)}) copy-start(bf16[1024,1024]{1,0:T(8,128)(2,1)} %all-gather.5.cloned.1.call-done) | copy-start | bytes 6291460
  140.7 12.4 %collective-permute-start.28 = (bf16[256,1024]{1,0:T(8,128)(2,1)S(1)}, bf16[256,1024]{1,0:T(8,128)(2,1)S(1)}, u32[]{:S(2)}, u32[]{:S(2)}) collective-permute-start(bf16[256,1024]{1,0:T(8,128)(2,1)S(1)} %copy-done.34), channel_id=1, source_target_pairs={{0,8},{4,12},{8,0},{12,4},{1,9},{5,13},{9,1},{13,5},{2,10},{6,14},... | collective-permute-start | bytes 1572872 | tf_op jit(solution)/shard_map/ppermute | solution.py:178
  143.1 24.9 %collective-permute-start.22 = (bf16[256,1024]{1,0:T(8,128)(2,1)}, bf16[256,1024]{1,0:T(8,128)(2,1)}, u32[]{:S(2)}, u32[]{:S(2)}) collective-permute-start(bf16[256,1024]{1,0:T(8,128)(2,1)} %shard_map.120.refs_4_.refs_14_), channel_id=1, source_target_pairs={{0,4},{4,0},{8,12},{12,8},{1,5},{5,1},{9,13},{13,9},{2,6},{6,2},{1... | collective-permute-start | bytes 1572872 | tf_op jit(solution)/shard_map/ppermute | solution.py:178
  147.7 19.9 %collective-permute-start.29 = (bf16[256,1024]{1,0:T(8,128)(2,1)}, bf16[256,1024]{1,0:T(8,128)(2,1)}, u32[]{:S(2)}, u32[]{:S(2)}) collective-permute-start(bf16[256,1024]{1,0:T(8,128)(2,1)} %shard_map.124.refs_3_), channel_id=1, source_target_pairs={{0,16},{16,0},{1,17},{17,1},{2,18},{18,2},{3,19},{19,3},{4,20},{20... | collective-permute-start | bytes 1572872 | tf_op jit(solution)/shard_map/ppermute | solution.py:178
  149.9 10.5 %copy-start = (bf16[4,256,1024]{2,1,0:T(8,128)(2,1)}, bf16[4,256,1024]{2,1,0:T(8,128)(2,1)S(1)}, u32[]{:S(2)}) copy-start(bf16[4,256,1024]{2,1,0:T(8,128)(2,1)S(1)} %fusion.2.refs_0_) | copy-start | bytes 6291460
  153.1 7.3 %copy-start.1 = (bf16[256,1024]{1,0:T(8,128)(2,1)}, bf16[256,1024]{1,0:T(8,128)(2,1)S(1)}, u32[]{:S(2)}) copy-start(bf16[256,1024]{1,0:T(8,128)(2,1)S(1)} %collective-permute-done.28.refs_0_) | copy-start | bytes 1572868
  153.1 14.4 %collective-permute-start.30 = (bf16[128,1024]{1,0:T(8,128)(2,1)S(1)}, bf16[128,1024]{1,0:T(8,128)(2,1)}, u32[]{:S(2)}, u32[]{:S(2)}) collective-permute-start(bf16[128,1024]{1,0:T(8,128)(2,1)S(1)} %collective-permute-done.27.refs_4_), channel_id=1, source_target_pairs={{0,16},{16,0},{1,17},{17,1},{2,18},{18,2},{3,19},{19,3},{4,20},{20... | collective-permute-start | bytes 786440 | tf_op jit(solution)/shard_map/ppermute | solution.py:178
  154.4 13.7 %collective-permute-start.23 = (bf16[256,1024]{1,0:T(8,128)(2,1)}, bf16[256,1024]{1,0:T(8,128)(2,1)S(1)}, u32[]{:S(2)}, u32[]{:S(2)}) collective-permute-start(bf16[256,1024]{1,0:T(8,128)(2,1)} %collective-permute-done.19.refs_5_.refs_1_.refs_15_), channel_id=1, source_target_pairs={{0,4},{4,0},{8,12},{12,8},{1,5},{5,1},{9,13},{13,9},{2,6},{6,2},{1... | collective-permute-start | bytes 1572872 | tf_op jit(solution)/shard_map/ppermute | solution.py:178
  154.4 14.1 %collective-permute-start.24 = (bf16[256,1024]{1,0:T(8,128)(2,1)}, bf16[256,1024]{1,0:T(8,128)(2,1)S(1)}, u32[]{:S(2)}, u32[]{:S(2)}) collective-permute-start(bf16[256,1024]{1,0:T(8,128)(2,1)} %collective-permute-done.20.refs_6_.refs_1_.refs_16_), channel_id=1, source_target_pairs={{0,4},{4,0},{8,12},{12,8},{1,5},{5,1},{9,13},{13,9},{2,6},{6,2},{1... | collective-permute-start | bytes 1572872 | tf_op jit(solution)/shard_map/ppermute | solution.py:178
  167.5 12.4 %collective-permute-start.31 = (bf16[256,1024]{1,0:T(8,128)(2,1)}, bf16[256,1024]{1,0:T(8,128)(2,1)}, u32[]{:S(2)}, u32[]{:S(2)}) collective-permute-start(bf16[256,1024]{1,0:T(8,128)(2,1)} %shard_map.124.refs_3_), channel_id=1, source_target_pairs={{0,4},{4,0},{8,12},{12,8},{1,5},{5,1},{9,13},{13,9},{2,6},{6,2},{1... | collective-permute-start | bytes 1572872 | tf_op jit(solution)/shard_map/ppermute | solution.py:178
  167.6 12.3 %collective-permute-start.34 = (bf16[256,1024]{1,0:T(8,128)(2,1)}, bf16[256,1024]{1,0:T(8,128)(2,1)}, u32[]{:S(2)}, u32[]{:S(2)}) collective-permute-start(bf16[256,1024]{1,0:T(8,128)(2,1)} %collective-permute-done.29.refs_6_), channel_id=1, source_target_pairs={{0,4},{4,0},{8,12},{12,8},{1,5},{5,1},{9,13},{13,9},{2,6},{6,2},{1... | collective-permute-start | bytes 1572872 | tf_op jit(solution)/shard_map/ppermute | solution.py:178
  168.0 11.9 %collective-permute-start.33 = (bf16[256,1024]{1,0:T(8,128)(2,1)}, bf16[256,1024]{1,0:T(8,128)(2,1)}, u32[]{:S(2)}, u32[]{:S(2)}) collective-permute-start(bf16[256,1024]{1,0:T(8,128)(2,1)} %shard_map.125.refs_5_.refs_8_), channel_id=1, source_target_pairs={{0,4},{4,0},{8,12},{12,8},{1,5},{5,1},{9,13},{13,9},{2,6},{6,2},{1... | collective-permute-start | bytes 1572872 | tf_op jit(solution)/shard_map/ppermute | solution.py:178
  168.1 11.7 %collective-permute-start.32 = (bf16[128,1024]{1,0:T(8,128)(2,1)S(1)}, bf16[128,1024]{1,0:T(8,128)(2,1)}, u32[]{:S(2)}, u32[]{:S(2)}) collective-permute-start(bf16[128,1024]{1,0:T(8,128)(2,1)S(1)} %collective-permute-done.27.refs_4_), channel_id=1, source_target_pairs={{0,4},{4,0},{8,12},{12,8},{1,5},{5,1},{9,13},{13,9},{2,6},{6,2},{1... | collective-permute-start | bytes 786440 | tf_op jit(solution)/shard_map/ppermute | solution.py:178
  168.6 11.3 %collective-permute-start.35 = (bf16[128,1024]{1,0:T(8,128)(2,1)}, bf16[128,1024]{1,0:T(8,128)(2,1)}, u32[]{:S(2)}, u32[]{:S(2)}) collective-permute-start(bf16[128,1024]{1,0:T(8,128)(2,1)} %collective-permute-done.30.refs_7_), channel_id=1, source_target_pairs={{0,4},{4,0},{8,12},{12,8},{1,5},{5,1},{9,13},{13,9},{2,6},{6,2},{1... | collective-permute-start | bytes 786440 | tf_op jit(solution)/shard_map/ppermute | solution.py:178
  186.5 90.2 %reduce-scatter.5.cloned.1.call-start = ((), (), s32[]{:S(2)}) async-start(), calls=%async_computation.3 | async-start | bytes 2621440 | tf_op jit(solution)/shard_map/reduce_scatter | solution.py:562
  232.4 8.3 %copy-start.16 = (bf16[4,256,1024]{2,1,0:T(8,128)(2,1)S(1)}, bf16[4,256,1024]{2,1,0:T(8,128)(2,1)}, u32[]{:S(2)}) copy-start(bf16[4,256,1024]{2,1,0:T(8,128)(2,1)} %shard_map.131) | copy-start | bytes 6291460
  232.4 8.4 %copy-start.18 = (bf16[1024,1024]{1,0:T(8,128)(2,1)S(1)}, bf16[1024,1024]{1,0:T(8,128)(2,1)}, u32[]{:S(2)}) copy-start(bf16[1024,1024]{1,0:T(8,128)(2,1)} %all-gather.5.cloned.1.call-done) | copy-start | bytes 6291460
  232.7 7.9 %collective-permute-start.36 = (bf16[128,1024]{1,0:T(8,128)(2,1)S(1)}, bf16[128,1024]{1,0:T(8,128)(2,1)S(1)}, u32[]{:S(2)}, u32[]{:S(2)}) collective-permute-start(bf16[128,1024]{1,0:T(8,128)(2,1)S(1)} %get-tuple-element.29), channel_id=1, source_target_pairs={{0,8},{4,12},{8,0},{12,4},{1,9},{5,13},{9,1},{13,5},{2,10},{6,14},... | collective-permute-start | bytes 786440 | tf_op jit(solution)/shard_map/ppermute | solution.py:178
  240.7 9.3 %collective-permute-start.37 = (bf16[2,128,1024]{2,1,0:T(8,128)(2,1)S(1)}, bf16[2,128,1024]{2,1,0:T(8,128)(2,1)S(1)}, u32[]{:S(2)}, u32[]{:S(2)}) collective-permute-start(bf16[2,128,1024]{2,1,0:T(8,128)(2,1)S(1)} %pad_maximum_fusion.4), channel_id=1, source_target_pairs={{0,4},{4,0},{8,12},{12,8},{1,5},{5,1},{9,13},{13,9},{2,6},{6,2},{1... | collective-permute-start | bytes 1572872 | tf_op jit(solution)/shard_map/ppermute | solution.py:178
  241.7 35.0 %copy-start.6 = (bf16[256,1024]{1,0:T(8,128)(2,1)S(1)}, bf16[256,1024]{1,0:T(8,128)(2,1)}, u32[]{:S(2)}) copy-start(bf16[256,1024]{1,0:T(8,128)(2,1)} %pad_maximum_fusion.3.refs_2_.g_ref) | copy-start | bytes 1572868
  241.7 3.7 %collective-permute-start.38 = (f32[2,128]{1,0:T(2,128)S(1)}, f32[2,128]{1,0:T(2,128)S(1)}, u32[]{:S(2)}, u32[]{:S(2)}) collective-permute-start(f32[2,128]{1,0:T(2,128)S(1)} %bitcast.107), channel_id=1, source_target_pairs={{0,1},{1,0},{2,3},{3,2},{4,5},{5,4},{6,7},{7,6},{8,9},{9,8},{10,11... | collective-permute-start | bytes 3080 | tf_op jit(solution)/shard_map/ppermute | solution.py:178
  245.4 4.5 %collective-permute-start.39 = (f32[2,128]{1,0:T(2,128)S(1)}, f32[2,128]{1,0:T(2,128)S(1)}, u32[]{:S(2)}, u32[]{:S(2)}) collective-permute-start(f32[2,128]{1,0:T(2,128)S(1)} %bitcast_add_fusion), channel_id=1, source_target_pairs={{0,2},{1,3},{2,0},{3,1},{4,6},{5,7},{6,4},{7,5},{8,10},{9,11},{10,... | collective-permute-start | bytes 3080 | tf_op jit(solution)/shard_map/ppermute | solution.py:178
  250.2 28.1 %copy-start.11 = (bf16[4,128,1024]{2,1,0:T(8,128)(2,1)}, bf16[4,128,1024]{2,1,0:T(8,128)(2,1)S(1)}, u32[]{:S(2)}) copy-start(bf16[4,128,1024]{2,1,0:T(8,128)(2,1)S(1)} %pad_maximum_fusion.refs_0_) | copy-start | bytes 3145732
  278.3 7.9 %collective-permute-start.40 = (bf16[128,1024]{1,0:T(8,128)(2,1)S(1)}, bf16[128,1024]{1,0:T(8,128)(2,1)S(1)}, u32[]{:S(2)}, u32[]{:S(2)}) collective-permute-start(bf16[128,1024]{1,0:T(8,128)(2,1)S(1)} %get-tuple-element.25), channel_id=1, source_target_pairs={{0,8},{4,12},{8,0},{12,4},{1,9},{5,13},{9,1},{13,5},{2,10},{6,14},... | collective-permute-start | bytes 786440 | tf_op jit(solution)/shard_map/ppermute | solution.py:178
  286.3 6.2 %collective-permute-start.41 = (bf16[2,128,1024]{2,1,0:T(8,128)(2,1)S(1)}, bf16[2,128,1024]{2,1,0:T(8,128)(2,1)S(1)}, u32[]{:S(2)}, u32[]{:S(2)}) collective-permute-start(bf16[2,128,1024]{2,1,0:T(8,128)(2,1)S(1)} %pad_maximum_fusion.5), channel_id=1, source_target_pairs={{0,4},{4,0},{8,12},{12,8},{1,5},{5,1},{9,13},{13,9},{2,6},{6,2},{1... | collective-permute-start | bytes 1572872 | tf_op jit(solution)/shard_map/ppermute | solution.py:178
  286.4 1.9 collective-permute-start.42
  288.3 3.6 %collective-permute-start.43 = (f32[8,128]{1,0:T(8,128)S(1)}, f32[8,128]{1,0:T(8,128)S(1)}, u32[]{:S(2)}, u32[]{:S(2)}) collective-permute-start(f32[8,128]{1,0:T(8,128)S(1)} %add.57), channel_id=1, source_target_pairs={{0,8},{4,12},{8,0},{12,4},{1,9},{5,13},{9,1},{13,5},{2,10},{6,14},... | collective-permute-start | bytes 12296 | tf_op jit(solution)/shard_map/ppermute | solution.py:178
  (24 other events, 50.6 us)
Sparse Core Ops, SparseCore 0:
  31.1 46.2 all-gather.4
  99.2 47.0 all-gather.6
  186.6 44.5 reduce-scatter.2
  233.4 43.1 reduce-scatter.4

commit v4 on v3

--- a/solution.py
+++ b/solution.py
@@ -9,6 +9,7 @@
 BAL = 2
 EPSILON = 1e-06
 VMEM_LIMIT = 50 * 2**20
+LITTLE = pl.CostEstimate(flops=1, bytes_accessed=1, transcendentals=0)
 
 
 def entering(shard, axis, combine, identity):
@@ -223,40 +224,55 @@
     def ready(w, i):
         for copy in started[w, i]:
             copy.wait()
-        return held[w, i]
+        return held.at[w, i]
 
     return ready
+
+
+TILES = [pl.ds(256 * t, 256) for t in range(4)]
 
 
 def project_kernel(weights, pos, dense, out, held, sems):
     ready = stream(weights, pos, held, sems)
-    total = 0.0
+    totals = [0.0] * 4
     for i in range(4):
-        total += dot_nn(dense[0][pos[0] ^ i], ready(0, i))
-    out[...] = total.astype(out.dtype)
+        block = ready(0, i)
+        rows = dense[0][pos[0] ^ i]
+        for t, tile in enumerate(TILES):
+            totals[t] += dot_nn(rows, block[:, tile])
+    for total, tile in zip(totals, TILES):
+        out[:, tile] = total.astype(out.dtype)
 
 
 def project_out_kernel(weights, pos, dense, out, held, sems):
     ready = stream(weights, pos, held, sems)
-    total = 0.0
+    totals = [0.0] * 4
     for i in range(4):
-        total += dot_nt(dense[0][pos[0] ^ i], ready(0, i))
-    out[...] = total.astype(out.dtype)
+        block = ready(0, i)
+        rows = dense[0][pos[0] ^ i]
+        for t, tile in enumerate(TILES):
+            totals[t] += dot_nt(rows, block[tile])
+    for total, tile in zip(totals, TILES):
+        out[:, tile] = total.astype(out.dtype)
 
 
 def emit_kernel(weights, pos, dense, out, held, sems):
     ready = stream(weights, pos, held, sems)
     rows = dense[0][...]
     for i in range(4):
-        out[pos[0] ^ i] = dot_nn(rows, ready(0, i)).astype(out.dtype)
+        block = ready(0, i)
+        for tile in TILES:
+            out[pos[0] ^ i, :, tile] = dot_nn(rows, block[:, tile]).astype(out.dtype)
 
 
 def back_kernel(weights, pos, dense, out, held, sems):
     ready = stream(weights, pos, held, sems)
     grads = [d[...] for d in dense]
     for i in range(4):
-        total = sum(dot_nt(g, ready(w, i)) for w, g in enumerate(grads))
-        out[pos[0] ^ i] = total.astype(out.dtype)
+        blocks = [ready(w, i) for w in range(3)]
+        for tile in TILES:
+            total = sum(dot_nt(g, block[tile]) for g, block in zip(grads, blocks))
+            out[pos[0] ^ i, :, tile] = total.astype(out.dtype)
 
 
 def call(kernel, pos, dense, weights, out_shape, *earlier):
@@ -281,8 +297,8 @@
             pltpu.VMEM((count, 4, 1024, 1024), jnp.bfloat16),
             pltpu.SemaphoreType.DMA((count, 4, 6)),
         ],
-        cost_estimate=pl.CostEstimate(flops=512 * size, bytes_accessed=2 * size, transcendentals=0),
-        compiler_params=pltpu.CompilerParams(vmem_limit_bytes=VMEM_LIMIT),
+        cost_estimate=LITTLE,
+        compiler_params=pltpu.CompilerParams(vmem_limit_bytes=(8 * count + 8) * 2**20),
     )(pos, *dense, *flat, *earlier)
 
 
@@ -353,9 +369,7 @@
         in_specs=[spec] * len(arrays),
         out_specs=[spec] * outputs,
         out_shape=[shape] * outputs,
-        cost_estimate=pl.CostEstimate(
-            flops=32 * 8 * 128 * 128 * 128, bytes_accessed=many * 2 * rows * cols, transcendentals=2**19
-        ),
+        cost_estimate=LITTLE,
         compiler_params=pltpu.CompilerParams(vmem_limit_bytes=VMEM_LIMIT),
     )(*arrays)
 
@@ -374,7 +388,7 @@
             out_specs=pl.BlockSpec((rows, 1024), lambda i, block: (0, 0)),
         ),
         out_shape=jax.ShapeDtypeStruct((rows, 1024), weight.dtype),
-        cost_estimate=pl.CostEstimate(flops=0, bytes_accessed=4096 * rows, transcendentals=0),
+        cost_estimate=LITTLE,
     )(block.reshape(1), weight, *earlier)
 
 
@@ -393,7 +407,7 @@
         + [ANYWHERE] * len(earlier),
         out_specs=pl.BlockSpec((256, 1024), lambda i: (0, 0)),
         out_shape=jax.ShapeDtypeStruct((256, 1024), weight.dtype),
-        cost_estimate=pl.CostEstimate(flops=0, bytes_accessed=2**20, transcendentals=0),
+        cost_estimate=LITTLE,
     )(weight, weight, *earlier)
 
 
@@ -415,9 +429,7 @@
             jax.ShapeDtypeStruct(grads.shape, grads.dtype),
             jax.ShapeDtypeStruct((1, grads.shape[1]), jnp.float32),
         ],
-        cost_estimate=pl.CostEstimate(
-            flops=8 * grads.size, bytes_accessed=8 * grads.size, transcendentals=0
-        ),
+        cost_estimate=LITTLE,
         compiler_params=pltpu.CompilerParams(vmem_limit_bytes=VMEM_LIMIT),
     )(d_part, tokens, grads, inverse, row_mean, gain, *earlier)
 
@@ -538,17 +550,17 @@
     send(over_x[5], over_y[3])
     forward(cuts[7])
     send(over_x[6], over_y[4])
-    forward(cuts[8])
     keys = project(key_w)
-    query = project(query_w)
-    over_x[8] = after(over_x[8], over_y[5], keys, query)
+    forward(cuts[8], keys)
+    query = project(query_w, all_grads)
+    over_x[8] = after(over_x[8], over_y[5], query)
     forward()
     far = over_x[4:6] + over_y[4:6]
     value_w = [w_value, swap(w_value, "pas", 1), far, [swap(c, "pas", 1) for c in far]]
     far = over_x[6:9] + over_y[6:8]
     far_core = [swap(c, "pas", 1) for c in far]
     out_w = [w_out, swap(w_out, "pas", 1), far + far[2:3], far_core + far_core[2:3]]
-    values = project(value_w, all_grads)
+    values = project(value_w)
     (context,) = attend(attention_kernel, (query, keys, values), 1)
     partial_out = call(emit_kernel, pos, [context], [out_w], wide_shape)
     attention = lax.psum_scatter(partial_out, "fsdp", scatter_dimension=0)
@@ -574,11 +586,12 @@
         local = local.reshape(2, seq, 1024)
         back = local[1]
         over_x = swap(back, "pas", 2)
-        over_core = swap(jnp.stack([back, over_x]), "pas", 1)
+        over_core = swap(back, "pas", 1)
+        over_both = swap(over_x, "pas", 1)
 
         def pick(host):
             way = host ^ me
-            return jnp.where(way == 1, over_core[0], jnp.where(way == 2, over_x, over_core[1]))
+            return jnp.where(way == 1, over_core, jnp.where(way == 2, over_x, over_both))
 
         zero = jnp.zeros_like(back)
         return jnp.stack(
@@ -602,8 +615,8 @@
     )
     input_grad = home(input_local)
     gain_grad = gain_grad.reshape(8, 128)
-    gain_grad += swap(gain_grad, "pas", 1)
-    gain_grad += swap(gain_grad, "pas", 2)
+    others = [swap(gain_grad, "pas", bits) for bits in (1, 2, 3)]
+    gain_grad = (gain_grad + others[0]) + (others[1] + others[2])
     return encoded, input_grad, gain_grad.reshape(1024)
 
 

time: 301 us -> 292 us (0.970)
  waiting for transfers between devices: 135 us -> 124 us
  local copies, waits for them, and re-layouts: 12.9 us -> 23.9 us
  Pallas kernels: 73.4 us -> 67.3 us
  starting transfers between devices: 36.5 us -> 32 us
    unnamed x83 -> x111, local copies, waits for them, and re-layouts: 10.5 us -> 21.6 us
    ppermute x44 -> x47, waiting for transfers between devices: 91.3 us -> 80.9 us  [swap(): lax.ppermute(array, axis, [(i, i ^ bit) for i in range(lax.axis_size(axis...]
    pallas_call x6, Pallas kernels: 43.9 us -> 37.9 us  [call(): pl.pallas_call(run, in_specs=[pl.BlockSpec(memory_space=pltpu.SMEM)] + [p...]
    ppermute x44 -> x47, starting transfers between devices: 36.2 us -> 31.6 us  [swap(): lax.ppermute(array, axis, [(i, i ^ bit) for i in range(lax.axis_size(axis...]
    reduce_scatter x1, waiting for transfers between devices: 17 us -> 13.3 us  [fast_body(): attention = lax.psum_scatter(partial_out, 'fsdp', scatter_dimension=0)]
    reduce_scatter x1, waiting for transfers between devices: 26.5 us -> 29.5 us  [fast_body(): d_part = lax.psum_scatter(d_normed, 'fsdp', scatter_dimension=0)]
  transfers between devices with their start and end apart: 48 -> 51, of which waited for: 20 -> 20; matrix products, arithmetic and copies ran while one was open for 6% -> 7% of each run, Pallas kernels for 22% -> 21%
where the time goes in v4:
time: 292 us; the launch traced here: 291 us
  waiting for transfers between devices  124 us (42%)
  Pallas kernels  67.3 us (23%)
  starting transfers between devices  32 us (11%)
  local copies, waits for them, and re-layouts  23.9 us (8%)
  other arithmetic  19 us (7%)
  between operations  18.8 us (6%)
  blocking collectives  5.92 us (2%)
    ppermute x47, waiting for transfers between devices, swap(): lax.ppermute(array, axis, [(i, i ^ bit) for i in range(lax.axis_size(axis...  80.9 us
    pallas_call x6, Pallas kernels, call(): pl.pallas_call(run, in_specs=[pl.BlockSpec(memory_space=pltpu.SMEM)] + [p...  37.9 us
    ppermute x47, starting transfers between devices, swap(): lax.ppermute(array, axis, [(i, i ^ bit) for i in range(lax.axis_size(axis...  31.6 us
    reduce_scatter x1, waiting for transfers between devices, fast_body(): d_part = lax.psum_scatter(d_normed, 'fsdp', scatter_dimension=0)  29.5 us
    unnamed x111, local copies, waits for them, and re-layouts  21.6 us
    pallas_call x8, Pallas kernels, cut(): pl.pallas_call(copy, grid_spec=pltpu.PrefetchScalarGridSpec(num_scalar_pr...  14.9 us
    reduce_scatter x1, waiting for transfers between devices, fast_body(): attention = lax.psum_scatter(partial_out, 'fsdp', scatter_dimension=0)  13.3 us
    pallas_call x2, Pallas kernels, attend(): pl.pallas_call(kernel, grid=(BAL, 2), in_specs=[spec] * len(arrays), out_...  11.6 us
  transfers between devices with their start and end apart: 51, of which 20 were waited for; matrix products, arithmetic and copies ran while one was open for 7% of the time, Pallas kernels for 21%

profile of v4, /device:TPU:0, one launch (start us, length us, event | category | flops | bytes accessed | tf_op | source)
XLA Modules:
  0.0 290.7 jit_solution(9123836451343701597)
XLA Ops:
  7.2 1.2 slice.64
  8.9 1.9 shard_map.103.refs_1_
  12.6 1.4 dynamic-update-slice
  14.0 5.9 %all-reduce = s32[4]{0:T(128)S(1)} all-reduce(s32[4]{0:T(128)S(1)} %dynamic-update-slice), channel_id=1, replica_groups=mesh['grp'=2,'pas'=4,'fsdp'=4] {'pas'}, use_global_device_ids=true, to_apply=%add | all-reduce | flops 4 | bytes 32
  24.1 1.9 shard_map.105.refs_1_
  25.9 3.9 %collective-permute-done.1.refs_1_ = bf16[128,1024]{1,0:T(8,128)(2,1)S(1)} collective-permute-done((bf16[128,1024]{1,0:T(8,128)(2,1)S(1)}, bf16[128,1024]{1,0:T(8,128)(2,1)S(1)}, u32[]{:S(2)}, u32[]{:S(2)}) %collective-permute-start.1) | collective-permute-done | bytes 262176 | tf_op jit(solution)/shard_map/ppermute | solution.py:179
  32.8 1.5 collective-permute-start.6
  34.3 11.7 %collective-permute-done.3.refs_0_ = bf16[256,1024]{1,0:T(8,128)(2,1)S(1)} collective-permute-done((bf16[256,1024]{1,0:T(8,128)(2,1)}, bf16[256,1024]{1,0:T(8,128)(2,1)S(1)}, u32[]{:S(2)}, u32[]{:S(2)}) %collective-permute-start.3) | collective-permute-done | bytes 524320 | tf_op jit(solution)/shard_map/ppermute | solution.py:179
  46.7 1.9 shard_map.107.refs_1_
  49.2 1.5 collective-permute-start.5
  50.8 1.5 collective-permute-start.10
  52.4 4.8 %collective-permute-done.6.refs_0_ = bf16[256,1024]{1,0:T(8,128)(2,1)S(1)} collective-permute-done((bf16[256,1024]{1,0:T(8,128)(2,1)}, bf16[256,1024]{1,0:T(8,128)(2,1)S(1)}, u32[]{:S(2)}, u32[]{:S(2)}) %collective-permute-start.6) | collective-permute-done | bytes 524320 | tf_op jit(solution)/shard_map/ppermute | solution.py:179
  58.0 1.9 shard_map.111.refs_1_
  60.4 1.5 collective-permute-start.9
  62.0 6.5 %collective-permute-done.4.refs_0_ = bf16[256,1024]{1,0:T(8,128)(2,1)S(1)} collective-permute-done((bf16[256,1024]{1,0:T(8,128)(2,1)}, bf16[256,1024]{1,0:T(8,128)(2,1)S(1)}, u32[]{:S(2)}, u32[]{:S(2)}) %collective-permute-start.4) | collective-permute-done | bytes 524320 | tf_op jit(solution)/shard_map/ppermute | solution.py:179
  69.2 1.9 shard_map.109.refs_1_
  71.7 2.5 collective-permute-done.10
  74.1 1.5 collective-permute-start.11
  75.7 1.2 fusion.7
  77.7 7.6 %collective-permute-done.8.refs_0_ = bf16[256,1024]{1,0:T(8,128)(2,1)S(1)} collective-permute-done((bf16[256,1024]{1,0:T(8,128)(2,1)}, bf16[256,1024]{1,0:T(8,128)(2,1)S(1)}, u32[]{:S(2)}, u32[]{:S(2)}) %collective-permute-start.8) | collective-permute-done | bytes 524320 | tf_op jit(solution)/shard_map/ppermute | solution.py:179
  86.1 1.9 shard_map.113.refs_1_
  88.0 1.5 collective-permute-start.12
  90.1 6.4 %collective-permute-done.17.refs_0_ = bf16[256,1024]{1,0:T(8,128)(2,1)S(1)} collective-permute-done((bf16[256,1024]{1,0:T(8,128)(2,1)}, bf16[256,1024]{1,0:T(8,128)(2,1)S(1)}, u32[]{:S(2)}, u32[]{:S(2)}) %collective-permute-start.17) | collective-permute-done | bytes 524320 | tf_op jit(solution)/shard_map/ppermute | solution.py:179
  97.4 1.9 shard_map.117.refs_1_
  99.2 1.5 collective-permute-start.19
  101.1 3.6 %maximum_select_fusion.1.refs_3_.refs_9_ = bf16[1024,1024]{1,0:T(8,128)(2,1)} fusion(bf16[256,1024]{1,0:T(8,128)(2,1)} %copy-done.42, bf16[256,1024]{1,0:T(8,128)(2,1)} %copy-done.44, bf16[256,1024]{1,0:T(8,128)(2,1)} %shard_map.112, bf16[256,1024]{1,0:T(8,128)(2,1)} %shard_map.108, pred[]{:T(512)S(6)} %eq.57), kind=kLoop, calls=%fused_computation.8 | loop fusion | flops 17825792 | bytes 4194305 | tf_op jit(solution)/shard_map/jit(_where)/select_n | solution.py:452
  106.1 2.8 collective-permute-done.19.refs_5_.refs_1_.refs_15_
  109.2 3.1 %maximum_select_fusion.refs_3_.refs_5_ = bf16[1024,1024]{1,0:T(8,128)(2,1)} fusion(bf16[256,1024]{1,0:T(8,128)(2,1)} %collective-permute-done.12.refs_1_, bf16[256,1024]{1,0:T(8,128)(2,1)S(1)} %copy-done.46, bf16[256,1024]{1,0:T(8,128)(2,1)S(1)} %copy-done.35, bf16[256,1024]{1,0:T(8,128)(2,1)S(1)} %copy-done.37, pred[]{:T(512)S(6)} %eq.57), kind=kLoop, calls=%fused_computation.7 | loop fusion | flops 17825792 | bytes 4194305 | tf_op jit(solution)/shard_map/jit(_where)/select_n | solution.py:452
  112.3 7.7 %collective-permute-done.26.refs_0_ = bf16[256,1024]{1,0:T(8,128)(2,1)S(1)} collective-permute-done((bf16[256,1024]{1,0:T(8,128)(2,1)S(1)}, bf16[256,1024]{1,0:T(8,128)(2,1)S(1)}, u32[]{:S(2)}, u32[]{:S(2)}) %collective-permute-start.26) | collective-permute-done | bytes 524320 | tf_op jit(solution)/shard_map/ppermute | solution.py:179
  120.1 1.8 shard_map.119.refs_1_
  121.9 1.9 shard_map.123.refs_1_
  123.8 2.2 fusion.4
  126.8 1.4 collective-permute-start.20
  128.2 1.7 collective-permute-start.28
  130.0 2.4 fusion.2.refs_0_
  132.3 5.5 %shard_map.116.k_ref.refs_2_ = bf16[256,1024]{1,0:T(8,128)(2,1)S(1)} custom-call(s32[2]{0:T(128)S(1)} %pad_add_fusion.pos_ref, bf16[4,256,1024]{2,1,0:T(8,128)(2,1)S(1)} %fusion.2.refs_0_, bf16[1024,1024]{1,0:T(8,128)(2,1)} %refs_7_.1, bf16[1024,1024]{1,0:T(8,128)(2,1)} %collective-permute-done.14.refs_2_.refs_8_, ...), custom_call_target="tpu_custom_call" | custom-call | flops 1 | bytes 1 | tf_op jit(solution)/shard_map/pallas_call | solution.py:289
  139.1 1.7 collective-permute-done.20.refs_6_.refs_1_.refs_16_
  140.8 1.5 collective-permute-start.30
  142.3 3.9 %collective-permute-done.28.refs_0_ = bf16[256,1024]{1,0:T(8,128)(2,1)S(1)} collective-permute-done((bf16[256,1024]{1,0:T(8,128)(2,1)}, bf16[256,1024]{1,0:T(8,128)(2,1)S(1)}, u32[]{:S(2)}, u32[]{:S(2)}) %collective-permute-start.28) | collective-permute-done | bytes 524320 | tf_op jit(solution)/shard_map/ppermute | solution.py:179
  146.7 1.6 copy-done.4
  148.3 5.4 %shard_map.115.q_ref.refs_2_ = bf16[256,1024]{1,0:T(8,128)(2,1)S(1)} custom-call(s32[2]{0:T(128)S(1)} %pad_add_fusion.pos_ref, bf16[4,256,1024]{2,1,0:T(8,128)(2,1)S(1)} %fusion.2.refs_0_, bf16[1024,1024]{1,0:T(8,128)(2,1)} %refs_3_.1, bf16[1024,1024]{1,0:T(8,128)(2,1)} %collective-permute-done.2.refs_2_.refs_4_, ...), custom_call_target="tpu_custom_call" | custom-call | flops 1 | bytes 1 | tf_op jit(solution)/shard_map/pallas_call | solution.py:289
  154.6 4.3 %collective-permute-done.30.refs_7_ = bf16[128,1024]{1,0:T(8,128)(2,1)} collective-permute-done((bf16[128,1024]{1,0:T(8,128)(2,1)S(1)}, bf16[128,1024]{1,0:T(8,128)(2,1)}, u32[]{:S(2)}, u32[]{:S(2)}) %collective-permute-start.30) | collective-permute-done | bytes 262176 | tf_op jit(solution)/shard_map/ppermute | solution.py:179
  161.0 5.4 %shard_map.121.v_ref = bf16[256,1024]{1,0:T(8,128)(2,1)S(1)} custom-call(s32[2]{0:T(128)S(1)} %pad_add_fusion.pos_ref, bf16[4,256,1024]{2,1,0:T(8,128)(2,1)S(1)} %fusion.2.refs_0_, bf16[1024,1024]{1,0:T(8,128)(2,1)} %refs_11_.1, bf16[1024,1024]{1,0:T(8,128)(2,1)} %collective-permute-done.16.refs_2_.refs_12_, bf16[256,1024]{1,0:T(8,128)(2,1)S(1)} %copy-done.11, ...), custom_call_target="tpu_custom_call" | custom-call | flops 1 | bytes 1 | tf_op jit(solution)/shard_map/pallas_call | solution.py:289
  166.5 3.8 %shard_map.122.refs_0_ = bf16[256,1024]{1,0:T(8,128)(2,1)S(1)} custom-call(bf16[256,1024]{1,0:T(8,128)(2,1)S(1)} %copy-done.19, bf16[256,1024]{1,0:T(8,128)(2,1)S(1)} %copy-done.16, bf16[256,1024]{1,0:T(8,128)(2,1)S(1)} %shard_map.121.v_ref), custom_call_target="tpu_custom_call" | custom-call | flops 1 | bytes 1 | tf_op jit(solution)/shard_map/pallas_call | solution.py:366
  170.4 4.7 %shard_map.126.refs_1_ = bf16[4,256,1024]{2,1,0:T(8,128)(2,1)S(1)} custom-call(s32[2]{0:T(128)S(1)} %pad_add_fusion.pos_ref, bf16[256,1024]{1,0:T(8,128)(2,1)S(1)} %shard_map.122.refs_0_, bf16[1024,1024]{1,0:T(8,128)(2,1)S(1)} %copy-done.1, bf16[1024,1024]{1,0:T(8,128)(2,1)} %collective-permute-done.25.refs_2_, bf16[256,1024]{1,0:T(8,128)(2,1)S(1)} %copy-done.22, ...), custom_call_target="tpu_custom_call" | custom-call | flops 1 | bytes 1 | tf_op jit(solution)/shard_map/pallas_call | solution.py:289
  175.1 1.3 copy-done.6
  178.1 1.6 copy-done.5
  179.7 1.0 copy-done.13
  182.8 5.4 %shard_map.128.dc_ref = bf16[256,1024]{1,0:T(8,128)(2,1)S(1)} custom-call(s32[2]{0:T(128)S(1)} %pad_add_fusion.pos_ref, bf16[4,256,1024]{2,1,0:T(8,128)(2,1)S(1)} %copy-done.5, bf16[1024,1024]{1,0:T(8,128)(2,1)S(1)} %copy-done.1, bf16[1024,1024]{1,0:T(8,128)(2,1)} %collective-permute-done.25.refs_2_, bf16[256,1024]{1,0:T(8,128)(2,1)S(1)} %copy-done.23, ...), custom_call_target="tpu_custom_call" | custom-call | flops 1 | bytes 1 | tf_op jit(solution)/shard_map/pallas_call | solution.py:289
  188.2 7.9 %shard_map.129 = (bf16[256,1024]{1,0:T(8,128)(2,1)S(1)}, bf16[256,1024]{1,0:T(8,128)(2,1)S(1)}, bf16[256,1024]{1,0:T(8,128)(2,1)S(1)}) custom-call(bf16[256,1024]{1,0:T(8,128)(2,1)S(1)} %copy-done.20, bf16[256,1024]{1,0:T(8,128)(2,1)S(1)} %copy-done.17, bf16[256,1024]{1,0:T(8,128)(2,1)S(1)} %copy-done.28, bf16[256,1024]{1,0:T(8,128)(2,1)S(1)} %shard_map.128.dc_ref), custom_call_target="tpu_custom_call" | custom-call | flops 1 | bytes 1 | tf_op jit(solution)/shard_map/pallas_call | solution.py:366
  196.1 11.5 %shard_map.130.refs_0_ = bf16[4,256,1024]{2,1,0:T(8,128)(2,1)S(1)} custom-call(s32[2]{0:T(128)S(1)} %pad_add_fusion.pos_ref, bf16[256,1024]{1,0:T(8,128)(2,1)S(1)} %get-tuple-element.8.refs_0_, bf16[256,1024]{1,0:T(8,128)(2,1)S(1)} %get-tuple-element.9.refs_1_, bf16[256,1024]{1,0:T(8,128)(2,1)S(1)} %get-tuple-element.10.refs_2_, bf16[1024,1024]{1,0:T(8,128)(2,1)} %refs_3_.1, ...), custom_call_target="tpu_custom_call" | custom-call | flops 1 | bytes 1 | tf_op jit(solution)/shard_map/pallas_call | solution.py:289
  207.6 1.4 copy-done.2
  209.0 13.3 %reduce-scatter.3.cloned.1.call-done = bf16[1,256,1024]{2,1,0:T(8,128)(2,1)} async-done(((bf16[4,256,1024]{2,1,0:T(8,128)(2,1)}), bf16[1,256,1024]{2,1,0:T(8,128)(2,1)}) %reduce-scatter.3.cloned.1.call-update) | async-done | bytes 524304 | tf_op jit(solution)/shard_map/reduce_scatter | solution.py:566
  224.5 1.5 collective-permute-start.37
  227.1 5.5 %collective-permute-done.37 = bf16[128,1024]{1,0:T(8,128)(2,1)S(1)} collective-permute-done((bf16[128,1024]{1,0:T(8,128)(2,1)}, bf16[128,1024]{1,0:T(8,128)(2,1)S(1)}, u32[]{:S(2)}, u32[]{:S(2)}) %collective-permute-start.37) | collective-permute-done | bytes 262176 | tf_op jit(solution)/shard_map/ppermute | solution.py:179
  232.6 2.0 collective-permute-start.40
  236.1 1.9 collective-permute-done.40
  238.4 29.5 %reduce-scatter.5.cloned.1.call-done = bf16[1,256,1024]{2,1,0:T(8,128)(2,1)} async-done(((bf16[4,256,1024]{2,1,0:T(8,128)(2,1)}), bf16[1,256,1024]{2,1,0:T(8,128)(2,1)}) %reduce-scatter.5.cloned.1.call-update) | async-done | bytes 524304 | tf_op jit(solution)/shard_map/reduce_scatter | solution.py:574
  267.9 1.0 copy-done.32
  269.5 1.5 collective-permute-start.42
  271.0 6.4 %collective-permute-done.42 = bf16[128,1024]{1,0:T(8,128)(2,1)S(1)} collective-permute-done((bf16[128,1024]{1,0:T(8,128)(2,1)S(1)}, bf16[128,1024]{1,0:T(8,128)(2,1)S(1)}, u32[]{:S(2)}, u32[]{:S(2)}) %collective-permute-start.42) | collective-permute-done | bytes 262176 | tf_op jit(solution)/shard_map/ppermute | solution.py:179
  277.9 1.5 collective-permute-start.45
  279.4 2.1 collective-permute-done.45
  283.0 1.1 pad_maximum_fusion.1
  (218 shorter events, 31.5 us)
Async XLA Ops:
  7.2 14.6 %copy-start.40 = (bf16[4,128,1024]{2,1,0:T(8,128)(2,1)S(1)}, bf16[4,128,1024]{2,1,0:T(8,128)(2,1)}, u32[]{:S(2)}) copy-start(bf16[4,128,1024]{2,1,0:T(8,128)(2,1)} %param.8) | copy-start | bytes 3145732
  7.2 116.6 %all-gather.5.cloned.1.call-start = ((), (), s32[]{:S(2)}) async-start(), calls=%async_computation.4 | async-start | bytes 2621440 | tf_op jit(solution)/shard_map/all_gather | solution.py:521
  8.4 13.4 %collective-permute-start = (bf16[2,128,1024]{2,1,0:T(8,128)(2,1)S(1)}, bf16[2,128,1024]{2,1,0:T(8,128)(2,1)S(1)}, u32[]{:S(2)}, u32[]{:S(2)}) collective-permute-start(bf16[2,128,1024]{2,1,0:T(8,128)(2,1)S(1)} %slice.64), channel_id=1, source_target_pairs={{0,4},{4,0},{8,12},{12,8},{1,5},{5,1},{9,13},{13,9},{2,6},{6,2},{1... | collective-permute-start | bytes 1572872 | tf_op jit(solution)/shard_map/ppermute | solution.py:179
  21.9 7.9 %collective-permute-start.1 = (bf16[128,1024]{1,0:T(8,128)(2,1)S(1)}, bf16[128,1024]{1,0:T(8,128)(2,1)S(1)}, u32[]{:S(2)}, u32[]{:S(2)}) collective-permute-start(bf16[128,1024]{1,0:T(8,128)(2,1)S(1)} %fusion.9.refs_0_), channel_id=1, source_target_pairs={{0,8},{4,12},{8,0},{12,4},{1,9},{5,13},{9,1},{13,5},{2,10},{6,14},... | collective-permute-start | bytes 786440 | tf_op jit(solution)/shard_map/ppermute | solution.py:179
  30.8 116.0 %all-gather.7.cloned.1.call-start = ((), (), s32[]{:S(2)}) async-start(), calls=%async_computation.5 | async-start | bytes 2621440 | tf_op jit(solution)/shard_map/all_gather | solution.py:522
  30.8 15.1 %collective-permute-start.3 = (bf16[256,1024]{1,0:T(8,128)(2,1)}, bf16[256,1024]{1,0:T(8,128)(2,1)S(1)}, u32[]{:S(2)}, u32[]{:S(2)}) collective-permute-start(bf16[256,1024]{1,0:T(8,128)(2,1)} %shard_map.103.refs_1_), channel_id=1, source_target_pairs={{0,8},{4,12},{8,0},{12,4},{1,9},{5,13},{9,1},{13,5},{2,10},{6,14},... | collective-permute-start | bytes 1572872 | tf_op jit(solution)/shard_map/ppermute | solution.py:179
  32.3 18.4 %collective-permute-start.7 = (bf16[2,128,1024]{2,1,0:T(8,128)(2,1)}, bf16[2,128,1024]{2,1,0:T(8,128)(2,1)S(1)}, u32[]{:S(2)}, u32[]{:S(2)}) collective-permute-start(bf16[2,128,1024]{2,1,0:T(8,128)(2,1)} %slice.69), channel_id=1, source_target_pairs={{0,4},{4,0},{8,12},{12,8},{1,5},{5,1},{9,13},{13,9},{2,6},{6,2},{1... | collective-permute-start | bytes 1572872 | tf_op jit(solution)/shard_map/ppermute | solution.py:179
  32.3 73.3 %collective-permute-start.2 = (bf16[1024,1024]{1,0:T(8,128)(2,1)}, bf16[1024,1024]{1,0:T(8,128)(2,1)}, u32[]{:S(2)}, u32[]{:S(2)}) collective-permute-start(bf16[1024,1024]{1,0:T(8,128)(2,1)} %refs_3_.1), channel_id=1, source_target_pairs={{0,4},{4,0},{8,12},{12,8},{1,5},{5,1},{9,13},{13,9},{2,6},{6,2},{1... | collective-permute-start | bytes 6291464 | tf_op jit(solution)/shard_map/ppermute | solution.py:179
  32.8 24.4 %collective-permute-start.6 = (bf16[256,1024]{1,0:T(8,128)(2,1)}, bf16[256,1024]{1,0:T(8,128)(2,1)S(1)}, u32[]{:S(2)}, u32[]{:S(2)}) collective-permute-start(bf16[256,1024]{1,0:T(8,128)(2,1)} %shard_map.105.refs_1_), channel_id=1, source_target_pairs={{0,8},{4,12},{8,0},{12,4},{1,9},{5,13},{9,1},{13,5},{2,10},{6,14},... | collective-permute-start | bytes 1572872 | tf_op jit(solution)/shard_map/ppermute | solution.py:179
  48.6 19.8 %collective-permute-start.4 = (bf16[256,1024]{1,0:T(8,128)(2,1)}, bf16[256,1024]{1,0:T(8,128)(2,1)S(1)}, u32[]{:S(2)}, u32[]{:S(2)}) collective-permute-start(bf16[256,1024]{1,0:T(8,128)(2,1)} %shard_map.107.refs_1_), channel_id=1, source_target_pairs={{0,8},{4,12},{8,0},{12,4},{1,9},{5,13},{9,1},{13,5},{2,10},{6,14},... | collective-permute-start | bytes 1572872 | tf_op jit(solution)/shard_map/ppermute | solution.py:179
  49.2 11.2 %collective-permute-start.5 = (bf16[256,1024]{1,0:T(8,128)(2,1)}, bf16[256,1024]{1,0:T(8,128)(2,1)S(1)}, u32[]{:S(2)}, u32[]{:S(2)}) collective-permute-start(bf16[256,1024]{1,0:T(8,128)(2,1)} %shard_map.108), channel_id=1, source_target_pairs={{0,16},{16,0},{1,17},{17,1},{2,18},{18,2},{3,19},{19,3},{4,20},{20... | collective-permute-start | bytes 1572872 | tf_op jit(solution)/shard_map/ppermute | solution.py:179
  50.8 23.3 %collective-permute-start.10 = (bf16[128,1024]{1,0:T(8,128)(2,1)S(1)}, bf16[128,1024]{1,0:T(8,128)(2,1)}, u32[]{:S(2)}, u32[]{:S(2)}) collective-permute-start(bf16[128,1024]{1,0:T(8,128)(2,1)S(1)} %fusion.8.refs_1_), channel_id=1, source_target_pairs={{0,8},{4,12},{8,0},{12,4},{1,9},{5,13},{9,1},{13,5},{2,10},{6,14},... | collective-permute-start | bytes 786440 | tf_op jit(solution)/shard_map/ppermute | solution.py:179
  59.9 25.4 %collective-permute-start.8 = (bf16[256,1024]{1,0:T(8,128)(2,1)}, bf16[256,1024]{1,0:T(8,128)(2,1)S(1)}, u32[]{:S(2)}, u32[]{:S(2)}) collective-permute-start(bf16[256,1024]{1,0:T(8,128)(2,1)} %shard_map.111.refs_1_), channel_id=1, source_target_pairs={{0,8},{4,12},{8,0},{12,4},{1,9},{5,13},{9,1},{13,5},{2,10},{6,14},... | collective-permute-start | bytes 1572872 | tf_op jit(solution)/shard_map/ppermute | solution.py:179
  60.4 8.0 %copy-start.44 = (bf16[256,1024]{1,0:T(8,128)(2,1)}, bf16[256,1024]{1,0:T(8,128)(2,1)S(1)}, u32[]{:S(2)}) copy-start(bf16[256,1024]{1,0:T(8,128)(2,1)S(1)} %collective-permute-done.5.refs_1_) | copy-start | bytes 1572868
  60.4 17.2 %collective-permute-start.9 = (bf16[256,1024]{1,0:T(8,128)(2,1)}, bf16[256,1024]{1,0:T(8,128)(2,1)S(1)}, u32[]{:S(2)}, u32[]{:S(2)}) collective-permute-start(bf16[256,1024]{1,0:T(8,128)(2,1)} %shard_map.112), channel_id=1, source_target_pairs={{0,16},{16,0},{1,17},{17,1},{2,18},{18,2},{3,19},{19,3},{4,20},{20... | collective-permute-start | bytes 1572872 | tf_op jit(solution)/shard_map/ppermute | solution.py:179
  71.1 25.4 %collective-permute-start.17 = (bf16[256,1024]{1,0:T(8,128)(2,1)}, bf16[256,1024]{1,0:T(8,128)(2,1)S(1)}, u32[]{:S(2)}, u32[]{:S(2)}) collective-permute-start(bf16[256,1024]{1,0:T(8,128)(2,1)} %shard_map.109.refs_1_), channel_id=1, source_target_pairs={{0,8},{4,12},{8,0},{12,4},{1,9},{5,13},{9,1},{13,5},{2,10},{6,14},... | collective-permute-start | bytes 1572872 | tf_op jit(solution)/shard_map/ppermute | solution.py:179
  74.1 15.9 %collective-permute-start.11 = (bf16[256,1024]{1,0:T(8,128)(2,1)}, bf16[256,1024]{1,0:T(8,128)(2,1)S(1)}, u32[]{:S(2)}, u32[]{:S(2)}) collective-permute-start(bf16[256,1024]{1,0:T(8,128)(2,1)} %shard_map.110), channel_id=1, source_target_pairs={{0,16},{16,0},{1,17},{17,1},{2,18},{18,2},{3,19},{19,3},{4,20},{20... | collective-permute-start | bytes 1572872 | tf_op jit(solution)/shard_map/ppermute | solution.py:179
  88.0 16.7 %collective-permute-start.12 = (bf16[256,1024]{1,0:T(8,128)(2,1)}, bf16[256,1024]{1,0:T(8,128)(2,1)}, u32[]{:S(2)}, u32[]{:S(2)}) collective-permute-start(bf16[256,1024]{1,0:T(8,128)(2,1)} %shard_map.114), channel_id=1, source_target_pairs={{0,16},{16,0},{1,17},{17,1},{2,18},{18,2},{3,19},{19,3},{4,20},{20... | collective-permute-start | bytes 1572872 | tf_op jit(solution)/shard_map/ppermute | solution.py:179
  89.5 16.1 %collective-permute-start.18 = (bf16[256,1024]{1,0:T(8,128)(2,1)}, bf16[256,1024]{1,0:T(8,128)(2,1)}, u32[]{:S(2)}, u32[]{:S(2)}) collective-permute-start(bf16[256,1024]{1,0:T(8,128)(2,1)} %shard_map.113.refs_1_), channel_id=1, source_target_pairs={{0,8},{4,12},{8,0},{12,4},{1,9},{5,13},{9,1},{13,5},{2,10},{6,14},... | collective-permute-start | bytes 1572872 | tf_op jit(solution)/shard_map/ppermute | solution.py:179
  99.2 9.6 %collective-permute-start.19 = (bf16[256,1024]{1,0:T(8,128)(2,1)}, bf16[256,1024]{1,0:T(8,128)(2,1)S(1)}, u32[]{:S(2)}, u32[]{:S(2)}) collective-permute-start(bf16[256,1024]{1,0:T(8,128)(2,1)} %shard_map.118.refs_3_.refs_13_), channel_id=1, source_target_pairs={{0,16},{16,0},{1,17},{17,1},{2,18},{18,2},{3,19},{19,3},{4,20},{20... | collective-permute-start | bytes 1572872 | tf_op jit(solution)/shard_map/ppermute | solution.py:179
  100.8 25.2 %collective-permute-start.14 = (bf16[1024,1024]{1,0:T(8,128)(2,1)}, bf16[1024,1024]{1,0:T(8,128)(2,1)}, u32[]{:S(2)}, u32[]{:S(2)}) collective-permute-start(bf16[1024,1024]{1,0:T(8,128)(2,1)} %refs_7_.1), channel_id=1, source_target_pairs={{0,4},{4,0},{8,12},{12,8},{1,5},{5,1},{9,13},{13,9},{2,6},{6,2},{1... | collective-permute-start | bytes 6291464 | tf_op jit(solution)/shard_map/ppermute | solution.py:179
  100.8 121.5 %reduce-scatter.3.cloned.1.call-start = ((), (), s32[]{:S(2)}) async-start(), calls=%async_computation.2 | async-start | bytes 2621440 | tf_op jit(solution)/shard_map/reduce_scatter | solution.py:566
  101.0 8.2 %copy-start.35 = (bf16[256,1024]{1,0:T(8,128)(2,1)S(1)}, bf16[256,1024]{1,0:T(8,128)(2,1)}, u32[]{:S(2)}) copy-start(bf16[256,1024]{1,0:T(8,128)(2,1)} %shard_map.114) | copy-start | bytes 1572868
  101.0 8.2 %copy-start.37 = (bf16[256,1024]{1,0:T(8,128)(2,1)S(1)}, bf16[256,1024]{1,0:T(8,128)(2,1)}, u32[]{:S(2)}) copy-start(bf16[256,1024]{1,0:T(8,128)(2,1)} %shard_map.110) | copy-start | bytes 1572868
  101.1 8.2 %copy-start.46 = (bf16[256,1024]{1,0:T(8,128)(2,1)S(1)}, bf16[256,1024]{1,0:T(8,128)(2,1)}, u32[]{:S(2)}) copy-start(bf16[256,1024]{1,0:T(8,128)(2,1)} %copy-done.45) | copy-start | bytes 1572868
  104.7 15.3 %copy-start.52 = (f32[4096]{0:T(1024)S(1)}, f32[4096]{0:T(1024)}, u32[]{:S(2)}) copy-start(f32[4096]{0:T(1024)} %param.11) | copy-start | bytes 49156
  104.7 21.7 %collective-permute-start.16 = (bf16[1024,1024]{1,0:T(8,128)(2,1)}, bf16[1024,1024]{1,0:T(8,128)(2,1)}, u32[]{:S(2)}, u32[]{:S(2)}) collective-permute-start(bf16[1024,1024]{1,0:T(8,128)(2,1)} %refs_11_.1), channel_id=1, source_target_pairs={{0,4},{4,0},{8,12},{12,8},{1,5},{5,1},{9,13},{13,9},{2,6},{6,2},{1... | collective-permute-start | bytes 6291464 | tf_op jit(solution)/shard_map/ppermute | solution.py:179
  105.5 21.2 %collective-permute-start.25 = (bf16[1024,1024]{1,0:T(8,128)(2,1)S(1)}, bf16[1024,1024]{1,0:T(8,128)(2,1)}, u32[]{:S(2)}, u32[]{:S(2)}) collective-permute-start(bf16[1024,1024]{1,0:T(8,128)(2,1)S(1)} %copy-done), channel_id=1, source_target_pairs={{0,4},{4,0},{8,12},{12,8},{1,5},{5,1},{9,13},{13,9},{2,6},{6,2},{1... | collective-permute-start | bytes 6291464 | tf_op jit(solution)/shard_map/ppermute | solution.py:179
  105.5 22.7 %collective-permute-start.15 = (bf16[1024,1024]{1,0:T(8,128)(2,1)}, bf16[1024,1024]{1,0:T(8,128)(2,1)}, u32[]{:S(2)}, u32[]{:S(2)}) collective-permute-start(bf16[1024,1024]{1,0:T(8,128)(2,1)} %maximum_select_fusion.1.refs_3_.refs_9_), channel_id=1, source_target_pairs={{0,4},{4,0},{8,12},{12,8},{1,5},{5,1},{9,13},{13,9},{2,6},{6,2},{1... | collective-permute-start | bytes 6291464 | tf_op jit(solution)/shard_map/ppermute | solution.py:179
  108.9 11.1 %collective-permute-start.26 = (bf16[256,1024]{1,0:T(8,128)(2,1)S(1)}, bf16[256,1024]{1,0:T(8,128)(2,1)S(1)}, u32[]{:S(2)}, u32[]{:S(2)}) collective-permute-start(bf16[256,1024]{1,0:T(8,128)(2,1)S(1)} %copy-done.48), channel_id=1, source_target_pairs={{0,8},{4,12},{8,0},{12,4},{1,9},{5,13},{9,1},{13,5},{2,10},{6,14},... | collective-permute-start | bytes 1572872 | tf_op jit(solution)/shard_map/ppermute | solution.py:179
  120.0 26.2 %collective-permute-start.13 = (bf16[1024,1024]{1,0:T(8,128)(2,1)}, bf16[1024,1024]{1,0:T(8,128)(2,1)}, u32[]{:S(2)}, u32[]{:S(2)}) collective-permute-start(bf16[1024,1024]{1,0:T(8,128)(2,1)} %maximum_select_fusion.refs_3_.refs_5_), channel_id=1, source_target_pairs={{0,4},{4,0},{8,12},{12,8},{1,5},{5,1},{9,13},{13,9},{2,6},{6,2},{1... | collective-permute-start | bytes 6291464 | tf_op jit(solution)/shard_map/ppermute | solution.py:179
  125.9 12.6 %collective-permute-start.21 = (bf16[256,1024]{1,0:T(8,128)(2,1)S(1)}, bf16[256,1024]{1,0:T(8,128)(2,1)}, u32[]{:S(2)}, u32[]{:S(2)}) collective-permute-start(bf16[256,1024]{1,0:T(8,128)(2,1)S(1)} %copy-done.11), channel_id=1, source_target_pairs={{0,4},{4,0},{8,12},{12,8},{1,5},{5,1},{9,13},{13,9},{2,6},{6,2},{1... | collective-permute-start | bytes 1572872 | tf_op jit(solution)/shard_map/ppermute | solution.py:179
  126.4 12.2 %collective-permute-start.27 = (bf16[128,1024]{1,0:T(8,128)(2,1)}, bf16[128,1024]{1,0:T(8,128)(2,1)S(1)}, u32[]{:S(2)}, u32[]{:S(2)}) collective-permute-start(bf16[128,1024]{1,0:T(8,128)(2,1)} %shard_map.119.refs_1_), channel_id=1, source_target_pairs={{0,8},{4,12},{8,0},{12,4},{1,9},{5,13},{9,1},{13,5},{2,10},{6,14},... | collective-permute-start | bytes 786440 | tf_op jit(solution)/shard_map/ppermute | solution.py:179
  126.8 14.0 %collective-permute-start.20 = (bf16[256,1024]{1,0:T(8,128)(2,1)}, bf16[256,1024]{1,0:T(8,128)(2,1)}, u32[]{:S(2)}, u32[]{:S(2)}) collective-permute-start(bf16[256,1024]{1,0:T(8,128)(2,1)} %shard_map.120.refs_4_.refs_14_), channel_id=1, source_target_pairs={{0,16},{16,0},{1,17},{17,1},{2,18},{18,2},{3,19},{19,3},{4,20},{20... | collective-permute-start | bytes 1572872 | tf_op jit(solution)/shard_map/ppermute | solution.py:179
  128.2 18.0 %collective-permute-start.28 = (bf16[256,1024]{1,0:T(8,128)(2,1)}, bf16[256,1024]{1,0:T(8,128)(2,1)S(1)}, u32[]{:S(2)}, u32[]{:S(2)}) collective-permute-start(bf16[256,1024]{1,0:T(8,128)(2,1)} %shard_map.123.refs_1_), channel_id=1, source_target_pairs={{0,8},{4,12},{8,0},{12,4},{1,9},{5,13},{9,1},{13,5},{2,10},{6,14},... | collective-permute-start | bytes 1572872 | tf_op jit(solution)/shard_map/ppermute | solution.py:179
  138.6 20.3 %collective-permute-start.22 = (bf16[256,1024]{1,0:T(8,128)(2,1)}, bf16[256,1024]{1,0:T(8,128)(2,1)}, u32[]{:S(2)}, u32[]{:S(2)}) collective-permute-start(bf16[256,1024]{1,0:T(8,128)(2,1)} %shard_map.120.refs_4_.refs_14_), channel_id=1, source_target_pairs={{0,4},{4,0},{8,12},{12,8},{1,5},{5,1},{9,13},{13,9},{2,6},{6,2},{1... | collective-permute-start | bytes 1572872 | tf_op jit(solution)/shard_map/ppermute | solution.py:179
  138.6 20.8 %collective-permute-start.29 = (bf16[256,1024]{1,0:T(8,128)(2,1)}, bf16[256,1024]{1,0:T(8,128)(2,1)}, u32[]{:S(2)}, u32[]{:S(2)}) collective-permute-start(bf16[256,1024]{1,0:T(8,128)(2,1)} %shard_map.124.refs_3_), channel_id=1, source_target_pairs={{0,16},{16,0},{1,17},{17,1},{2,18},{18,2},{3,19},{19,3},{4,20},{20... | collective-permute-start | bytes 1572872 | tf_op jit(solution)/shard_map/ppermute | solution.py:179
  140.8 18.1 %collective-permute-start.30 = (bf16[128,1024]{1,0:T(8,128)(2,1)S(1)}, bf16[128,1024]{1,0:T(8,128)(2,1)}, u32[]{:S(2)}, u32[]{:S(2)}) collective-permute-start(bf16[128,1024]{1,0:T(8,128)(2,1)S(1)} %collective-permute-done.27.refs_4_), channel_id=1, source_target_pairs={{0,16},{16,0},{1,17},{17,1},{2,18},{18,2},{3,19},{19,3},{4,20},{20... | collective-permute-start | bytes 786440 | tf_op jit(solution)/shard_map/ppermute | solution.py:179
  146.2 13.2 %collective-permute-start.23 = (bf16[256,1024]{1,0:T(8,128)(2,1)}, bf16[256,1024]{1,0:T(8,128)(2,1)}, u32[]{:S(2)}, u32[]{:S(2)}) collective-permute-start(bf16[256,1024]{1,0:T(8,128)(2,1)} %copy-done.24), channel_id=1, source_target_pairs={{0,4},{4,0},{8,12},{12,8},{1,5},{5,1},{9,13},{13,9},{2,6},{6,2},{1... | collective-permute-start | bytes 1572872 | tf_op jit(solution)/shard_map/ppermute | solution.py:179
  146.2 13.7 %collective-permute-start.24 = (bf16[256,1024]{1,0:T(8,128)(2,1)}, bf16[256,1024]{1,0:T(8,128)(2,1)}, u32[]{:S(2)}, u32[]{:S(2)}) collective-permute-start(bf16[256,1024]{1,0:T(8,128)(2,1)} %collective-permute-done.20.refs_6_.refs_1_.refs_16_), channel_id=1, source_target_pairs={{0,4},{4,0},{8,12},{12,8},{1,5},{5,1},{9,13},{13,9},{2,6},{6,2},{1... | collective-permute-start | bytes 1572872 | tf_op jit(solution)/shard_map/ppermute | solution.py:179
  154.6 11.9 %copy-start.16 = (bf16[256,1024]{1,0:T(8,128)(2,1)S(1)}, bf16[256,1024]{1,0:T(8,128)(2,1)}, u32[]{:S(2)}) copy-start(bf16[256,1024]{1,0:T(8,128)(2,1)} %copy-done.15) | copy-start | bytes 1572868
  154.6 11.9 %copy-start.19 = (bf16[256,1024]{1,0:T(8,128)(2,1)S(1)}, bf16[256,1024]{1,0:T(8,128)(2,1)}, u32[]{:S(2)}) copy-start(bf16[256,1024]{1,0:T(8,128)(2,1)} %copy-done.18) | copy-start | bytes 1572868
  158.8 11.4 %collective-permute-start.31 = (bf16[256,1024]{1,0:T(8,128)(2,1)}, bf16[256,1024]{1,0:T(8,128)(2,1)S(1)}, u32[]{:S(2)}, u32[]{:S(2)}) collective-permute-start(bf16[256,1024]{1,0:T(8,128)(2,1)} %shard_map.124.refs_3_), channel_id=1, source_target_pairs={{0,4},{4,0},{8,12},{12,8},{1,5},{5,1},{9,13},{13,9},{2,6},{6,2},{1... | collective-permute-start | bytes 1572872 | tf_op jit(solution)/shard_map/ppermute | solution.py:179
  158.9 11.4 %collective-permute-start.33 = (bf16[256,1024]{1,0:T(8,128)(2,1)}, bf16[256,1024]{1,0:T(8,128)(2,1)S(1)}, u32[]{:S(2)}, u32[]{:S(2)}) collective-permute-start(bf16[256,1024]{1,0:T(8,128)(2,1)} %shard_map.125.refs_5_.refs_8_), channel_id=1, source_target_pairs={{0,4},{4,0},{8,12},{12,8},{1,5},{5,1},{9,13},{13,9},{2,6},{6,2},{1... | collective-permute-start | bytes 1572872 | tf_op jit(solution)/shard_map/ppermute | solution.py:179
  159.4 11.0 %collective-permute-start.34 = (bf16[256,1024]{1,0:T(8,128)(2,1)}, bf16[256,1024]{1,0:T(8,128)(2,1)}, u32[]{:S(2)}, u32[]{:S(2)}) collective-permute-start(bf16[256,1024]{1,0:T(8,128)(2,1)} %collective-permute-done.29.refs_6_), channel_id=1, source_target_pairs={{0,4},{4,0},{8,12},{12,8},{1,5},{5,1},{9,13},{13,9},{2,6},{6,2},{1... | collective-permute-start | bytes 1572872 | tf_op jit(solution)/shard_map/ppermute | solution.py:179
  159.4 10.8 %collective-permute-start.32 = (bf16[128,1024]{1,0:T(8,128)(2,1)S(1)}, bf16[128,1024]{1,0:T(8,128)(2,1)}, u32[]{:S(2)}, u32[]{:S(2)}) collective-permute-start(bf16[128,1024]{1,0:T(8,128)(2,1)S(1)} %collective-permute-done.27.refs_4_), channel_id=1, source_target_pairs={{0,4},{4,0},{8,12},{12,8},{1,5},{5,1},{9,13},{13,9},{2,6},{6,2},{1... | collective-permute-start | bytes 786440 | tf_op jit(solution)/shard_map/ppermute | solution.py:179
  159.9 10.4 %collective-permute-start.35 = (bf16[128,1024]{1,0:T(8,128)(2,1)}, bf16[128,1024]{1,0:T(8,128)(2,1)}, u32[]{:S(2)}, u32[]{:S(2)}) collective-permute-start(bf16[128,1024]{1,0:T(8,128)(2,1)} %collective-permute-done.30.refs_7_), channel_id=1, source_target_pairs={{0,4},{4,0},{8,12},{12,8},{1,5},{5,1},{9,13},{13,9},{2,6},{6,2},{1... | collective-permute-start | bytes 786440 | tf_op jit(solution)/shard_map/ppermute | solution.py:179
  161.0 9.3 %copy-start.8 = (bf16[256,1024]{1,0:T(8,128)(2,1)S(1)}, bf16[256,1024]{1,0:T(8,128)(2,1)}, u32[]{:S(2)}) copy-start(bf16[256,1024]{1,0:T(8,128)(2,1)} %shard_map.125.refs_5_.refs_8_) | copy-start | bytes 1572868
  161.0 9.3 %copy-start.22 = (bf16[256,1024]{1,0:T(8,128)(2,1)S(1)}, bf16[256,1024]{1,0:T(8,128)(2,1)}, u32[]{:S(2)}) copy-start(bf16[256,1024]{1,0:T(8,128)(2,1)} %shard_map.124.refs_3_) | copy-start | bytes 1572868
  178.0 89.8 %reduce-scatter.5.cloned.1.call-start = ((), (), s32[]{:S(2)}) async-start(), calls=%async_computation.3 | async-start | bytes 2621440 | tf_op jit(solution)/shard_map/reduce_scatter | solution.py:574
  188.2 7.9 %copy-start.26 = (bf16[256,1024]{1,0:T(8,128)(2,1)S(1)}, bf16[256,1024]{1,0:T(8,128)(2,1)}, u32[]{:S(2)}) copy-start(bf16[256,1024]{1,0:T(8,128)(2,1)} %copy-done.24) | copy-start | bytes 1572868
  224.5 8.1 %collective-permute-start.37 = (bf16[128,1024]{1,0:T(8,128)(2,1)}, bf16[128,1024]{1,0:T(8,128)(2,1)S(1)}, u32[]{:S(2)}, u32[]{:S(2)}) collective-permute-start(bf16[128,1024]{1,0:T(8,128)(2,1)} %get-tuple-element.27), channel_id=1, source_target_pairs={{0,8},{4,12},{8,0},{12,4},{1,9},{5,13},{9,1},{13,5},{2,10},{6,14},... | collective-permute-start | bytes 786440 | tf_op jit(solution)/shard_map/ppermute | solution.py:179
  226.9 40.9 %copy-start.14 = (bf16[256,1024]{1,0:T(8,128)(2,1)S(1)}, bf16[256,1024]{1,0:T(8,128)(2,1)}, u32[]{:S(2)}) copy-start(bf16[256,1024]{1,0:T(8,128)(2,1)} %pad_maximum_fusion.3.refs_2_.g_ref) | copy-start | bytes 1572868
  226.9 5.7 %collective-permute-start.39 = (f32[2,128]{1,0:T(2,128)S(1)}, f32[2,128]{1,0:T(2,128)S(1)}, u32[]{:S(2)}, u32[]{:S(2)}) collective-permute-start(f32[2,128]{1,0:T(2,128)S(1)} %bitcast.77), channel_id=1, source_target_pairs={{0,1},{1,0},{2,3},{3,2},{4,5},{5,4},{6,7},{7,6},{8,9},{9,8},{10,11... | collective-permute-start | bytes 3080 | tf_op jit(solution)/shard_map/ppermute | solution.py:179
  227.0 11.1 %collective-permute-start.36 = (bf16[128,1024]{1,0:T(8,128)(2,1)}, bf16[128,1024]{1,0:T(8,128)(2,1)S(1)}, u32[]{:S(2)}, u32[]{:S(2)}) collective-permute-start(bf16[128,1024]{1,0:T(8,128)(2,1)} %get-tuple-element.27), channel_id=1, source_target_pairs={{0,4},{4,0},{8,12},{12,8},{1,5},{5,1},{9,13},{13,9},{2,6},{6,2},{1... | collective-permute-start | bytes 786440 | tf_op jit(solution)/shard_map/ppermute | solution.py:179
  232.6 5.5 %collective-permute-start.38 = (bf16[128,1024]{1,0:T(8,128)(2,1)S(1)}, bf16[128,1024]{1,0:T(8,128)(2,1)S(1)}, u32[]{:S(2)}, u32[]{:S(2)}) collective-permute-start(bf16[128,1024]{1,0:T(8,128)(2,1)S(1)} %collective-permute-done.37), channel_id=1, source_target_pairs={{0,4},{4,0},{8,12},{12,8},{1,5},{5,1},{9,13},{13,9},{2,6},{6,2},{1... | collective-permute-start | bytes 786440 | tf_op jit(solution)/shard_map/ppermute | solution.py:179
  232.6 5.3 %collective-permute-start.40 = (f32[2,128]{1,0:T(2,128)S(1)}, f32[2,128]{1,0:T(2,128)S(1)}, u32[]{:S(2)}, u32[]{:S(2)}) collective-permute-start(f32[2,128]{1,0:T(2,128)S(1)} %bitcast_add_fusion), channel_id=1, source_target_pairs={{0,2},{1,3},{2,0},{3,1},{4,6},{5,7},{6,4},{7,5},{8,10},{9,11},{10,... | collective-permute-start | bytes 3080 | tf_op jit(solution)/shard_map/ppermute | solution.py:179
  238.3 31.1 %copy-start.29 = (bf16[4,128,1024]{2,1,0:T(8,128)(2,1)}, bf16[4,128,1024]{2,1,0:T(8,128)(2,1)S(1)}, u32[]{:S(2)}) copy-start(bf16[4,128,1024]{2,1,0:T(8,128)(2,1)S(1)} %pad_maximum_fusion.refs_0_) | copy-start | bytes 3145732
  269.5 7.9 %collective-permute-start.42 = (bf16[128,1024]{1,0:T(8,128)(2,1)S(1)}, bf16[128,1024]{1,0:T(8,128)(2,1)S(1)}, u32[]{:S(2)}, u32[]{:S(2)}) collective-permute-start(bf16[128,1024]{1,0:T(8,128)(2,1)S(1)} %get-tuple-element.24), channel_id=1, source_target_pairs={{0,8},{4,12},{8,0},{12,4},{1,9},{5,13},{9,1},{13,5},{2,10},{6,14},... | collective-permute-start | bytes 786440 | tf_op jit(solution)/shard_map/ppermute | solution.py:179
  271.0 12.0 %collective-permute-start.41 = (bf16[128,1024]{1,0:T(8,128)(2,1)S(1)}, bf16[128,1024]{1,0:T(8,128)(2,1)S(1)}, u32[]{:S(2)}, u32[]{:S(2)}) collective-permute-start(bf16[128,1024]{1,0:T(8,128)(2,1)S(1)} %get-tuple-element.24), channel_id=1, source_target_pairs={{0,4},{4,0},{8,12},{12,8},{1,5},{5,1},{9,13},{13,9},{2,6},{6,2},{1... | collective-permute-start | bytes 786440 | tf_op jit(solution)/shard_map/ppermute | solution.py:179
  277.4 5.6 %collective-permute-start.43 = (bf16[128,1024]{1,0:T(8,128)(2,1)S(1)}, bf16[128,1024]{1,0:T(8,128)(2,1)S(1)}, u32[]{:S(2)}, u32[]{:S(2)}) collective-permute-start(bf16[128,1024]{1,0:T(8,128)(2,1)S(1)} %collective-permute-done.42), channel_id=1, source_target_pairs={{0,4},{4,0},{8,12},{12,8},{1,5},{5,1},{9,13},{13,9},{2,6},{6,2},{1... | collective-permute-start | bytes 786440 | tf_op jit(solution)/shard_map/ppermute | solution.py:179
  277.4 2.0 collective-permute-start.44
  277.9 3.6 %collective-permute-start.45 = (f32[8,128]{1,0:T(8,128)S(1)}, f32[8,128]{1,0:T(8,128)S(1)}, u32[]{:S(2)}, u32[]{:S(2)}) collective-permute-start(f32[8,128]{1,0:T(8,128)S(1)} %bitcast.70), channel_id=1, source_target_pairs={{0,8},{4,12},{8,0},{12,4},{1,9},{5,13},{9,1},{13,5},{2,10},{6,14},... | collective-permute-start | bytes 12296 | tf_op jit(solution)/shard_map/ppermute | solution.py:179
  279.3 3.0 %collective-permute-start.46 = (f32[8,128]{1,0:T(8,128)S(1)}, f32[8,128]{1,0:T(8,128)S(1)}, u32[]{:S(2)}, u32[]{:S(2)}) collective-permute-start(f32[8,128]{1,0:T(8,128)S(1)} %bitcast.71), channel_id=1, source_target_pairs={{0,12},{4,8},{8,4},{12,0},{1,13},{5,9},{9,5},{13,1},{2,14},{6,10},... | collective-permute-start | bytes 12296 | tf_op jit(solution)/shard_map/ppermute | solution.py:179
  (41 other events, 113.9 us)
Sparse Core Ops, SparseCore 0:
  30.9 46.2 all-gather.4
  100.9 45.4 all-gather.6
  178.2 44.1 reduce-scatter.2
  224.6 43.2 reduce-scatter.4

commit v5 on v4

--- a/solution.py
+++ b/solution.py
@@ -413,22 +413,17 @@
 
 def finish(d_part, tokens, grads, inverse, row_mean, gain, *earlier):
     def kernel(d_ref, x_ref, g_ref, inverse_ref, mean_ref, gain_ref, *refs):
-        grad_out, gain_out = refs[-2:]
         d = d_ref[...].astype(jnp.float32)
         scale = inverse_ref[...]
         unit = x_ref[...].astype(jnp.float32) * scale
         d_tokens = scale * (d * gain_ref[...] - unit * mean_ref[...])
-        grad_out[...] = (g_ref[...].astype(jnp.float32) + d_tokens).astype(grad_out.dtype)
-        gain_out[...] = jnp.sum(d * unit, axis=0, keepdims=True)
+        refs[-1][...] = (g_ref[...].astype(jnp.float32) + d_tokens).astype(grads.dtype)
 
     return pl.pallas_call(
         kernel,
         in_specs=[pl.BlockSpec(memory_space=pltpu.VMEM)] * 6 + [ANYWHERE] * len(earlier),
-        out_specs=[pl.BlockSpec(memory_space=pltpu.VMEM)] * 2,
-        out_shape=[
-            jax.ShapeDtypeStruct(grads.shape, grads.dtype),
-            jax.ShapeDtypeStruct((1, grads.shape[1]), jnp.float32),
-        ],
+        out_specs=pl.BlockSpec(memory_space=pltpu.VMEM),
+        out_shape=jax.ShapeDtypeStruct(grads.shape, grads.dtype),
         cost_estimate=LITTLE,
         compiler_params=pltpu.CompilerParams(vmem_limit_bytes=VMEM_LIMIT),
     )(d_part, tokens, grads, inverse, row_mean, gain, *earlier)
@@ -573,11 +568,15 @@
     d_normed = after(d_normed, attention)
     d_part = lax.psum_scatter(d_normed, "fsdp", scatter_dimension=0)
 
-    row_total = jnp.sum(
-        d_normed.astype(jnp.float32) * gain * (tokens_f32 * inverse), axis=(0, 2)
-    ).reshape(2, seq)
-    row_total += swap(row_total, "fsdp", 1)
-    row_total += swap(row_total, "fsdp", 2)
+    terms = d_normed.astype(jnp.float32) * (tokens_f32 * inverse)
+    row_total = jnp.sum(terms * gain, axis=(0, 2)).reshape(2, seq)
+    gain_total = jnp.sum(terms, axis=1).reshape(32, 128)
+    for bit in (1, 2):
+        row_total += swap(row_total, "fsdp", bit)
+        gain_total += swap(gain_total, "fsdp", bit)
+    gain_grad = lax.dynamic_slice_in_dim(gain_total, feature * 8, 8, 0)
+    for bit in (1, 2):
+        gain_grad += swap(gain_grad, "pas", bit)
     row_mean = row_total.reshape(2 * seq, 1) / width
 
     gain_part = lax.dynamic_slice_in_dim(norm_gain, feature * 1024, 1024, 0)
@@ -604,7 +603,7 @@
         )
 
     encoded = home(states)
-    input_local, gain_grad = finish(
+    input_local = finish(
         d_part.reshape(2 * seq, 1024),
         tokens,
         grads,
@@ -612,11 +611,9 @@
         row_mean,
         gain_part.reshape(1, 1024),
         encoded,
+        gain_grad,
     )
     input_grad = home(input_local)
-    gain_grad = gain_grad.reshape(8, 128)
-    others = [swap(gain_grad, "pas", bits) for bits in (1, 2, 3)]
-    gain_grad = (gain_grad + others[0]) + (others[1] + others[2])
     return encoded, input_grad, gain_grad.reshape(1024)
 
 

time: 292 us -> 288 us (0.986)
  waiting for transfers between devices: 124 us -> 118 us
    reduce_scatter x1, waiting for transfers between devices: 29.5 us -> 23.6 us  [fast_body(): d_part = lax.psum_scatter(d_normed, 'fsdp', scatter_dimension=0)]
    ppermute x47 -> x48, starting transfers between devices: 31.6 us -> 32.8 us  [swap(): lax.ppermute(array, axis, [(i, i ^ bit) for i in range(lax.axis_size(axis...]
    ppermute x47 -> x48, waiting for transfers between devices: 80.9 us -> 81.4 us  [swap(): lax.ppermute(array, axis, [(i, i ^ bit) for i in range(lax.axis_size(axis...]
    unnamed x111 -> x113, local copies, waits for them, and re-layouts: 21.6 us -> 21.6 us
  transfers between devices with their start and end apart: 51 -> 52, of which waited for: 20 -> 21; matrix products, arithmetic and copies ran while one was open for 7% -> 7% of each run, Pallas kernels for 21% -> 22%
where the time goes in v5:
time: 288 us; the launch traced here: 287 us
  waiting for transfers between devices  118 us (41%)
  Pallas kernels  67.1 us (23%)
  starting transfers between devices  33.1 us (11%)
  local copies, waits for them, and re-layouts  23.9 us (8%)
  other arithmetic  19.5 us (7%)
  between operations  19 us (7%)
  blocking collectives  5.92 us (2%)
    ppermute x48, waiting for transfers between devices, swap(): lax.ppermute(array, axis, [(i, i ^ bit) for i in range(lax.axis_size(axis...  81.4 us
    pallas_call x6, Pallas kernels, call(): pl.pallas_call(run, in_specs=[pl.BlockSpec(memory_space=pltpu.SMEM)] + [p...  37.9 us
    ppermute x48, starting transfers between devices, swap(): lax.ppermute(array, axis, [(i, i ^ bit) for i in range(lax.axis_size(axis...  32.8 us
    reduce_scatter x1, waiting for transfers between devices, fast_body(): d_part = lax.psum_scatter(d_normed, 'fsdp', scatter_dimension=0)  23.6 us
    unnamed x113, local copies, waits for them, and re-layouts  21.6 us
    pallas_call x8, Pallas kernels, cut(): pl.pallas_call(copy, grid_spec=pltpu.PrefetchScalarGridSpec(num_scalar_pr...  14.9 us
    reduce_scatter x1, waiting for transfers between devices, fast_body(): attention = lax.psum_scatter(partial_out, 'fsdp', scatter_dimension=0)  13.3 us
    pallas_call x2, Pallas kernels, attend(): pl.pallas_call(kernel, grid=(BAL, 2), in_specs=[spec] * len(arrays), out_...  11.6 us
  transfers between devices with their start and end apart: 52, of which 21 were waited for; matrix products, arithmetic and copies ran while one was open for 7% of the time, Pallas kernels for 22%

profile of v5, /device:TPU:0, one launch (start us, length us, event | category | flops | bytes accessed | tf_op | source)
XLA Modules:
  0.0 287.1 jit_solution(18128650250926351458)
XLA Ops:
  7.2 1.2 slice.64
  8.9 1.9 shard_map.103.refs_1_
  12.6 1.4 dynamic-update-slice
  14.0 5.9 %all-reduce = s32[4]{0:T(128)S(1)} all-reduce(s32[4]{0:T(128)S(1)} %dynamic-update-slice), channel_id=1, replica_groups=mesh['grp'=2,'pas'=4,'fsdp'=4] {'pas'}, use_global_device_ids=true, to_apply=%add | all-reduce | flops 4 | bytes 32
  24.4 1.9 shard_map.105.refs_1_
  26.2 3.8 %collective-permute-done.1.refs_1_ = bf16[128,1024]{1,0:T(8,128)(2,1)S(1)} collective-permute-done((bf16[128,1024]{1,0:T(8,128)(2,1)S(1)}, bf16[128,1024]{1,0:T(8,128)(2,1)S(1)}, u32[]{:S(2)}, u32[]{:S(2)}) %collective-permute-start.1) | collective-permute-done | bytes 262176 | tf_op jit(solution)/shard_map/ppermute | solution.py:179
  33.0 1.5 collective-permute-start.6
  34.4 11.7 %collective-permute-done.3.refs_0_ = bf16[256,1024]{1,0:T(8,128)(2,1)S(1)} collective-permute-done((bf16[256,1024]{1,0:T(8,128)(2,1)}, bf16[256,1024]{1,0:T(8,128)(2,1)S(1)}, u32[]{:S(2)}, u32[]{:S(2)}) %collective-permute-start.3) | collective-permute-done | bytes 524320 | tf_op jit(solution)/shard_map/ppermute | solution.py:179
  46.9 1.9 shard_map.107.refs_1_
  49.4 1.5 collective-permute-start.5
  51.0 1.5 collective-permute-start.10
  52.5 4.8 %collective-permute-done.6.refs_0_ = bf16[256,1024]{1,0:T(8,128)(2,1)S(1)} collective-permute-done((bf16[256,1024]{1,0:T(8,128)(2,1)}, bf16[256,1024]{1,0:T(8,128)(2,1)S(1)}, u32[]{:S(2)}, u32[]{:S(2)}) %collective-permute-start.6) | collective-permute-done | bytes 524320 | tf_op jit(solution)/shard_map/ppermute | solution.py:179
  58.2 1.9 shard_map.111.refs_1_
  60.6 1.5 collective-permute-start.9
  62.2 6.5 %collective-permute-done.4.refs_0_ = bf16[256,1024]{1,0:T(8,128)(2,1)S(1)} collective-permute-done((bf16[256,1024]{1,0:T(8,128)(2,1)}, bf16[256,1024]{1,0:T(8,128)(2,1)S(1)}, u32[]{:S(2)}, u32[]{:S(2)}) %collective-permute-start.4) | collective-permute-done | bytes 524320 | tf_op jit(solution)/shard_map/ppermute | solution.py:179
  69.4 1.9 shard_map.109.refs_1_
  71.8 2.5 collective-permute-done.10
  74.3 1.5 collective-permute-start.11
  75.9 1.1 fusion.7
  77.8 7.7 %collective-permute-done.8.refs_0_ = bf16[256,1024]{1,0:T(8,128)(2,1)S(1)} collective-permute-done((bf16[256,1024]{1,0:T(8,128)(2,1)}, bf16[256,1024]{1,0:T(8,128)(2,1)S(1)}, u32[]{:S(2)}, u32[]{:S(2)}) %collective-permute-start.8) | collective-permute-done | bytes 524320 | tf_op jit(solution)/shard_map/ppermute | solution.py:179
  86.3 1.9 shard_map.113.refs_1_
  88.1 1.5 collective-permute-start.12
  90.2 6.5 %collective-permute-done.17.refs_0_ = bf16[256,1024]{1,0:T(8,128)(2,1)S(1)} collective-permute-done((bf16[256,1024]{1,0:T(8,128)(2,1)}, bf16[256,1024]{1,0:T(8,128)(2,1)S(1)}, u32[]{:S(2)}, u32[]{:S(2)}) %collective-permute-start.17) | collective-permute-done | bytes 524320 | tf_op jit(solution)/shard_map/ppermute | solution.py:179
  97.6 1.9 shard_map.117.refs_1_
  99.4 1.5 collective-permute-start.19
  101.3 3.6 %maximum_select_fusion.1.refs_3_.refs_9_ = bf16[1024,1024]{1,0:T(8,128)(2,1)} fusion(bf16[256,1024]{1,0:T(8,128)(2,1)} %copy-done.43, bf16[256,1024]{1,0:T(8,128)(2,1)} %copy-done.45, bf16[256,1024]{1,0:T(8,128)(2,1)} %shard_map.112, bf16[256,1024]{1,0:T(8,128)(2,1)} %shard_map.108, pred[]{:T(512)S(6)} %eq.57), kind=kLoop, calls=%fused_computation.9 | loop fusion | flops 17825792 | bytes 4194305 | tf_op jit(solution)/shard_map/jit(_where)/select_n | solution.py:447
  106.2 2.8 collective-permute-done.19.refs_5_.refs_1_.refs_15_
  109.4 3.1 %maximum_select_fusion.refs_3_.refs_5_ = bf16[1024,1024]{1,0:T(8,128)(2,1)} fusion(bf16[256,1024]{1,0:T(8,128)(2,1)} %collective-permute-done.12.refs_1_, bf16[256,1024]{1,0:T(8,128)(2,1)S(1)} %copy-done.47, bf16[256,1024]{1,0:T(8,128)(2,1)S(1)} %copy-done.36, bf16[256,1024]{1,0:T(8,128)(2,1)S(1)} %copy-done.38, pred[]{:T(512)S(6)} %eq.57), kind=kLoop, calls=%fused_computation.8 | loop fusion | flops 17825792 | bytes 4194305 | tf_op jit(solution)/shard_map/jit(_where)/select_n | solution.py:447
  112.5 7.7 %collective-permute-done.26.refs_0_ = bf16[256,1024]{1,0:T(8,128)(2,1)S(1)} collective-permute-done((bf16[256,1024]{1,0:T(8,128)(2,1)S(1)}, bf16[256,1024]{1,0:T(8,128)(2,1)S(1)}, u32[]{:S(2)}, u32[]{:S(2)}) %collective-permute-start.26) | collective-permute-done | bytes 524320 | tf_op jit(solution)/shard_map/ppermute | solution.py:179
  120.3 1.8 shard_map.119.refs_1_
  122.1 1.9 shard_map.123.refs_1_
  124.0 2.2 fusion.3
  127.0 1.4 collective-permute-start.20
  128.4 1.7 collective-permute-start.28
  130.1 2.4 fusion.2.refs_0_
  132.5 5.5 %shard_map.116.k_ref.refs_2_ = bf16[256,1024]{1,0:T(8,128)(2,1)S(1)} custom-call(s32[2]{0:T(128)S(1)} %pad_add_fusion.pos_ref, bf16[4,256,1024]{2,1,0:T(8,128)(2,1)S(1)} %fusion.2.refs_0_, bf16[1024,1024]{1,0:T(8,128)(2,1)} %refs_7_.1, bf16[1024,1024]{1,0:T(8,128)(2,1)} %collective-permute-done.14.refs_2_.refs_8_, ...), custom_call_target="tpu_custom_call" | custom-call | flops 1 | bytes 1 | tf_op jit(solution)/shard_map/pallas_call | solution.py:289
  139.3 1.7 collective-permute-done.20.refs_6_.refs_1_.refs_16_
  141.0 1.5 collective-permute-start.30
  142.5 3.9 %collective-permute-done.28.refs_0_ = bf16[256,1024]{1,0:T(8,128)(2,1)S(1)} collective-permute-done((bf16[256,1024]{1,0:T(8,128)(2,1)}, bf16[256,1024]{1,0:T(8,128)(2,1)S(1)}, u32[]{:S(2)}, u32[]{:S(2)}) %collective-permute-start.28) | collective-permute-done | bytes 524320 | tf_op jit(solution)/shard_map/ppermute | solution.py:179
  146.9 1.6 copy-done.4
  148.5 5.4 %shard_map.115.q_ref.refs_2_ = bf16[256,1024]{1,0:T(8,128)(2,1)S(1)} custom-call(s32[2]{0:T(128)S(1)} %pad_add_fusion.pos_ref, bf16[4,256,1024]{2,1,0:T(8,128)(2,1)S(1)} %fusion.2.refs_0_, bf16[1024,1024]{1,0:T(8,128)(2,1)} %refs_3_.1, bf16[1024,1024]{1,0:T(8,128)(2,1)} %collective-permute-done.2.refs_2_.refs_4_, ...), custom_call_target="tpu_custom_call" | custom-call | flops 1 | bytes 1 | tf_op jit(solution)/shard_map/pallas_call | solution.py:289
  154.7 4.3 %collective-permute-done.30.refs_7_ = bf16[128,1024]{1,0:T(8,128)(2,1)} collective-permute-done((bf16[128,1024]{1,0:T(8,128)(2,1)S(1)}, bf16[128,1024]{1,0:T(8,128)(2,1)}, u32[]{:S(2)}, u32[]{:S(2)}) %collective-permute-start.30) | collective-permute-done | bytes 262176 | tf_op jit(solution)/shard_map/ppermute | solution.py:179
  161.2 5.4 %shard_map.121.v_ref = bf16[256,1024]{1,0:T(8,128)(2,1)S(1)} custom-call(s32[2]{0:T(128)S(1)} %pad_add_fusion.pos_ref, bf16[4,256,1024]{2,1,0:T(8,128)(2,1)S(1)} %fusion.2.refs_0_, bf16[1024,1024]{1,0:T(8,128)(2,1)} %refs_11_.1, bf16[1024,1024]{1,0:T(8,128)(2,1)} %collective-permute-done.16.refs_2_.refs_12_, bf16[256,1024]{1,0:T(8,128)(2,1)S(1)} %copy-done.11, ...), custom_call_target="tpu_custom_call" | custom-call | flops 1 | bytes 1 | tf_op jit(solution)/shard_map/pallas_call | solution.py:289
  166.7 3.8 %shard_map.122.refs_0_ = bf16[256,1024]{1,0:T(8,128)(2,1)S(1)} custom-call(bf16[256,1024]{1,0:T(8,128)(2,1)S(1)} %copy-done.19, bf16[256,1024]{1,0:T(8,128)(2,1)S(1)} %copy-done.16, bf16[256,1024]{1,0:T(8,128)(2,1)S(1)} %shard_map.121.v_ref), custom_call_target="tpu_custom_call" | custom-call | flops 1 | bytes 1 | tf_op jit(solution)/shard_map/pallas_call | solution.py:366
  170.5 4.7 %shard_map.126.refs_1_ = bf16[4,256,1024]{2,1,0:T(8,128)(2,1)S(1)} custom-call(s32[2]{0:T(128)S(1)} %pad_add_fusion.pos_ref, bf16[256,1024]{1,0:T(8,128)(2,1)S(1)} %shard_map.122.refs_0_, bf16[1024,1024]{1,0:T(8,128)(2,1)S(1)} %copy-done.1, bf16[1024,1024]{1,0:T(8,128)(2,1)} %collective-permute-done.25.refs_2_, bf16[256,1024]{1,0:T(8,128)(2,1)S(1)} %copy-done.22, ...), custom_call_target="tpu_custom_call" | custom-call | flops 1 | bytes 1 | tf_op jit(solution)/shard_map/pallas_call | solution.py:289
  175.3 1.3 copy-done.6
  178.3 1.6 copy-done.5
  183.0 5.4 %shard_map.128.dc_ref = bf16[256,1024]{1,0:T(8,128)(2,1)S(1)} custom-call(s32[2]{0:T(128)S(1)} %pad_add_fusion.pos_ref, bf16[4,256,1024]{2,1,0:T(8,128)(2,1)S(1)} %copy-done.5, bf16[1024,1024]{1,0:T(8,128)(2,1)S(1)} %copy-done.1, bf16[1024,1024]{1,0:T(8,128)(2,1)} %collective-permute-done.25.refs_2_, bf16[256,1024]{1,0:T(8,128)(2,1)S(1)} %copy-done.23, ...), custom_call_target="tpu_custom_call" | custom-call | flops 1 | bytes 1 | tf_op jit(solution)/shard_map/pallas_call | solution.py:289
  188.4 7.9 %shard_map.129 = (bf16[256,1024]{1,0:T(8,128)(2,1)S(1)}, bf16[256,1024]{1,0:T(8,128)(2,1)S(1)}, bf16[256,1024]{1,0:T(8,128)(2,1)S(1)}) custom-call(bf16[256,1024]{1,0:T(8,128)(2,1)S(1)} %copy-done.20, bf16[256,1024]{1,0:T(8,128)(2,1)S(1)} %copy-done.17, bf16[256,1024]{1,0:T(8,128)(2,1)S(1)} %copy-done.28, bf16[256,1024]{1,0:T(8,128)(2,1)S(1)} %shard_map.128.dc_ref), custom_call_target="tpu_custom_call" | custom-call | flops 1 | bytes 1 | tf_op jit(solution)/shard_map/pallas_call | solution.py:366
  196.3 11.5 %shard_map.130.refs_0_ = bf16[4,256,1024]{2,1,0:T(8,128)(2,1)S(1)} custom-call(s32[2]{0:T(128)S(1)} %pad_add_fusion.pos_ref, bf16[256,1024]{1,0:T(8,128)(2,1)S(1)} %get-tuple-element.6.refs_0_, bf16[256,1024]{1,0:T(8,128)(2,1)S(1)} %get-tuple-element.7.refs_1_, bf16[256,1024]{1,0:T(8,128)(2,1)S(1)} %get-tuple-element.8.refs_2_, bf16[1024,1024]{1,0:T(8,128)(2,1)} %refs_3_.1, ...), custom_call_target="tpu_custom_call" | custom-call | flops 1 | bytes 1 | tf_op jit(solution)/shard_map/pallas_call | solution.py:289
  207.8 1.4 copy-done.2
  209.2 13.3 %reduce-scatter.3.cloned.1.call-done = bf16[1,256,1024]{2,1,0:T(8,128)(2,1)} async-done(((bf16[4,256,1024]{2,1,0:T(8,128)(2,1)}), bf16[1,256,1024]{2,1,0:T(8,128)(2,1)}) %reduce-scatter.3.cloned.1.call-update) | async-done | bytes 524304 | tf_op jit(solution)/shard_map/reduce_scatter | solution.py:561
  224.7 1.5 collective-permute-start.37
  226.2 2.1 fusion.4
  228.3 3.7 %collective-permute-done.41 = f32[32,128]{1,0:T(8,128)S(1)} collective-permute-done((f32[32,128]{1,0:T(8,128)S(1)}, f32[32,128]{1,0:T(8,128)S(1)}, u32[]{:S(2)}, u32[]{:S(2)}) %collective-permute-start.41) | collective-permute-done | bytes 16416 | tf_op jit(solution)/shard_map/ppermute | solution.py:179
  232.1 1.7 collective-permute-start.42
  234.3 2.9 %collective-permute-done.42 = f32[32,128]{1,0:T(8,128)S(1)} collective-permute-done((f32[32,128]{1,0:T(8,128)S(1)}, f32[32,128]{1,0:T(8,128)S(1)}, u32[]{:S(2)}, u32[]{:S(2)}) %collective-permute-start.42) | collective-permute-done | bytes 16416 | tf_op jit(solution)/shard_map/ppermute | solution.py:179
  237.7 1.7 collective-permute-start.40
  242.3 2.1 collective-permute-done.44
  244.7 23.6 %reduce-scatter.5.cloned.1.call-done = bf16[1,256,1024]{2,1,0:T(8,128)(2,1)} async-done(((bf16[4,256,1024]{2,1,0:T(8,128)(2,1)}), bf16[1,256,1024]{2,1,0:T(8,128)(2,1)}) %reduce-scatter.5.cloned.1.call-update) | async-done | bytes 524304 | tf_op jit(solution)/shard_map/reduce_scatter | solution.py:569
  269.8 1.4 collective-permute-start.46
  271.3 6.6 %collective-permute-done.46 = bf16[128,1024]{1,0:T(8,128)(2,1)S(1)} collective-permute-done((bf16[128,1024]{1,0:T(8,128)(2,1)S(1)}, bf16[128,1024]{1,0:T(8,128)(2,1)S(1)}, u32[]{:S(2)}, u32[]{:S(2)}) %collective-permute-start.46) | collective-permute-done | bytes 262176 | tf_op jit(solution)/shard_map/ppermute | solution.py:179
  277.8 1.5 collective-permute-done.47
  279.4 1.1 pad_maximum_fusion.1
  (226 shorter events, 32.9 us)
Async XLA Ops:
  7.2 14.8 %copy-start.41 = (bf16[4,128,1024]{2,1,0:T(8,128)(2,1)S(1)}, bf16[4,128,1024]{2,1,0:T(8,128)(2,1)}, u32[]{:S(2)}) copy-start(bf16[4,128,1024]{2,1,0:T(8,128)(2,1)} %param.8) | copy-start | bytes 3145732
  7.2 116.8 %all-gather.5.cloned.1.call-start = ((), (), s32[]{:S(2)}) async-start(), calls=%async_computation.4 | async-start | bytes 2621440 | tf_op jit(solution)/shard_map/all_gather | solution.py:516
  8.4 13.6 %collective-permute-start = (bf16[2,128,1024]{2,1,0:T(8,128)(2,1)S(1)}, bf16[2,128,1024]{2,1,0:T(8,128)(2,1)S(1)}, u32[]{:S(2)}, u32[]{:S(2)}) collective-permute-start(bf16[2,128,1024]{2,1,0:T(8,128)(2,1)S(1)} %slice.64), channel_id=1, source_target_pairs={{0,4},{4,0},{8,12},{12,8},{1,5},{5,1},{9,13},{13,9},{2,6},{6,2},{1... | collective-permute-start | bytes 1572872 | tf_op jit(solution)/shard_map/ppermute | solution.py:179
  22.1 7.9 %collective-permute-start.1 = (bf16[128,1024]{1,0:T(8,128)(2,1)S(1)}, bf16[128,1024]{1,0:T(8,128)(2,1)S(1)}, u32[]{:S(2)}, u32[]{:S(2)}) collective-permute-start(bf16[128,1024]{1,0:T(8,128)(2,1)S(1)} %fusion.9.refs_0_), channel_id=1, source_target_pairs={{0,8},{4,12},{8,0},{12,4},{1,9},{5,13},{9,1},{13,5},{2,10},{6,14},... | collective-permute-start | bytes 786440 | tf_op jit(solution)/shard_map/ppermute | solution.py:179
  30.9 116.0 %all-gather.7.cloned.1.call-start = ((), (), s32[]{:S(2)}) async-start(), calls=%async_computation.5 | async-start | bytes 2621440 | tf_op jit(solution)/shard_map/all_gather | solution.py:517
  31.0 15.1 %collective-permute-start.3 = (bf16[256,1024]{1,0:T(8,128)(2,1)}, bf16[256,1024]{1,0:T(8,128)(2,1)S(1)}, u32[]{:S(2)}, u32[]{:S(2)}) collective-permute-start(bf16[256,1024]{1,0:T(8,128)(2,1)} %shard_map.103.refs_1_), channel_id=1, source_target_pairs={{0,8},{4,12},{8,0},{12,4},{1,9},{5,13},{9,1},{13,5},{2,10},{6,14},... | collective-permute-start | bytes 1572872 | tf_op jit(solution)/shard_map/ppermute | solution.py:179
  32.5 18.4 %collective-permute-start.7 = (bf16[2,128,1024]{2,1,0:T(8,128)(2,1)}, bf16[2,128,1024]{2,1,0:T(8,128)(2,1)S(1)}, u32[]{:S(2)}, u32[]{:S(2)}) collective-permute-start(bf16[2,128,1024]{2,1,0:T(8,128)(2,1)} %slice.69), channel_id=1, source_target_pairs={{0,4},{4,0},{8,12},{12,8},{1,5},{5,1},{9,13},{13,9},{2,6},{6,2},{1... | collective-permute-start | bytes 1572872 | tf_op jit(solution)/shard_map/ppermute | solution.py:179
  32.5 73.3 %collective-permute-start.2 = (bf16[1024,1024]{1,0:T(8,128)(2,1)}, bf16[1024,1024]{1,0:T(8,128)(2,1)}, u32[]{:S(2)}, u32[]{:S(2)}) collective-permute-start(bf16[1024,1024]{1,0:T(8,128)(2,1)} %refs_3_.1), channel_id=1, source_target_pairs={{0,4},{4,0},{8,12},{12,8},{1,5},{5,1},{9,13},{13,9},{2,6},{6,2},{1... | collective-permute-start | bytes 6291464 | tf_op jit(solution)/shard_map/ppermute | solution.py:179
  33.0 24.4 %collective-permute-start.6 = (bf16[256,1024]{1,0:T(8,128)(2,1)}, bf16[256,1024]{1,0:T(8,128)(2,1)S(1)}, u32[]{:S(2)}, u32[]{:S(2)}) collective-permute-start(bf16[256,1024]{1,0:T(8,128)(2,1)} %shard_map.105.refs_1_), channel_id=1, source_target_pairs={{0,8},{4,12},{8,0},{12,4},{1,9},{5,13},{9,1},{13,5},{2,10},{6,14},... | collective-permute-start | bytes 1572872 | tf_op jit(solution)/shard_map/ppermute | solution.py:179
  48.8 19.8 %collective-permute-start.4 = (bf16[256,1024]{1,0:T(8,128)(2,1)}, bf16[256,1024]{1,0:T(8,128)(2,1)S(1)}, u32[]{:S(2)}, u32[]{:S(2)}) collective-permute-start(bf16[256,1024]{1,0:T(8,128)(2,1)} %shard_map.107.refs_1_), channel_id=1, source_target_pairs={{0,8},{4,12},{8,0},{12,4},{1,9},{5,13},{9,1},{13,5},{2,10},{6,14},... | collective-permute-start | bytes 1572872 | tf_op jit(solution)/shard_map/ppermute | solution.py:179
  49.4 11.2 %collective-permute-start.5 = (bf16[256,1024]{1,0:T(8,128)(2,1)}, bf16[256,1024]{1,0:T(8,128)(2,1)S(1)}, u32[]{:S(2)}, u32[]{:S(2)}) collective-permute-start(bf16[256,1024]{1,0:T(8,128)(2,1)} %shard_map.108), channel_id=1, source_target_pairs={{0,16},{16,0},{1,17},{17,1},{2,18},{18,2},{3,19},{19,3},{4,20},{20... | collective-permute-start | bytes 1572872 | tf_op jit(solution)/shard_map/ppermute | solution.py:179
  51.0 23.3 %collective-permute-start.10 = (bf16[128,1024]{1,0:T(8,128)(2,1)S(1)}, bf16[128,1024]{1,0:T(8,128)(2,1)}, u32[]{:S(2)}, u32[]{:S(2)}) collective-permute-start(bf16[128,1024]{1,0:T(8,128)(2,1)S(1)} %fusion.8.refs_1_), channel_id=1, source_target_pairs={{0,8},{4,12},{8,0},{12,4},{1,9},{5,13},{9,1},{13,5},{2,10},{6,14},... | collective-permute-start | bytes 786440 | tf_op jit(solution)/shard_map/ppermute | solution.py:179
  60.1 25.4 %collective-permute-start.8 = (bf16[256,1024]{1,0:T(8,128)(2,1)}, bf16[256,1024]{1,0:T(8,128)(2,1)S(1)}, u32[]{:S(2)}, u32[]{:S(2)}) collective-permute-start(bf16[256,1024]{1,0:T(8,128)(2,1)} %shard_map.111.refs_1_), channel_id=1, source_target_pairs={{0,8},{4,12},{8,0},{12,4},{1,9},{5,13},{9,1},{13,5},{2,10},{6,14},... | collective-permute-start | bytes 1572872 | tf_op jit(solution)/shard_map/ppermute | solution.py:179
  60.6 17.2 %collective-permute-start.9 = (bf16[256,1024]{1,0:T(8,128)(2,1)}, bf16[256,1024]{1,0:T(8,128)(2,1)S(1)}, u32[]{:S(2)}, u32[]{:S(2)}) collective-permute-start(bf16[256,1024]{1,0:T(8,128)(2,1)} %shard_map.112), channel_id=1, source_target_pairs={{0,16},{16,0},{1,17},{17,1},{2,18},{18,2},{3,19},{19,3},{4,20},{20... | collective-permute-start | bytes 1572872 | tf_op jit(solution)/shard_map/ppermute | solution.py:179
  71.3 25.4 %collective-permute-start.17 = (bf16[256,1024]{1,0:T(8,128)(2,1)}, bf16[256,1024]{1,0:T(8,128)(2,1)S(1)}, u32[]{:S(2)}, u32[]{:S(2)}) collective-permute-start(bf16[256,1024]{1,0:T(8,128)(2,1)} %shard_map.109.refs_1_), channel_id=1, source_target_pairs={{0,8},{4,12},{8,0},{12,4},{1,9},{5,13},{9,1},{13,5},{2,10},{6,14},... | collective-permute-start | bytes 1572872 | tf_op jit(solution)/shard_map/ppermute | solution.py:179
  74.3 15.9 %collective-permute-start.11 = (bf16[256,1024]{1,0:T(8,128)(2,1)}, bf16[256,1024]{1,0:T(8,128)(2,1)S(1)}, u32[]{:S(2)}, u32[]{:S(2)}) collective-permute-start(bf16[256,1024]{1,0:T(8,128)(2,1)} %shard_map.110), channel_id=1, source_target_pairs={{0,16},{16,0},{1,17},{17,1},{2,18},{18,2},{3,19},{19,3},{4,20},{20... | collective-permute-start | bytes 1572872 | tf_op jit(solution)/shard_map/ppermute | solution.py:179
  88.1 16.8 %collective-permute-start.12 = (bf16[256,1024]{1,0:T(8,128)(2,1)}, bf16[256,1024]{1,0:T(8,128)(2,1)}, u32[]{:S(2)}, u32[]{:S(2)}) collective-permute-start(bf16[256,1024]{1,0:T(8,128)(2,1)} %shard_map.114), channel_id=1, source_target_pairs={{0,16},{16,0},{1,17},{17,1},{2,18},{18,2},{3,19},{19,3},{4,20},{20... | collective-permute-start | bytes 1572872 | tf_op jit(solution)/shard_map/ppermute | solution.py:179
  89.7 16.1 %collective-permute-start.18 = (bf16[256,1024]{1,0:T(8,128)(2,1)}, bf16[256,1024]{1,0:T(8,128)(2,1)}, u32[]{:S(2)}, u32[]{:S(2)}) collective-permute-start(bf16[256,1024]{1,0:T(8,128)(2,1)} %shard_map.113.refs_1_), channel_id=1, source_target_pairs={{0,8},{4,12},{8,0},{12,4},{1,9},{5,13},{9,1},{13,5},{2,10},{6,14},... | collective-permute-start | bytes 1572872 | tf_op jit(solution)/shard_map/ppermute | solution.py:179
  99.4 9.6 %collective-permute-start.19 = (bf16[256,1024]{1,0:T(8,128)(2,1)}, bf16[256,1024]{1,0:T(8,128)(2,1)S(1)}, u32[]{:S(2)}, u32[]{:S(2)}) collective-permute-start(bf16[256,1024]{1,0:T(8,128)(2,1)} %shard_map.118.refs_3_.refs_13_), channel_id=1, source_target_pairs={{0,16},{16,0},{1,17},{17,1},{2,18},{18,2},{3,19},{19,3},{4,20},{20... | collective-permute-start | bytes 1572872 | tf_op jit(solution)/shard_map/ppermute | solution.py:179
  101.0 25.2 %collective-permute-start.14 = (bf16[1024,1024]{1,0:T(8,128)(2,1)}, bf16[1024,1024]{1,0:T(8,128)(2,1)}, u32[]{:S(2)}, u32[]{:S(2)}) collective-permute-start(bf16[1024,1024]{1,0:T(8,128)(2,1)} %refs_7_.1), channel_id=1, source_target_pairs={{0,4},{4,0},{8,12},{12,8},{1,5},{5,1},{9,13},{13,9},{2,6},{6,2},{1... | collective-permute-start | bytes 6291464 | tf_op jit(solution)/shard_map/ppermute | solution.py:179
  101.0 121.5 %reduce-scatter.3.cloned.1.call-start = ((), (), s32[]{:S(2)}) async-start(), calls=%async_computation.2 | async-start | bytes 2621440 | tf_op jit(solution)/shard_map/reduce_scatter | solution.py:561
  101.2 8.2 %copy-start.36 = (bf16[256,1024]{1,0:T(8,128)(2,1)S(1)}, bf16[256,1024]{1,0:T(8,128)(2,1)}, u32[]{:S(2)}) copy-start(bf16[256,1024]{1,0:T(8,128)(2,1)} %shard_map.114) | copy-start | bytes 1572868
  101.2 8.2 %copy-start.38 = (bf16[256,1024]{1,0:T(8,128)(2,1)S(1)}, bf16[256,1024]{1,0:T(8,128)(2,1)}, u32[]{:S(2)}) copy-start(bf16[256,1024]{1,0:T(8,128)(2,1)} %shard_map.110) | copy-start | bytes 1572868
  101.3 8.2 %copy-start.47 = (bf16[256,1024]{1,0:T(8,128)(2,1)S(1)}, bf16[256,1024]{1,0:T(8,128)(2,1)}, u32[]{:S(2)}) copy-start(bf16[256,1024]{1,0:T(8,128)(2,1)} %copy-done.46) | copy-start | bytes 1572868
  104.9 15.3 %copy-start.53 = (f32[4096]{0:T(1024)S(1)}, f32[4096]{0:T(1024)}, u32[]{:S(2)}) copy-start(f32[4096]{0:T(1024)} %param.11) | copy-start | bytes 49156
  104.9 21.7 %collective-permute-start.16 = (bf16[1024,1024]{1,0:T(8,128)(2,1)}, bf16[1024,1024]{1,0:T(8,128)(2,1)}, u32[]{:S(2)}, u32[]{:S(2)}) collective-permute-start(bf16[1024,1024]{1,0:T(8,128)(2,1)} %refs_11_.1), channel_id=1, source_target_pairs={{0,4},{4,0},{8,12},{12,8},{1,5},{5,1},{9,13},{13,9},{2,6},{6,2},{1... | collective-permute-start | bytes 6291464 | tf_op jit(solution)/shard_map/ppermute | solution.py:179
  105.7 21.2 %collective-permute-start.25 = (bf16[1024,1024]{1,0:T(8,128)(2,1)S(1)}, bf16[1024,1024]{1,0:T(8,128)(2,1)}, u32[]{:S(2)}, u32[]{:S(2)}) collective-permute-start(bf16[1024,1024]{1,0:T(8,128)(2,1)S(1)} %copy-done), channel_id=1, source_target_pairs={{0,4},{4,0},{8,12},{12,8},{1,5},{5,1},{9,13},{13,9},{2,6},{6,2},{1... | collective-permute-start | bytes 6291464 | tf_op jit(solution)/shard_map/ppermute | solution.py:179
  105.7 22.7 %collective-permute-start.15 = (bf16[1024,1024]{1,0:T(8,128)(2,1)}, bf16[1024,1024]{1,0:T(8,128)(2,1)}, u32[]{:S(2)}, u32[]{:S(2)}) collective-permute-start(bf16[1024,1024]{1,0:T(8,128)(2,1)} %maximum_select_fusion.1.refs_3_.refs_9_), channel_id=1, source_target_pairs={{0,4},{4,0},{8,12},{12,8},{1,5},{5,1},{9,13},{13,9},{2,6},{6,2},{1... | collective-permute-start | bytes 6291464 | tf_op jit(solution)/shard_map/ppermute | solution.py:179
  109.1 11.1 %collective-permute-start.26 = (bf16[256,1024]{1,0:T(8,128)(2,1)S(1)}, bf16[256,1024]{1,0:T(8,128)(2,1)S(1)}, u32[]{:S(2)}, u32[]{:S(2)}) collective-permute-start(bf16[256,1024]{1,0:T(8,128)(2,1)S(1)} %copy-done.49), channel_id=1, source_target_pairs={{0,8},{4,12},{8,0},{12,4},{1,9},{5,13},{9,1},{13,5},{2,10},{6,14},... | collective-permute-start | bytes 1572872 | tf_op jit(solution)/shard_map/ppermute | solution.py:179
  120.2 26.2 %collective-permute-start.13 = (bf16[1024,1024]{1,0:T(8,128)(2,1)}, bf16[1024,1024]{1,0:T(8,128)(2,1)}, u32[]{:S(2)}, u32[]{:S(2)}) collective-permute-start(bf16[1024,1024]{1,0:T(8,128)(2,1)} %maximum_select_fusion.refs_3_.refs_5_), channel_id=1, source_target_pairs={{0,4},{4,0},{8,12},{12,8},{1,5},{5,1},{9,13},{13,9},{2,6},{6,2},{1... | collective-permute-start | bytes 6291464 | tf_op jit(solution)/shard_map/ppermute | solution.py:179
  126.1 12.6 %collective-permute-start.21 = (bf16[256,1024]{1,0:T(8,128)(2,1)S(1)}, bf16[256,1024]{1,0:T(8,128)(2,1)}, u32[]{:S(2)}, u32[]{:S(2)}) collective-permute-start(bf16[256,1024]{1,0:T(8,128)(2,1)S(1)} %copy-done.11), channel_id=1, source_target_pairs={{0,4},{4,0},{8,12},{12,8},{1,5},{5,1},{9,13},{13,9},{2,6},{6,2},{1... | collective-permute-start | bytes 1572872 | tf_op jit(solution)/shard_map/ppermute | solution.py:179
  126.6 12.2 %collective-permute-start.27 = (bf16[128,1024]{1,0:T(8,128)(2,1)}, bf16[128,1024]{1,0:T(8,128)(2,1)S(1)}, u32[]{:S(2)}, u32[]{:S(2)}) collective-permute-start(bf16[128,1024]{1,0:T(8,128)(2,1)} %shard_map.119.refs_1_), channel_id=1, source_target_pairs={{0,8},{4,12},{8,0},{12,4},{1,9},{5,13},{9,1},{13,5},{2,10},{6,14},... | collective-permute-start | bytes 786440 | tf_op jit(solution)/shard_map/ppermute | solution.py:179
  127.0 14.0 %collective-permute-start.20 = (bf16[256,1024]{1,0:T(8,128)(2,1)}, bf16[256,1024]{1,0:T(8,128)(2,1)}, u32[]{:S(2)}, u32[]{:S(2)}) collective-permute-start(bf16[256,1024]{1,0:T(8,128)(2,1)} %shard_map.120.refs_4_.refs_14_), channel_id=1, source_target_pairs={{0,16},{16,0},{1,17},{17,1},{2,18},{18,2},{3,19},{19,3},{4,20},{20... | collective-permute-start | bytes 1572872 | tf_op jit(solution)/shard_map/ppermute | solution.py:179
  128.4 18.0 %collective-permute-start.28 = (bf16[256,1024]{1,0:T(8,128)(2,1)}, bf16[256,1024]{1,0:T(8,128)(2,1)S(1)}, u32[]{:S(2)}, u32[]{:S(2)}) collective-permute-start(bf16[256,1024]{1,0:T(8,128)(2,1)} %shard_map.123.refs_1_), channel_id=1, source_target_pairs={{0,8},{4,12},{8,0},{12,4},{1,9},{5,13},{9,1},{13,5},{2,10},{6,14},... | collective-permute-start | bytes 1572872 | tf_op jit(solution)/shard_map/ppermute | solution.py:179
  138.8 20.3 %collective-permute-start.22 = (bf16[256,1024]{1,0:T(8,128)(2,1)}, bf16[256,1024]{1,0:T(8,128)(2,1)}, u32[]{:S(2)}, u32[]{:S(2)}) collective-permute-start(bf16[256,1024]{1,0:T(8,128)(2,1)} %shard_map.120.refs_4_.refs_14_), channel_id=1, source_target_pairs={{0,4},{4,0},{8,12},{12,8},{1,5},{5,1},{9,13},{13,9},{2,6},{6,2},{1... | collective-permute-start | bytes 1572872 | tf_op jit(solution)/shard_map/ppermute | solution.py:179
  138.8 20.8 %collective-permute-start.29 = (bf16[256,1024]{1,0:T(8,128)(2,1)}, bf16[256,1024]{1,0:T(8,128)(2,1)}, u32[]{:S(2)}, u32[]{:S(2)}) collective-permute-start(bf16[256,1024]{1,0:T(8,128)(2,1)} %shard_map.124.refs_3_), channel_id=1, source_target_pairs={{0,16},{16,0},{1,17},{17,1},{2,18},{18,2},{3,19},{19,3},{4,20},{20... | collective-permute-start | bytes 1572872 | tf_op jit(solution)/shard_map/ppermute | solution.py:179
  141.0 18.1 %collective-permute-start.30 = (bf16[128,1024]{1,0:T(8,128)(2,1)S(1)}, bf16[128,1024]{1,0:T(8,128)(2,1)}, u32[]{:S(2)}, u32[]{:S(2)}) collective-permute-start(bf16[128,1024]{1,0:T(8,128)(2,1)S(1)} %collective-permute-done.27.refs_4_), channel_id=1, source_target_pairs={{0,16},{16,0},{1,17},{17,1},{2,18},{18,2},{3,19},{19,3},{4,20},{20... | collective-permute-start | bytes 786440 | tf_op jit(solution)/shard_map/ppermute | solution.py:179
  146.4 13.2 %collective-permute-start.23 = (bf16[256,1024]{1,0:T(8,128)(2,1)}, bf16[256,1024]{1,0:T(8,128)(2,1)}, u32[]{:S(2)}, u32[]{:S(2)}) collective-permute-start(bf16[256,1024]{1,0:T(8,128)(2,1)} %copy-done.24), channel_id=1, source_target_pairs={{0,4},{4,0},{8,12},{12,8},{1,5},{5,1},{9,13},{13,9},{2,6},{6,2},{1... | collective-permute-start | bytes 1572872 | tf_op jit(solution)/shard_map/ppermute | solution.py:179
  146.4 13.7 %collective-permute-start.24 = (bf16[256,1024]{1,0:T(8,128)(2,1)}, bf16[256,1024]{1,0:T(8,128)(2,1)}, u32[]{:S(2)}, u32[]{:S(2)}) collective-permute-start(bf16[256,1024]{1,0:T(8,128)(2,1)} %collective-permute-done.20.refs_6_.refs_1_.refs_16_), channel_id=1, source_target_pairs={{0,4},{4,0},{8,12},{12,8},{1,5},{5,1},{9,13},{13,9},{2,6},{6,2},{1... | collective-permute-start | bytes 1572872 | tf_op jit(solution)/shard_map/ppermute | solution.py:179
  154.7 11.9 %copy-start.16 = (bf16[256,1024]{1,0:T(8,128)(2,1)S(1)}, bf16[256,1024]{1,0:T(8,128)(2,1)}, u32[]{:S(2)}) copy-start(bf16[256,1024]{1,0:T(8,128)(2,1)} %copy-done.15) | copy-start | bytes 1572868
  154.7 11.9 %copy-start.19 = (bf16[256,1024]{1,0:T(8,128)(2,1)S(1)}, bf16[256,1024]{1,0:T(8,128)(2,1)}, u32[]{:S(2)}) copy-start(bf16[256,1024]{1,0:T(8,128)(2,1)} %copy-done.18) | copy-start | bytes 1572868
  159.0 11.4 %collective-permute-start.31 = (bf16[256,1024]{1,0:T(8,128)(2,1)}, bf16[256,1024]{1,0:T(8,128)(2,1)S(1)}, u32[]{:S(2)}, u32[]{:S(2)}) collective-permute-start(bf16[256,1024]{1,0:T(8,128)(2,1)} %shard_map.124.refs_3_), channel_id=1, source_target_pairs={{0,4},{4,0},{8,12},{12,8},{1,5},{5,1},{9,13},{13,9},{2,6},{6,2},{1... | collective-permute-start | bytes 1572872 | tf_op jit(solution)/shard_map/ppermute | solution.py:179
  159.0 11.4 %collective-permute-start.33 = (bf16[256,1024]{1,0:T(8,128)(2,1)}, bf16[256,1024]{1,0:T(8,128)(2,1)S(1)}, u32[]{:S(2)}, u32[]{:S(2)}) collective-permute-start(bf16[256,1024]{1,0:T(8,128)(2,1)} %shard_map.125.refs_5_.refs_8_), channel_id=1, source_target_pairs={{0,4},{4,0},{8,12},{12,8},{1,5},{5,1},{9,13},{13,9},{2,6},{6,2},{1... | collective-permute-start | bytes 1572872 | tf_op jit(solution)/shard_map/ppermute | solution.py:179
  159.6 11.0 %collective-permute-start.34 = (bf16[256,1024]{1,0:T(8,128)(2,1)}, bf16[256,1024]{1,0:T(8,128)(2,1)}, u32[]{:S(2)}, u32[]{:S(2)}) collective-permute-start(bf16[256,1024]{1,0:T(8,128)(2,1)} %collective-permute-done.29.refs_6_), channel_id=1, source_target_pairs={{0,4},{4,0},{8,12},{12,8},{1,5},{5,1},{9,13},{13,9},{2,6},{6,2},{1... | collective-permute-start | bytes 1572872 | tf_op jit(solution)/shard_map/ppermute | solution.py:179
  159.6 10.8 %collective-permute-start.32 = (bf16[128,1024]{1,0:T(8,128)(2,1)S(1)}, bf16[128,1024]{1,0:T(8,128)(2,1)}, u32[]{:S(2)}, u32[]{:S(2)}) collective-permute-start(bf16[128,1024]{1,0:T(8,128)(2,1)S(1)} %collective-permute-done.27.refs_4_), channel_id=1, source_target_pairs={{0,4},{4,0},{8,12},{12,8},{1,5},{5,1},{9,13},{13,9},{2,6},{6,2},{1... | collective-permute-start | bytes 786440 | tf_op jit(solution)/shard_map/ppermute | solution.py:179
  160.1 10.4 %collective-permute-start.35 = (bf16[128,1024]{1,0:T(8,128)(2,1)}, bf16[128,1024]{1,0:T(8,128)(2,1)}, u32[]{:S(2)}, u32[]{:S(2)}) collective-permute-start(bf16[128,1024]{1,0:T(8,128)(2,1)} %collective-permute-done.30.refs_7_), channel_id=1, source_target_pairs={{0,4},{4,0},{8,12},{12,8},{1,5},{5,1},{9,13},{13,9},{2,6},{6,2},{1... | collective-permute-start | bytes 786440 | tf_op jit(solution)/shard_map/ppermute | solution.py:179
  161.2 9.3 %copy-start.8 = (bf16[256,1024]{1,0:T(8,128)(2,1)S(1)}, bf16[256,1024]{1,0:T(8,128)(2,1)}, u32[]{:S(2)}) copy-start(bf16[256,1024]{1,0:T(8,128)(2,1)} %shard_map.125.refs_5_.refs_8_) | copy-start | bytes 1572868
  161.2 9.3 %copy-start.22 = (bf16[256,1024]{1,0:T(8,128)(2,1)S(1)}, bf16[256,1024]{1,0:T(8,128)(2,1)}, u32[]{:S(2)}) copy-start(bf16[256,1024]{1,0:T(8,128)(2,1)} %shard_map.124.refs_3_) | copy-start | bytes 1572868
  178.2 90.1 %reduce-scatter.5.cloned.1.call-start = ((), (), s32[]{:S(2)}) async-start(), calls=%async_computation.3 | async-start | bytes 2621440 | tf_op jit(solution)/shard_map/reduce_scatter | solution.py:569
  224.7 12.5 %collective-permute-start.37 = (bf16[128,1024]{1,0:T(8,128)(2,1)}, bf16[128,1024]{1,0:T(8,128)(2,1)S(1)}, u32[]{:S(2)}, u32[]{:S(2)}) collective-permute-start(bf16[128,1024]{1,0:T(8,128)(2,1)} %get-tuple-element.25), channel_id=1, source_target_pairs={{0,8},{4,12},{8,0},{12,4},{1,9},{5,13},{9,1},{13,5},{2,10},{6,14},... | collective-permute-start | bytes 786440 | tf_op jit(solution)/shard_map/ppermute | solution.py:179
  228.2 40.1 %copy-start.14 = (bf16[256,1024]{1,0:T(8,128)(2,1)S(1)}, bf16[256,1024]{1,0:T(8,128)(2,1)}, u32[]{:S(2)}) copy-start(bf16[256,1024]{1,0:T(8,128)(2,1)} %pad_maximum_fusion.3.refs_2_.g_ref) | copy-start | bytes 1572868
  228.3 3.8 %collective-permute-start.41 = (f32[32,128]{1,0:T(8,128)S(1)}, f32[32,128]{1,0:T(8,128)S(1)}, u32[]{:S(2)}, u32[]{:S(2)}) collective-permute-start(f32[32,128]{1,0:T(8,128)S(1)} %reshape.101), channel_id=1, source_target_pairs={{0,1},{1,0},{2,3},{3,2},{4,5},{5,4},{6,7},{7,6},{8,9},{9,8},{10,11... | collective-permute-start | bytes 49160 | tf_op jit(solution)/shard_map/ppermute | solution.py:179
  232.1 5.1 %collective-permute-start.42 = (f32[32,128]{1,0:T(8,128)S(1)}, f32[32,128]{1,0:T(8,128)S(1)}, u32[]{:S(2)}, u32[]{:S(2)}) collective-permute-start(f32[32,128]{1,0:T(8,128)S(1)} %add.66), channel_id=1, source_target_pairs={{0,2},{1,3},{2,0},{3,1},{4,6},{5,7},{6,4},{7,5},{8,10},{9,11},{10,... | collective-permute-start | bytes 49160 | tf_op jit(solution)/shard_map/ppermute | solution.py:179
  233.8 10.7 %collective-permute-start.36 = (bf16[128,1024]{1,0:T(8,128)(2,1)}, bf16[128,1024]{1,0:T(8,128)(2,1)S(1)}, u32[]{:S(2)}, u32[]{:S(2)}) collective-permute-start(bf16[128,1024]{1,0:T(8,128)(2,1)} %get-tuple-element.25), channel_id=1, source_target_pairs={{0,4},{4,0},{8,12},{12,8},{1,5},{5,1},{9,13},{13,9},{2,6},{6,2},{1... | collective-permute-start | bytes 786440 | tf_op jit(solution)/shard_map/ppermute | solution.py:179
  233.8 3.9 %collective-permute-start.39 = (f32[2,128]{1,0:T(2,128)S(1)}, f32[2,128]{1,0:T(2,128)S(1)}, u32[]{:S(2)}, u32[]{:S(2)}) collective-permute-start(f32[2,128]{1,0:T(2,128)S(1)} %bitcast.73), channel_id=1, source_target_pairs={{0,1},{1,0},{2,3},{3,2},{4,5},{5,4},{6,7},{7,6},{8,9},{9,8},{10,11... | collective-permute-start | bytes 3080 | tf_op jit(solution)/shard_map/ppermute | solution.py:179
  237.2 3.6 %collective-permute-start.43 = (f32[8,128]{1,0:T(8,128)S(1)}, f32[8,128]{1,0:T(8,128)S(1)}, u32[]{:S(2)}, u32[]{:S(2)}) collective-permute-start(f32[8,128]{1,0:T(8,128)S(1)} %dynamic-slice_add_fusion), channel_id=1, source_target_pairs={{0,4},{4,0},{8,12},{12,8},{1,5},{5,1},{9,13},{13,9},{2,6},{6,2},{1... | collective-permute-start | bytes 12296 | tf_op jit(solution)/shard_map/ppermute | solution.py:179
  237.2 7.3 %collective-permute-start.38 = (bf16[128,1024]{1,0:T(8,128)(2,1)S(1)}, bf16[128,1024]{1,0:T(8,128)(2,1)S(1)}, u32[]{:S(2)}, u32[]{:S(2)}) collective-permute-start(bf16[128,1024]{1,0:T(8,128)(2,1)S(1)} %collective-permute-done.37), channel_id=1, source_target_pairs={{0,4},{4,0},{8,12},{12,8},{1,5},{5,1},{9,13},{13,9},{2,6},{6,2},{1... | collective-permute-start | bytes 786440 | tf_op jit(solution)/shard_map/ppermute | solution.py:179
  237.7 4.5 %collective-permute-start.40 = (f32[2,128]{1,0:T(2,128)S(1)}, f32[2,128]{1,0:T(2,128)S(1)}, u32[]{:S(2)}, u32[]{:S(2)}) collective-permute-start(f32[2,128]{1,0:T(2,128)S(1)} %bitcast_add_fusion), channel_id=1, source_target_pairs={{0,2},{1,3},{2,0},{3,1},{4,6},{5,7},{6,4},{7,5},{8,10},{9,11},{10,... | collective-permute-start | bytes 3080 | tf_op jit(solution)/shard_map/ppermute | solution.py:179
  240.8 3.7 %collective-permute-start.44 = (f32[8,128]{1,0:T(8,128)S(1)}, f32[8,128]{1,0:T(8,128)S(1)}, u32[]{:S(2)}, u32[]{:S(2)}) collective-permute-start(f32[8,128]{1,0:T(8,128)S(1)} %add.69), channel_id=1, source_target_pairs={{0,8},{4,12},{8,0},{12,4},{1,9},{5,13},{9,1},{13,5},{2,10},{6,14},... | collective-permute-start | bytes 12296 | tf_op jit(solution)/shard_map/ppermute | solution.py:179
  244.5 25.3 %copy-start.33 = (f32[8,128]{1,0:T(8,128)}, f32[8,128]{1,0:T(8,128)S(1)}, u32[]{:S(2)}) copy-start(f32[8,128]{1,0:T(8,128)S(1)} %add.70.refs_1_) | copy-start | bytes 12292
  244.7 25.1 %copy-start.29 = (bf16[4,128,1024]{2,1,0:T(8,128)(2,1)}, bf16[4,128,1024]{2,1,0:T(8,128)(2,1)S(1)}, u32[]{:S(2)}) copy-start(bf16[4,128,1024]{2,1,0:T(8,128)(2,1)S(1)} %pad_maximum_fusion.refs_0_) | copy-start | bytes 3145732
  269.8 8.0 %collective-permute-start.46 = (bf16[128,1024]{1,0:T(8,128)(2,1)S(1)}, bf16[128,1024]{1,0:T(8,128)(2,1)S(1)}, u32[]{:S(2)}, u32[]{:S(2)}) collective-permute-start(bf16[128,1024]{1,0:T(8,128)(2,1)S(1)} %get-tuple-element.22), channel_id=1, source_target_pairs={{0,8},{4,12},{8,0},{12,4},{1,9},{5,13},{9,1},{13,5},{2,10},{6,14},... | collective-permute-start | bytes 786440 | tf_op jit(solution)/shard_map/ppermute | solution.py:179
  271.3 6.6 %collective-permute-start.45 = (bf16[128,1024]{1,0:T(8,128)(2,1)S(1)}, bf16[128,1024]{1,0:T(8,128)(2,1)S(1)}, u32[]{:S(2)}, u32[]{:S(2)}) collective-permute-start(bf16[128,1024]{1,0:T(8,128)(2,1)S(1)} %get-tuple-element.22), channel_id=1, source_target_pairs={{0,4},{4,0},{8,12},{12,8},{1,5},{5,1},{9,13},{13,9},{2,6},{6,2},{1... | collective-permute-start | bytes 786440 | tf_op jit(solution)/shard_map/ppermute | solution.py:179
  277.8 1.5 collective-permute-start.47
  (43 other events, 130.0 us)
Sparse Core Ops, SparseCore 0:
  31.1 46.2 all-gather.4
  101.1 45.4 all-gather.6
  178.3 44.1 reduce-scatter.2
  224.8 43.4 reduce-scatter.4

commit v6 on v5

--- a/solution.py
+++ b/solution.py
@@ -256,13 +256,18 @@
         out[:, tile] = total.astype(out.dtype)
 
 
-def emit_kernel(weights, pos, dense, out, held, sems):
+def emit_kernel(weights, pos, dense, out, held, sems, blocks, out_sems):
     ready = stream(weights, pos, held, sems)
     rows = dense[0][...]
+    written = []
     for i in range(4):
         block = ready(0, i)
         for tile in TILES:
-            out[pos[0] ^ i, :, tile] = dot_nn(rows, block[:, tile]).astype(out.dtype)
+            blocks[i, :, tile] = dot_nn(rows, block[:, tile]).astype(out.dtype)
+        written.append(pltpu.make_async_copy(blocks.at[i], out.at[pos[0] ^ i], out_sems.at[i]))
+        written[i].start()
+    for copy in written:
+        copy.wait()
 
 
 def back_kernel(weights, pos, dense, out, held, sems):
@@ -278,12 +283,14 @@
 def call(kernel, pos, dense, weights, out_shape, *earlier):
     flat, tree = jax.tree.flatten(weights)
     count = len(weights)
+    direct = kernel is emit_kernel
+    staging = [pltpu.VMEM(out_shape.shape, out_shape.dtype), pltpu.SemaphoreType.DMA((4,))]
 
     def run(pos_ref, *refs):
         dense_refs = refs[: len(dense)]
         weight_refs = jax.tree.unflatten(tree, refs[len(dense) : len(dense) + len(flat)])
-        out, held, sems = refs[-3:]
-        kernel(weight_refs, pos_ref, dense_refs, out, held, sems)
+        own = refs[-5:] if direct else refs[-3:]
+        kernel(weight_refs, pos_ref, dense_refs, *own)
 
     size = count * 2**22
     return pl.pallas_call(
@@ -291,12 +298,13 @@
         in_specs=[pl.BlockSpec(memory_space=pltpu.SMEM)]
         + [pl.BlockSpec(memory_space=pltpu.VMEM)] * len(dense)
         + [ANYWHERE] * (len(flat) + len(earlier)),
-        out_specs=pl.BlockSpec(memory_space=pltpu.VMEM),
+        out_specs=ANYWHERE if direct else pl.BlockSpec(memory_space=pltpu.VMEM),
         out_shape=out_shape,
         scratch_shapes=[
             pltpu.VMEM((count, 4, 1024, 1024), jnp.bfloat16),
             pltpu.SemaphoreType.DMA((count, 4, 6)),
-        ],
+        ]
+        + (staging if direct else []),
         cost_estimate=LITTLE,
         compiler_params=pltpu.CompilerParams(vmem_limit_bytes=(8 * count + 8) * 2**20),
     )(pos, *dense, *flat, *earlier)

time: 288 us -> 288 us (level)
  no operation moved by 1% of the time
where the time goes in v6:
time: 288 us; the launch traced here: 287 us
  waiting for transfers between devices  118 us (41%)
  Pallas kernels  67.4 us (23%)
  starting transfers between devices  33.1 us (11%)
  local copies, waits for them, and re-layouts  23.9 us (8%)
  other arithmetic  19.6 us (7%)
  between operations  19 us (7%)
  blocking collectives  5.92 us (2%)
    ppermute x48, waiting for transfers between devices, swap(): lax.ppermute(array, axis, [(i, i ^ bit) for i in range(lax.axis_size(axis...  81.4 us
    pallas_call x6, Pallas kernels, call(): pl.pallas_call(run, in_specs=[pl.BlockSpec(memory_space=pltpu.SMEM)] + [p...  38.2 us
    ppermute x48, starting transfers between devices, swap(): lax.ppermute(array, axis, [(i, i ^ bit) for i in range(lax.axis_size(axis...  32.8 us
    reduce_scatter x1, waiting for transfers between devices, fast_body(): d_part = lax.psum_scatter(d_normed, 'fsdp', scatter_dimension=0)  23.6 us
    unnamed x113, local copies, waits for them, and re-layouts  21.6 us
    pallas_call x8, Pallas kernels, cut(): pl.pallas_call(copy, grid_spec=pltpu.PrefetchScalarGridSpec(num_scalar_pr...  14.9 us
    reduce_scatter x1, waiting for transfers between devices, fast_body(): attention = lax.psum_scatter(partial_out, 'fsdp', scatter_dimension=0)  13.4 us
    pallas_call x2, Pallas kernels, attend(): pl.pallas_call(kernel, grid=(BAL, 2), in_specs=[spec] * len(arrays), out_...  11.6 us
  transfers between devices with their start and end apart: 52, of which 21 were waited for; matrix products, arithmetic and copies ran while one was open for 7% of the time, Pallas kernels for 22%

profile of v6, /device:TPU:0, one launch (start us, length us, event | category | flops | bytes accessed | tf_op | source)
XLA Modules:
  0.0 287.4 jit_solution(11605373486215395116)
XLA Ops:
  7.2 1.2 slice.64
  8.9 1.9 shard_map.103.refs_1_
  12.6 1.4 dynamic-update-slice
  14.0 5.9 %all-reduce = s32[4]{0:T(128)S(1)} all-reduce(s32[4]{0:T(128)S(1)} %dynamic-update-slice), channel_id=1, replica_groups=mesh['grp'=2,'pas'=4,'fsdp'=4] {'pas'}, use_global_device_ids=true, to_apply=%add | all-reduce | flops 4 | bytes 32
  24.4 1.9 shard_map.105.refs_1_
  26.2 3.8 %collective-permute-done.1.refs_1_ = bf16[128,1024]{1,0:T(8,128)(2,1)S(1)} collective-permute-done((bf16[128,1024]{1,0:T(8,128)(2,1)S(1)}, bf16[128,1024]{1,0:T(8,128)(2,1)S(1)}, u32[]{:S(2)}, u32[]{:S(2)}) %collective-permute-start.1) | collective-permute-done | bytes 262176 | tf_op jit(solution)/shard_map/ppermute | solution.py:179
  33.0 1.5 collective-permute-start.6
  34.4 11.7 %collective-permute-done.3.refs_0_ = bf16[256,1024]{1,0:T(8,128)(2,1)S(1)} collective-permute-done((bf16[256,1024]{1,0:T(8,128)(2,1)}, bf16[256,1024]{1,0:T(8,128)(2,1)S(1)}, u32[]{:S(2)}, u32[]{:S(2)}) %collective-permute-start.3) | collective-permute-done | bytes 524320 | tf_op jit(solution)/shard_map/ppermute | solution.py:179
  46.9 1.9 shard_map.107.refs_1_
  49.4 1.5 collective-permute-start.5
  51.0 1.5 collective-permute-start.10
  52.5 4.8 %collective-permute-done.6.refs_0_ = bf16[256,1024]{1,0:T(8,128)(2,1)S(1)} collective-permute-done((bf16[256,1024]{1,0:T(8,128)(2,1)}, bf16[256,1024]{1,0:T(8,128)(2,1)S(1)}, u32[]{:S(2)}, u32[]{:S(2)}) %collective-permute-start.6) | collective-permute-done | bytes 524320 | tf_op jit(solution)/shard_map/ppermute | solution.py:179
  58.2 1.9 shard_map.111.refs_1_
  60.6 1.5 collective-permute-start.9
  62.2 6.5 %collective-permute-done.4.refs_0_ = bf16[256,1024]{1,0:T(8,128)(2,1)S(1)} collective-permute-done((bf16[256,1024]{1,0:T(8,128)(2,1)}, bf16[256,1024]{1,0:T(8,128)(2,1)S(1)}, u32[]{:S(2)}, u32[]{:S(2)}) %collective-permute-start.4) | collective-permute-done | bytes 524320 | tf_op jit(solution)/shard_map/ppermute | solution.py:179
  69.4 1.9 shard_map.109.refs_1_
  71.8 2.5 collective-permute-done.10
  74.3 1.5 collective-permute-start.11
  75.9 1.2 fusion.7
  77.9 7.6 %collective-permute-done.8.refs_0_ = bf16[256,1024]{1,0:T(8,128)(2,1)S(1)} collective-permute-done((bf16[256,1024]{1,0:T(8,128)(2,1)}, bf16[256,1024]{1,0:T(8,128)(2,1)S(1)}, u32[]{:S(2)}, u32[]{:S(2)}) %collective-permute-start.8) | collective-permute-done | bytes 524320 | tf_op jit(solution)/shard_map/ppermute | solution.py:179
  86.3 1.9 shard_map.113.refs_1_
  88.1 1.5 collective-permute-start.12
  90.2 6.5 %collective-permute-done.17.refs_0_ = bf16[256,1024]{1,0:T(8,128)(2,1)S(1)} collective-permute-done((bf16[256,1024]{1,0:T(8,128)(2,1)}, bf16[256,1024]{1,0:T(8,128)(2,1)S(1)}, u32[]{:S(2)}, u32[]{:S(2)}) %collective-permute-start.17) | collective-permute-done | bytes 524320 | tf_op jit(solution)/shard_map/ppermute | solution.py:179
  97.6 1.9 shard_map.117.refs_1_
  99.4 1.5 collective-permute-start.19
  101.3 3.6 %maximum_select_fusion.1.refs_3_.refs_9_ = bf16[1024,1024]{1,0:T(8,128)(2,1)} fusion(bf16[256,1024]{1,0:T(8,128)(2,1)} %copy-done.43, bf16[256,1024]{1,0:T(8,128)(2,1)} %copy-done.45, bf16[256,1024]{1,0:T(8,128)(2,1)} %shard_map.112, bf16[256,1024]{1,0:T(8,128)(2,1)} %shard_map.108, pred[]{:T(512)S(6)} %eq.57), kind=kLoop, calls=%fused_computation.9 | loop fusion | flops 17825792 | bytes 4194305 | tf_op jit(solution)/shard_map/jit(_where)/select_n | solution.py:455
  106.2 2.8 collective-permute-done.19.refs_5_.refs_1_.refs_15_
  109.4 3.1 %maximum_select_fusion.refs_3_.refs_5_ = bf16[1024,1024]{1,0:T(8,128)(2,1)} fusion(bf16[256,1024]{1,0:T(8,128)(2,1)} %collective-permute-done.12.refs_1_, bf16[256,1024]{1,0:T(8,128)(2,1)S(1)} %copy-done.47, bf16[256,1024]{1,0:T(8,128)(2,1)S(1)} %copy-done.36, bf16[256,1024]{1,0:T(8,128)(2,1)S(1)} %copy-done.38, pred[]{:T(512)S(6)} %eq.57), kind=kLoop, calls=%fused_computation.8 | loop fusion | flops 17825792 | bytes 4194305 | tf_op jit(solution)/shard_map/jit(_where)/select_n | solution.py:455
  112.5 7.7 %collective-permute-done.26.refs_0_ = bf16[256,1024]{1,0:T(8,128)(2,1)S(1)} collective-permute-done((bf16[256,1024]{1,0:T(8,128)(2,1)S(1)}, bf16[256,1024]{1,0:T(8,128)(2,1)S(1)}, u32[]{:S(2)}, u32[]{:S(2)}) %collective-permute-start.26) | collective-permute-done | bytes 524320 | tf_op jit(solution)/shard_map/ppermute | solution.py:179
  120.3 1.8 shard_map.119.refs_1_
  122.1 1.9 shard_map.123.refs_1_
  124.0 2.2 fusion.3
  127.0 1.4 collective-permute-start.20
  128.4 1.7 collective-permute-start.28
  130.1 2.4 fusion.2.refs_0_
  132.5 5.5 %shard_map.116.k_ref.refs_2_ = bf16[256,1024]{1,0:T(8,128)(2,1)S(1)} custom-call(s32[2]{0:T(128)S(1)} %pad_add_fusion.pos_ref, bf16[4,256,1024]{2,1,0:T(8,128)(2,1)S(1)} %fusion.2.refs_0_, bf16[1024,1024]{1,0:T(8,128)(2,1)} %refs_7_.1, bf16[1024,1024]{1,0:T(8,128)(2,1)} %collective-permute-done.14.refs_2_.refs_8_, ...), custom_call_target="tpu_custom_call" | custom-call | flops 1 | bytes 1 | tf_op jit(solution)/shard_map/pallas_call | solution.py:296
  139.3 1.7 collective-permute-done.20.refs_6_.refs_1_.refs_16_
  141.0 1.5 collective-permute-start.30
  142.5 3.9 %collective-permute-done.28.refs_0_ = bf16[256,1024]{1,0:T(8,128)(2,1)S(1)} collective-permute-done((bf16[256,1024]{1,0:T(8,128)(2,1)}, bf16[256,1024]{1,0:T(8,128)(2,1)S(1)}, u32[]{:S(2)}, u32[]{:S(2)}) %collective-permute-start.28) | collective-permute-done | bytes 524320 | tf_op jit(solution)/shard_map/ppermute | solution.py:179
  146.9 1.6 copy-done.4
  148.5 5.4 %shard_map.115.q_ref.refs_2_ = bf16[256,1024]{1,0:T(8,128)(2,1)S(1)} custom-call(s32[2]{0:T(128)S(1)} %pad_add_fusion.pos_ref, bf16[4,256,1024]{2,1,0:T(8,128)(2,1)S(1)} %fusion.2.refs_0_, bf16[1024,1024]{1,0:T(8,128)(2,1)} %refs_3_.1, bf16[1024,1024]{1,0:T(8,128)(2,1)} %collective-permute-done.2.refs_2_.refs_4_, ...), custom_call_target="tpu_custom_call" | custom-call | flops 1 | bytes 1 | tf_op jit(solution)/shard_map/pallas_call | solution.py:296
  154.7 4.3 %collective-permute-done.30.refs_7_ = bf16[128,1024]{1,0:T(8,128)(2,1)} collective-permute-done((bf16[128,1024]{1,0:T(8,128)(2,1)S(1)}, bf16[128,1024]{1,0:T(8,128)(2,1)}, u32[]{:S(2)}, u32[]{:S(2)}) %collective-permute-start.30) | collective-permute-done | bytes 262176 | tf_op jit(solution)/shard_map/ppermute | solution.py:179
  161.2 5.4 %shard_map.121.v_ref = bf16[256,1024]{1,0:T(8,128)(2,1)S(1)} custom-call(s32[2]{0:T(128)S(1)} %pad_add_fusion.pos_ref, bf16[4,256,1024]{2,1,0:T(8,128)(2,1)S(1)} %fusion.2.refs_0_, bf16[1024,1024]{1,0:T(8,128)(2,1)} %refs_11_.1, bf16[1024,1024]{1,0:T(8,128)(2,1)} %collective-permute-done.16.refs_2_.refs_12_, bf16[256,1024]{1,0:T(8,128)(2,1)S(1)} %copy-done.11, ...), custom_call_target="tpu_custom_call" | custom-call | flops 1 | bytes 1 | tf_op jit(solution)/shard_map/pallas_call | solution.py:296
  166.7 3.8 %shard_map.122.refs_0_ = bf16[256,1024]{1,0:T(8,128)(2,1)S(1)} custom-call(bf16[256,1024]{1,0:T(8,128)(2,1)S(1)} %copy-done.19, bf16[256,1024]{1,0:T(8,128)(2,1)S(1)} %copy-done.16, bf16[256,1024]{1,0:T(8,128)(2,1)S(1)} %shard_map.121.v_ref), custom_call_target="tpu_custom_call" | custom-call | flops 1 | bytes 1 | tf_op jit(solution)/shard_map/pallas_call | solution.py:374
  170.5 5.0 %shard_map.126.refs_1_ = bf16[4,256,1024]{2,1,0:T(8,128)(2,1)S(1)} custom-call(s32[2]{0:T(128)S(1)} %pad_add_fusion.pos_ref, bf16[256,1024]{1,0:T(8,128)(2,1)S(1)} %shard_map.122.refs_0_, bf16[1024,1024]{1,0:T(8,128)(2,1)S(1)} %copy-done.1, bf16[1024,1024]{1,0:T(8,128)(2,1)} %collective-permute-done.25.refs_2_, bf16[256,1024]{1,0:T(8,128)(2,1)S(1)} %copy-done.22, ...), custom_call_target="tpu_custom_call" | custom-call | flops 1 | bytes 1 | tf_op jit(solution)/shard_map/pallas_call | solution.py:296
  175.6 1.3 copy-done.6
  178.6 1.6 copy-done.5
  183.3 5.4 %shard_map.128.dc_ref = bf16[256,1024]{1,0:T(8,128)(2,1)S(1)} custom-call(s32[2]{0:T(128)S(1)} %pad_add_fusion.pos_ref, bf16[4,256,1024]{2,1,0:T(8,128)(2,1)S(1)} %copy-done.5, bf16[1024,1024]{1,0:T(8,128)(2,1)S(1)} %copy-done.1, bf16[1024,1024]{1,0:T(8,128)(2,1)} %collective-permute-done.25.refs_2_, bf16[256,1024]{1,0:T(8,128)(2,1)S(1)} %copy-done.23, ...), custom_call_target="tpu_custom_call" | custom-call | flops 1 | bytes 1 | tf_op jit(solution)/shard_map/pallas_call | solution.py:296
  188.7 7.9 %shard_map.129 = (bf16[256,1024]{1,0:T(8,128)(2,1)S(1)}, bf16[256,1024]{1,0:T(8,128)(2,1)S(1)}, bf16[256,1024]{1,0:T(8,128)(2,1)S(1)}) custom-call(bf16[256,1024]{1,0:T(8,128)(2,1)S(1)} %copy-done.20, bf16[256,1024]{1,0:T(8,128)(2,1)S(1)} %copy-done.17, bf16[256,1024]{1,0:T(8,128)(2,1)S(1)} %copy-done.28, bf16[256,1024]{1,0:T(8,128)(2,1)S(1)} %shard_map.128.dc_ref), custom_call_target="tpu_custom_call" | custom-call | flops 1 | bytes 1 | tf_op jit(solution)/shard_map/pallas_call | solution.py:374
  196.6 11.5 %shard_map.130.refs_0_ = bf16[4,256,1024]{2,1,0:T(8,128)(2,1)S(1)} custom-call(s32[2]{0:T(128)S(1)} %pad_add_fusion.pos_ref, bf16[256,1024]{1,0:T(8,128)(2,1)S(1)} %get-tuple-element.6.refs_0_, bf16[256,1024]{1,0:T(8,128)(2,1)S(1)} %get-tuple-element.7.refs_1_, bf16[256,1024]{1,0:T(8,128)(2,1)S(1)} %get-tuple-element.8.refs_2_, bf16[1024,1024]{1,0:T(8,128)(2,1)} %refs_3_.1, ...), custom_call_target="tpu_custom_call" | custom-call | flops 1 | bytes 1 | tf_op jit(solution)/shard_map/pallas_call | solution.py:296
  208.1 1.4 copy-done.2
  209.5 13.4 %reduce-scatter.3.cloned.1.call-done = bf16[1,256,1024]{2,1,0:T(8,128)(2,1)} async-done(((bf16[4,256,1024]{2,1,0:T(8,128)(2,1)}), bf16[1,256,1024]{2,1,0:T(8,128)(2,1)}) %reduce-scatter.3.cloned.1.call-update) | async-done | bytes 524304 | tf_op jit(solution)/shard_map/reduce_scatter | solution.py:569
  225.0 1.5 collective-permute-start.37
  226.5 2.1 fusion.4
  228.7 3.7 %collective-permute-done.41 = f32[32,128]{1,0:T(8,128)S(1)} collective-permute-done((f32[32,128]{1,0:T(8,128)S(1)}, f32[32,128]{1,0:T(8,128)S(1)}, u32[]{:S(2)}, u32[]{:S(2)}) %collective-permute-start.41) | collective-permute-done | bytes 16416 | tf_op jit(solution)/shard_map/ppermute | solution.py:179
  232.4 1.7 collective-permute-start.42
  234.6 2.9 %collective-permute-done.42 = f32[32,128]{1,0:T(8,128)S(1)} collective-permute-done((f32[32,128]{1,0:T(8,128)S(1)}, f32[32,128]{1,0:T(8,128)S(1)}, u32[]{:S(2)}, u32[]{:S(2)}) %collective-permute-start.42) | collective-permute-done | bytes 16416 | tf_op jit(solution)/shard_map/ppermute | solution.py:179
  238.0 1.7 collective-permute-start.40
  242.7 2.1 collective-permute-done.44
  245.0 23.6 %reduce-scatter.5.cloned.1.call-done = bf16[1,256,1024]{2,1,0:T(8,128)(2,1)} async-done(((bf16[4,256,1024]{2,1,0:T(8,128)(2,1)}), bf16[1,256,1024]{2,1,0:T(8,128)(2,1)}) %reduce-scatter.5.cloned.1.call-update) | async-done | bytes 524304 | tf_op jit(solution)/shard_map/reduce_scatter | solution.py:577
  270.1 1.4 collective-permute-start.46
  271.6 6.6 %collective-permute-done.46 = bf16[128,1024]{1,0:T(8,128)(2,1)S(1)} collective-permute-done((bf16[128,1024]{1,0:T(8,128)(2,1)S(1)}, bf16[128,1024]{1,0:T(8,128)(2,1)S(1)}, u32[]{:S(2)}, u32[]{:S(2)}) %collective-permute-start.46) | collective-permute-done | bytes 262176 | tf_op jit(solution)/shard_map/ppermute | solution.py:179
  278.2 1.5 collective-permute-done.47
  279.8 1.1 pad_maximum_fusion.1
  (226 shorter events, 32.9 us)
Async XLA Ops:
  7.2 14.8 %copy-start.41 = (bf16[4,128,1024]{2,1,0:T(8,128)(2,1)S(1)}, bf16[4,128,1024]{2,1,0:T(8,128)(2,1)}, u32[]{:S(2)}) copy-start(bf16[4,128,1024]{2,1,0:T(8,128)(2,1)} %param.8) | copy-start | bytes 3145732
  7.2 116.8 %all-gather.5.cloned.1.call-start = ((), (), s32[]{:S(2)}) async-start(), calls=%async_computation.4 | async-start | bytes 2621440 | tf_op jit(solution)/shard_map/all_gather | solution.py:524
  8.4 13.6 %collective-permute-start = (bf16[2,128,1024]{2,1,0:T(8,128)(2,1)S(1)}, bf16[2,128,1024]{2,1,0:T(8,128)(2,1)S(1)}, u32[]{:S(2)}, u32[]{:S(2)}) collective-permute-start(bf16[2,128,1024]{2,1,0:T(8,128)(2,1)S(1)} %slice.64), channel_id=1, source_target_pairs={{0,4},{4,0},{8,12},{12,8},{1,5},{5,1},{9,13},{13,9},{2,6},{6,2},{1... | collective-permute-start | bytes 1572872 | tf_op jit(solution)/shard_map/ppermute | solution.py:179
  22.1 7.9 %collective-permute-start.1 = (bf16[128,1024]{1,0:T(8,128)(2,1)S(1)}, bf16[128,1024]{1,0:T(8,128)(2,1)S(1)}, u32[]{:S(2)}, u32[]{:S(2)}) collective-permute-start(bf16[128,1024]{1,0:T(8,128)(2,1)S(1)} %fusion.9.refs_0_), channel_id=1, source_target_pairs={{0,8},{4,12},{8,0},{12,4},{1,9},{5,13},{9,1},{13,5},{2,10},{6,14},... | collective-permute-start | bytes 786440 | tf_op jit(solution)/shard_map/ppermute | solution.py:179
  30.9 116.0 %all-gather.7.cloned.1.call-start = ((), (), s32[]{:S(2)}) async-start(), calls=%async_computation.5 | async-start | bytes 2621440 | tf_op jit(solution)/shard_map/all_gather | solution.py:525
  31.0 15.1 %collective-permute-start.3 = (bf16[256,1024]{1,0:T(8,128)(2,1)}, bf16[256,1024]{1,0:T(8,128)(2,1)S(1)}, u32[]{:S(2)}, u32[]{:S(2)}) collective-permute-start(bf16[256,1024]{1,0:T(8,128)(2,1)} %shard_map.103.refs_1_), channel_id=1, source_target_pairs={{0,8},{4,12},{8,0},{12,4},{1,9},{5,13},{9,1},{13,5},{2,10},{6,14},... | collective-permute-start | bytes 1572872 | tf_op jit(solution)/shard_map/ppermute | solution.py:179
  32.5 18.4 %collective-permute-start.7 = (bf16[2,128,1024]{2,1,0:T(8,128)(2,1)}, bf16[2,128,1024]{2,1,0:T(8,128)(2,1)S(1)}, u32[]{:S(2)}, u32[]{:S(2)}) collective-permute-start(bf16[2,128,1024]{2,1,0:T(8,128)(2,1)} %slice.69), channel_id=1, source_target_pairs={{0,4},{4,0},{8,12},{12,8},{1,5},{5,1},{9,13},{13,9},{2,6},{6,2},{1... | collective-permute-start | bytes 1572872 | tf_op jit(solution)/shard_map/ppermute | solution.py:179
  32.5 73.3 %collective-permute-start.2 = (bf16[1024,1024]{1,0:T(8,128)(2,1)}, bf16[1024,1024]{1,0:T(8,128)(2,1)}, u32[]{:S(2)}, u32[]{:S(2)}) collective-permute-start(bf16[1024,1024]{1,0:T(8,128)(2,1)} %refs_3_.1), channel_id=1, source_target_pairs={{0,4},{4,0},{8,12},{12,8},{1,5},{5,1},{9,13},{13,9},{2,6},{6,2},{1... | collective-permute-start | bytes 6291464 | tf_op jit(solution)/shard_map/ppermute | solution.py:179
  33.0 24.4 %collective-permute-start.6 = (bf16[256,1024]{1,0:T(8,128)(2,1)}, bf16[256,1024]{1,0:T(8,128)(2,1)S(1)}, u32[]{:S(2)}, u32[]{:S(2)}) collective-permute-start(bf16[256,1024]{1,0:T(8,128)(2,1)} %shard_map.105.refs_1_), channel_id=1, source_target_pairs={{0,8},{4,12},{8,0},{12,4},{1,9},{5,13},{9,1},{13,5},{2,10},{6,14},... | collective-permute-start | bytes 1572872 | tf_op jit(solution)/shard_map/ppermute | solution.py:179
  48.8 19.8 %collective-permute-start.4 = (bf16[256,1024]{1,0:T(8,128)(2,1)}, bf16[256,1024]{1,0:T(8,128)(2,1)S(1)}, u32[]{:S(2)}, u32[]{:S(2)}) collective-permute-start(bf16[256,1024]{1,0:T(8,128)(2,1)} %shard_map.107.refs_1_), channel_id=1, source_target_pairs={{0,8},{4,12},{8,0},{12,4},{1,9},{5,13},{9,1},{13,5},{2,10},{6,14},... | collective-permute-start | bytes 1572872 | tf_op jit(solution)/shard_map/ppermute | solution.py:179
  49.4 11.2 %collective-permute-start.5 = (bf16[256,1024]{1,0:T(8,128)(2,1)}, bf16[256,1024]{1,0:T(8,128)(2,1)S(1)}, u32[]{:S(2)}, u32[]{:S(2)}) collective-permute-start(bf16[256,1024]{1,0:T(8,128)(2,1)} %shard_map.108), channel_id=1, source_target_pairs={{0,16},{16,0},{1,17},{17,1},{2,18},{18,2},{3,19},{19,3},{4,20},{20... | collective-permute-start | bytes 1572872 | tf_op jit(solution)/shard_map/ppermute | solution.py:179
  51.0 23.3 %collective-permute-start.10 = (bf16[128,1024]{1,0:T(8,128)(2,1)S(1)}, bf16[128,1024]{1,0:T(8,128)(2,1)}, u32[]{:S(2)}, u32[]{:S(2)}) collective-permute-start(bf16[128,1024]{1,0:T(8,128)(2,1)S(1)} %fusion.8.refs_1_), channel_id=1, source_target_pairs={{0,8},{4,12},{8,0},{12,4},{1,9},{5,13},{9,1},{13,5},{2,10},{6,14},... | collective-permute-start | bytes 786440 | tf_op jit(solution)/shard_map/ppermute | solution.py:179
  60.1 25.4 %collective-permute-start.8 = (bf16[256,1024]{1,0:T(8,128)(2,1)}, bf16[256,1024]{1,0:T(8,128)(2,1)S(1)}, u32[]{:S(2)}, u32[]{:S(2)}) collective-permute-start(bf16[256,1024]{1,0:T(8,128)(2,1)} %shard_map.111.refs_1_), channel_id=1, source_target_pairs={{0,8},{4,12},{8,0},{12,4},{1,9},{5,13},{9,1},{13,5},{2,10},{6,14},... | collective-permute-start | bytes 1572872 | tf_op jit(solution)/shard_map/ppermute | solution.py:179
  60.6 17.2 %collective-permute-start.9 = (bf16[256,1024]{1,0:T(8,128)(2,1)}, bf16[256,1024]{1,0:T(8,128)(2,1)S(1)}, u32[]{:S(2)}, u32[]{:S(2)}) collective-permute-start(bf16[256,1024]{1,0:T(8,128)(2,1)} %shard_map.112), channel_id=1, source_target_pairs={{0,16},{16,0},{1,17},{17,1},{2,18},{18,2},{3,19},{19,3},{4,20},{20... | collective-permute-start | bytes 1572872 | tf_op jit(solution)/shard_map/ppermute | solution.py:179
  71.3 25.4 %collective-permute-start.17 = (bf16[256,1024]{1,0:T(8,128)(2,1)}, bf16[256,1024]{1,0:T(8,128)(2,1)S(1)}, u32[]{:S(2)}, u32[]{:S(2)}) collective-permute-start(bf16[256,1024]{1,0:T(8,128)(2,1)} %shard_map.109.refs_1_), channel_id=1, source_target_pairs={{0,8},{4,12},{8,0},{12,4},{1,9},{5,13},{9,1},{13,5},{2,10},{6,14},... | collective-permute-start | bytes 1572872 | tf_op jit(solution)/shard_map/ppermute | solution.py:179
  74.3 15.9 %collective-permute-start.11 = (bf16[256,1024]{1,0:T(8,128)(2,1)}, bf16[256,1024]{1,0:T(8,128)(2,1)S(1)}, u32[]{:S(2)}, u32[]{:S(2)}) collective-permute-start(bf16[256,1024]{1,0:T(8,128)(2,1)} %shard_map.110), channel_id=1, source_target_pairs={{0,16},{16,0},{1,17},{17,1},{2,18},{18,2},{3,19},{19,3},{4,20},{20... | collective-permute-start | bytes 1572872 | tf_op jit(solution)/shard_map/ppermute | solution.py:179
  88.1 16.8 %collective-permute-start.12 = (bf16[256,1024]{1,0:T(8,128)(2,1)}, bf16[256,1024]{1,0:T(8,128)(2,1)}, u32[]{:S(2)}, u32[]{:S(2)}) collective-permute-start(bf16[256,1024]{1,0:T(8,128)(2,1)} %shard_map.114), channel_id=1, source_target_pairs={{0,16},{16,0},{1,17},{17,1},{2,18},{18,2},{3,19},{19,3},{4,20},{20... | collective-permute-start | bytes 1572872 | tf_op jit(solution)/shard_map/ppermute | solution.py:179
  89.7 16.1 %collective-permute-start.18 = (bf16[256,1024]{1,0:T(8,128)(2,1)}, bf16[256,1024]{1,0:T(8,128)(2,1)}, u32[]{:S(2)}, u32[]{:S(2)}) collective-permute-start(bf16[256,1024]{1,0:T(8,128)(2,1)} %shard_map.113.refs_1_), channel_id=1, source_target_pairs={{0,8},{4,12},{8,0},{12,4},{1,9},{5,13},{9,1},{13,5},{2,10},{6,14},... | collective-permute-start | bytes 1572872 | tf_op jit(solution)/shard_map/ppermute | solution.py:179
  99.4 9.6 %collective-permute-start.19 = (bf16[256,1024]{1,0:T(8,128)(2,1)}, bf16[256,1024]{1,0:T(8,128)(2,1)S(1)}, u32[]{:S(2)}, u32[]{:S(2)}) collective-permute-start(bf16[256,1024]{1,0:T(8,128)(2,1)} %shard_map.118.refs_3_.refs_13_), channel_id=1, source_target_pairs={{0,16},{16,0},{1,17},{17,1},{2,18},{18,2},{3,19},{19,3},{4,20},{20... | collective-permute-start | bytes 1572872 | tf_op jit(solution)/shard_map/ppermute | solution.py:179
  101.0 25.2 %collective-permute-start.14 = (bf16[1024,1024]{1,0:T(8,128)(2,1)}, bf16[1024,1024]{1,0:T(8,128)(2,1)}, u32[]{:S(2)}, u32[]{:S(2)}) collective-permute-start(bf16[1024,1024]{1,0:T(8,128)(2,1)} %refs_7_.1), channel_id=1, source_target_pairs={{0,4},{4,0},{8,12},{12,8},{1,5},{5,1},{9,13},{13,9},{2,6},{6,2},{1... | collective-permute-start | bytes 6291464 | tf_op jit(solution)/shard_map/ppermute | solution.py:179
  101.0 121.9 %reduce-scatter.3.cloned.1.call-start = ((), (), s32[]{:S(2)}) async-start(), calls=%async_computation.2 | async-start | bytes 2621440 | tf_op jit(solution)/shard_map/reduce_scatter | solution.py:569
  101.2 8.2 %copy-start.36 = (bf16[256,1024]{1,0:T(8,128)(2,1)S(1)}, bf16[256,1024]{1,0:T(8,128)(2,1)}, u32[]{:S(2)}) copy-start(bf16[256,1024]{1,0:T(8,128)(2,1)} %shard_map.114) | copy-start | bytes 1572868
  101.2 8.2 %copy-start.38 = (bf16[256,1024]{1,0:T(8,128)(2,1)S(1)}, bf16[256,1024]{1,0:T(8,128)(2,1)}, u32[]{:S(2)}) copy-start(bf16[256,1024]{1,0:T(8,128)(2,1)} %shard_map.110) | copy-start | bytes 1572868
  101.3 8.2 %copy-start.47 = (bf16[256,1024]{1,0:T(8,128)(2,1)S(1)}, bf16[256,1024]{1,0:T(8,128)(2,1)}, u32[]{:S(2)}) copy-start(bf16[256,1024]{1,0:T(8,128)(2,1)} %copy-done.46) | copy-start | bytes 1572868
  104.9 15.3 %copy-start.53 = (f32[4096]{0:T(1024)S(1)}, f32[4096]{0:T(1024)}, u32[]{:S(2)}) copy-start(f32[4096]{0:T(1024)} %param.11) | copy-start | bytes 49156
  104.9 21.7 %collective-permute-start.16 = (bf16[1024,1024]{1,0:T(8,128)(2,1)}, bf16[1024,1024]{1,0:T(8,128)(2,1)}, u32[]{:S(2)}, u32[]{:S(2)}) collective-permute-start(bf16[1024,1024]{1,0:T(8,128)(2,1)} %refs_11_.1), channel_id=1, source_target_pairs={{0,4},{4,0},{8,12},{12,8},{1,5},{5,1},{9,13},{13,9},{2,6},{6,2},{1... | collective-permute-start | bytes 6291464 | tf_op jit(solution)/shard_map/ppermute | solution.py:179
  105.7 21.2 %collective-permute-start.25 = (bf16[1024,1024]{1,0:T(8,128)(2,1)S(1)}, bf16[1024,1024]{1,0:T(8,128)(2,1)}, u32[]{:S(2)}, u32[]{:S(2)}) collective-permute-start(bf16[1024,1024]{1,0:T(8,128)(2,1)S(1)} %copy-done), channel_id=1, source_target_pairs={{0,4},{4,0},{8,12},{12,8},{1,5},{5,1},{9,13},{13,9},{2,6},{6,2},{1... | collective-permute-start | bytes 6291464 | tf_op jit(solution)/shard_map/ppermute | solution.py:179
  105.7 22.7 %collective-permute-start.15 = (bf16[1024,1024]{1,0:T(8,128)(2,1)}, bf16[1024,1024]{1,0:T(8,128)(2,1)}, u32[]{:S(2)}, u32[]{:S(2)}) collective-permute-start(bf16[1024,1024]{1,0:T(8,128)(2,1)} %maximum_select_fusion.1.refs_3_.refs_9_), channel_id=1, source_target_pairs={{0,4},{4,0},{8,12},{12,8},{1,5},{5,1},{9,13},{13,9},{2,6},{6,2},{1... | collective-permute-start | bytes 6291464 | tf_op jit(solution)/shard_map/ppermute | solution.py:179
  109.1 11.1 %collective-permute-start.26 = (bf16[256,1024]{1,0:T(8,128)(2,1)S(1)}, bf16[256,1024]{1,0:T(8,128)(2,1)S(1)}, u32[]{:S(2)}, u32[]{:S(2)}) collective-permute-start(bf16[256,1024]{1,0:T(8,128)(2,1)S(1)} %copy-done.49), channel_id=1, source_target_pairs={{0,8},{4,12},{8,0},{12,4},{1,9},{5,13},{9,1},{13,5},{2,10},{6,14},... | collective-permute-start | bytes 1572872 | tf_op jit(solution)/shard_map/ppermute | solution.py:179
  120.2 26.2 %collective-permute-start.13 = (bf16[1024,1024]{1,0:T(8,128)(2,1)}, bf16[1024,1024]{1,0:T(8,128)(2,1)}, u32[]{:S(2)}, u32[]{:S(2)}) collective-permute-start(bf16[1024,1024]{1,0:T(8,128)(2,1)} %maximum_select_fusion.refs_3_.refs_5_), channel_id=1, source_target_pairs={{0,4},{4,0},{8,12},{12,8},{1,5},{5,1},{9,13},{13,9},{2,6},{6,2},{1... | collective-permute-start | bytes 6291464 | tf_op jit(solution)/shard_map/ppermute | solution.py:179
  126.1 12.6 %collective-permute-start.21 = (bf16[256,1024]{1,0:T(8,128)(2,1)S(1)}, bf16[256,1024]{1,0:T(8,128)(2,1)}, u32[]{:S(2)}, u32[]{:S(2)}) collective-permute-start(bf16[256,1024]{1,0:T(8,128)(2,1)S(1)} %copy-done.11), channel_id=1, source_target_pairs={{0,4},{4,0},{8,12},{12,8},{1,5},{5,1},{9,13},{13,9},{2,6},{6,2},{1... | collective-permute-start | bytes 1572872 | tf_op jit(solution)/shard_map/ppermute | solution.py:179
  126.6 12.2 %collective-permute-start.27 = (bf16[128,1024]{1,0:T(8,128)(2,1)}, bf16[128,1024]{1,0:T(8,128)(2,1)S(1)}, u32[]{:S(2)}, u32[]{:S(2)}) collective-permute-start(bf16[128,1024]{1,0:T(8,128)(2,1)} %shard_map.119.refs_1_), channel_id=1, source_target_pairs={{0,8},{4,12},{8,0},{12,4},{1,9},{5,13},{9,1},{13,5},{2,10},{6,14},... | collective-permute-start | bytes 786440 | tf_op jit(solution)/shard_map/ppermute | solution.py:179
  127.0 14.0 %collective-permute-start.20 = (bf16[256,1024]{1,0:T(8,128)(2,1)}, bf16[256,1024]{1,0:T(8,128)(2,1)}, u32[]{:S(2)}, u32[]{:S(2)}) collective-permute-start(bf16[256,1024]{1,0:T(8,128)(2,1)} %shard_map.120.refs_4_.refs_14_), channel_id=1, source_target_pairs={{0,16},{16,0},{1,17},{17,1},{2,18},{18,2},{3,19},{19,3},{4,20},{20... | collective-permute-start | bytes 1572872 | tf_op jit(solution)/shard_map/ppermute | solution.py:179
  128.4 18.0 %collective-permute-start.28 = (bf16[256,1024]{1,0:T(8,128)(2,1)}, bf16[256,1024]{1,0:T(8,128)(2,1)S(1)}, u32[]{:S(2)}, u32[]{:S(2)}) collective-permute-start(bf16[256,1024]{1,0:T(8,128)(2,1)} %shard_map.123.refs_1_), channel_id=1, source_target_pairs={{0,8},{4,12},{8,0},{12,4},{1,9},{5,13},{9,1},{13,5},{2,10},{6,14},... | collective-permute-start | bytes 1572872 | tf_op jit(solution)/shard_map/ppermute | solution.py:179
  138.8 20.3 %collective-permute-start.22 = (bf16[256,1024]{1,0:T(8,128)(2,1)}, bf16[256,1024]{1,0:T(8,128)(2,1)}, u32[]{:S(2)}, u32[]{:S(2)}) collective-permute-start(bf16[256,1024]{1,0:T(8,128)(2,1)} %shard_map.120.refs_4_.refs_14_), channel_id=1, source_target_pairs={{0,4},{4,0},{8,12},{12,8},{1,5},{5,1},{9,13},{13,9},{2,6},{6,2},{1... | collective-permute-start | bytes 1572872 | tf_op jit(solution)/shard_map/ppermute | solution.py:179
  138.8 20.8 %collective-permute-start.29 = (bf16[256,1024]{1,0:T(8,128)(2,1)}, bf16[256,1024]{1,0:T(8,128)(2,1)}, u32[]{:S(2)}, u32[]{:S(2)}) collective-permute-start(bf16[256,1024]{1,0:T(8,128)(2,1)} %shard_map.124.refs_3_), channel_id=1, source_target_pairs={{0,16},{16,0},{1,17},{17,1},{2,18},{18,2},{3,19},{19,3},{4,20},{20... | collective-permute-start | bytes 1572872 | tf_op jit(solution)/shard_map/ppermute | solution.py:179
  141.0 18.1 %collective-permute-start.30 = (bf16[128,1024]{1,0:T(8,128)(2,1)S(1)}, bf16[128,1024]{1,0:T(8,128)(2,1)}, u32[]{:S(2)}, u32[]{:S(2)}) collective-permute-start(bf16[128,1024]{1,0:T(8,128)(2,1)S(1)} %collective-permute-done.27.refs_4_), channel_id=1, source_target_pairs={{0,16},{16,0},{1,17},{17,1},{2,18},{18,2},{3,19},{19,3},{4,20},{20... | collective-permute-start | bytes 786440 | tf_op jit(solution)/shard_map/ppermute | solution.py:179
  146.4 13.2 %collective-permute-start.23 = (bf16[256,1024]{1,0:T(8,128)(2,1)}, bf16[256,1024]{1,0:T(8,128)(2,1)}, u32[]{:S(2)}, u32[]{:S(2)}) collective-permute-start(bf16[256,1024]{1,0:T(8,128)(2,1)} %copy-done.24), channel_id=1, source_target_pairs={{0,4},{4,0},{8,12},{12,8},{1,5},{5,1},{9,13},{13,9},{2,6},{6,2},{1... | collective-permute-start | bytes 1572872 | tf_op jit(solution)/shard_map/ppermute | solution.py:179
  146.4 13.7 %collective-permute-start.24 = (bf16[256,1024]{1,0:T(8,128)(2,1)}, bf16[256,1024]{1,0:T(8,128)(2,1)}, u32[]{:S(2)}, u32[]{:S(2)}) collective-permute-start(bf16[256,1024]{1,0:T(8,128)(2,1)} %collective-permute-done.20.refs_6_.refs_1_.refs_16_), channel_id=1, source_target_pairs={{0,4},{4,0},{8,12},{12,8},{1,5},{5,1},{9,13},{13,9},{2,6},{6,2},{1... | collective-permute-start | bytes 1572872 | tf_op jit(solution)/shard_map/ppermute | solution.py:179
  154.7 11.9 %copy-start.16 = (bf16[256,1024]{1,0:T(8,128)(2,1)S(1)}, bf16[256,1024]{1,0:T(8,128)(2,1)}, u32[]{:S(2)}) copy-start(bf16[256,1024]{1,0:T(8,128)(2,1)} %copy-done.15) | copy-start | bytes 1572868
  154.7 11.9 %copy-start.19 = (bf16[256,1024]{1,0:T(8,128)(2,1)S(1)}, bf16[256,1024]{1,0:T(8,128)(2,1)}, u32[]{:S(2)}) copy-start(bf16[256,1024]{1,0:T(8,128)(2,1)} %copy-done.18) | copy-start | bytes 1572868
  159.0 11.4 %collective-permute-start.31 = (bf16[256,1024]{1,0:T(8,128)(2,1)}, bf16[256,1024]{1,0:T(8,128)(2,1)S(1)}, u32[]{:S(2)}, u32[]{:S(2)}) collective-permute-start(bf16[256,1024]{1,0:T(8,128)(2,1)} %shard_map.124.refs_3_), channel_id=1, source_target_pairs={{0,4},{4,0},{8,12},{12,8},{1,5},{5,1},{9,13},{13,9},{2,6},{6,2},{1... | collective-permute-start | bytes 1572872 | tf_op jit(solution)/shard_map/ppermute | solution.py:179
  159.0 11.4 %collective-permute-start.33 = (bf16[256,1024]{1,0:T(8,128)(2,1)}, bf16[256,1024]{1,0:T(8,128)(2,1)S(1)}, u32[]{:S(2)}, u32[]{:S(2)}) collective-permute-start(bf16[256,1024]{1,0:T(8,128)(2,1)} %shard_map.125.refs_5_.refs_8_), channel_id=1, source_target_pairs={{0,4},{4,0},{8,12},{12,8},{1,5},{5,1},{9,13},{13,9},{2,6},{6,2},{1... | collective-permute-start | bytes 1572872 | tf_op jit(solution)/shard_map/ppermute | solution.py:179
  159.6 11.0 %collective-permute-start.34 = (bf16[256,1024]{1,0:T(8,128)(2,1)}, bf16[256,1024]{1,0:T(8,128)(2,1)}, u32[]{:S(2)}, u32[]{:S(2)}) collective-permute-start(bf16[256,1024]{1,0:T(8,128)(2,1)} %collective-permute-done.29.refs_6_), channel_id=1, source_target_pairs={{0,4},{4,0},{8,12},{12,8},{1,5},{5,1},{9,13},{13,9},{2,6},{6,2},{1... | collective-permute-start | bytes 1572872 | tf_op jit(solution)/shard_map/ppermute | solution.py:179
  159.6 10.8 %collective-permute-start.32 = (bf16[128,1024]{1,0:T(8,128)(2,1)S(1)}, bf16[128,1024]{1,0:T(8,128)(2,1)}, u32[]{:S(2)}, u32[]{:S(2)}) collective-permute-start(bf16[128,1024]{1,0:T(8,128)(2,1)S(1)} %collective-permute-done.27.refs_4_), channel_id=1, source_target_pairs={{0,4},{4,0},{8,12},{12,8},{1,5},{5,1},{9,13},{13,9},{2,6},{6,2},{1... | collective-permute-start | bytes 786440 | tf_op jit(solution)/shard_map/ppermute | solution.py:179
  160.1 10.4 %collective-permute-start.35 = (bf16[128,1024]{1,0:T(8,128)(2,1)}, bf16[128,1024]{1,0:T(8,128)(2,1)}, u32[]{:S(2)}, u32[]{:S(2)}) collective-permute-start(bf16[128,1024]{1,0:T(8,128)(2,1)} %collective-permute-done.30.refs_7_), channel_id=1, source_target_pairs={{0,4},{4,0},{8,12},{12,8},{1,5},{5,1},{9,13},{13,9},{2,6},{6,2},{1... | collective-permute-start | bytes 786440 | tf_op jit(solution)/shard_map/ppermute | solution.py:179
  161.2 9.3 %copy-start.8 = (bf16[256,1024]{1,0:T(8,128)(2,1)S(1)}, bf16[256,1024]{1,0:T(8,128)(2,1)}, u32[]{:S(2)}) copy-start(bf16[256,1024]{1,0:T(8,128)(2,1)} %shard_map.125.refs_5_.refs_8_) | copy-start | bytes 1572868
  161.2 9.3 %copy-start.22 = (bf16[256,1024]{1,0:T(8,128)(2,1)S(1)}, bf16[256,1024]{1,0:T(8,128)(2,1)}, u32[]{:S(2)}) copy-start(bf16[256,1024]{1,0:T(8,128)(2,1)} %shard_map.124.refs_3_) | copy-start | bytes 1572868
  178.5 90.1 %reduce-scatter.5.cloned.1.call-start = ((), (), s32[]{:S(2)}) async-start(), calls=%async_computation.3 | async-start | bytes 2621440 | tf_op jit(solution)/shard_map/reduce_scatter | solution.py:577
  225.0 12.5 %collective-permute-start.37 = (bf16[128,1024]{1,0:T(8,128)(2,1)}, bf16[128,1024]{1,0:T(8,128)(2,1)S(1)}, u32[]{:S(2)}, u32[]{:S(2)}) collective-permute-start(bf16[128,1024]{1,0:T(8,128)(2,1)} %get-tuple-element.25), channel_id=1, source_target_pairs={{0,8},{4,12},{8,0},{12,4},{1,9},{5,13},{9,1},{13,5},{2,10},{6,14},... | collective-permute-start | bytes 786440 | tf_op jit(solution)/shard_map/ppermute | solution.py:179
  228.6 40.1 %copy-start.14 = (bf16[256,1024]{1,0:T(8,128)(2,1)S(1)}, bf16[256,1024]{1,0:T(8,128)(2,1)}, u32[]{:S(2)}) copy-start(bf16[256,1024]{1,0:T(8,128)(2,1)} %pad_maximum_fusion.3.refs_2_.g_ref) | copy-start | bytes 1572868
  228.6 3.8 %collective-permute-start.41 = (f32[32,128]{1,0:T(8,128)S(1)}, f32[32,128]{1,0:T(8,128)S(1)}, u32[]{:S(2)}, u32[]{:S(2)}) collective-permute-start(f32[32,128]{1,0:T(8,128)S(1)} %reshape.101), channel_id=1, source_target_pairs={{0,1},{1,0},{2,3},{3,2},{4,5},{5,4},{6,7},{7,6},{8,9},{9,8},{10,11... | collective-permute-start | bytes 49160 | tf_op jit(solution)/shard_map/ppermute | solution.py:179
  232.4 5.1 %collective-permute-start.42 = (f32[32,128]{1,0:T(8,128)S(1)}, f32[32,128]{1,0:T(8,128)S(1)}, u32[]{:S(2)}, u32[]{:S(2)}) collective-permute-start(f32[32,128]{1,0:T(8,128)S(1)} %add.66), channel_id=1, source_target_pairs={{0,2},{1,3},{2,0},{3,1},{4,6},{5,7},{6,4},{7,5},{8,10},{9,11},{10,... | collective-permute-start | bytes 49160 | tf_op jit(solution)/shard_map/ppermute | solution.py:179
  234.1 10.7 %collective-permute-start.36 = (bf16[128,1024]{1,0:T(8,128)(2,1)}, bf16[128,1024]{1,0:T(8,128)(2,1)S(1)}, u32[]{:S(2)}, u32[]{:S(2)}) collective-permute-start(bf16[128,1024]{1,0:T(8,128)(2,1)} %get-tuple-element.25), channel_id=1, source_target_pairs={{0,4},{4,0},{8,12},{12,8},{1,5},{5,1},{9,13},{13,9},{2,6},{6,2},{1... | collective-permute-start | bytes 786440 | tf_op jit(solution)/shard_map/ppermute | solution.py:179
  234.1 3.9 %collective-permute-start.39 = (f32[2,128]{1,0:T(2,128)S(1)}, f32[2,128]{1,0:T(2,128)S(1)}, u32[]{:S(2)}, u32[]{:S(2)}) collective-permute-start(f32[2,128]{1,0:T(2,128)S(1)} %bitcast.73), channel_id=1, source_target_pairs={{0,1},{1,0},{2,3},{3,2},{4,5},{5,4},{6,7},{7,6},{8,9},{9,8},{10,11... | collective-permute-start | bytes 3080 | tf_op jit(solution)/shard_map/ppermute | solution.py:179
  237.5 3.6 %collective-permute-start.43 = (f32[8,128]{1,0:T(8,128)S(1)}, f32[8,128]{1,0:T(8,128)S(1)}, u32[]{:S(2)}, u32[]{:S(2)}) collective-permute-start(f32[8,128]{1,0:T(8,128)S(1)} %dynamic-slice_add_fusion), channel_id=1, source_target_pairs={{0,4},{4,0},{8,12},{12,8},{1,5},{5,1},{9,13},{13,9},{2,6},{6,2},{1... | collective-permute-start | bytes 12296 | tf_op jit(solution)/shard_map/ppermute | solution.py:179
  237.5 7.3 %collective-permute-start.38 = (bf16[128,1024]{1,0:T(8,128)(2,1)S(1)}, bf16[128,1024]{1,0:T(8,128)(2,1)S(1)}, u32[]{:S(2)}, u32[]{:S(2)}) collective-permute-start(bf16[128,1024]{1,0:T(8,128)(2,1)S(1)} %collective-permute-done.37), channel_id=1, source_target_pairs={{0,4},{4,0},{8,12},{12,8},{1,5},{5,1},{9,13},{13,9},{2,6},{6,2},{1... | collective-permute-start | bytes 786440 | tf_op jit(solution)/shard_map/ppermute | solution.py:179
  238.0 4.5 %collective-permute-start.40 = (f32[2,128]{1,0:T(2,128)S(1)}, f32[2,128]{1,0:T(2,128)S(1)}, u32[]{:S(2)}, u32[]{:S(2)}) collective-permute-start(f32[2,128]{1,0:T(2,128)S(1)} %bitcast_add_fusion), channel_id=1, source_target_pairs={{0,2},{1,3},{2,0},{3,1},{4,6},{5,7},{6,4},{7,5},{8,10},{9,11},{10,... | collective-permute-start | bytes 3080 | tf_op jit(solution)/shard_map/ppermute | solution.py:179
  241.1 3.7 %collective-permute-start.44 = (f32[8,128]{1,0:T(8,128)S(1)}, f32[8,128]{1,0:T(8,128)S(1)}, u32[]{:S(2)}, u32[]{:S(2)}) collective-permute-start(f32[8,128]{1,0:T(8,128)S(1)} %add.69), channel_id=1, source_target_pairs={{0,8},{4,12},{8,0},{12,4},{1,9},{5,13},{9,1},{13,5},{2,10},{6,14},... | collective-permute-start | bytes 12296 | tf_op jit(solution)/shard_map/ppermute | solution.py:179
  244.8 25.3 %copy-start.33 = (f32[8,128]{1,0:T(8,128)}, f32[8,128]{1,0:T(8,128)S(1)}, u32[]{:S(2)}) copy-start(f32[8,128]{1,0:T(8,128)S(1)} %add.70.refs_1_) | copy-start | bytes 12292
  245.0 25.1 %copy-start.29 = (bf16[4,128,1024]{2,1,0:T(8,128)(2,1)}, bf16[4,128,1024]{2,1,0:T(8,128)(2,1)S(1)}, u32[]{:S(2)}) copy-start(bf16[4,128,1024]{2,1,0:T(8,128)(2,1)S(1)} %pad_maximum_fusion.refs_0_) | copy-start | bytes 3145732
  270.1 8.0 %collective-permute-start.46 = (bf16[128,1024]{1,0:T(8,128)(2,1)S(1)}, bf16[128,1024]{1,0:T(8,128)(2,1)S(1)}, u32[]{:S(2)}, u32[]{:S(2)}) collective-permute-start(bf16[128,1024]{1,0:T(8,128)(2,1)S(1)} %get-tuple-element.22), channel_id=1, source_target_pairs={{0,8},{4,12},{8,0},{12,4},{1,9},{5,13},{9,1},{13,5},{2,10},{6,14},... | collective-permute-start | bytes 786440 | tf_op jit(solution)/shard_map/ppermute | solution.py:179
  271.6 6.6 %collective-permute-start.45 = (bf16[128,1024]{1,0:T(8,128)(2,1)S(1)}, bf16[128,1024]{1,0:T(8,128)(2,1)S(1)}, u32[]{:S(2)}, u32[]{:S(2)}) collective-permute-start(bf16[128,1024]{1,0:T(8,128)(2,1)S(1)} %get-tuple-element.22), channel_id=1, source_target_pairs={{0,4},{4,0},{8,12},{12,8},{1,5},{5,1},{9,13},{13,9},{2,6},{6,2},{1... | collective-permute-start | bytes 786440 | tf_op jit(solution)/shard_map/ppermute | solution.py:179
  278.2 1.5 collective-permute-start.47
  (43 other events, 129.9 us)
Sparse Core Ops, SparseCore 0:
  31.1 46.2 all-gather.4
  101.1 45.4 all-gather.6
  178.7 44.1 reduce-scatter.2
  225.1 43.4 reduce-scatter.4
